TPU v7x, 32 devices: a whole 2x2x4 slice. The times are simulated.
32 devices in a mesh: dp: 4 (over x, core), fsdp: 8 (over z, y).
Axes of the slice: x: 2, y: 2, z: 4, core: 2. Of those that a mesh axis runs over, the one named last changes fastest.
Arguments:
- tokens: bfloat16 [192, 296, 512], P(('dp', 'fsdp')), as said below
- cotangent: bfloat16 [192, 296, 512], P(('dp', 'fsdp')), may hold values from -6 to 6
- lengths: int32 [192], P(('dp', 'fsdp')), may hold values from 37 to 296, as said below
- valid_mask: int32 [192, 296], P(('dp', 'fsdp')), may hold values 0 or 1
- action_bins: int32 [192, 296, 11], P(('dp', 'fsdp')), may hold values from 0 to 255
- value_head: bfloat16 [2816, 512], replicated, may hold values from -0.25 to 0.25
- w_triple: float32 [512, 1536], P('fsdp')
- w_mixer: float32 [512, 512], P('fsdp')
- w_expand: float32 [512, 2048], P('fsdp')
- w_reduce: float32 [2048, 512], P('fsdp')
- norm_params: float32 [512, 4], replicated, as said below
- first_triple: float32 [512, 1536], P('fsdp')
- first_mixer: float32 [512, 512], P('fsdp')
- first_expand: float32 [512, 2048], P('fsdp')
- first_reduce: float32 [2048, 512], P('fsdp')
- first_norms: float32 [512, 4], replicated
- second_triple: float32 [512, 1536], P('fsdp'), as said below
- second_mixer: float32 [512, 512], P('fsdp'), as said below
- second_expand: float32 [512, 2048], P('fsdp'), as said below
- second_reduce: float32 [2048, 512], P('fsdp'), as said below
- second_norms: float32 [512, 4], replicated, as said below
Outputs:
- block_out: bfloat16 [192, 296, 512], P(('dp', 'fsdp'))
- input_grad: bfloat16 [192, 296, 512], P(('dp', 'fsdp'))
- new_triple: float32 [512, 1536], P('fsdp')
- new_mixer: float32 [512, 512], P('fsdp')
- new_expand: float32 [512, 2048], P('fsdp')
- new_reduce: float32 [2048, 512], P('fsdp')
- momentum_triple: float32 [512, 1536], P('fsdp')
- momentum_mixer: float32 [512, 512], P('fsdp')
- momentum_expand: float32 [512, 2048], P('fsdp')
- momentum_reduce: float32 [2048, 512], P('fsdp')
- variance_triple: float32 [512, 1536], P('fsdp')
- variance_mixer: float32 [512, 512], P('fsdp')
- variance_expand: float32 [512, 2048], P('fsdp')
- variance_reduce: float32 [2048, 512], P('fsdp')
- new_norms: float32 [512, 4], replicated
- momentum_norms: float32 [512, 4], replicated
- variance_norms: float32 [512, 4], replicated
- norm_table: float32 [2, 8], replicated
- value_mean: float32 [11], replicated
- value_peak: float32 [11], replicated
Inputs may be any that keep to these rules, and one draw needn't show every extreme that they name: `lengths`: every episode has at least 37 rows; an episode of the first device has exactly 37 and one of the last device exactly 296. `tokens`: rows of order one. `norm_params`: gains positive. `second_triple`: positive. `second_mixer`: positive. `second_expand`: positive. `second_reduce`: positive. `second_norms`: positive.
All inputs are finite; a program needn't handle non-finite values. No bound on the sum of `valid_mask` on one device may be relied on, other than what follows from the above.
Results may differ from a plain program's by a relative error of at most 0.012.
The roundings to bfloat16 on the way count: a program that leaves them out, or rounds other values in their place, can miss the bound.
Values may be sent and summed in bfloat16 or wider, within the bound.
No kernel may reach another device: no remote copies, remote signals or barrier semaphores. Data moves between devices by JAX's collectives and lax.ppermute only.
A program may use at most 256 MiB of HBM per device.

v0:
```python
import jax
import jax.numpy as jnp
from jax import lax
from jax.sharding import PartitionSpec as P

HEADS = 8
HEAD_DIM = 64
ACT = 11
NBINS = 256
STEP = 5


NORM_EPSILON = 1e-05
BETA_FIRST = 0.9
BETA_SECOND = 0.999
ADAM_EPSILON = 1e-06
RATIO_EPSILON = 1e-06
WEIGHT_DECAY = 0.01
LEARNING_RATE = 0.5
MASKED = -1e30


def for_sending(shard):

    def short(part):
        return part.astype(jnp.bfloat16) if part.dtype == jnp.float32 else part

    return jax.tree.map(short, shard)


def layer_norm(row_block, gain_vector, bias_vector):
    center = row_block - jnp.mean(row_block, axis=-1, keepdims=True)
    spread = jnp.mean(center * center, axis=-1, keepdims=True)
    return center * lax.rsqrt(spread + NORM_EPSILON) * gain_vector + bias_vector


def gelu_exact(expanded_in):
    return jax.nn.gelu(expanded_in, approximate=False)


def masked_scores(queries, key_rows, allowed):
    scores = jnp.einsum(
        "ehqd,ehkd->ehqk", queries, key_rows, preferred_element_type=jnp.float32
    ) * HEAD_DIM ** (-0.5)
    return jnp.where(allowed, scores, MASKED)


def lamb_moments(weight, gradient, moment_one, moment_two):
    first_new = BETA_FIRST * moment_one + (1.0 - BETA_FIRST) * gradient
    second_new = BETA_SECOND * moment_two + (1.0 - BETA_SECOND) * gradient * gradient
    update = (
        first_new
        / (1.0 - BETA_FIRST**STEP)
        / (jnp.sqrt(second_new / (1.0 - BETA_SECOND**STEP)) + ADAM_EPSILON)
        + WEIGHT_DECAY * weight
    )
    return (first_new, second_new, update)


def body(
    tokens,
    cotangent,
    lengths,
    valid_mask,
    action_bins,
    value_head,
    w_triple,
    w_mixer,
    w_expand,
    w_reduce,
    norm_params,
    first_triple,
    first_mixer,
    first_expand,
    first_reduce,
    first_norms,
    second_triple,
    second_mixer,
    second_expand,
    second_reduce,
    second_norms,
):
    episodes, length_rows, features = tokens.shape
    masters = (w_triple, w_mixer, w_expand, w_reduce)
    shards_low = tuple((master.astype(jnp.bfloat16) for master in masters))
    gathered = jax.tree.map(
        lambda part, own: part.astype(own.dtype),
        lax.all_gather(for_sending(shards_low), "fsdp", axis=0, tiled=True),
        shards_low,
    )
    flattened = tokens.reshape(episodes * length_rows, features).astype(jnp.float32)
    places = jnp.arange(length_rows)
    inside = places[None, :] < lengths[:, None]
    allowed = ((places[None, :] <= places[:, None])[None] & inside[:, None, :])[:, None]
    gain_one, bias_one = (norm_params[:, 0], norm_params[:, 1])
    gain_two, bias_two = (norm_params[:, 2], norm_params[:, 3])
    normed_one = layer_norm(flattened, gain_one, bias_one).astype(jnp.bfloat16)
    triple = jnp.dot(normed_one, gathered[0], preferred_element_type=jnp.float32).astype(
        jnp.bfloat16
    )
    triple = triple.reshape(episodes, length_rows, 3, HEADS, HEAD_DIM)
    queries = triple[:, :, 0].transpose(0, 2, 1, 3)
    key_rows = triple[:, :, 1].transpose(0, 2, 1, 3)
    value_rows = triple[:, :, 2].transpose(0, 2, 1, 3)
    scores = masked_scores(queries, key_rows, allowed)
    row_peak = jnp.max(scores, axis=-1, keepdims=True)
    shifted = jnp.exp(scores - row_peak)
    totals = jnp.sum(shifted, axis=-1, keepdims=True)
    log_totals = row_peak + jnp.log(totals)
    probs_low = (shifted / totals).astype(jnp.bfloat16)
    mixture = jnp.einsum(
        "ehqk,ehkd->eqhd", probs_low, value_rows, preferred_element_type=jnp.float32
    )
    attended = mixture.reshape(episodes * length_rows, features).astype(jnp.bfloat16)
    hidden = flattened + jnp.dot(attended, gathered[1], preferred_element_type=jnp.float32)
    normed_two = layer_norm(hidden, gain_two, bias_two).astype(jnp.bfloat16)
    expanded = jnp.dot(normed_two, gathered[2], preferred_element_type=jnp.float32)
    activated = gelu_exact(expanded).astype(jnp.bfloat16)
    block_flat = (
        hidden + jnp.dot(activated, gathered[3], preferred_element_type=jnp.float32)
    ).astype(jnp.bfloat16)
    bin_rows = action_bins.reshape(-1, ACT) + (jnp.arange(ACT) * NBINS)[None, :]
    picked = jnp.take(value_head, bin_rows, axis=0)
    value_scores = jnp.einsum("tad,td->ta", picked, block_flat, preferred_element_type=jnp.float32)
    counted = ((valid_mask == 1) & inside).reshape(-1, 1).astype(jnp.float32)
    value_sum = jnp.sum(value_scores * counted, axis=0)
    value_count = jnp.sum(counted)
    value_top = jnp.max(jnp.where(counted > 0, value_scores, MASKED), axis=0)
    value_peak = lax.pmax(value_top, ("dp", "fsdp"))
    live_rows = inside.reshape(-1, 1).astype(jnp.float32)
    grad_out = cotangent.reshape(-1, features).astype(jnp.float32) * live_rows
    gathered = jax.tree.map(
        lambda part, own: part.astype(own.dtype),
        lax.all_gather(for_sending(shards_low), "fsdp", axis=0, tiled=True),
        shards_low,
    )
    grad_low = grad_out.astype(jnp.bfloat16)
    grad_reduce_w = jnp.einsum("tf,td->fd", activated, grad_low, preferred_element_type=jnp.float32)
    grad_act = jnp.einsum("td,fd->tf", grad_low, gathered[3], preferred_element_type=jnp.float32)
    _, gelu_pull = jax.vjp(gelu_exact, expanded)
    grad_expanded = gelu_pull(grad_act)[0].astype(jnp.bfloat16)
    grad_expand_w = jnp.einsum(
        "td,tf->df", normed_two, grad_expanded, preferred_element_type=jnp.float32
    )
    grad_two = jnp.einsum(
        "tf,df->td", grad_expanded, gathered[2], preferred_element_type=jnp.float32
    )
    _, second_pull = jax.vjp(layer_norm, hidden, gain_two, bias_two)
    back_hidden, grad_gain_two, grad_bias_two = second_pull(grad_two)
    grad_hidden = grad_out + back_hidden
    grad_branch = grad_hidden.astype(jnp.bfloat16)
    grad_mixer_w = jnp.einsum(
        "ti,to->io", attended, grad_branch, preferred_element_type=jnp.float32
    )
    grad_attended = jnp.einsum(
        "to,io->ti", grad_branch, gathered[1], preferred_element_type=jnp.float32
    ).astype(jnp.bfloat16)
    grad_mixture = grad_attended.reshape(episodes, length_rows, HEADS, HEAD_DIM)
    softmax_rows = jnp.exp(masked_scores(queries, key_rows, allowed) - log_totals)
    grad_soft = jnp.einsum(
        "eqhd,ehkd->ehqk", grad_mixture, value_rows, preferred_element_type=jnp.float32
    )
    grad_values = jnp.einsum(
        "ehqk,eqhd->ekhd",
        softmax_rows.astype(jnp.bfloat16),
        grad_mixture,
        preferred_element_type=jnp.float32,
    )
    grad_scores = (
        softmax_rows * (grad_soft - jnp.sum(grad_soft * softmax_rows, axis=-1, keepdims=True))
    ).astype(jnp.bfloat16)
    grad_queries = jnp.einsum(
        "ehqk,ehkd->eqhd", grad_scores, key_rows, preferred_element_type=jnp.float32
    ) * HEAD_DIM ** (-0.5)
    grad_keys = jnp.einsum(
        "ehqk,ehqd->ekhd", grad_scores, queries, preferred_element_type=jnp.float32
    ) * HEAD_DIM ** (-0.5)
    grad_triple = (
        jnp.stack([grad_queries, grad_keys, grad_values], axis=2)
        .reshape(-1, 3 * features)
        .astype(jnp.bfloat16)
    )
    grad_triple_w = jnp.einsum(
        "ti,tj->ij", normed_one, grad_triple, preferred_element_type=jnp.float32
    )
    grad_one = jnp.einsum("tj,ij->ti", grad_triple, gathered[0], preferred_element_type=jnp.float32)
    _, first_pull = jax.vjp(layer_norm, flattened, gain_one, bias_one)
    back_input, grad_gain_one, grad_bias_one = first_pull(grad_one)
    input_grad = (grad_hidden + back_input).astype(jnp.bfloat16)
    norm_local = jnp.stack([grad_gain_one, grad_bias_one, grad_gain_two, grad_bias_two], axis=1)
    norm_grads, value_sums, value_counts = lax.psum(
        (norm_local, value_sum, value_count), ("dp", "fsdp")
    )
    value_mean = value_sums / jnp.maximum(value_counts, 1.0)
    local_grads = (grad_triple_w, grad_mixer_w, grad_expand_w, grad_reduce_w)
    owner_sums = (
        lax.psum_scatter(local_grads[0], "fsdp", scatter_dimension=0, tiled=True),
        lax.psum_scatter(local_grads[1], "fsdp", scatter_dimension=0, tiled=True),
        lax.psum_scatter(local_grads[2], "fsdp", scatter_dimension=0, tiled=True),
        lax.psum_scatter(local_grads[3], "fsdp", scatter_dimension=0, tiled=True),
    )
    shard_grads = lax.psum((owner_sums[0], owner_sums[1], owner_sums[2], owner_sums[3]), "dp")
    firsts = (first_triple, first_mixer, first_expand, first_reduce)
    seconds = (second_triple, second_mixer, second_expand, second_reduce)
    results = []
    weight_squares = []
    update_squares = []
    for master, gradient, moment_one, moment_two in zip(masters, shard_grads, firsts, seconds):
        first_new, second_new, update = lamb_moments(master, gradient, moment_one, moment_two)
        results.append((first_new, second_new, update))
        weight_squares.append(jnp.sum(master * master))
        update_squares.append(jnp.sum(update * update))
    weight_total, update_total = lax.psum(
        (jnp.stack(weight_squares), jnp.stack(update_squares)), "fsdp"
    )
    weight_norms = jnp.sqrt(weight_total)
    update_norms = jnp.sqrt(update_total)
    new_list = []
    for position_index in range(4):
        ratio = weight_norms[position_index] / (update_norms[position_index] + RATIO_EPSILON)
        new_list.append(
            masters[position_index] - LEARNING_RATE * ratio * results[position_index][2]
        )
    small_first, small_second, small_update = lamb_moments(
        norm_params, norm_grads, first_norms, second_norms
    )
    small_weight = jnp.sqrt(jnp.sum(norm_params * norm_params, axis=0))
    small_norm = jnp.sqrt(jnp.sum(small_update * small_update, axis=0))
    new_norms = (
        norm_params
        - LEARNING_RATE * (small_weight / (small_norm + RATIO_EPSILON))[None, :] * small_update
    )
    norm_table = jnp.stack(
        [jnp.concatenate([weight_norms, small_weight]), jnp.concatenate([update_norms, small_norm])]
    )
    block_out = block_flat.reshape(episodes, length_rows, features)
    input_grad = input_grad.reshape(episodes, length_rows, features)
    return (
        block_out,
        input_grad,
        new_list[0],
        new_list[1],
        new_list[2],
        new_list[3],
        results[0][0],
        results[1][0],
        results[2][0],
        results[3][0],
        results[0][1],
        results[1][1],
        results[2][1],
        results[3][1],
        new_norms,
        small_first,
        small_second,
        norm_table,
        value_mean,
        value_peak,
    )


def solution(mesh):
    in_specs = (
        P(("dp", "fsdp"), None, None),
        P(("dp", "fsdp"), None, None),
        P(("dp", "fsdp")),
        P(("dp", "fsdp"), None),
        P(("dp", "fsdp"), None, None),
        P(),
        P("fsdp", None),
        P("fsdp", None),
        P("fsdp", None),
        P("fsdp", None),
        P(),
        P("fsdp", None),
        P("fsdp", None),
        P("fsdp", None),
        P("fsdp", None),
        P(),
        P("fsdp", None),
        P("fsdp", None),
        P("fsdp", None),
        P("fsdp", None),
        P(),
    )
    out_specs = (
        P(("dp", "fsdp"), None, None),
        P(("dp", "fsdp"), None, None),
        P("fsdp", None),
        P("fsdp", None),
        P("fsdp", None),
        P("fsdp", None),
        P("fsdp", None),
        P("fsdp", None),
        P("fsdp", None),
        P("fsdp", None),
        P("fsdp", None),
        P("fsdp", None),
        P("fsdp", None),
        P("fsdp", None),
        P(),
        P(),
        P(),
        P(),
        P(),
        P(),
    )
    return jax.shard_map(body, mesh=mesh, in_specs=in_specs, out_specs=out_specs, check_vma=False)
```

profile of v0, /device:TPU:0, one launch (start us, length us, event | category | flops | bytes accessed | tf_op | source)
XLA Modules:
  0.0 741.7 jit_solution(123519239920081982)
XLA Ops:
  20.4 34.3 %all_gather.17 = bf16[512,512]{1,0:T(8,128)(2,1)S(1)} all-gather(bf16[64,512]{1,0:T(8,128)(2,1)S(1)} %convert_element_type.133), channel_id=1, replica_groups=mesh['dp'=4,'fsdp'=8] {'fsdp'}, dimensions={0}, use_global_device_ids=true | all-gather | bytes 589824 | tf_op jit(solution)/shard_map/all_gather | solution.py:88
  61.8 7.5 %convolution_convert_fusion = bf16[1776,1536]{1,0:T(8,128)(2,1)} fusion(bf16[512,1536]{1,0:T(8,128)(2,1)} %all-gather.4.cloned.1.call-done, f32[512]{0:T(512)S(1)} %bitcast.140, f32[512]{0:T(512)S(1)} %bitcast.132, f32[1776]{0:T(1024)S(1)} %copy-done.42, f32[1776]{0:T(1024)S(1)} %copy-done.40, bf16[1776,512]{1,0:T(8,128)(2,1)} %bitcast.126), kind=kOutput, calls=%fused_computation.34 | convolution fusion | flops 2801590272 | bytes 8865664 | tf_op jit(solution)/shard_map/dot_general | solution.py:98
  69.3 14.4 %reshape.361 = bf16[6,296,3,8,64]{4,3,2,1,0:T(8,128)(2,1)} reshape(bf16[1776,1536]{1,0:T(8,128)(2,1)} %convolution_convert_fusion) | data formatting | bytes 10911744 | tf_op jit(solution)/shard_map/reshape | solution.py:101
  83.7 7.8 %fusion.64 = (bf16[6,296,1,8,64]{4,3,2,1,0:T(8,128)(2,1)}, bf16[6,296,1,8,64]{4,3,2,1,0:T(8,128)(2,1)}, bf16[6,296,1,8,64]{4,3,2,1,0:T(8,128)(2,1)}) fusion(bf16[6,296,3,8,64]{4,3,2,1,0:T(8,128)(2,1)} %reshape.361), kind=kLoop, calls=%fused_computation.148 | loop fusion | bytes 10911744 | tf_op jit(solution)/shard_map/slice | solution.py:104
  97.5 6.0 copy.107
  103.5 6.0 copy.106
  109.5 14.2 %fusion.69 = (f32[6,8,296]{2,1,0:T(8,128)S(1)}, f32[6,8,296,296]{2,3,1,0:T(8,128)}) fusion(bf16[6,296,1,8,64]{1,4,3,0,2:T(8,128)(2,1)} %copy.108, bf16[6,296,1,8,64]{1,4,3,0,2:T(8,128)(2,1)} %copy.107, pred[6,296,296]{1,2,0:T(8,128)(4,1)} %broadcast_and_fusion), kind=kOutput, calls=%fused_computation.153 | convolution fusion | flops 550915200 | bytes 21042048 | tf_op jit(solution)/shard_map/ehqd,ehkd->ehqk/dot_general | solution.py:42
  123.8 9.5 %fusion.3 = f32[6,8,296]{2,1,0:T(8,128)S(1)} fusion(f32[6,8,296,296]{2,3,1,0:T(8,128)} %get-tuple-element.87, f32[6,8,296]{2,1,0:T(8,128)S(1)} %get-tuple-element.86), kind=kLoop, calls=%fused_computation.11 | loop fusion | flops 8396928 | bytes 16935936 | tf_op jit(solution)/shard_map/reduce_sum | solution.py:108
  133.9 10.1 %convert_bitcast_fusion = bf16[6,296,8,64]{1,3,2,0:T(8,128)(2,1)S(1)} fusion(f32[6,8,296,296]{2,3,1,0:T(8,128)} %get-tuple-element.87, f32[6,8,296]{2,1,0:T(8,128)S(1)} %fusion.3, f32[6,8,296]{2,1,0:T(8,128)S(1)} %get-tuple-element.86, bf16[6,296,1,8,64]{1,4,3,0,2:T(8,128)(2,1)S(1)} %copy-done.8), kind=kOutput, calls=%fused_computation.66 | convolution fusion | flops 551838720 | bytes 20573184 | tf_op jit(solution)/shard_map/ehqk,ehkd->eqhd/dot_general | solution.py:111
  158.7 38.4 %multiply_convert_fusion.1 = (bf16[1776,2048]{1,0:T(8,128)(2,1)}, f32[1776,2048]{1,0:T(8,128)}, f32[1776,2048]{1,0:T(8,128)}) fusion(bf16[512,2048]{1,0:T(8,128)(2,1)} %all-gather.6.cloned.1.call-done, f32[1776,512]{1,0:T(8,128)} %copy-done.3, f32[512]{0:T(512)S(1)} %bitcast.141, f32[512]{0:T(512)S(1)} %bitcast.135, f32[1776]{0:T(1024)S(1)} %fusion.49, ...), kind=kOutput, calls=%fused_computation.16 | convolution fusion | flops 3965509632 | bytes 42125184 | tf_op jit(solution)/shard_map/dot_general | solution.py:117
  197.1 18.1 %add_convert_fusion = bf16[1776,2048]{1,0:T(8,128)(2,1)} fusion(f32[1776,2048]{1,0:T(8,128)} %get-tuple-element.62, f32[1776,2048]{1,0:T(8,128)} %get-tuple-element.90, bf16[1776,512]{1,0:T(8,128)(2,1)} %fusion.17, bf16[2048,512]{1,0:T(8,128)(2,1)} %all-gather.8.cloned.1.call-done), kind=kOutput, calls=%fused_computation.15 | convolution fusion | flops 3775463424 | bytes 40288256 | tf_op jit(solution)/shard_map/td,fd->tf/dot_general | solution.py:139
  215.2 8.9 %multiply_reduce_fusion.1 = (f32[512]{0:T(512)}, f32[1776]{0:T(1024)S(1)}, f32[512]{0:T(512)}, f32[1776,512]{1,0:T(8,128)S(1)}) fusion(f32[1776,512]{1,0:T(8,128)S(1)} %copy-done.4, f32[1776]{0:T(1024)S(1)} %fusion.49, f32[1776]{0:T(1024)S(1)} %broadcast_multiply_fusion.1, f32[512]{0:T(512)S(1)} %bitcast.136, bf16[1776,2048]{1,0:T(8,128)(2,1)} %add_convert_fusion, ...), kind=kOutput, calls=%fused_computation.43 | convolution fusion | flops 3731813632 | bytes 16673600 | tf_op jit(solution)/shard_map/tf,df->td/dot_general | solution.py:145
  237.2 6.2 copy.88
  243.4 13.1 %fusion.28 = bf16[6,296,1,8,64]{1,4,3,0,2:T(8,128)(2,1)} fusion(bf16[6,296,8,64]{1,3,2,0:T(8,128)(2,1)} %copy.88, f32[6,8,296,296]{2,3,1,0:T(8,128)} %get-tuple-element.87, f32[6,8,296]{2,1,0:T(8,128)S(1)} %copy-done.20), kind=kOutput, calls=%fused_computation.67 | convolution fusion | flops 546723840 | bytes 20516352 | tf_op jit(solution)/shard_map/ehqk,eqhd->ekhd/dot_general | solution.py:163
  256.5 20.2 %multiply_reduce_fusion = (f32[6,8,296]{2,1,0:T(8,128)S(1)}, f32[6,8,296,296]{2,3,1,0:T(8,128)}) fusion(f32[6,8,296,296]{2,3,1,0:T(8,128)} %get-tuple-element.87, f32[6,8,296]{2,1,0:T(8,128)S(1)} %copy-done.20, bf16[6,296,8,64]{1,3,2,0:T(8,128)(2,1)} %copy.88, bf16[6,296,1,8,64]{1,4,3,0,2:T(8,128)(2,1)} %copy.106), kind=kOutput, calls=%fused_computation.5 | convolution fusion | flops 550915200 | bytes 37395456 | tf_op jit(solution)/shard_map/eqhd,ehkd->ehqk/dot_general | solution.py:160
  281.0 18.9 %multiply_convert_fusion = bf16[6,8,296,296]{2,3,1,0:T(8,128)(2,1)} fusion(f32[6,8,296,296]{2,3,1,0:T(8,128)} %get-tuple-element.93, f32[6,8,296,296]{2,3,1,0:T(8,128)} %get-tuple-element.87, f32[6,8,296]{2,1,0:T(8,128)S(1)} %get-tuple-element.92, f32[6,8,296]{2,1,0:T(8,128)S(1)} %copy-done.20), kind=kLoop, calls=%fused_computation.4 | loop fusion | flops 16822272 | bytes 42169344 | tf_op jit(solution)/shard_map/convert_element_type | solution.py:171
  299.9 9.4 %multiply_bitcast_fusion = bf16[6,296,1,8,64]{1,4,3,0,2:T(8,128)(2,1)} fusion(bf16[6,8,296,296]{2,3,1,0:T(8,128)(2,1)} %multiply_convert_fusion, bf16[6,296,1,8,64]{1,4,3,0,2:T(8,128)(2,1)S(1)} %copy-done.6), kind=kOutput, calls=%fused_computation.37 | convolution fusion | flops 540131328 | bytes 12048384 | tf_op jit(solution)/shard_map/ehqk,ehqd->ekhd/dot_general | solution.py:175
  309.8 7.4 multiply_bitcast_fusion.1
  321.1 12.5 %copy.93 = bf16[6,296,3,8,64]{1,0,4,3,2:T(8,128)(2,1)} copy(bf16[6,296,3,8,64]{1,4,3,0,2:T(8,128)(2,1)} %maximum_convert_fusion) | data formatting | bytes 10911744 | tf_op jit(solution)/shard_map/convert_element_type | solution.py:181
  333.6 13.2 %convert_element_type.150 = bf16[1776,1536]{0,1:T(8,128)(2,1)} reshape(bf16[6,296,3,8,64]{1,0,4,3,2:T(8,128)(2,1)} %copy.93) | data formatting | bytes 10911744 | tf_op jit(solution)/shard_map/convert_element_type | solution.py:181
  346.8 7.9 %fusion.72 = f32[512,1536]{1,0:T(8,128)} fusion(bf16[1776,512]{1,0:T(8,128)(2,1)} %bitcast.130, bf16[1776,1536]{0,1:T(8,128)(2,1)} %convert_element_type.150), kind=kOutput, calls=%fused_computation.156 | convolution fusion | flops 2793406464 | bytes 10420224 | tf_op jit(solution)/shard_map/ti,tj->ij/dot_general | solution.py:183
  354.9 9.6 %fusion.74 = f32[2048,512]{1,0:T(8,128)} fusion(bf16[1776,2048]{1,0:T(8,128)(2,1)} %get-tuple-element.61, bf16[1776,512]{1,0:T(8,128)(2,1)} %fusion.17), kind=kOutput, calls=%fused_computation.158 | convolution fusion | flops 3724541952 | bytes 13287424 | tf_op jit(solution)/shard_map/tf,td->fd/dot_general | solution.py:138
  365.6 10.5 %fusion.54 = f32[512,2048]{1,0:T(8,128)} fusion(bf16[1776,2048]{1,0:T(8,128)(2,1)} %add_convert_fusion, f32[1776,512]{1,0:T(8,128)} %copy-done.3, f32[512]{0:T(512)S(1)} %bitcast.142, f32[512]{0:T(512)S(1)} %bitcast.138, f32[1776]{0:T(1024)S(1)} %fusion.49, f32[1776]{0:T(1024)S(1)} %broadcast_multiply_fusion.1), kind=kOutput, calls=%fused_computation.144 | convolution fusion | flops 3729088512 | bytes 15124352 | tf_op jit(solution)/shard_map/td,tf->df/dot_general | solution.py:142
  379.3 55.3 %gather_fusion = bf16[19536,512]{1,0:T(8,128)(2,1)} fusion(bf16[2816,512]{1,0:T(8,128)(2,1)S(1)} %copy-done, s32[20480]{0:T(1024)S(1)} %pad_clamp_fusion), kind=kCustom, calls=%fused_computation | custom fusion | bytes 40087872 | tf_op jit(solution)/shard_map/jit(_take)/gather | solution.py:123
  434.5 34.2 %reshape.351 = bf16[1776,11,512]{2,1,0:T(8,128)(2,1)} reshape(bf16[19536,512]{1,0:T(8,128)(2,1)} %gather_fusion) | data formatting | bytes 40009728 | tf_op jit(solution)/shard_map/jit(_take)/gather | solution.py:123
  470.7 10.2 %add_convert_fusion.3 = bf16[1776,512]{1,0:T(8,128)(2,1)} fusion(f32[1776,512]{1,0:T(8,128)} %copy-done.3, bf16[1776,2048]{1,0:T(8,128)(2,1)} %get-tuple-element.61, bf16[2048,512]{1,0:T(8,128)(2,1)} %all-gather.8.cloned.1.call-done), kind=kOutput, calls=%fused_computation.49 | convolution fusion | flops 3726360576 | bytes 14827520 | tf_op jit(solution)/shard_map/dot_general | solution.py:120
  485.0 15.0 %fusion = f32[1776,1,11]{2,1,0:T(1,128)} fusion(bf16[1776,11,512]{2,1,0:T(8,128)(2,1)S(1)} %copy-done.7, pred[1776,11]{1,0:T(8,128)(4,1)} %copy.94, bf16[1776,512,1]{1,0,2:T(8,128)(2,1)} %bitcast.147), kind=kOutput, calls=%fused_computation.1 | convolution fusion | flops 30007296 | bytes 21921168 | tf_op jit(solution)/shard_map/tad,td->ta/dot_general | solution.py:124
  502.4 9.1 %multiply_reduce_fusion.2 = (f32[512]{0:T(512)S(1)}, f32[1776]{0:T(1024)S(1)}, f32[512]{0:T(512)S(1)}, f32[1776,512]{1,0:T(8,128)S(1)}) fusion(f32[1776]{0:T(1024)S(1)} %copy-done.43, f32[1776]{0:T(1024)S(1)} %copy-done.41, bf16[6,296,512]{2,1,0:T(8,128)(2,1)} %param.21, f32[512]{0:T(512)S(1)} %bitcast.133, bf16[1776,1536]{0,1:T(8,128)(2,1)} %convert_element_type.150, ...), kind=kOutput, calls=%fused_computation.44 | convolution fusion | flops 2803406080 | bytes 14330688 | tf_op jit(solution)/shard_map/tj,ij->ti/dot_general | solution.py:186
  516.7 41.0 %all-reduce = (f32[512,4]{0,1:T(4,128)S(1)}, f32[11]{0:T(128)S(1)}, f32[]{:T(128)}) all-reduce(f32[512,4]{0,1:T(4,128)S(1)} %pad_maximum_fusion, f32[11]{0:T(128)S(1)} %get-tuple-element.35, f32[]{:T(128)} %get-tuple-element.49), channel_id=1, replica_groups=mesh['dp'=4,'fsdp'=8] {'dp','fsdp'}, use_global_device_ids=true, to_apply=%region_34.35 | all-reduce | flops 2060 | bytes 16480 | tf_op jit(solution)/shard_map/psum | solution.py:191
  559.8 74.4 %reduce-scatter.9.cloned.1.call-done = f32[64,2048]{1,0:T(8,128)} async-done(((f32[512,2048]{1,0:T(8,128)}), f32[64,2048]{1,0:T(8,128)}) %reduce-scatter.9.cloned.1.call-update) | async-done | bytes 524304 | tf_op jit(solution)/shard_map/reduce_scatter | solution.py:199
  634.8 40.9 %pmax.7 = f32[11]{0:T(128)} all-reduce(f32[11]{0:T(128)S(1)} %get-tuple-element.34), channel_id=1, replica_groups=mesh['dp'=4,'fsdp'=8] {'dp','fsdp'}, use_global_device_ids=true, to_apply=%region_41.42 | all-reduce | flops 11 | bytes 88 | tf_op jit(solution)/shard_map/pmax | solution.py:129
  696.7 21.9 %all-reduce.1 = (f32[4]{0:T(128)}, f32[4]{0:T(128)}) all-reduce(f32[4]{0:T(128)S(1)} %get-tuple-element.95, f32[4]{0:T(128)S(1)} %get-tuple-element.96), channel_id=1, replica_groups=mesh['dp'=4,'fsdp'=8] {'fsdp'}, use_global_device_ids=true, to_apply=%region_15.16 | all-reduce | flops 8 | bytes 64 | tf_op jit(solution)/shard_map/psum | solution.py:213
  (209 shorter events, 114.6 us)
Async XLA Ops:
  7.2 372.1 %copy-start = (bf16[2816,512]{1,0:T(8,128)(2,1)S(1)}, bf16[2816,512]{1,0:T(8,128)(2,1)}, u32[]{:S(2)}) copy-start(bf16[2816,512]{1,0:T(8,128)(2,1)} %param.26) | copy-start | bytes 8650756
  7.2 10.6 %copy-start.35 = (f32[512,4]{0,1:T(4,128)S(1)}, f32[512,4]{0,1:T(4,128)}, u32[]{:S(2)}) copy-start(f32[512,4]{0,1:T(4,128)} %param.31) | copy-start | bytes 24580
  7.2 12.5 %copy-start.51 = (s32[6]{0:T(128)S(1)}, s32[6]{0:T(128)}, u32[]{:S(2)}) copy-start(s32[6]{0:T(128)} %param.23) | copy-start | bytes 76
  7.2 13.1 %copy-start.21 = (f32[64,512]{1,0:T(8,128)S(1)}, f32[64,512]{1,0:T(8,128)}, u32[]{:S(2)}) copy-start(f32[64,512]{1,0:T(8,128)} %param.28) | copy-start | bytes 393220
  7.2 54.5 %all-gather.4.cloned.1.call-start = ((), (), s32[]{:S(2)}) async-start(), calls=%async_computation.4 | async-start | bytes 1769472 | tf_op jit(solution)/shard_map/all_gather | solution.py:88
  9.2 149.5 %all-gather.6.cloned.1.call-start = ((), (), s32[]{:S(2)}) async-start(), calls=%async_computation.5 | async-start | bytes 2359296 | tf_op jit(solution)/shard_map/all_gather | solution.py:88
  11.0 186.1 %all-gather.8.cloned.1.call-start = ((), (), s32[]{:S(2)}) async-start(), calls=%async_computation.6 | async-start | bytes 2359296 | tf_op jit(solution)/shard_map/all_gather | solution.py:88
  12.9 547.0 %reduce-scatter.7.cloned.1.call-start = ((), (), s32[]{:S(2)}) async-start(), calls=%async_computation.8 | async-start | bytes 1179648 | tf_op jit(solution)/shard_map/reduce_scatter | solution.py:198
  54.6 98.1 %copy-start.15 = (bf16[512,512]{1,0:T(8,128)(2,1)}, bf16[512,512]{1,0:T(8,128)(2,1)S(1)}, u32[]{:S(2)}) copy-start(bf16[512,512]{1,0:T(8,128)(2,1)S(1)} %all_gather.17) | copy-start | bytes 1572868
  123.7 10.1 %copy-start.8 = (bf16[6,296,1,8,64]{1,4,3,0,2:T(8,128)(2,1)S(1)}, bf16[6,296,1,8,64]{1,4,3,0,2:T(8,128)(2,1)}, u32[]{:S(2)}) copy-start(bf16[6,296,1,8,64]{1,4,3,0,2:T(8,128)(2,1)} %copy.106) | copy-start | bytes 5455876
  197.1 18.1 %copy-start.4 = (f32[1776,512]{1,0:T(8,128)S(1)}, f32[1776,512]{1,0:T(8,128)}, u32[]{:S(2)}) copy-start(f32[1776,512]{1,0:T(8,128)} %copy-done.3) | copy-start | bytes 10911748
  281.0 18.9 %copy-start.6 = (bf16[6,296,1,8,64]{1,4,3,0,2:T(8,128)(2,1)S(1)}, bf16[6,296,1,8,64]{1,4,3,0,2:T(8,128)(2,1)}, u32[]{:S(2)}) copy-start(bf16[6,296,1,8,64]{1,4,3,0,2:T(8,128)(2,1)} %copy.107) | copy-start | bytes 5455876
  309.3 250.5 %reduce-scatter.5.cloned.1.call-start = ((), (), s32[]{:S(2)}) async-start(), calls=%async_computation.7 | async-start | bytes 3538944 | tf_op jit(solution)/shard_map/reduce_scatter | solution.py:197
  354.7 205.1 %reduce-scatter.11.cloned.1.call-start = ((), (), s32[]{:S(2)}) async-start(), calls=%async_computation.10 | async-start | bytes 4718592 | tf_op jit(solution)/shard_map/reduce_scatter | solution.py:200
  364.5 269.7 %reduce-scatter.9.cloned.1.call-start = ((), (), s32[]{:S(2)}) async-start(), calls=%async_computation.9 | async-start | bytes 4718592 | tf_op jit(solution)/shard_map/reduce_scatter | solution.py:199
  376.1 305.0 %all-reduce.5.cloned.1.call-start = ((), (), s32[]{:S(2)}) async-start(), calls=%async_computation.11 | async-start | bytes 3145728 | tf_op jit(solution)/shard_map/psum | solution.py:202
  434.5 35.4 %copy-start.46 = (s32[6,296]{1,0:T(8,128)S(1)}, s32[6,296]{1,0:T(8,128)}, u32[]{:S(2)}) copy-start(s32[6,296]{1,0:T(8,128)} %param.24) | copy-start | bytes 21316
  434.5 35.4 %copy-start.52 = (s32[6]{0:T(128)S(1)}, s32[6]{0:T(128)}, u32[]{:S(2)}) copy-start(s32[6]{0:T(128)} %param.23) | copy-start | bytes 76
  470.7 14.4 %copy-start.7 = (bf16[1776,11,512]{2,1,0:T(8,128)(2,1)S(1)}, bf16[1776,11,512]{2,1,0:T(8,128)(2,1)}, u32[]{:S(2)}) copy-start(bf16[1776,11,512]{2,1,0:T(8,128)(2,1)} %reshape.351) | copy-start | bytes 60014596
  485.0 17.3 %copy-start.41 = (f32[1776]{0:T(1024)S(1)}, f32[1776]{0:T(1024)}, u32[]{:S(2)}) copy-start(f32[1776]{0:T(1024)} %div.155) | copy-start | bytes 21316
  485.0 17.3 %copy-start.43 = (f32[1776]{0:T(1024)S(1)}, f32[1776]{0:T(1024)}, u32[]{:S(2)}) copy-start(f32[1776]{0:T(1024)} %rsqrt.25) | copy-start | bytes 21316
  485.0 17.3 %copy-start.45 = (f32[512,1]{0,1:T(1,128)S(1)}, f32[512,1]{0,1:T(1,128)}, u32[]{:S(2)}) copy-start(f32[512,1]{0,1:T(1,128)} %get-tuple-element.72) | copy-start | bytes 6148
  502.4 9.2 %copy-start.38 = (f32[1776]{0:T(1024)S(1)}, f32[1776]{0:T(1024)}, u32[]{:S(2)}) copy-start(f32[1776]{0:T(1024)} %copy-done.37) | copy-start | bytes 21316
  502.4 9.2 %copy-start.2 = (bf16[6,296,512]{2,1,0:T(8,128)(2,1)S(1)}, bf16[6,296,512]{2,1,0:T(8,128)(2,1)}, u32[]{:S(2)}) copy-start(bf16[6,296,512]{2,1,0:T(8,128)(2,1)} %param.21) | copy-start | bytes 5455876
  514.1 44.3 %copy-start.36 = (f32[512,4]{0,1:T(4,128)S(1)}, f32[512,4]{0,1:T(4,128)}, u32[]{:S(2)}) copy-start(f32[512,4]{0,1:T(4,128)} %param.31) | copy-start | bytes 24580
  514.1 44.3 %copy-start.49 = (f32[512,4]{0,1:T(4,128)S(1)}, f32[512,4]{0,1:T(4,128)}, u32[]{:S(2)}) copy-start(f32[512,4]{0,1:T(4,128)} %param.36) | copy-start | bytes 24580
  514.1 44.3 %copy-start.50 = (f32[512,4]{0,1:T(4,128)S(1)}, f32[512,4]{0,1:T(4,128)}, u32[]{:S(2)}) copy-start(f32[512,4]{0,1:T(4,128)} %param.41) | copy-start | bytes 24580
  514.1 161.6 %copy-start.29 = (f32[1776]{0:T(1024)S(1)}, f32[1776]{0:T(1024)}, u32[]{:S(2)}) copy-start(f32[1776]{0:T(1024)} %copy-done.27) | copy-start | bytes 21316
  514.1 161.6 %copy-start.34 = (f32[1776]{0:T(1024)S(1)}, f32[1776]{0:T(1024)}, u32[]{:S(2)}) copy-start(f32[1776]{0:T(1024)} %copy-done.33) | copy-start | bytes 21316
  718.6 14.8 %copy-start.13 = (f32[256,512]{1,0:T(8,128)S(1)}, f32[256,512]{1,0:T(8,128)}, u32[]{:S(2)}) copy-start(f32[256,512]{1,0:T(8,128)} %param.30) | copy-start | bytes 1572868
  718.6 14.8 %copy-start.17 = (f32[256,512]{1,0:T(8,128)S(1)}, f32[256,512]{1,0:T(8,128)}, u32[]{:S(2)}) copy-start(f32[256,512]{1,0:T(8,128)} %get-tuple-element.57) | copy-start | bytes 1572868
  718.6 14.8 %copy-start.18 = (f32[256,512]{1,0:T(8,128)S(1)}, f32[256,512]{1,0:T(8,128)}, u32[]{:S(2)}) copy-start(f32[256,512]{1,0:T(8,128)} %get-tuple-element.58) | copy-start | bytes 1572868
  (32 other events, 156.3 us)
Sparse Core Ops, SparseCore 0:
  10.8 50.0 all-gather.3
  63.6 48.5 all-gather.5
  114.9 47.7 all-gather.7
  309.4 64.2 reduce-scatter.6
  377.5 73.5 reduce-scatter.4
  455.0 87.6 reduce-scatter.10
  546.4 87.8 reduce-scatter.8
  637.0 44.0 all-reduce.4
where the time goes:
time: 754 us; the launch traced here: 742 us
  matrix products  220 us (29%)
  local copies, waits for them, and re-layouts  196 us (26%)
  blocking collectives  138 us (18%)
  other arithmetic  91.2 us (12%)
  waiting for transfers between devices  74.8 us (10%)
  between operations  21.1 us (3%)
    gather x2, local copies, waits for them, and re-layouts, body(): picked = jnp.take(value_head, bin_rows, axis=0)  89.5 us
    reduce_scatter x1, waiting for transfers between devices, body(): lax.psum_scatter(local_grads[2], 'fsdp', scatter_dimension=0, tiled=True)  74.4 us
    psum x1, blocking collectives, body(): lax.psum((norm_local, value_sum, value_count), ('dp', 'fsdp'))  41 us
    pmax x1, blocking collectives, body(): value_peak = lax.pmax(value_top, ('dp', 'fsdp'))  40.9 us
    dot_general x1, matrix products, body(): jnp.dot(normed_two, gathered[2], preferred_element_type=jnp.float32)  38.4 us
    all_gather x1, blocking collectives, body(): lax.all_gather(for_sending(shards_low), 'fsdp', axis=0, tiled=True)  34.3 us
    unnamed x115, local copies, waits for them, and re-layouts  27 us
    convert_element_type x2, local copies, waits for them, and re-layouts, body(): grad_triple = jnp.stack([grad_queries, grad_keys, grad_values], axis=2).r...  25.7 us
  transfers between devices with their start and end apart: 8, of which 2 were waited for; matrix products, arithmetic and copies ran while one was open for 49% of the time, Pallas kernels for 0%

commit v1 on v0

v1 whole, which is shorter than its diff:
```python
import functools

import jax
import jax.numpy as jnp
from jax import lax
from jax.experimental import pallas as pl
from jax.experimental.pallas import tpu as pltpu
from jax.sharding import PartitionSpec as P

HEADS = 8
HEAD_DIM = 64
ACT = 11
NBINS = 256
STEP = 5

NORM_EPSILON = 1e-05
BETA_FIRST = 0.9
BETA_SECOND = 0.999
ADAM_EPSILON = 1e-06
RATIO_EPSILON = 1e-06
WEIGHT_DECAY = 0.01
LEARNING_RATE = 0.5
MASKED = -1e30

D = 512
FF = 2048
QB = 64
QUAD = 256
F32 = jnp.float32
BF16 = jnp.bfloat16
VMEM_LIMIT = 60 * 1024 * 1024

NT = (((1,), (1,)), ((), ()))
NN = (((1,), (0,)), ((), ()))
TN = (((0,), (0,)), ((), ()))


def mm(a, b, dims=NN):
    return lax.dot_general(a, b, dims, preferred_element_type=F32)


def pad_rows(v, rows):
    return jnp.concatenate([v, jnp.zeros((rows - v.shape[0], v.shape[1]), v.dtype)], axis=0)


def ln_parts(x):
    center = x - jnp.mean(x, axis=-1, keepdims=True)
    spread = jnp.mean(center * center, axis=-1, keepdims=True)
    rstd = lax.rsqrt(spread + NORM_EPSILON)
    return center * rstd, rstd


def ln_back(grad, xhat, rstd, gain):
    t = grad * gain
    m1 = jnp.mean(t, axis=-1, keepdims=True)
    m2 = jnp.mean(t * xhat, axis=-1, keepdims=True)
    return rstd * (t - m1 - xhat * m2)


def head_masks():
    lane = lax.broadcasted_iota(jnp.int32, (1, QUAD), 1)
    return [jnp.where(lane // HEAD_DIM == h, 1.0, 0.0).astype(BF16) for h in range(4)]


def stack_heads(block, masks):
    return jnp.concatenate([block * m for m in masks], axis=0)


def pair_rows(t):
    tt = t.T
    lane = lax.broadcasted_iota(jnp.int32, (QB, 2 * HEAD_DIM), 1)
    return jnp.where(lane < HEAD_DIM, tt[:QB], tt[QB:])


def sides(refs, core):
    return [(refs[0], 0)] if len(refs) == 1 else [(refs[0], core), (refs[1], 1 - core)]


def load_triple(refs, dst, sem, me, core, rels, start):
    half = refs[0].shape[1]
    for p, rel in enumerate(rels):
        block = jnp.bitwise_xor(me, rel)
        for src, c in sides(refs, core):
            row = pl.multiple_of(block * (len(refs) * half) + c * half, half)
            copy = pltpu.make_async_copy(src.at[p], dst.at[pl.ds(row, half)], sem)
            copy.start() if start else copy.wait()


def load_rest(refs, wm, we, wr, sem, me, core, rels, start):
    hm = D // len(rels) // len(refs)
    hr = FF // len(rels) // len(refs)
    nc = FF // D
    for p, rel in enumerate(rels):
        block = jnp.bitwise_xor(me, rel)
        for src, c in sides(refs, core):
            row = pl.multiple_of(block * (len(refs) * hm) + c * hm, hm)
            rowr = pl.multiple_of(block * (len(refs) * hr) + c * hr, hr)
            copies = [pltpu.make_async_copy(src.at[p, pl.ds(0, hm)], wm.at[pl.ds(row, hm)], sem)]
            for q in range(nc):
                copies.append(
                    pltpu.make_async_copy(
                        src.at[p, pl.ds(hm * (1 + q), hm)],
                        we.at[pl.ds(row, hm), pl.ds(q * D, D)],
                        sem,
                    )
                )
            copies.append(
                pltpu.make_async_copy(src.at[p, pl.ds(hm * (1 + nc), hr)], wr.at[pl.ds(rowr, hr)], sem)
            )
            for copy in copies:
                copy.start() if start else copy.wait()


def f1_kernel(rels, nh, idx, lens, tok, norm, *refs):
    w_refs, (tri_out, att_out, lse_out, wt, tri, sem) = refs[:nh], refs[nh:]
    e = pl.program_id(0)
    rows = tok.shape[1]
    padded = tri.shape[0]
    rows16 = -(-rows // 16) * 16

    @pl.when(e == 0)
    def _():
        load_triple(w_refs, wt, sem, idx[0], idx[1], rels, True)
        tri[rows16:padded] = jnp.zeros((padded - rows16, 3 * D), BF16)
        load_triple(w_refs, wt, sem, idx[0], idx[1], rels, False)

    x = pad_rows(tok[0].astype(F32), rows16)
    xhat, _ = ln_parts(x)
    n1 = (xhat * norm[0:1] + norm[1:2]).astype(BF16)
    t = mm(n1, wt[...]).astype(BF16)
    tri[0:rows16, 0:D] = t[:, 0:D] * jnp.asarray(HEAD_DIM**-0.5, BF16)
    tri[0:rows16, D:] = t[:, D:]
    tri_out[0] = tri[0:rows]

    length = lens[e]
    masks = head_masks()
    lane = lax.broadcasted_iota(jnp.int32, (1, QUAD), 1) % QB
    blocks = -(-rows // QB)
    for g in range(HEADS // 4):
        gl = g * QUAD
        for j in range(blocks):
            ext = min(QB * (j + 1), rows16)
            q4 = stack_heads(tri[QB * j : QB * (j + 1), gl : gl + QUAD], masks)
            s = mm(tri[0:ext, D + gl : D + gl + QUAD], q4, NT)
            kmax = jnp.minimum(lane + QB * j, length - 1)
            krow = lax.broadcasted_iota(jnp.int32, (ext, QUAD), 0)
            s = jnp.where(krow <= kmax, s, MASKED)
            m = jnp.max(s, axis=0, keepdims=True)
            p = jnp.exp(s - m)
            total = jnp.sum(p, axis=0, keepdims=True)
            lse_out[0, pl.ds(g * blocks + j, 1), :] = m + jnp.log(total)
            pb = (p * (1.0 / total)).astype(BF16)
            live = min(QB, rows - QB * j)
            for t2 in range(2):
                cl = 2 * D + gl + 128 * t2
                o = mm(tri[0:ext, cl : cl + 128], pb[:, 128 * t2 : 128 * t2 + 128], TN)
                o = pair_rows(o).astype(BF16)
                att_out[0, QB * j : QB * j + live, gl + 128 * t2 : gl + 128 * t2 + 128] = o[:live]


def f2_kernel(rels, pos, nh, idx, att_ref, tok, gl_ref, norm, *refs):
    w_refs, refs = refs[:nh], refs[nh:]
    (block_out, gh_out, ga_out), grads, refs = refs[:3], refs[3 : 3 + nh], refs[3 + nh :]
    ln_out, wm, we, wr, acc_m, acc_e, acc_r, sem = refs
    e = pl.program_id(0)
    rows = tok.shape[1]
    rows16 = -(-rows // 16) * 16

    @pl.when(e == 0)
    def _():
        load_rest(w_refs, wm, we, wr, sem, idx[0], idx[1], rels, True)
        acc_m[...] = jnp.zeros_like(acc_m)
        acc_e[...] = jnp.zeros_like(acc_e)
        acc_r[...] = jnp.zeros_like(acc_r)
        ln_out[...] = jnp.zeros_like(ln_out)
        load_rest(w_refs, wm, we, wr, sem, idx[0], idx[1], rels, False)

    gain = norm[2:3]
    att = pad_rows(att_ref[0], rows16)
    glow = pad_rows(gl_ref[0], rows16)
    hidden = pad_rows(tok[0].astype(F32), rows16) + mm(att, wm[...])
    xhat, rstd = ln_parts(hidden)
    n2 = (xhat * gain + norm[3:4]).astype(BF16)
    out = hidden
    g2 = jnp.zeros_like(hidden)
    for c in range(FF // D):
        cs = slice(c * D, c * D + D)
        ex = mm(n2, we[:, cs])
        phi = 0.5 + 0.5 * lax.erf(ex * 0.7071067811865476)
        act = (ex * phi).astype(BF16)
        gp = phi + ex * (jnp.exp(-0.5 * ex * ex) * 0.3989422804014327)
        out = out + mm(act, wr[cs])
        gact = mm(glow, wr[cs], NT)
        ge = (gp * gact).astype(BF16)
        g2 = g2 + mm(ge, we[:, cs], NT)
        acc_r[:, cs] += mm(glow, act, TN)
        acc_e[:, cs] += mm(n2, ge, TN)
    block_out[0] = out[:rows].astype(BF16)
    gh = glow.astype(F32) + ln_back(g2, xhat, rstd, gain)
    ln_out[0:1] += jnp.sum(g2 * xhat, axis=0, keepdims=True)
    ln_out[1:2] += jnp.sum(g2, axis=0, keepdims=True)
    gb = gh.astype(BF16)
    gh_out[0] = gh[:rows]
    acc_m[...] += mm(att, gb, TN)
    ga_out[0] = mm(gb, wm[...], NT)[:rows].astype(BF16)

    @pl.when(e == pl.num_programs(0) - 1)
    def _():
        me, core = idx[0], idx[1]
        hm = D // len(rels) // nh
        hr = FF // len(rels) // nh
        nc = FF // D
        for c in range(nc):
            wr[c * D : c * D + D] = acc_r[:, c * D : c * D + D].T.astype(BF16)
        for p, rel in enumerate(pos):
            block = jnp.bitwise_xor(me, rel)
            for dst, c in sides(grads, core):
                row = pl.multiple_of(block * (nh * hm) + c * hm, hm)
                rowr = pl.multiple_of(block * (nh * hr) + c * hr, hr)
                dst[p, 0:hm] = acc_m[pl.ds(row, hm)].astype(BF16)
                for q in range(nc):
                    dst[p, hm * (1 + q) : hm * (2 + q)] = acc_e[
                        pl.ds(row, hm), q * D : q * D + D
                    ].astype(BF16)
                dst[p, hm * (1 + nc) :] = wr[pl.ds(rowr, hr)]


def b1_kernel(pos, nh, idx, lens, tri_ref, ga_ref, lse, tok, norm, gtri_out, *refs):
    grads, (tri, ga, gtri, dk, dv, acc) = refs[:nh], refs[nh:]
    e = pl.program_id(0)
    rows = tok.shape[1]
    padded = tri.shape[0]
    rows16 = -(-rows // 16) * 16
    rows8 = rows // 16 * 16

    @pl.when(e == 0)
    def _():
        acc[...] = jnp.zeros_like(acc)
        tri[rows8:padded] = jnp.zeros((padded - rows8, 3 * D), BF16)
        ga[rows8:padded] = jnp.zeros((padded - rows8, D), BF16)

    tri[0:rows] = tri_ref[0]
    ga[0:rows] = ga_ref[0]
    dk[...] = jnp.zeros_like(dk)
    dv[...] = jnp.zeros_like(dv)
    gtri[:, 0:D] = jnp.zeros((padded, D), BF16)

    length = lens[e]
    masks = head_masks()
    lane = lax.broadcasted_iota(jnp.int32, (1, QUAD), 1) % QB
    blocks = -(-rows // QB)
    for j in range(blocks):

        @pl.when(length > QB * j)
        def _(j=j):
            ext = min(QB * (j + 1), rows16)
            kmax = jnp.minimum(lane + QB * j, length - 1)
            krow = lax.broadcasted_iota(jnp.int32, (ext, QUAD), 0)
            allowed = krow <= kmax
            for g in range(HEADS // 4):
                gl = g * QUAD
                q4 = stack_heads(tri[QB * j : QB * (j + 1), gl : gl + QUAD], masks)
                do4 = stack_heads(ga[QB * j : QB * (j + 1), gl : gl + QUAD], masks)
                s = mm(tri[0:ext, D + gl : D + gl + QUAD], q4, NT)
                s = jnp.where(allowed, s - lse[0, pl.ds(g * blocks + j, 1), :], MASKED)
                p = jnp.exp(s)
                dp = mm(tri[0:ext, 2 * D + gl : 2 * D + gl + QUAD], do4, NT)
                delta = jnp.sum(p * dp, axis=0, keepdims=True)
                ds = (p * (dp - delta)).astype(BF16)
                dv[0:ext, gl : gl + QUAD] += mm(p.astype(BF16), do4)
                dk[0:ext, gl : gl + QUAD] += mm(ds, q4)
                for t2 in range(2):
                    cl = D + gl + 128 * t2
                    dq = mm(tri[0:ext, cl : cl + 128], ds[:, 128 * t2 : 128 * t2 + 128], TN)
                    dq = pair_rows(dq) * HEAD_DIM**-0.5
                    gtri[QB * j : QB * (j + 1), gl + 128 * t2 : gl + 128 * t2 + 128] = dq.astype(BF16)

    gtri[0:rows16, D : 2 * D] = dk[...].astype(BF16)
    gtri[0:rows16, 2 * D :] = dv[...].astype(BF16)
    gtri_out[0] = gtri[0:rows]
    xhat, _ = ln_parts(pad_rows(tok[0].astype(F32), rows16))
    n1 = (xhat * norm[0:1] + norm[1:2]).astype(BF16)
    acc[...] += mm(n1, gtri[0:rows16], TN)

    @pl.when(e == pl.num_programs(0) - 1)
    def _():
        me, core = idx[0], idx[1]
        hm = D // len(pos) // nh
        for p, rel in enumerate(pos):
            block = jnp.bitwise_xor(me, rel)
            for dst, c in sides(grads, core):
                row = pl.multiple_of(block * (nh * hm) + c * hm, hm)
                for q in range(3):
                    dst[p, hm * q : hm * (q + 1)] = acc[pl.ds(row, hm), q * D : q * D + D].astype(BF16)


def b2_kernel(rels, nh, idx, gtri, tok, gh, norm, *refs):
    w_refs, (ig_out, ln_out, wt, sem) = refs[:nh], refs[nh:]
    e = pl.program_id(0)

    @pl.when(e == 0)
    def _():
        load_triple(w_refs, wt, sem, idx[0], idx[1], rels, True)
        ln_out[...] = jnp.zeros_like(ln_out)
        load_triple(w_refs, wt, sem, idx[0], idx[1], rels, False)

    g1 = mm(gtri[0], wt[...], NT)
    xhat, rstd = ln_parts(tok[0].astype(F32))
    ig_out[0] = (gh[0] + ln_back(g1, xhat, rstd, norm[0:1])).astype(BF16)
    ln_out[0:1] += jnp.sum(g1 * xhat, axis=0, keepdims=True)
    ln_out[1:2] += jnp.sum(g1, axis=0, keepdims=True)


def q_kernel(total_rows, bo, vh, bins, cnt, sum_out, top_out):
    s = pl.program_id(0)
    block = bo.shape[0]

    @pl.when(s == 0)
    def _():
        sum_out[...] = jnp.zeros_like(sum_out)
        top_out[...] = jnp.full_like(top_out, MASKED)

    place = lax.broadcasted_iota(jnp.int32, (1, block), 1) + s * block
    counted = (cnt[...] > 0) & (place < total_rows)
    binrow = lax.broadcasted_iota(jnp.int32, (NBINS, block), 0)
    for a in range(ACT):
        sc = mm(vh[a * NBINS : (a + 1) * NBINS], bo[...], NT)
        picked = jnp.sum(jnp.where(binrow == bins[a : a + 1], sc, 0.0), axis=0, keepdims=True)
        sum_out[a : a + 1] += jnp.where(counted, picked, 0.0)
        top_out[a : a + 1] = jnp.maximum(top_out[a : a + 1], jnp.where(counted, picked, MASKED))


def xor_step(v, axis, size, bit):
    return lax.ppermute(v, axis, [(i, i ^ bit) for i in range(size)])


def axis_bits(size):
    bits = []
    b = 1
    while b < size:
        bits.append(b)
        b *= 2
    return bits


def gather_half(piece, n_f, n_d, order, nh):
    buf, rels = piece[None], [0]
    for b in order:
        buf = jnp.concatenate([buf, xor_step(buf, "fsdp", n_f, b)], axis=0)
        rels = rels + [r ^ b for r in rels]
    if nh == 1:
        return [buf], rels
    return [buf, xor_step(buf, "dp", n_d, 1)], rels


def halving_positions(order):
    rels = [0]
    for b in reversed(order):
        rels = rels + [r ^ b for r in rels]
    return rels


def add_low(a, b):
    return (a.astype(F32) + b.astype(F32)).astype(BF16)


def reduce_halves(parts, n_f, n_d, order):
    total = parts[0]
    if len(parts) == 2:
        total = add_low(total, xor_step(parts[1], "dp", n_d, 1))
    for b in order:
        n = total.shape[0] // 2
        total = add_low(total[:n], xor_step(total[n:], "fsdp", n_f, b))
    total = total[0].astype(F32)
    for b in axis_bits(n_d)[len(parts) - 1 :]:
        total = total + xor_step(total.astype(BF16), "dp", n_d, b).astype(F32)
    return total


def lamb_moments(weight, gradient, moment_one, moment_two):
    first_new = BETA_FIRST * moment_one + (1.0 - BETA_FIRST) * gradient
    second_new = BETA_SECOND * moment_two + (1.0 - BETA_SECOND) * gradient * gradient
    update = (
        first_new
        / (1.0 - BETA_FIRST**STEP)
        / (jnp.sqrt(second_new / (1.0 - BETA_SECOND**STEP)) + ADAM_EPSILON)
        + WEIGHT_DECAY * weight
    )
    return (first_new, second_new, update)


def const_spec(shape):
    return pl.BlockSpec(shape, lambda *a: (0,) * len(shape))


SMEM = pl.BlockSpec(memory_space=pltpu.SMEM)
ANY = pl.BlockSpec(memory_space=pl.ANY)


def params():
    return pltpu.CompilerParams(dimension_semantics=("arbitrary",), vmem_limit_bytes=VMEM_LIMIT)


def body(n_d, n_f, *args):
    (
        tokens, cotangent, lengths, valid_mask, action_bins, value_head,
        w_triple, w_mixer, w_expand, w_reduce, norm_params,
        first_triple, first_mixer, first_expand, first_reduce, first_norms,
        second_triple, second_mixer, second_expand, second_reduce, second_norms,
    ) = args
    ep, rows, _ = tokens.shape
    flat = ep * rows
    rows16 = -(-rows // 16) * 16
    padded = -(-rows // QB) * QB
    blocks = padded // QB
    me = lax.axis_index("fsdp")
    core = lax.axis_index("dp") % 2
    idx = jnp.stack([me, core]).astype(jnp.int32)
    nh = 2 if D // n_f >= 32 else 1
    hm = D // n_f // nh
    hr = FF // n_f // nh
    nc = FF // D

    order_g = list(reversed(axis_bits(n_f)))

    def own_half(w):
        n = w.shape[0] // nh
        return lax.dynamic_slice_in_dim(w, core * n, n, 0) if nh == 2 else w

    own_t = own_half(w_triple).astype(BF16)
    own_m = own_half(w_mixer).astype(BF16)
    own_e = own_half(w_expand).astype(BF16)
    own_r = own_half(w_reduce).astype(BF16)
    own_rest = jnp.concatenate(
        [own_m] + [own_e[:, q * D : (q + 1) * D] for q in range(nc)] + [own_r], axis=0
    )
    t_parts, rels = gather_half(own_t, n_f, n_d, order_g, nh)
    r_parts, _ = gather_half(own_rest, n_f, n_d, order_g, nh)

    norm = jnp.concatenate([norm_params.T, jnp.zeros((4, D), F32)], axis=0)
    places = jnp.arange(rows)
    inside = places[None, :] < lengths[:, None]
    glow = jnp.where(inside[:, :, None], cotangent, jnp.zeros((), BF16))

    ep_block = lambda width: pl.BlockSpec((1, rows, width), lambda e: (e, 0, 0))

    triple, attended, lse = pl.pallas_call(
        functools.partial(f1_kernel, rels, nh),
        grid=(ep,),
        in_specs=[SMEM, SMEM, ep_block(D), const_spec((8, D))] + [ANY] * nh,
        out_specs=[
            ep_block(3 * D), ep_block(D), pl.BlockSpec((1, 16, QUAD), lambda e: (e, 0, 0)),
        ],
        out_shape=[
            jax.ShapeDtypeStruct((ep, rows, 3 * D), BF16),
            jax.ShapeDtypeStruct((ep, rows, D), BF16),
            jax.ShapeDtypeStruct((ep, 16, QUAD), F32),
        ],
        scratch_shapes=[
            pltpu.VMEM((D, 3 * D), BF16), pltpu.VMEM((padded, 3 * D), BF16), pltpu.SemaphoreType.DMA,
        ],
        compiler_params=params(),
        cost_estimate=pl.CostEstimate(flops=20_000_000_000, bytes_accessed=14_000_000, transcendentals=0),
        name="f1",
    )(idx, lengths, tokens, norm, *t_parts)

    order_s = axis_bits(n_f)
    pos = halving_positions(order_s)
    width = hm * (1 + nc) + hr
    block_out, gh, ga, *grads_r, ln2 = pl.pallas_call(
        functools.partial(f2_kernel, rels, pos, nh),
        grid=(ep,),
        in_specs=[SMEM, ep_block(D), ep_block(D), ep_block(D), const_spec((8, D))] + [ANY] * nh,
        out_specs=[
            ep_block(D), ep_block(D), ep_block(D),
            *[const_spec((n_f, width, D))] * nh, const_spec((8, D)),
        ],
        out_shape=[
            jax.ShapeDtypeStruct((ep, rows, D), BF16),
            jax.ShapeDtypeStruct((ep, rows, D), F32),
            jax.ShapeDtypeStruct((ep, rows, D), BF16),
            *[jax.ShapeDtypeStruct((n_f, width, D), BF16)] * nh,
            jax.ShapeDtypeStruct((8, D), F32),
        ],
        scratch_shapes=[
            pltpu.VMEM((D, D), BF16), pltpu.VMEM((D, FF), BF16), pltpu.VMEM((FF, D), BF16),
            pltpu.VMEM((D, D), F32), pltpu.VMEM((D, FF), F32), pltpu.VMEM((D, FF), F32),
            pltpu.SemaphoreType.DMA,
        ],
        compiler_params=params(),
        cost_estimate=pl.CostEstimate(flops=40_000_000_000, bytes_accessed=20_000_000, transcendentals=0),
        name="f2",
    )(idx, attended, tokens, glow, norm, *r_parts)

    gtri, *grads_t = pl.pallas_call(
        functools.partial(b1_kernel, pos, nh),
        grid=(ep,),
        in_specs=[
            SMEM, SMEM, ep_block(3 * D), ep_block(D),
            pl.BlockSpec((1, 16, QUAD), lambda e: (e, 0, 0)), ep_block(D), const_spec((8, D)),
        ],
        out_specs=[ep_block(3 * D)] + [const_spec((n_f, 3 * hm, D))] * nh,
        out_shape=[
            jax.ShapeDtypeStruct((ep, rows, 3 * D), BF16),
            *[jax.ShapeDtypeStruct((n_f, 3 * hm, D), BF16)] * nh,
        ],
        scratch_shapes=[
            pltpu.VMEM((padded, 3 * D), BF16), pltpu.VMEM((padded, D), BF16),
            pltpu.VMEM((padded, 3 * D), BF16), pltpu.VMEM((rows16, D), F32),
            pltpu.VMEM((rows16, D), F32), pltpu.VMEM((D, 3 * D), F32),
        ],
        compiler_params=params(),
        cost_estimate=pl.CostEstimate(flops=25_000_000_000, bytes_accessed=20_000_000, transcendentals=0),
        name="b1",
    )(idx, lengths, triple, ga, lse, tokens, norm)

    input_grad, ln1 = pl.pallas_call(
        functools.partial(b2_kernel, rels, nh),
        grid=(ep,),
        in_specs=[SMEM, ep_block(3 * D), ep_block(D), ep_block(D), const_spec((8, D))] + [ANY] * nh,
        out_specs=[ep_block(D), const_spec((8, D))],
        out_shape=[
            jax.ShapeDtypeStruct((ep, rows, D), BF16),
            jax.ShapeDtypeStruct((8, D), F32),
        ],
        scratch_shapes=[pltpu.VMEM((D, 3 * D), BF16), pltpu.SemaphoreType.DMA],
        compiler_params=params(),
        cost_estimate=pl.CostEstimate(flops=5_000_000_000, bytes_accessed=16_000_000, transcendentals=0),
        name="b2",
    )(idx, gtri, tokens, gh, norm, *t_parts)

    counted = ((valid_mask == 1) & inside).reshape(1, flat)
    bins_t = action_bins.reshape(flat, ACT).T
    qb = 256
    steps = -(-flat // qb)
    q_sum, q_top = pl.pallas_call(
        functools.partial(q_kernel, flat),
        grid=(steps,),
        in_specs=[
            pl.BlockSpec((qb, D), lambda s: (s, 0)), const_spec((ACT * NBINS, D)),
            pl.BlockSpec((ACT, qb), lambda s: (0, s)), pl.BlockSpec((1, qb), lambda s: (0, s)),
        ],
        out_specs=[const_spec((16, qb)), const_spec((16, qb))],
        out_shape=[jax.ShapeDtypeStruct((16, qb), F32), jax.ShapeDtypeStruct((16, qb), F32)],
        compiler_params=params(),
        cost_estimate=pl.CostEstimate(flops=6_000_000_000, bytes_accessed=6_000_000, transcendentals=0),
        name="qstat",
    )(block_out.reshape(flat, D), value_head, bins_t, counted.astype(jnp.int32))
    value_sum = jnp.sum(q_sum[:ACT], axis=1)
    value_top = jnp.max(q_top[:ACT], axis=1)
    value_count = jnp.sum(counted.astype(F32))

    small = jnp.concatenate(
        [ln1[0], ln1[1], ln2[0], ln2[1], value_sum, value_count[None], value_top,
         jnp.zeros((512 - 2 * ACT - 1,), F32)]
    )
    tops_at = 4 * D + ACT + 1
    lane = jnp.arange(small.shape[0])
    is_top = (lane >= tops_at) & (lane < tops_at + ACT)
    for axis, size in (("dp", n_d), ("fsdp", n_f)):
        for b in axis_bits(size):
            other = xor_step(small, axis, size, b)
            small = jnp.where(is_top, jnp.maximum(small, other), small + other)
    norm_grads = small[: 4 * D].reshape(4, D).T
    value_mean = small[4 * D : 4 * D + ACT] / jnp.maximum(small[4 * D + ACT], 1.0)
    value_peak = small[tops_at : tops_at + ACT]

    def both_cores(mine):
        if nh == 1:
            return (mine,)
        theirs = xor_step(mine, "dp", n_d, 1)
        return jnp.where(core == 0, mine, theirs), jnp.where(core == 0, theirs, mine)

    both_r = both_cores(reduce_halves(grads_r, n_f, n_d, order_s))
    both_t = both_cores(reduce_halves(grads_t, n_f, n_d, order_s))

    def columns(v, at, parts):
        return jnp.concatenate([v[at + hm * q : at + hm * (q + 1)] for q in range(parts)], axis=1)

    shard_grads = (
        jnp.concatenate([columns(v, 0, 3) for v in both_t], axis=0),
        jnp.concatenate([v[:hm] for v in both_r], axis=0),
        jnp.concatenate([columns(v, hm, nc) for v in both_r], axis=0),
        jnp.concatenate([v[hm * (1 + nc) :] for v in both_r], axis=0),
    )
    masters = (w_triple, w_mixer, w_expand, w_reduce)
    firsts = (first_triple, first_mixer, first_expand, first_reduce)
    seconds = (second_triple, second_mixer, second_expand, second_reduce)
    results = []
    squares = []
    for master, gradient, moment_one, moment_two in zip(masters, shard_grads, firsts, seconds):
        first_new, second_new, update = lamb_moments(master, gradient, moment_one, moment_two)
        results.append((first_new, second_new, update))
        squares.append(jnp.sum(master * master))
        squares.append(jnp.sum(update * update))
    totals = jnp.stack(squares)
    for b in axis_bits(n_f):
        totals = totals + xor_step(totals, "fsdp", n_f, b)
    roots = jnp.sqrt(totals)
    weight_norms, update_norms = roots[0::2], roots[1::2]
    new_list = []
    for i in range(4):
        ratio = weight_norms[i] / (update_norms[i] + RATIO_EPSILON)
        new_list.append(masters[i] - LEARNING_RATE * ratio * results[i][2])
    small_first, small_second, small_update = lamb_moments(
        norm_params, norm_grads, first_norms, second_norms
    )
    small_weight = jnp.sqrt(jnp.sum(norm_params * norm_params, axis=0))
    small_norm = jnp.sqrt(jnp.sum(small_update * small_update, axis=0))
    new_norms = (
        norm_params
        - LEARNING_RATE * (small_weight / (small_norm + RATIO_EPSILON))[None, :] * small_update
    )
    norm_table = jnp.stack(
        [jnp.concatenate([weight_norms, small_weight]), jnp.concatenate([update_norms, small_norm])]
    )
    return (
        block_out, input_grad,
        new_list[0], new_list[1], new_list[2], new_list[3],
        results[0][0], results[1][0], results[2][0], results[3][0],
        results[0][1], results[1][1], results[2][1], results[3][1],
        new_norms, small_first, small_second, norm_table, value_mean, value_peak,
    )


def solution(mesh):
    n_d, n_f = mesh.shape["dp"], mesh.shape["fsdp"]
    both = ("dp", "fsdp")
    row, rep = P("fsdp", None), P()
    in_specs = (
        P(both, None, None), P(both, None, None), P(both), P(both, None), P(both, None, None), rep,
        row, row, row, row, rep,
        row, row, row, row, rep,
        row, row, row, row, rep,
    )
    out_specs = (
        (P(both, None, None),) * 2 + (row,) * 12 + (rep,) * 6
    )
    return jax.shard_map(
        functools.partial(body, n_d, n_f), mesh=mesh, in_specs=in_specs, out_specs=out_specs,
        check_vma=False,
    )
```

time: 754 us -> 326 us (0.43); the launches traced: 742 us -> 323 us
  matrix products: 220 us -> 0 us
  local copies, waits for them, and re-layouts: 196 us -> 24 us
  blocking collectives: 138 us -> 0 us
  Pallas kernels: 0 us -> 110 us
  other arithmetic: 91.2 us -> 28.1 us
  starting transfers between devices: 0.91 us -> 46.4 us
  waiting for transfers between devices: 74.8 us -> 107 us
  between operations: 21.1 us -> 6.9 us
    dot_general x19 -> x0, matrix products: 220 us -> none  [the longest x1 38.4 us: body(): jnp.dot(normed_two, gathered[2], preferred_element_type=jnp.float32)]
    pallas_call x0 -> x5, Pallas kernels: none -> 110 us  [the longest x1 46.4 us: body(): pl.pallas_call(functools.partial(f2_kernel, rels, pos, nh), grid=(ep,), i...]
    ppermute x0 -> x28, waiting for transfers between devices: none -> 107 us  [xor_step(): return lax.ppermute(v, axis, [(i, i ^ bit) for i in range(size)])]
    gather x2 -> x0, local copies, waits for them, and re-layouts: 89.5 us -> none  [body(): picked = jnp.take(value_head, bin_rows, axis=0)]
    reduce_scatter x4 -> x0, waiting for transfers between devices: 74.4 us -> none  [the longest x1 74.4 us: body(): lax.psum_scatter(local_grads[2], 'fsdp', scatter_dimension=0, tiled=True)]
    psum x2 -> x0, blocking collectives: 62.8 us -> none  [the longest x1 41 us: body(): lax.psum((norm_local, value_sum, value_count), ('dp', 'fsdp'))]
    ppermute x0 -> x28, starting transfers between devices: none -> 46.4 us  [xor_step(): return lax.ppermute(v, axis, [(i, i ^ bit) for i in range(size)])]
    pmax x1 -> x0, blocking collectives: 40.9 us -> none  [body(): value_peak = lax.pmax(value_top, ('dp', 'fsdp'))]
  transfers between devices with their start and end apart: 8 -> 28, of which waited for: 2 -> 18; matrix products, arithmetic and copies ran while one was open for 49% -> 9% of each run, Pallas kernels for 0% -> 20%
where the time goes in v1:
time: 326 us; the launch traced here: 323 us
  Pallas kernels  110 us (34%)
  waiting for transfers between devices  107 us (33%)
  starting transfers between devices  46.4 us (14%)
  other arithmetic  28.1 us (9%)
  local copies, waits for them, and re-layouts  24 us (7%)
  between operations  6.9 us (2%)
    ppermute x28, waiting for transfers between devices, xor_step(): return lax.ppermute(v, axis, [(i, i ^ bit) for i in range(size)])  107 us
    ppermute x28, starting transfers between devices, xor_step(): return lax.ppermute(v, axis, [(i, i ^ bit) for i in range(size)])  46.4 us
    pallas_call x1, Pallas kernels, body(): pl.pallas_call(functools.partial(f2_kernel, rels, pos, nh), grid=(ep,), i...  46.4 us
    pallas_call x1, Pallas kernels, body(): pl.pallas_call(functools.partial(f1_kernel, rels, nh), grid=(ep,), in_spe...  22.4 us
    pallas_call x1, Pallas kernels, body(): pl.pallas_call(functools.partial(b1_kernel, pos, nh), grid=(ep,), in_spec...  20.6 us
    pallas_call x1, Pallas kernels, body(): pl.pallas_call(functools.partial(b2_kernel, rels, nh), grid=(ep,), in_spe...  10.8 us
    pallas_call x1, Pallas kernels, body(): pl.pallas_call(functools.partial(q_kernel, flat), grid=(steps,), in_specs...  9.5 us
  transfers between devices with their start and end apart: 28, of which 18 were waited for; matrix products, arithmetic and copies ran while one was open for 9% of the time, Pallas kernels for 20%

profile of v1, /device:TPU:0, one launch (start us, length us, event | category | flops | bytes accessed | tf_op | source)
XLA Modules:
  0.0 322.6 jit_solution(7488186258383153316)
XLA Ops:
  3.5 4.1 %collective-permute-start.4 = (bf16[1,288,512]{2,1,0:T(8,128)(2,1)S(1)}, bf16[1,288,512]{2,1,0:T(8,128)(2,1)S(1)}, u32[]{:S(2)}, u32[]{:S(2)}) collective-permute-start(bf16[1,288,512]{2,1,0:T(8,128)(2,1)S(1)} %bitcast.43), channel_id=1, source_target_pairs={{0,4},{1,5},{2,6},{3,7},{4,0},{5,1},{6,2},{7,3},{8,12},{9,13},{10,... | collective-permute-start | bytes 884744 | tf_op jit(solution)/shard_map/ppermute | solution.py:334
  7.6 13.3 %collective-permute-done.4 = bf16[1,288,512]{2,1,0:T(8,128)(2,1)S(1)} collective-permute-done((bf16[1,288,512]{2,1,0:T(8,128)(2,1)S(1)}, bf16[1,288,512]{2,1,0:T(8,128)(2,1)S(1)}, u32[]{:S(2)}, u32[]{:S(2)}) %collective-permute-start.4) | collective-permute-done | bytes 294944 | tf_op jit(solution)/shard_map/ppermute | solution.py:334
  22.8 3.4 %collective-permute-start = (bf16[1,32,1536]{2,1,0:T(8,128)(2,1)S(1)}, bf16[1,32,1536]{2,1,0:T(8,128)(2,1)S(1)}, u32[]{:S(2)}, u32[]{:S(2)}) collective-permute-start(bf16[1,32,1536]{2,1,0:T(8,128)(2,1)S(1)} %fusion.6), channel_id=1, source_target_pairs={{0,4},{1,5},{2,6},{3,7},{4,0},{5,1},{6,2},{7,3},{8,12},{9,13},{10,... | collective-permute-start | bytes 294920 | tf_op jit(solution)/shard_map/ppermute | solution.py:334
  26.2 10.5 %collective-permute-done = bf16[1,32,1536]{2,1,0:T(8,128)(2,1)S(1)} collective-permute-done((bf16[1,32,1536]{2,1,0:T(8,128)(2,1)S(1)}, bf16[1,32,1536]{2,1,0:T(8,128)(2,1)S(1)}, u32[]{:S(2)}, u32[]{:S(2)}) %collective-permute-start) | collective-permute-done | bytes 98336 | tf_op jit(solution)/shard_map/ppermute | solution.py:334
  36.7 4.2 %collective-permute-start.1 = (bf16[2,32,1536]{2,1,0:T(8,128)(2,1)S(1)}, bf16[2,32,1536]{2,1,0:T(8,128)(2,1)S(1)}, u32[]{:S(2)}, u32[]{:S(2)}) collective-permute-start(bf16[2,32,1536]{2,1,0:T(8,128)(2,1)S(1)} %pad_maximum_fusion.6), channel_id=1, source_target_pairs={{0,2},{1,3},{2,0},{3,1},{4,6},{5,7},{6,4},{7,5},{8,10},{9,11},{10,... | collective-permute-start | bytes 589832 | tf_op jit(solution)/shard_map/ppermute | solution.py:334
  42.6 2.8 collective-permute-done.1
  48.5 28.1 %collective-permute-done.2 = bf16[4,32,1536]{2,1,0:T(8,128)(2,1)S(1)} collective-permute-done((bf16[4,32,1536]{2,1,0:T(8,128)(2,1)S(1)}, bf16[4,32,1536]{2,1,0:T(8,128)(2,1)S(1)}, u32[]{:S(2)}, u32[]{:S(2)}) %collective-permute-start.2) | collective-permute-done | bytes 393248 | tf_op jit(solution)/shard_map/ppermute | solution.py:334
  85.0 22.4 %f1.1 = (bf16[6,296,1536]{2,1,0:T(8,128)(2,1)}, bf16[6,296,512]{2,1,0:T(8,128)(2,1)}, f32[6,16,256]{2,1,0:T(8,128)}) custom-call(s32[2]{0:T(128)} %pad_add_fusion.idx, s32[6]{0:T(128)} %lens.3, bf16[6,296,512]{2,1,0:T(8,128)(2,1)} %tok.7, f32[8,512]{1,0:T(8,128)} %concatenate.61.norm, bf16[8,32,1536]{2,1,0:T(8,128)(2,1)} %pad_maximum_fusion.2.refs_0_, ...), custom_call_target="tpu_custom_call" | custom-call | flops 20000000000 | bytes 14000000 | tf_op jit(solution)/shard_map/f1/pallas_call | solution.py:447
  107.4 46.4 %f2.1 = (bf16[6,296,512]{2,1,0:T(8,128)(2,1)}, f32[6,296,512]{2,1,0:T(8,128)}, bf16[6,296,512]{2,1,0:T(8,128)(2,1)}, bf16[8,288,512]{2,1,0:T(8,128)(2,1)}, bf16[...) custom-call(s32[2]{0:T(128)} %pad_add_fusion.idx, bf16[6,296,512]{2,1,0:T(8,128)(2,1)} %get-tuple-element.36.att_ref, ...), custom_call_target="tpu_custom_call" | custom-call | flops 40000000000 | bytes 20000000 | tf_op jit(solution)/shard_map/f2/pallas_call | solution.py:470
  154.2 20.6 %b1.1 = (bf16[6,296,1536]{2,1,0:T(8,128)(2,1)}, bf16[8,96,512]{2,1,0:T(8,128)(2,1)}, bf16[8,96,512]{2,1,0:T(8,128)(2,1)}) custom-call(s32[2]{0:T(128)} %pad_add_fusion.idx, s32[6]{0:T(128)} %lens.3, bf16[6,296,1536]{2,1,0:T(8,128)(2,1)} %get-tuple-element.38.tri_ref, bf16[6,296,512]{2,1,0:T(8,128)(2,1)} %get-tuple-element.39.ga_ref, ...), custom_call_target="tpu_custom_call" | custom-call | flops 24999999488 | bytes 20000000 | tf_op jit(solution)/shard_map/b1/pallas_call | solution.py:495
  174.8 9.5 %qstat.1 = (f32[16,256]{1,0:T(8,128)}, f32[16,256]{1,0:T(8,128)}) custom-call(bf16[1776,512]{1,0:T(8,128)(2,1)} %bitcast.53, bf16[2816,512]{1,0:T(8,128)(2,1)} %vh.1, s32[11,1776]{1,0:T(8,128)} %bitcast.47, s32[1,1776]{1,0:T(1,128)} %reshape.128.cnt), custom_call_target="tpu_custom_call" | custom-call | flops 6000000000 | bytes 6000000 | tf_op jit(solution)/shard_map/qstat/pallas_call | solution.py:536
  185.2 10.8 %b2.1 = (bf16[6,296,512]{2,1,0:T(8,128)(2,1)}, f32[8,512]{1,0:T(8,128)}) custom-call(s32[2]{0:T(128)} %pad_add_fusion.idx, bf16[6,296,1536]{2,1,0:T(8,128)(2,1)} %get-tuple-element.41.gtri, bf16[6,296,512]{2,1,0:T(8,128)(2,1)} %tok.7, f32[6,296,512]{2,1,0:T(8,128)} %get-tuple-element.42.gh, f32[8,512]{1,0:T(8,128)} %concatenate.61.norm, ...), custom_call_target="tpu_custom_call" | custom-call | flops 5000000000 | bytes 16000000 | tf_op jit(solution)/shard_map/b2/pallas_call | solution.py:517
  200.2 3.4 %collective-permute-start.24 = (f32[2560]{0:T(1024)S(1)}, f32[2560]{0:T(1024)S(1)}, u32[]{:S(2)}, u32[]{:S(2)}) collective-permute-start(f32[2560]{0:T(1024)S(1)} %add_select_fusion.4), channel_id=1, source_target_pairs={{0,16},{8,24},{16,0},{24,8},{1,17},{9,25},{17,1},{25,9},{2,18},{10... | collective-permute-start | bytes 30728 | tf_op jit(solution)/shard_map/ppermute | solution.py:334
  205.3 2.4 collective-permute-start.25
  209.1 3.1 add_convert_fusion
  213.3 3.4 %collective-permute-start.26 = (f32[2560]{0:T(1024)S(1)}, f32[2560]{0:T(1024)S(1)}, u32[]{:S(2)}, u32[]{:S(2)}) collective-permute-start(f32[2560]{0:T(1024)S(1)} %add_select_fusion.2), channel_id=1, source_target_pairs={{0,2},{1,3},{2,0},{3,1},{4,6},{5,7},{6,4},{7,5},{8,10},{9,11},{10,... | collective-permute-start | bytes 30728 | tf_op jit(solution)/shard_map/ppermute | solution.py:334
  216.7 1.7 collective-permute-done.26
  218.9 4.3 %collective-permute-start.27 = (f32[2560]{0:T(1024)}, f32[2560]{0:T(1024)}, u32[]{:S(2)}, u32[]{:S(2)}) collective-permute-start(f32[2560]{0:T(1024)} %add_select_fusion.1), channel_id=1, source_target_pairs={{0,4},{1,5},{2,6},{3,7},{4,0},{5,1},{6,2},{7,3},{8,12},{9,13},{10,... | collective-permute-start | bytes 30728 | tf_op jit(solution)/shard_map/ppermute | solution.py:334
  223.2 2.0 collective-permute-done.27
  230.4 12.0 %collective-permute-done.15 = bf16[4,288,512]{2,1,0:T(8,128)(2,1)S(1)} collective-permute-done((bf16[4,288,512]{2,1,0:T(8,128)(2,1)}, bf16[4,288,512]{2,1,0:T(8,128)(2,1)S(1)}, u32[]{:S(2)}, u32[]{:S(2)}) %collective-permute-start.15) | collective-permute-done | bytes 1179680 | tf_op jit(solution)/shard_map/ppermute | solution.py:334
  244.1 4.9 %collective-permute-done.9 = bf16[4,96,512]{2,1,0:T(8,128)(2,1)S(1)} collective-permute-done((bf16[4,96,512]{2,1,0:T(8,128)(2,1)S(1)}, bf16[4,96,512]{2,1,0:T(8,128)(2,1)S(1)}, u32[]{:S(2)}, u32[]{:S(2)}) %collective-permute-start.9) | collective-permute-done | bytes 393248 | tf_op jit(solution)/shard_map/ppermute | solution.py:334
  250.8 8.1 %collective-permute-done.10 = bf16[2,96,512]{2,1,0:T(8,128)(2,1)S(1)} collective-permute-done((bf16[2,96,512]{2,1,0:T(8,128)(2,1)S(1)}, bf16[2,96,512]{2,1,0:T(8,128)(2,1)S(1)}, u32[]{:S(2)}, u32[]{:S(2)}) %collective-permute-start.10) | collective-permute-done | bytes 196640 | tf_op jit(solution)/shard_map/ppermute | solution.py:334
  258.9 5.4 %collective-permute-start.11 = (bf16[1,96,512]{2,1,0:T(8,128)(2,1)S(1)}, bf16[1,96,512]{2,1,0:T(8,128)(2,1)S(1)}, u32[]{:S(2)}, u32[]{:S(2)}) collective-permute-start(bf16[1,96,512]{2,1,0:T(8,128)(2,1)S(1)} %slice.236), channel_id=1, source_target_pairs={{0,4},{1,5},{2,6},{3,7},{4,0},{5,1},{6,2},{7,3},{8,12},{9,13},{10,... | collective-permute-start | bytes 294920 | tf_op jit(solution)/shard_map/ppermute | solution.py:334
  267.2 6.4 %collective-permute-done.11 = bf16[1,96,512]{2,1,0:T(8,128)(2,1)S(1)} collective-permute-done((bf16[1,96,512]{2,1,0:T(8,128)(2,1)S(1)}, bf16[1,96,512]{2,1,0:T(8,128)(2,1)S(1)}, u32[]{:S(2)}, u32[]{:S(2)}) %collective-permute-start.11) | collective-permute-done | bytes 98336 | tf_op jit(solution)/shard_map/ppermute | solution.py:334
  274.9 3.2 collective-permute-done.17
  280.7 4.7 %collective-permute-done.18 = bf16[288,512]{1,0:T(8,128)(2,1)S(1)} collective-permute-done((bf16[288,512]{1,0:T(8,128)(2,1)S(1)}, bf16[288,512]{1,0:T(8,128)(2,1)S(1)}, u32[]{:S(2)}, u32[]{:S(2)}) %collective-permute-start.18) | collective-permute-done | bytes 294944 | tf_op jit(solution)/shard_map/ppermute | solution.py:334
  285.6 1.8 multiply_reduce_fusion.4
  293.0 5.1 %stack.56 = f32[8]{0:T(128)S(1)} concatenate(f32[1]{0:T(128)} %bitcast.5, f32[1]{0:T(128)} %bitcast.7, f32[1]{0:T(128)} %bitcast.8, f32[1]{0:T(128)} %bitcast.10, f32[1]{0:T(128)} %bitcast.11, f32[1]{0:T(128)} %bitcast.12, f32[1]{0:T(128)} %bitcast.13, f32[1]{0:T(128)} %bitcast.14), dimensions={0} | concatenate | bytes 64 | tf_op jit(solution)/shard_map/stack | solution.py:596
  299.0 2.6 collective-permute-done.20
  302.7 2.5 collective-permute-done.21
  305.2 2.4 collective-permute-start.22
  307.6 2.1 collective-permute-done.22
  (167 shorter events, 58.1 us)
Async XLA Ops:
  3.5 17.4 %collective-permute-start.4 = (bf16[1,288,512]{2,1,0:T(8,128)(2,1)S(1)}, bf16[1,288,512]{2,1,0:T(8,128)(2,1)S(1)}, u32[]{:S(2)}, u32[]{:S(2)}) collective-permute-start(bf16[1,288,512]{2,1,0:T(8,128)(2,1)S(1)} %bitcast.43), channel_id=1, source_target_pairs={{0,4},{1,5},{2,6},{3,7},{4,0},{5,1},{6,2},{7,3},{8,12},{9,13},{10,... | collective-permute-start | bytes 884744 | tf_op jit(solution)/shard_map/ppermute | solution.py:334
  21.0 19.9 %collective-permute-start.5 = (bf16[2,288,512]{2,1,0:T(8,128)(2,1)S(1)}, bf16[2,288,512]{2,1,0:T(8,128)(2,1)S(1)}, u32[]{:S(2)}, u32[]{:S(2)}) collective-permute-start(bf16[2,288,512]{2,1,0:T(8,128)(2,1)S(1)} %pad_maximum_fusion.3), channel_id=1, source_target_pairs={{0,2},{1,3},{2,0},{3,1},{4,6},{5,7},{6,4},{7,5},{8,10},{9,11},{10,... | collective-permute-start | bytes 1769480 | tf_op jit(solution)/shard_map/ppermute | solution.py:334
  22.8 13.9 %collective-permute-start = (bf16[1,32,1536]{2,1,0:T(8,128)(2,1)S(1)}, bf16[1,32,1536]{2,1,0:T(8,128)(2,1)S(1)}, u32[]{:S(2)}, u32[]{:S(2)}) collective-permute-start(bf16[1,32,1536]{2,1,0:T(8,128)(2,1)S(1)} %fusion.6), channel_id=1, source_target_pairs={{0,4},{1,5},{2,6},{3,7},{4,0},{5,1},{6,2},{7,3},{8,12},{9,13},{10,... | collective-permute-start | bytes 294920 | tf_op jit(solution)/shard_map/ppermute | solution.py:334
  36.7 8.7 %collective-permute-start.1 = (bf16[2,32,1536]{2,1,0:T(8,128)(2,1)S(1)}, bf16[2,32,1536]{2,1,0:T(8,128)(2,1)S(1)}, u32[]{:S(2)}, u32[]{:S(2)}) collective-permute-start(bf16[2,32,1536]{2,1,0:T(8,128)(2,1)S(1)} %pad_maximum_fusion.6), channel_id=1, source_target_pairs={{0,2},{1,3},{2,0},{3,1},{4,6},{5,7},{6,4},{7,5},{8,10},{9,11},{10,... | collective-permute-start | bytes 589832 | tf_op jit(solution)/shard_map/ppermute | solution.py:334
  41.0 39.5 %copy-start.24 = (f32[512,4]{0,1:T(4,128)S(1)}, f32[512,4]{0,1:T(4,128)}, u32[]{:S(2)}) copy-start(f32[512,4]{0,1:T(4,128)} %param.31) | copy-start | bytes 24580
  41.0 40.1 %collective-permute-start.6 = (bf16[4,288,512]{2,1,0:T(8,128)(2,1)S(1)}, bf16[4,288,512]{2,1,0:T(8,128)(2,1)}, u32[]{:S(2)}, u32[]{:S(2)}) collective-permute-start(bf16[4,288,512]{2,1,0:T(8,128)(2,1)S(1)} %pad_maximum_fusion.1), channel_id=1, source_target_pairs={{0,1},{1,0},{2,3},{3,2},{4,5},{5,4},{6,7},{7,6},{8,9},{9,8},{10,11... | collective-permute-start | bytes 3538952 | tf_op jit(solution)/shard_map/ppermute | solution.py:334
  45.5 31.1 %collective-permute-start.2 = (bf16[4,32,1536]{2,1,0:T(8,128)(2,1)S(1)}, bf16[4,32,1536]{2,1,0:T(8,128)(2,1)S(1)}, u32[]{:S(2)}, u32[]{:S(2)}) collective-permute-start(bf16[4,32,1536]{2,1,0:T(8,128)(2,1)S(1)} %pad_maximum_fusion.5), channel_id=1, source_target_pairs={{0,1},{1,0},{2,3},{3,2},{4,5},{5,4},{6,7},{7,6},{8,9},{9,8},{10,11... | collective-permute-start | bytes 1179656 | tf_op jit(solution)/shard_map/ppermute | solution.py:334
  77.6 7.4 %collective-permute-start.3 = (bf16[8,32,1536]{2,1,0:T(8,128)(2,1)}, bf16[8,32,1536]{2,1,0:T(8,128)(2,1)}, u32[]{:S(2)}, u32[]{:S(2)}) collective-permute-start(bf16[8,32,1536]{2,1,0:T(8,128)(2,1)} %pad_maximum_fusion.2.refs_0_), channel_id=1, source_target_pairs={{0,8},{8,0},{16,24},{24,16},{1,9},{9,1},{17,25},{25,17},{2,10},{10... | collective-permute-start | bytes 2359304 | tf_op jit(solution)/shard_map/ppermute | solution.py:334
  82.8 24.7 %collective-permute-start.7 = (bf16[8,288,512]{2,1,0:T(8,128)(2,1)S(1)}, bf16[8,288,512]{2,1,0:T(8,128)(2,1)}, u32[]{:S(2)}, u32[]{:S(2)}) collective-permute-start(bf16[8,288,512]{2,1,0:T(8,128)(2,1)S(1)} %pad_maximum_fusion.refs_0_), channel_id=1, source_target_pairs={{0,8},{8,0},{16,24},{24,16},{1,9},{9,1},{17,25},{25,17},{2,10},{10... | collective-permute-start | bytes 7077896 | tf_op jit(solution)/shard_map/ppermute | solution.py:334
  153.8 53.8 %collective-permute-start.14 = (bf16[8,288,512]{2,1,0:T(8,128)(2,1)}, bf16[8,288,512]{2,1,0:T(8,128)(2,1)S(1)}, u32[]{:S(2)}, u32[]{:S(2)}) collective-permute-start(bf16[8,288,512]{2,1,0:T(8,128)(2,1)} %get-tuple-element.47), channel_id=1, source_target_pairs={{0,8},{8,0},{16,24},{24,16},{1,9},{9,1},{17,25},{25,17},{2,10},{10... | collective-permute-start | bytes 7077896 | tf_op jit(solution)/shard_map/ppermute | solution.py:334
  198.3 1.9 collective-permute-start.23
  200.2 5.0 %collective-permute-start.24 = (f32[2560]{0:T(1024)S(1)}, f32[2560]{0:T(1024)S(1)}, u32[]{:S(2)}, u32[]{:S(2)}) collective-permute-start(f32[2560]{0:T(1024)S(1)} %add_select_fusion.4), channel_id=1, source_target_pairs={{0,16},{8,24},{16,0},{24,8},{1,17},{9,25},{17,1},{25,9},{2,18},{10... | collective-permute-start | bytes 30728 | tf_op jit(solution)/shard_map/ppermute | solution.py:334
  203.6 24.3 %collective-permute-start.8 = (bf16[8,96,512]{2,1,0:T(8,128)(2,1)}, bf16[8,96,512]{2,1,0:T(8,128)(2,1)}, u32[]{:S(2)}, u32[]{:S(2)}) collective-permute-start(bf16[8,96,512]{2,1,0:T(8,128)(2,1)} %get-tuple-element.45), channel_id=1, source_target_pairs={{0,8},{8,0},{16,24},{24,16},{1,9},{9,1},{17,25},{25,17},{2,10},{10... | collective-permute-start | bytes 2359304 | tf_op jit(solution)/shard_map/ppermute | solution.py:334
  205.3 8.0 %collective-permute-start.25 = (f32[2560]{0:T(1024)S(1)}, f32[2560]{0:T(1024)S(1)}, u32[]{:S(2)}, u32[]{:S(2)}) collective-permute-start(f32[2560]{0:T(1024)S(1)} %add_select_fusion.3), channel_id=1, source_target_pairs={{0,1},{1,0},{2,3},{3,2},{4,5},{5,4},{6,7},{7,6},{8,9},{9,8},{10,11... | collective-permute-start | bytes 30728 | tf_op jit(solution)/shard_map/ppermute | solution.py:334
  213.3 29.1 %collective-permute-start.15 = (bf16[4,288,512]{2,1,0:T(8,128)(2,1)}, bf16[4,288,512]{2,1,0:T(8,128)(2,1)S(1)}, u32[]{:S(2)}, u32[]{:S(2)}) collective-permute-start(bf16[4,288,512]{2,1,0:T(8,128)(2,1)} %slice.244), channel_id=1, source_target_pairs={{0,1},{1,0},{2,3},{3,2},{4,5},{5,4},{6,7},{7,6},{8,9},{9,8},{10,11... | collective-permute-start | bytes 3538952 | tf_op jit(solution)/shard_map/ppermute | solution.py:334
  213.3 5.0 %collective-permute-start.26 = (f32[2560]{0:T(1024)S(1)}, f32[2560]{0:T(1024)S(1)}, u32[]{:S(2)}, u32[]{:S(2)}) collective-permute-start(f32[2560]{0:T(1024)S(1)} %add_select_fusion.2), channel_id=1, source_target_pairs={{0,2},{1,3},{2,0},{3,1},{4,6},{5,7},{6,4},{7,5},{8,10},{9,11},{10,... | collective-permute-start | bytes 30728 | tf_op jit(solution)/shard_map/ppermute | solution.py:334
  218.9 6.3 %collective-permute-start.27 = (f32[2560]{0:T(1024)}, f32[2560]{0:T(1024)}, u32[]{:S(2)}, u32[]{:S(2)}) collective-permute-start(f32[2560]{0:T(1024)} %add_select_fusion.1), channel_id=1, source_target_pairs={{0,4},{1,5},{2,6},{3,7},{4,0},{5,1},{6,2},{7,3},{8,12},{9,13},{10,... | collective-permute-start | bytes 30728 | tf_op jit(solution)/shard_map/ppermute | solution.py:334
  229.5 19.5 %collective-permute-start.9 = (bf16[4,96,512]{2,1,0:T(8,128)(2,1)S(1)}, bf16[4,96,512]{2,1,0:T(8,128)(2,1)S(1)}, u32[]{:S(2)}, u32[]{:S(2)}) collective-permute-start(bf16[4,96,512]{2,1,0:T(8,128)(2,1)S(1)} %slice.232), channel_id=1, source_target_pairs={{0,1},{1,0},{2,3},{3,2},{4,5},{5,4},{6,7},{7,6},{8,9},{9,8},{10,11... | collective-permute-start | bytes 1179656 | tf_op jit(solution)/shard_map/ppermute | solution.py:334
  242.8 21.6 %collective-permute-start.16 = (bf16[2,288,512]{2,1,0:T(8,128)(2,1)S(1)}, bf16[2,288,512]{2,1,0:T(8,128)(2,1)S(1)}, u32[]{:S(2)}, u32[]{:S(2)}) collective-permute-start(bf16[2,288,512]{2,1,0:T(8,128)(2,1)S(1)} %slice.246), channel_id=1, source_target_pairs={{0,2},{1,3},{2,0},{3,1},{4,6},{5,7},{6,4},{7,5},{8,10},{9,11},{10,... | collective-permute-start | bytes 1769480 | tf_op jit(solution)/shard_map/ppermute | solution.py:334
  249.1 9.7 %collective-permute-start.10 = (bf16[2,96,512]{2,1,0:T(8,128)(2,1)S(1)}, bf16[2,96,512]{2,1,0:T(8,128)(2,1)S(1)}, u32[]{:S(2)}, u32[]{:S(2)}) collective-permute-start(bf16[2,96,512]{2,1,0:T(8,128)(2,1)S(1)} %slice.234), channel_id=1, source_target_pairs={{0,2},{1,3},{2,0},{3,1},{4,6},{5,7},{6,4},{7,5},{8,10},{9,11},{10,... | collective-permute-start | bytes 589832 | tf_op jit(solution)/shard_map/ppermute | solution.py:334
  258.9 14.7 %collective-permute-start.11 = (bf16[1,96,512]{2,1,0:T(8,128)(2,1)S(1)}, bf16[1,96,512]{2,1,0:T(8,128)(2,1)S(1)}, u32[]{:S(2)}, u32[]{:S(2)}) collective-permute-start(bf16[1,96,512]{2,1,0:T(8,128)(2,1)S(1)} %slice.236), channel_id=1, source_target_pairs={{0,4},{1,5},{2,6},{3,7},{4,0},{5,1},{6,2},{7,3},{8,12},{9,13},{10,... | collective-permute-start | bytes 294920 | tf_op jit(solution)/shard_map/ppermute | solution.py:334
  264.5 13.5 %collective-permute-start.17 = (bf16[1,288,512]{2,1,0:T(8,128)(2,1)S(1)}, bf16[1,288,512]{2,1,0:T(8,128)(2,1)S(1)}, u32[]{:S(2)}, u32[]{:S(2)}) collective-permute-start(bf16[1,288,512]{2,1,0:T(8,128)(2,1)S(1)} %slice.248), channel_id=1, source_target_pairs={{0,4},{1,5},{2,6},{3,7},{4,0},{5,1},{6,2},{7,3},{8,12},{9,13},{10,... | collective-permute-start | bytes 884744 | tf_op jit(solution)/shard_map/ppermute | solution.py:334
  273.7 6.9 %collective-permute-start.12 = (bf16[96,512]{1,0:T(8,128)(2,1)S(1)}, bf16[96,512]{1,0:T(8,128)(2,1)S(1)}, u32[]{:S(2)}, u32[]{:S(2)}) collective-permute-start(bf16[96,512]{1,0:T(8,128)(2,1)S(1)} %fusion.7), channel_id=1, source_target_pairs={{0,16},{8,24},{16,0},{24,8},{1,17},{9,25},{17,1},{25,9},{2,18},{10... | collective-permute-start | bytes 294920 | tf_op jit(solution)/shard_map/ppermute | solution.py:334
  278.1 7.2 %collective-permute-start.18 = (bf16[288,512]{1,0:T(8,128)(2,1)S(1)}, bf16[288,512]{1,0:T(8,128)(2,1)S(1)}, u32[]{:S(2)}, u32[]{:S(2)}) collective-permute-start(bf16[288,512]{1,0:T(8,128)(2,1)S(1)} %fusion.3), channel_id=1, source_target_pairs={{0,16},{8,24},{16,0},{24,8},{1,17},{9,25},{17,1},{25,9},{2,18},{10... | collective-permute-start | bytes 884744 | tf_op jit(solution)/shard_map/ppermute | solution.py:334
  280.6 4.9 %collective-permute-start.13 = (f32[96,512]{1,0:T(8,128)S(1)}, f32[96,512]{1,0:T(8,128)S(1)}, u32[]{:S(2)}, u32[]{:S(2)}) collective-permute-start(f32[96,512]{1,0:T(8,128)S(1)} %convert_add_fusion.1), channel_id=1, source_target_pairs={{0,8},{8,0},{16,24},{24,16},{1,9},{9,1},{17,25},{25,17},{2,10},{10... | collective-permute-start | bytes 589832 | tf_op jit(solution)/shard_map/ppermute | solution.py:334
  285.4 2.1 collective-permute-start.19
  290.1 28.6 %copy-start.4 = (f32[256,512]{1,0:T(8,128)}, f32[256,512]{1,0:T(8,128)S(1)}, u32[]{:S(2)}) copy-start(f32[256,512]{1,0:T(8,128)S(1)} %get-tuple-element.66) | copy-start | bytes 1572868
  290.1 28.6 %copy-start.5 = (f32[256,512]{1,0:T(8,128)}, f32[256,512]{1,0:T(8,128)S(1)}, u32[]{:S(2)}) copy-start(f32[256,512]{1,0:T(8,128)S(1)} %get-tuple-element.67) | copy-start | bytes 1572868
  293.0 27.9 %copy-start.7 = (f32[64,2048]{1,0:T(8,128)}, f32[64,2048]{1,0:T(8,128)S(1)}, u32[]{:S(2)}) copy-start(f32[64,2048]{1,0:T(8,128)S(1)} %get-tuple-element.69) | copy-start | bytes 1572868
  298.1 3.5 %collective-permute-start.20 = (f32[8]{0:T(128)S(1)}, f32[8]{0:T(128)S(1)}, u32[]{:S(2)}, u32[]{:S(2)}) collective-permute-start(f32[8]{0:T(128)S(1)} %stack.56), channel_id=1, source_target_pairs={{0,1},{1,0},{2,3},{3,2},{4,5},{5,4},{6,7},{7,6},{8,9},{9,8},{10,11... | collective-permute-start | bytes 104 | tf_op jit(solution)/shard_map/ppermute | solution.py:334
  301.7 3.5 %collective-permute-start.21 = (f32[8]{0:T(128)S(1)}, f32[8]{0:T(128)S(1)}, u32[]{:S(2)}, u32[]{:S(2)}) collective-permute-start(f32[8]{0:T(128)S(1)} %add.199), channel_id=1, source_target_pairs={{0,2},{1,3},{2,0},{3,1},{4,6},{5,7},{6,4},{7,5},{8,10},{9,11},{10,... | collective-permute-start | bytes 104 | tf_op jit(solution)/shard_map/ppermute | solution.py:334
  305.2 4.4 %collective-permute-start.22 = (f32[8]{0:T(128)S(1)}, f32[8]{0:T(128)S(1)}, u32[]{:S(2)}, u32[]{:S(2)}) collective-permute-start(f32[8]{0:T(128)S(1)} %add.200), channel_id=1, source_target_pairs={{0,4},{1,5},{2,6},{3,7},{4,0},{5,1},{6,2},{7,3},{8,12},{9,13},{10,... | collective-permute-start | bytes 104 | tf_op jit(solution)/shard_map/ppermute | solution.py:334
  (25 other events, 124.5 us)

commit v2 on v1

v2 whole, which is shorter than its diff:
```python
import functools

import jax
import jax.numpy as jnp
from jax import lax
from jax.experimental import pallas as pl
from jax.experimental.pallas import tpu as pltpu
from jax.sharding import PartitionSpec as P

HEADS = 8
HEAD_DIM = 64
ACT = 11
NBINS = 256
STEP = 5

NORM_EPSILON = 1e-05
BETA_FIRST = 0.9
BETA_SECOND = 0.999
ADAM_EPSILON = 1e-06
RATIO_EPSILON = 1e-06
WEIGHT_DECAY = 0.01
LEARNING_RATE = 0.5
MASKED = -1e30

D = 512
FF = 2048
QB = 64
QUAD = 256
F32 = jnp.float32
BF16 = jnp.bfloat16
VMEM_LIMIT = 60 * 1024 * 1024

NT = (((1,), (1,)), ((), ()))
NN = (((1,), (0,)), ((), ()))
TN = (((0,), (0,)), ((), ()))


def mm(a, b, dims=NN):
    return lax.dot_general(a, b, dims, preferred_element_type=F32)


def pad_rows(v, rows):
    return jnp.concatenate([v, jnp.zeros((rows - v.shape[0], v.shape[1]), v.dtype)], axis=0)


def ln_parts(x):
    center = x - jnp.mean(x, axis=-1, keepdims=True)
    spread = jnp.mean(center * center, axis=-1, keepdims=True)
    rstd = lax.rsqrt(spread + NORM_EPSILON)
    return center * rstd, rstd


def ln_back(grad, xhat, rstd, gain):
    t = grad * gain
    m1 = jnp.mean(t, axis=-1, keepdims=True)
    m2 = jnp.mean(t * xhat, axis=-1, keepdims=True)
    return rstd * (t - m1 - xhat * m2)


def head_masks():
    lane = lax.broadcasted_iota(jnp.int32, (1, QUAD), 1)
    return [jnp.where(lane // HEAD_DIM == h, 1.0, 0.0).astype(BF16) for h in range(4)]


def stack_heads(block, masks):
    return jnp.concatenate([block * m for m in masks], axis=0)


def pair_rows(t):
    tt = t.T
    lane = lax.broadcasted_iota(jnp.int32, (QB, 2 * HEAD_DIM), 1)
    return jnp.where(lane < HEAD_DIM, tt[:QB], tt[QB:])


def place(block, size, side, core):
    if side == 0:
        return pl.multiple_of(block * size, size)
    c = core if side == 1 else 1 - core
    return pl.multiple_of(block * (2 * size) + c * size, size)


def run_copies(copies, start):
    for copy in copies:
        copy.start() if start else copy.wait()


def load_triple(refs, plan, dst, sem, me, core, start):
    for ref, (rels, side) in zip(refs, plan):
        half = ref.shape[1]
        for p, rel in enumerate(rels):
            row = place(jnp.bitwise_xor(me, rel), half, side, core)
            run_copies([pltpu.make_async_copy(ref.at[p], dst.at[pl.ds(row, half)], sem)], start)


def load_mixer(refs, plan, wm, sem, me, core, start):
    for ref, (rels, side) in zip(refs, plan):
        hm = D // wm_blocks(plan) // (1 if side == 0 else 2)
        for p, rel in enumerate(rels):
            row = place(jnp.bitwise_xor(me, rel), hm, side, core)
            run_copies([pltpu.make_async_copy(ref.at[p, pl.ds(0, hm)], wm.at[pl.ds(row, hm)], sem)], start)


def wm_blocks(plan):
    return sum(len(rels) for rels, side in plan if side != 2)


def load_ff(refs, plan, at_mixer, we, wr, sem, me, core, start):
    for ref, (rels, side) in zip(refs, plan):
        halves = 1 if side == 0 else 2
        hm = D // wm_blocks(plan) // halves
        hr = wr.shape[0] // wm_blocks(plan) // halves
        nc = we.shape[1] // D
        at = hm if at_mixer else 0
        for p, rel in enumerate(rels):
            block = jnp.bitwise_xor(me, rel)
            row, rowr = place(block, hm, side, core), place(block, hr, side, core)
            copies = []
            for q in range(nc):
                copies.append(
                    pltpu.make_async_copy(
                        ref.at[p, pl.ds(at + hm * q, hm)],
                        we.at[pl.ds(row, hm), pl.ds(q * D, D)],
                        sem,
                    )
                )
            copies.append(
                pltpu.make_async_copy(ref.at[p, pl.ds(at + hm * nc, hr)], wr.at[pl.ds(rowr, hr)], sem)
            )
            run_copies(copies, start)


def load_ff_true(ref, n_f, parts, we, wr, sem, start):
    hm = D // n_f // parts
    hr = wr.shape[0] // n_f // parts
    nc = we.shape[1] // D
    for d in range(parts):
        for i in range(n_f):
            row, rowr = (i * parts + d) * hm, (i * parts + d) * hr
            src = ref.at[d * n_f + i]
            copies = [
                pltpu.make_async_copy(
                    src.at[pl.ds(hm * q, hm)], we.at[pl.ds(row, hm), pl.ds(q * D, D)], sem
                )
                for q in range(nc)
            ]
            copies.append(pltpu.make_async_copy(src.at[pl.ds(hm * nc, hr)], wr.at[pl.ds(rowr, hr)], sem))
            run_copies(copies, start)


def f1_kernel(plan, nw, idx, lens, tok, norm, *refs):
    w_refs, (tri_out, n1_out, att_out, lse_out, wt, tri, sem) = refs[:nw], refs[nw:]
    e = pl.program_id(0)
    rows = tok.shape[1]
    padded = tri.shape[0]
    rows16 = -(-rows // 16) * 16

    @pl.when(e == 0)
    def _():
        load_triple(w_refs, plan, wt, sem, idx[0], idx[1], True)
        tri[rows16:padded] = jnp.zeros((padded - rows16, 3 * D), BF16)
        load_triple(w_refs, plan, wt, sem, idx[0], idx[1], False)

    xhat, _ = ln_parts(pad_rows(tok[0].astype(F32), rows16))
    n1 = (xhat * norm[0:1] + norm[1:2]).astype(BF16)
    n1_out[0] = n1[:rows]
    t = mm(n1, wt[...]).astype(BF16)
    tri[0:rows16, 0:D] = t[:, 0:D] * jnp.asarray(HEAD_DIM**-0.5, BF16)
    tri[0:rows16, D:] = t[:, D:]
    tri_out[0] = tri[0:rows]

    length = lens[e]
    masks = head_masks()
    lane = lax.broadcasted_iota(jnp.int32, (1, QUAD), 1) % QB
    blocks = -(-rows // QB)
    for g in range(HEADS // 4):
        gl = g * QUAD
        for j in range(blocks):
            ext = min(QB * (j + 1), rows16)
            q4 = stack_heads(tri[QB * j : QB * (j + 1), gl : gl + QUAD], masks)
            s = mm(tri[0:ext, D + gl : D + gl + QUAD], q4, NT)
            kmax = jnp.minimum(lane + QB * j, length - 1)
            krow = lax.broadcasted_iota(jnp.int32, (ext, QUAD), 0)
            s = jnp.where(krow <= kmax, s, MASKED)
            m = jnp.max(s, axis=0, keepdims=True)
            p = jnp.exp(s - m)
            total = jnp.sum(p, axis=0, keepdims=True)
            lse_out[0, pl.ds(g * blocks + j, 1), :] = m + jnp.log(total)
            pb = (p * (1.0 / total)).astype(BF16)
            live = min(QB, rows - QB * j)
            for t2 in range(2):
                cl = 2 * D + gl + 128 * t2
                o = mm(tri[0:ext, cl : cl + 128], pb[:, 128 * t2 : 128 * t2 + 128], TN)
                o = pair_rows(o).astype(BF16)
                att_out[0, QB * j : QB * j + live, gl + 128 * t2 : gl + 128 * t2 + 128] = o[:live]


def put_rows(dst, p, at, src, row, rows):
    for q in range(src.shape[1] // QUAD):
        dst[p, at : at + rows] = src[pl.ds(row, rows), q * QUAD : (q + 1) * QUAD].astype(BF16)
        at += rows
    return at


def grad_sides(refs):
    return [(refs[0], 0)] if len(refs) == 1 else [(refs[0], 1), (refs[1], 2)]


def put_ff_grads(grads, pos, idx, acc_e, acc_r, wr, acc_m=None):
    halves = len(grads)
    hm = D // len(pos) // halves
    hr = wr.shape[0] // len(pos) // halves
    for c in range(wr.shape[0] // D):
        wr[c * D : c * D + D] = acc_r[:, c * D : c * D + D].T.astype(BF16)
    for p, rel in enumerate(pos):
        block = jnp.bitwise_xor(idx[0], rel)
        for dst, side in grad_sides(grads):
            row, rowr = place(block, hm, side, idx[1]), place(block, hr, side, idx[1])
            at = put_rows(dst, p, 0, acc_e, row, hm)
            at = put_rows(dst, p, at, wr, rowr, hr)
            if acc_m is not None:
                put_rows(dst, p, at, acc_m, row, hm)


def ff_chunks(n2, glow, out, g2, we, wr, acc_e, acc_r):
    for c in range(we.shape[1] // D):
        cs = slice(c * D, c * D + D)
        ex = mm(n2, we[:, cs])
        phi = 0.5 + 0.5 * lax.erf(ex * 0.7071067811865476)
        act = (ex * phi).astype(BF16)
        gp = phi + ex * (jnp.exp(-0.5 * ex * ex) * 0.3989422804014327)
        out = out + mm(act, wr[cs])
        gact = mm(glow, wr[cs], NT)
        ge = (gp * gact).astype(BF16)
        g2 = g2 + mm(ge, we[:, cs], NT)
        acc_r[:, cs] += mm(glow, act, TN)
        acc_e[:, cs] += mm(n2, ge, TN)
    return out, g2


def f2a_kernel(plan, nw, pos, nh, idx, att_ref, tok, gl_ref, norm, *refs):
    w_refs, refs = refs[:nw], refs[nw:]
    (hid_out, out_out, g2_out, n2_out), grads, refs = refs[:4], refs[4 : 4 + nh], refs[4 + nh :]
    wm, we, wr, acc_e, acc_r, sem = refs
    e = pl.program_id(0)
    rows = tok.shape[1]
    rows16 = -(-rows // 16) * 16

    @pl.when(e == 0)
    def _():
        load_mixer(w_refs, plan, wm, sem, idx[0], idx[1], True)
        load_ff(w_refs, plan, True, we, wr, sem, idx[0], idx[1], True)
        acc_e[...] = jnp.zeros_like(acc_e)
        acc_r[...] = jnp.zeros_like(acc_r)
        load_mixer(w_refs, plan, wm, sem, idx[0], idx[1], False)
        load_ff(w_refs, plan, True, we, wr, sem, idx[0], idx[1], False)

    att = pad_rows(att_ref[0], rows16)
    glow = pad_rows(gl_ref[0], rows16)
    hidden = pad_rows(tok[0].astype(F32), rows16) + mm(att, wm[...])
    xhat, _ = ln_parts(hidden)
    n2 = (xhat * norm[2:3] + norm[3:4]).astype(BF16)
    hid_out[0] = hidden[:rows]
    n2_out[0] = n2[:rows]
    out, g2 = ff_chunks(n2, glow, hidden, jnp.zeros_like(hidden), we, wr, acc_e, acc_r)
    out_out[0] = out[:rows]
    g2_out[0] = g2[:rows]

    @pl.when(e == pl.num_programs(0) - 1)
    def _():
        put_ff_grads(grads, pos, idx, acc_e, acc_r, wr)


def f2b_kernel(plan, nw, parts, pos, nh, idx, att_ref, hid, out_ref, g2_ref, n2_ref, gl_ref, norm, wb, *refs):
    w_refs, refs = refs[:nw], refs[nw:]
    (block_out, gh_out, ga_out), grads, refs = refs[:3], refs[3 : 3 + nh], refs[3 + nh :]
    ln_out, wm, we, wr, acc_e, acc_r, acc_m, sem = refs
    e = pl.program_id(0)
    rows = hid.shape[1]
    rows16 = -(-rows // 16) * 16

    @pl.when(e == 0)
    def _():
        load_mixer(w_refs, plan, wm, sem, idx[0], idx[1], True)
        load_ff_true(wb, len(pos), parts, we, wr, sem, True)
        acc_e[...] = jnp.zeros_like(acc_e)
        acc_r[...] = jnp.zeros_like(acc_r)
        acc_m[...] = jnp.zeros_like(acc_m)
        ln_out[...] = jnp.zeros_like(ln_out)
        load_mixer(w_refs, plan, wm, sem, idx[0], idx[1], False)
        load_ff_true(wb, len(pos), parts, we, wr, sem, False)

    gain = norm[2:3]
    att = pad_rows(att_ref[0], rows16)
    glow = pad_rows(gl_ref[0], rows16)
    n2 = pad_rows(n2_ref[0], rows16)
    xhat, rstd = ln_parts(pad_rows(hid[0], rows16))
    out, g2 = ff_chunks(
        n2, glow, pad_rows(out_ref[0], rows16), pad_rows(g2_ref[0], rows16), we, wr, acc_e, acc_r
    )
    block_out[0] = out[:rows].astype(BF16)
    gh = glow.astype(F32) + ln_back(g2, xhat, rstd, gain)
    ln_out[0:1] += jnp.sum(g2 * xhat, axis=0, keepdims=True)
    ln_out[1:2] += jnp.sum(g2, axis=0, keepdims=True)
    gb = gh.astype(BF16)
    gh_out[0] = gh[:rows]
    acc_m[...] += mm(att, gb, TN)
    ga_out[0] = mm(gb, wm[...], NT)[:rows].astype(BF16)

    @pl.when(e == pl.num_programs(0) - 1)
    def _():
        put_ff_grads(grads, pos, idx, acc_e, acc_r, wr, acc_m)


def b1_kernel(pos, nh, idx, lens, tri_ref, ga_ref, lse, n1, gtri_out, *refs):
    grads, (tri, ga, gtri, dk, dv, acc) = refs[:nh], refs[nh:]
    e = pl.program_id(0)
    rows = n1.shape[1]
    padded = tri.shape[0]
    rows16 = -(-rows // 16) * 16
    low16 = rows // 16 * 16

    @pl.when(e == 0)
    def _():
        acc[...] = jnp.zeros_like(acc)
        tri[low16:padded] = jnp.zeros((padded - low16, 3 * D), BF16)
        ga[low16:padded] = jnp.zeros((padded - low16, D), BF16)

    tri[0:rows] = tri_ref[0]
    ga[0:rows] = ga_ref[0]
    dk[...] = jnp.zeros_like(dk)
    dv[...] = jnp.zeros_like(dv)
    gtri[:, 0:D] = jnp.zeros((padded, D), BF16)

    length = lens[e]
    masks = head_masks()
    lane = lax.broadcasted_iota(jnp.int32, (1, QUAD), 1) % QB
    blocks = -(-rows // QB)
    for j in range(blocks):

        @pl.when(length > QB * j)
        def _(j=j):
            ext = min(QB * (j + 1), rows16)
            kmax = jnp.minimum(lane + QB * j, length - 1)
            krow = lax.broadcasted_iota(jnp.int32, (ext, QUAD), 0)
            for g in range(HEADS // 4):
                gl = g * QUAD
                gs = slice(gl, gl + QUAD)
                q4 = stack_heads(tri[QB * j : QB * (j + 1), gs], masks)
                do4 = stack_heads(ga[QB * j : QB * (j + 1), gs], masks)
                s = mm(tri[0:ext, D + gl : D + gl + QUAD], q4, NT)
                s = jnp.where(krow <= kmax, s - lse[0, pl.ds(g * blocks + j, 1), :], MASKED)
                p = jnp.exp(s)
                dp = mm(tri[0:ext, 2 * D + gl : 2 * D + gl + QUAD], do4, NT)
                delta = jnp.sum(p * dp, axis=0, keepdims=True)
                ds = (p * (dp - delta)).astype(BF16)
                dv[0:ext, gs] += mm(p.astype(BF16), do4)
                dk[0:ext, gs] += mm(ds, q4)
                for t2 in range(2):
                    cl = D + gl + 128 * t2
                    dq = mm(tri[0:ext, cl : cl + 128], ds[:, 128 * t2 : 128 * t2 + 128], TN)
                    dq = pair_rows(dq) * HEAD_DIM**-0.5
                    gtri[QB * j : QB * (j + 1), gl + 128 * t2 : gl + 128 * t2 + 128] = dq.astype(BF16)

    gtri[0:rows16, D : 2 * D] = dk[...].astype(BF16)
    gtri[0:rows16, 2 * D :] = dv[...].astype(BF16)
    gtri_out[0] = gtri[0:rows]
    acc[...] += mm(pad_rows(n1[0], rows16), gtri[0:rows16], TN)

    @pl.when(e == pl.num_programs(0) - 1)
    def _():
        hm = D // len(pos) // nh
        for p, rel in enumerate(pos):
            block = jnp.bitwise_xor(idx[0], rel)
            for dst, side in grad_sides(grads):
                put_rows(dst, p, 0, acc, place(block, hm, side, idx[1]), hm)


def b2_kernel(plan, nw, idx, gtri, tok, gh, norm, ln2, q_sum, q_top, *refs):
    w_refs, (ig_out, ln_out, wt, sem) = refs[:nw], refs[nw:]
    e = pl.program_id(0)

    @pl.when(e == 0)
    def _():
        load_triple(w_refs, plan, wt, sem, idx[0], idx[1], True)
        ln_out[...] = jnp.zeros_like(ln_out)
        load_triple(w_refs, plan, wt, sem, idx[0], idx[1], False)

    g1 = mm(gtri[0], wt[...], NT)
    xhat, rstd = ln_parts(tok[0].astype(F32))
    ig_out[0] = (gh[0] + ln_back(g1, xhat, rstd, norm[0:1])).astype(BF16)
    ln_out[0:1] += jnp.sum(g1 * xhat, axis=0, keepdims=True)
    ln_out[1:2] += jnp.sum(g1, axis=0, keepdims=True)

    @pl.when(e == pl.num_programs(0) - 1)
    def _():
        ln_out[2:4] = ln2[0:2]
        ln_out[4:5, 0:16] = jnp.sum(q_sum[...].T, axis=0, keepdims=True)
        ln_out[5:6, 0:16] = jnp.max(q_top[...].T, axis=0, keepdims=True)


def q_kernel(total_rows, bo, vh, bins, cnt, sum_out, top_out):
    s = pl.program_id(0)
    block = bo.shape[0]

    @pl.when(s == 0)
    def _():
        sum_out[...] = jnp.zeros_like(sum_out)
        top_out[...] = jnp.full_like(top_out, MASKED)

    place = lax.broadcasted_iota(jnp.int32, (1, block), 1) + s * block
    counted = (cnt[...] > 0) & (place < total_rows)
    binrow = lax.broadcasted_iota(jnp.int32, (NBINS, block), 0)
    for a in range(ACT):
        sc = mm(vh[a * NBINS : (a + 1) * NBINS], bo[...], NT)
        picked = jnp.sum(jnp.where(binrow == bins[a : a + 1], sc, 0.0), axis=0, keepdims=True)
        sum_out[a : a + 1] += jnp.where(counted, picked, 0.0)
        top_out[a : a + 1] = jnp.maximum(top_out[a : a + 1], jnp.where(counted, picked, MASKED))
    sum_out[ACT : ACT + 1] += jnp.where(counted, 1.0, 0.0)


def lamb_moments(weight, gradient, moment_one, moment_two):
    first_new = BETA_FIRST * moment_one + (1.0 - BETA_FIRST) * gradient
    second_new = BETA_SECOND * moment_two + (1.0 - BETA_SECOND) * gradient * gradient
    update = (
        first_new
        * (1.0 / (1.0 - BETA_FIRST**STEP))
        / (jnp.sqrt(second_new * (1.0 / (1.0 - BETA_SECOND**STEP))) + ADAM_EPSILON)
        + WEIGHT_DECAY * weight
    )
    return (first_new, second_new, update)


class Squares:
    def __init__(self):
        self.total = jnp.zeros((8, 128), F32)

    def add(self, lane, weight, update):
        rows = lax.broadcasted_iota(jnp.int32, (8, 128), 0)
        lanes = lax.broadcasted_iota(jnp.int32, (8, 128), 1)
        for row, v in ((6, weight), (7, update)):
            one = jnp.sum(jnp.sum(v * v, axis=0, keepdims=True), axis=1, keepdims=True)
            self.total = self.total + jnp.where((rows == row) & (lanes == lane), one, 0.0)


def lamb_piece(state, outs, grad, rows, cols, squares, lane):
    weight = state[0][rows, cols]
    first_new, second_new, update = lamb_moments(weight, grad, state[1][rows, cols], state[2][rows, cols])
    for out, v in zip(outs, (first_new, second_new, update)):
        out[rows, cols] = v
    squares.add(lane, weight, update)


def core_halves(idx, parts):
    if len(parts) == 1:
        return [lambda rows: parts[0][rows]]
    own = idx[1] == 0
    return [
        lambda rows: jnp.where(own, parts[0][rows], parts[1][rows]),
        lambda rows: jnp.where(own, parts[1][rows], parts[0][rows]),
    ]


def lamb_mlp_kernel(n_f, nh, rows_a, idx, *refs):
    parts, refs = refs[:nh], refs[nh:]
    states = [refs[3 * i : 3 * i + 3] for i in range(3)]
    outs = [refs[9 + 3 * i : 12 + 3 * i] for i in range(3)]
    sq_out = refs[18]
    hm = D // n_f // nh
    h2 = FF // n_f // 2
    hr = h2 // nh
    ne, nd = FF // 2 // QUAD, D // QUAD
    squares = Squares()
    for c, take in enumerate(core_halves(idx, parts)):
        rows = slice(c * hm, c * hm + hm)
        for q in range(nd):
            at = 2 * rows_a + hm * q
            grad = take(slice(at, at + hm))
            lamb_piece(states[0], outs[0], grad, rows, slice(q * QUAD, (q + 1) * QUAD), squares, 1)
        for h in range(2):
            for q in range(ne):
                at = rows_a * h + hm * q
                grad = take(slice(at, at + hm))
                for k in range(QUAD // h2):
                    i = q * (QUAD // h2) + k
                    col = (2 * i + h) * h2
                    lamb_piece(
                        states[1], outs[1], grad[:, k * h2 : (k + 1) * h2], rows,
                        slice(col, col + h2), squares, 2,
                    )
            for q in range(nd):
                at = rows_a * h + hm * ne + hr * q
                grad = take(slice(at, at + hr))
                row = h * h2 + c * hr
                lamb_piece(
                    states[2], outs[2], grad, slice(row, row + hr),
                    slice(q * QUAD, (q + 1) * QUAD), squares, 3,
                )
    sq_out[...] = squares.total


def lamb_triple_kernel(n_f, nh, idx, *refs):
    parts, refs = refs[:nh], refs[nh:]
    sq_in, state, outs, sq_out = refs[0], refs[1:4], refs[4:7], refs[7]
    hm = D // n_f // nh
    squares = Squares()
    for c, take in enumerate(core_halves(idx, parts)):
        for q in range(3 * D // QUAD):
            lamb_piece(
                state, outs, take(slice(hm * q, hm * q + hm)), slice(c * hm, c * hm + hm),
                slice(q * QUAD, (q + 1) * QUAD), squares, 0,
            )
    sq_out[...] = squares.total + sq_in[...]


def merge_small(mine, other):
    row = lax.broadcasted_iota(jnp.int32, mine.shape, 0)
    return jnp.where(row == 5, jnp.maximum(mine, other), mine + other)


def final_kernel(one, two, norms, firsts, seconds, *refs):
    masters, updates, news = refs[:4], refs[4:8], refs[8:12]
    norms_out, first_out, second_out, table_out, mean_out, peak_out = refs[12:]
    small = merge_small(one[...], two[...])
    roots = jnp.sqrt(small[6:8, 0:128])
    for i in range(4):
        ratio = roots[0:1, i : i + 1] / (roots[1:2, i : i + 1] + RATIO_EPSILON)
        news[i][...] = masters[i][...] - LEARNING_RATE * ratio * updates[i][...]
    weight = norms[...]
    first_new, second_new, update = lamb_moments(weight, small[0:4], firsts[...], seconds[...])
    weight_norm = jnp.sqrt(jnp.sum(weight * weight, axis=1, keepdims=True))
    update_norm = jnp.sqrt(jnp.sum(update * update, axis=1, keepdims=True))
    norms_out[...] = weight - LEARNING_RATE * (weight_norm / (update_norm + RATIO_EPSILON)) * update
    first_out[...] = first_new
    second_out[...] = second_new
    row = lax.broadcasted_iota(jnp.int32, (4, 128), 0)
    lane = lax.broadcasted_iota(jnp.int32, (4, 128), 1)
    low = lax.broadcasted_iota(jnp.int32, (1, 128), 1) < 4
    for k, v in enumerate((weight_norm, update_norm)):
        spread = jnp.sum(jnp.where(lane == row + 4, v, 0.0), axis=0, keepdims=True)
        table_out[k : k + 1] = jnp.where(low, roots[k : k + 1], spread)[:, 0:8]
    sums = small[4:5, 0:128]
    mean_out[...] = (sums / jnp.maximum(sums[:, ACT : ACT + 1], 1.0))[:, 0:ACT]
    peak_out[...] = small[5:6, 0:ACT]


def xor_step(v, axis, size, bit):
    return lax.ppermute(v, axis, [(i, i ^ bit) for i in range(size)])


def axis_bits(size):
    bits = []
    b = 1
    while b < size:
        bits.append(b)
        b *= 2
    return bits


def sync(*vs):
    return lax.optimization_barrier(vs)


def halving_positions(order):
    rels = [0]
    for b in reversed(order):
        rels = rels + [r ^ b for r in rels]
    return rels


def add_low(a, b):
    return (a.astype(F32) + b.astype(F32)).astype(BF16)


def const_spec(shape):
    return pl.BlockSpec(shape, lambda *a: (0,) * len(shape))


SMEM = pl.BlockSpec(memory_space=pltpu.SMEM)
ANY = pl.BlockSpec(memory_space=pl.ANY)


def kernel_call(kernel, name, grid, in_specs, out, scratch, us, args, **more):
    return pl.pallas_call(
        kernel,
        grid=grid,
        in_specs=in_specs,
        out_specs=[spec for spec, _ in out],
        out_shape=[shape for _, shape in out],
        scratch_shapes=scratch,
        compiler_params=pltpu.CompilerParams(
            dimension_semantics=("arbitrary",) * len(grid), vmem_limit_bytes=VMEM_LIMIT
        ),
        cost_estimate=pl.CostEstimate(
            flops=us * 300_000_000, bytes_accessed=us * 300_000, transcendentals=0
        ),
        name=name,
        **more,
    )(*args)


def body(n_d, n_f, *args):
    (
        tokens, cotangent, lengths, valid_mask, action_bins, value_head,
        w_triple, w_mixer, w_expand, w_reduce, norm_params,
        first_triple, first_mixer, first_expand, first_reduce, first_norms,
        second_triple, second_mixer, second_expand, second_reduce, second_norms,
    ) = args
    ep, rows, _ = tokens.shape
    flat = ep * rows
    rows16 = -(-rows // 16) * 16
    padded = -(-rows // QB) * QB
    blocks = padded // QB
    me = lax.axis_index("fsdp")
    dp = lax.axis_index("dp")
    core = dp % 2
    idx = jnp.stack([me, core]).astype(jnp.int32)
    shard = D // n_f
    h2 = FF // n_f // 2
    half_ff = FF // 2
    nh = 2 if shard >= 32 else 1
    parts = n_d if shard // n_d >= 16 else 1
    f_bits, d_bits = axis_bits(n_f), axis_bits(n_d)
    steps_f = lambda v, b: xor_step(v, "fsdp", n_f, b)
    steps_d = lambda v, b: xor_step(v, "dp", n_d, b)

    def own_half(w):
        n = w.shape[0] // nh
        return lax.dynamic_slice_in_dim(w, core * n, n, 0) if nh == 2 else w

    def own_part(w):
        n = w.shape[0] // parts
        return lax.dynamic_slice_in_dim(w, dp * n, n, 0) if parts > 1 else w

    def ff_half(w, h):
        return jnp.concatenate([w[:, (2 * i + h) * h2 : (2 * i + h + 1) * h2] for i in range(n_f)], axis=1)

    def under(w):
        return [w[:, q * D : (q + 1) * D] for q in range(w.shape[1] // D)]

    own_t = own_half(w_triple).astype(BF16)
    near, rest_bits = f_bits[0], f_bits[1:]
    rels_a = [0]
    for b in rest_bits:
        rels_a = rels_a + [r ^ b for r in rels_a]
    t_one = jnp.stack([own_t] + [steps_f(own_t, r) for r in rels_a[1:]])
    rels_b = [r ^ near for r in rels_a]

    own_e = w_expand.astype(BF16)
    own_r = w_reduce.astype(BF16)
    own_a = jnp.concatenate(
        [own_half(w_mixer).astype(BF16)]
        + under(own_half(ff_half(own_e, 0)))
        + [own_half(own_r[:h2])],
        axis=0,
    )
    own_b = jnp.concatenate(under(own_part(ff_half(own_e, 1))) + [own_part(own_r[h2:])], axis=0)
    norm_t = norm_params.T
    norm = jnp.concatenate([norm_t, jnp.zeros((4, D), F32)], axis=0)
    places = jnp.arange(rows)
    inside = places[None, :] < lengths[:, None]
    glow = jnp.where(inside[:, :, None], cotangent, jnp.zeros((), BF16))
    counted = ((valid_mask == 1) & inside).astype(jnp.int32).reshape(1, flat)
    bins_t = action_bins.reshape(flat, ACT).T

    ep_block = lambda width: pl.BlockSpec((1, rows, width), lambda e: (e, 0, 0))
    ep_shape = lambda width, dtype: jax.ShapeDtypeStruct((ep, rows, width), dtype)
    low = lambda width: (ep_block(width), ep_shape(width, BF16))
    wide = lambda width: (ep_block(width), ep_shape(width, F32))
    whole = lambda shape: (const_spec(shape), jax.ShapeDtypeStruct(shape, F32))
    norm_spec = const_spec((8, D))
    lse_spec = pl.BlockSpec((1, 16, QUAD), lambda e: (e, 0, 0))
    dma = pltpu.SemaphoreType.DMA
    wt_scratch = pltpu.VMEM((D, 3 * D), BF16)

    waves = list(reversed(f_bits))
    a_buf, a_rels = own_a[None], [0]
    a_buf, own_b, t_one = sync(a_buf, own_b, t_one)
    b_all = lax.all_gather(own_b, ("dp", "fsdp") if parts > 1 else "fsdp", axis=0)
    t_refs, t_plan = [t_one, steps_f(t_one, near)], [(rels_a, nh - 1), (rels_b, nh - 1)]
    got = steps_f(a_buf, waves[0])
    if nh == 2:
        t_refs.append(steps_d(t_one, 1))
        t_plan.append((rels_a, 2))
    a_buf, got, *t_refs = sync(a_buf, got, *t_refs)
    if nh == 2:
        t_refs.append(steps_d(t_refs[1], 1))
        t_plan.append((rels_b, 2))
    nw = len(t_refs)
    a_buf, a_rels = jnp.concatenate([a_buf, got], axis=0), a_rels + [r ^ waves[0] for r in a_rels]
    for b in waves[1:-1]:
        a_buf = jnp.concatenate([a_buf, steps_f(a_buf, b)], axis=0)
        a_rels = a_rels + [r ^ b for r in a_rels]
    glow, bins_t, counted, norm, a_buf, *t_refs = sync(glow, bins_t, counted, norm, a_buf, *t_refs)

    last = waves[-1]
    a_two = steps_f(a_buf, last)
    a_refs, a_plan = [a_buf, a_two], [(a_rels, nh - 1), ([r ^ last for r in a_rels], nh - 1)]
    if nh == 2:
        a_refs.append(steps_d(a_buf, 1))
        a_plan.append((a_rels, 2))
    triple, n1, attended, lse = kernel_call(
        functools.partial(f1_kernel, t_plan, nw), "f1", (ep,),
        [SMEM, SMEM, ep_block(D), norm_spec] + [ANY] * nw,
        [low(3 * D), low(D), low(D), (lse_spec, jax.ShapeDtypeStruct((ep, 16, QUAD), F32))],
        [wt_scratch, pltpu.VMEM((padded, 3 * D), BF16), dma], 23,
        (idx, lengths, tokens, norm, *t_refs),
    )
    attended, *a_refs = sync(attended, *a_refs)
    if nh == 2:
        a_refs.append(steps_d(a_refs[1], 1))
        a_plan.append((a_plan[1][0], 2))
    na = len(a_refs)

    order = f_bits[1:2] + f_bits[:1] + f_bits[2:]
    pos = halving_positions(order)
    hm, hr = shard // nh, h2 // nh
    rows_a = hm * (half_ff // QUAD) + hr * (D // QUAD)
    rows_b = rows_a + hm * (D // QUAD)
    rows_t = 6 * hm
    half = n_f // 2
    grad_out = lambda n: [(const_spec((n_f, n, QUAD)), jax.ShapeDtypeStruct((n_f, n, QUAD), BF16))] * nh
    ff_scratch = [
        pltpu.VMEM((D, D), BF16), pltpu.VMEM((D, half_ff), BF16), pltpu.VMEM((half_ff, D), BF16),
        pltpu.VMEM((D, half_ff), F32), pltpu.VMEM((D, half_ff), F32),
    ]
    hidden, out_part, g2_part, n2, *grads_a = kernel_call(
        functools.partial(f2a_kernel, a_plan, na, pos, nh), "f2a", (ep,),
        [SMEM, ep_block(D), ep_block(D), ep_block(D), norm_spec] + [ANY] * na,
        [wide(D), wide(D), wide(D), low(D)] + grad_out(rows_a),
        ff_scratch + [dma], 25, (idx, attended, tokens, glow, norm, *a_refs),
    )

    def chip_halves(grads, other):
        if nh == 1:
            return grads[0][:half], grads[0][half:]
        return add_low(grads[0][:half], other[:half]), add_low(grads[0][half:], other[half:])

    def other_core(grads):
        return steps_d(grads[1], 1) if nh == 2 else grads[0]

    def halves(keep, got):
        n = keep.shape[0] // 2
        return add_low(keep[:n], got[:n]), add_low(keep[n:], got[n:])

    n2, *grads_a = sync(n2, *grads_a)
    other_a = other_core(grads_a)
    block_out, gh, ga, *rest = kernel_call(
        functools.partial(f2b_kernel, a_plan, na, parts, pos, nh), "f2b", (ep,),
        [SMEM] + [ep_block(D)] * 6 + [norm_spec, ANY] + [ANY] * na,
        [low(D), wide(D), low(D)] + grad_out(rows_b) + [whole((8, D))],
        ff_scratch + [pltpu.VMEM((D, D), F32), dma], 27,
        (idx, attended, hidden, out_part, g2_part, n2, glow, norm, b_all, *a_refs),
    )
    grads_b, ln2 = rest[:nh], rest[nh]
    ga, other_a, *grads_b = sync(ga, other_a, *grads_b)
    other_b = other_core(grads_b)
    keep_a, send_a = chip_halves(grads_a, other_a)
    keep_b, send_b = chip_halves(grads_b, other_b)
    send = jnp.concatenate([send_a, send_b], axis=1)
    keep = jnp.concatenate([keep_a, keep_b], axis=1)
    ga, send, keep = sync(ga, send, keep)

    got = steps_f(send, order[0])
    gtri, *grads_t = kernel_call(
        functools.partial(b1_kernel, pos, nh), "b1", (ep,),
        [SMEM, SMEM, ep_block(3 * D), ep_block(D), lse_spec, ep_block(D)],
        [low(3 * D)] + grad_out(rows_t),
        [
            pltpu.VMEM((padded, 3 * D), BF16), pltpu.VMEM((padded, D), BF16),
            pltpu.VMEM((padded, 3 * D), BF16), pltpu.VMEM((rows16, D), F32),
            pltpu.VMEM((rows16, D), F32), pltpu.VMEM((D, 3 * D), F32),
        ],
        27, (idx, lengths, triple, ga, lse, n1),
    )
    gtri, keep, got, *grads_t = sync(gtri, keep, got, *grads_t)
    other_t = other_core(grads_t)
    keep, send = halves(keep, got)
    keep_t, send_t = chip_halves(grads_t, other_t)
    block_out, keep, send, keep_t, send_t = sync(block_out, keep, send, keep_t, send_t)

    got_t, got = steps_f(send_t, order[0]), steps_f(send, order[1])
    qb = 256
    steps = -(-flat // qb)
    q_sum, q_top = kernel_call(
        functools.partial(q_kernel, flat), "qstat", (steps,),
        [
            pl.BlockSpec((qb, D), lambda s: (s, 0)), const_spec((ACT * NBINS, D)),
            pl.BlockSpec((ACT, qb), lambda s: (0, s)), pl.BlockSpec((1, qb), lambda s: (0, s)),
        ],
        [whole((16, qb))] * 2, [], 10, (block_out.reshape(flat, D), value_head, bins_t, counted),
    )
    gtri, q_sum, keep, got, keep_t, got_t = sync(gtri, q_sum, keep, got, keep_t, got_t)

    late = order[2:]
    keep_t, send_t = halves(keep_t, got_t)
    if late:
        keep, send = halves(keep, got)
    else:
        keep = add_low(keep, got)
    gtri, keep, keep_t, send_t = sync(gtri, keep, keep_t, send_t)
    got_t = steps_f(send_t, order[1])
    if late:
        got = steps_f(send, late[0])
    input_grad, small = kernel_call(
        functools.partial(b2_kernel, t_plan, nw), "b2", (ep,),
        [SMEM, ep_block(3 * D), ep_block(D), ep_block(D), norm_spec]
        + [const_spec((8, D)), const_spec((16, qb)), const_spec((16, qb))] + [ANY] * nw,
        [low(D), whole((8, D))], [wt_scratch, dma], 11,
        (idx, gtri, tokens, gh, norm, ln2, q_sum, q_top, *t_refs),
    )
    small, keep, got, keep_t, got_t = sync(small, keep, got, keep_t, got_t)

    x_bits = d_bits[nh - 1 :]
    if late:
        keep_t, send_t = halves(keep_t, got_t)
        keep = add_low(keep, got)
    else:
        keep_t = add_low(keep_t, got_t)
    for b in late[1:]:
        n = keep.shape[0] // 2
        keep = add_low(keep[:n], steps_f(keep[n:], b))
    red = keep[0]
    for b in x_bits[:-1]:
        red = add_low(red, steps_d(red, b))
    small, red, keep_t = sync(small, red, keep_t)
    if late:
        got_t = steps_f(send_t, late[0])
    got_red = steps_d(red, x_bits[-1])
    small = merge_small(small, steps_d(small, d_bits[0]))
    small, red, got_red, keep_t, got_t = sync(small, red, got_red, keep_t, got_t)
    red = red.astype(F32) + got_red.astype(F32)
    if late:
        keep_t = add_low(keep_t, got_t)
    for b in late[1:]:
        n = keep_t.shape[0] // 2
        keep_t = add_low(keep_t[:n], steps_f(keep_t[n:], b))
    red_t = keep_t[0]
    for b in x_bits[:-1]:
        red_t = add_low(red_t, steps_d(red_t, b))
    red, red_t, small = sync(red, red_t, small)
    got_rt = steps_d(red_t, x_bits[-1])
    for b in d_bits[1:]:
        small = merge_small(small, steps_d(small, b))
    red_parts = [red] + ([steps_d(red, 1)] if nh == 2 else [])

    like = lambda w: whole(w.shape)
    full = lambda *ws: [const_spec(w.shape) for w in ws]
    mlp_state = (
        w_mixer, first_mixer, second_mixer, w_expand, first_expand, second_expand,
        w_reduce, first_reduce, second_reduce,
    )
    *mlp_out, sq_mlp = kernel_call(
        functools.partial(lamb_mlp_kernel, n_f, nh, rows_a), "lamb_mlp", (1,),
        [SMEM] + full(*red_parts, *mlp_state),
        [like(w) for w in (w_mixer, w_expand, w_reduce) for _ in range(3)] + [whole((8, 128))],
        [], 4, (idx, *red_parts, *mlp_state),
    )
    small, sq_mlp, red_t, got_rt = sync(small, sq_mlp, red_t, got_rt)
    red_t = red_t.astype(F32) + got_rt.astype(F32)
    parts_t = [red_t] + ([steps_d(red_t, 1)] if nh == 2 else [])
    tri_state = (w_triple, first_triple, second_triple)
    *tri_out, squares = kernel_call(
        functools.partial(lamb_triple_kernel, n_f, nh), "lamb_triple", (1,),
        [SMEM] + full(*parts_t, sq_mlp, *tri_state),
        [like(w_triple)] * 3 + [whole((8, 128))],
        [], 2, (idx, *parts_t, sq_mlp, *tri_state),
    )

    small = small + jnp.pad(squares, ((0, 0), (0, D - 128)))
    for b in f_bits[:-1]:
        small = merge_small(small, steps_f(small, b))
    small_two = steps_f(small, f_bits[-1])
    masters = (w_triple, w_mixer, w_expand, w_reduce)
    updates = (tri_out[2], mlp_out[2], mlp_out[5], mlp_out[8])
    firsts_t, seconds_t = first_norms.T, second_norms.T
    *news, norms_out, first_out, second_out, norm_table, mean, peak = kernel_call(
        final_kernel, "final", (1,),
        full(small, small_two, norm_t, firsts_t, seconds_t, *masters, *updates),
        [like(w) for w in masters]
        + [whole((4, D))] * 3 + [whole((2, 8)), whole((1, ACT)), whole((1, ACT))],
        [], 3, (small, small_two, norm_t, firsts_t, seconds_t, *masters, *updates),
    )
    return (
        block_out, input_grad, *news,
        tri_out[0], mlp_out[0], mlp_out[3], mlp_out[6],
        tri_out[1], mlp_out[1], mlp_out[4], mlp_out[7],
        norms_out.T, first_out.T, second_out.T, norm_table, mean.reshape(ACT), peak.reshape(ACT),
    )


def solution(mesh):
    n_d, n_f = mesh.shape["dp"], mesh.shape["fsdp"]
    both = ("dp", "fsdp")
    row, rep = P("fsdp", None), P()
    in_specs = (
        P(both, None, None), P(both, None, None), P(both), P(both, None), P(both, None, None), rep,
        row, row, row, row, rep,
        row, row, row, row, rep,
        row, row, row, row, rep,
    )
    out_specs = (
        (P(both, None, None),) * 2 + (row,) * 12 + (rep,) * 6
    )
    return jax.shard_map(
        functools.partial(body, n_d, n_f), mesh=mesh, in_specs=in_specs, out_specs=out_specs,
        check_vma=False,
    )
```

time: 326 us -> 244 us (0.75)
  waiting for transfers between devices: 107 us -> 65.3 us
  starting transfers between devices: 46.4 us -> 22.3 us
  other arithmetic: 28.1 us -> 8.61 us
  local copies, waits for them, and re-layouts: 24 us -> 8.17 us
  Pallas kernels: 110 us -> 124 us
  between operations: 6.9 us -> 14.6 us
    ppermute x28 -> x29, waiting for transfers between devices: 107 us -> 65.2 us  [xor_step(): return lax.ppermute(v, axis, [(i, i ^ bit) for i in range(size)])]
    ppermute x28 -> x29, starting transfers between devices: 46.4 us -> 22.3 us  [xor_step(): return lax.ppermute(v, axis, [(i, i ^ bit) for i in range(size)])]
    pallas_call x5 -> x9, Pallas kernels: 110 us -> 124 us  [kernel_call(): pl.pallas_call(kernel, grid=grid, in_specs=in_specs, out_specs=[spec for...]
    reduce_sum x6 -> x0, other arithmetic: 8.05 us -> none  [the longest x4 5.92 us: body(): squares.append(jnp.sum(update * update))]
    slice x19 -> x3, local copies, waits for them, and re-layouts: 8.23 us -> 1.02 us  [the longest x2 1 us: under(): return [w[:, q * D:(q + 1) * D] for q in range(w.shape[1] // D)]]
    sub x5 -> x0, other arithmetic: 4.53 us -> none  [the longest x4 3.86 us: body(): new_list.append(masters[i] - LEARNING_RATE * ratio * results[i][2])]
    another operation x1, local copies, waits for them, and re-layouts: 5.14 us -> 0.94 us  [body(): t_one = jnp.stack([own_t] + [steps_f(own_t, r) for r in rels_a[1:]])]
    convert_element_type x6 -> x7, other arithmetic: 5.34 us -> 1.38 us  [add_low(): return (a.astype(F32) + b.astype(F32)).astype(BF16)]
  transfers between devices with their start and end apart: 28 -> 30, of which waited for: 18 -> 17; matrix products, arithmetic and copies ran while one was open for 9% -> 4% of each run, Pallas kernels for 20% -> 49%
where the time goes in v2:
time: 244 us; the launch traced here: 243 us
  Pallas kernels  124 us (51%)
  waiting for transfers between devices  65.3 us (27%)
  starting transfers between devices  22.3 us (9%)
  between operations  14.6 us (6%)
  other arithmetic  8.61 us (4%)
  local copies, waits for them, and re-layouts  8.17 us (3%)
    pallas_call x9, Pallas kernels, kernel_call(): pl.pallas_call(kernel, grid=grid, in_specs=in_specs, out_specs=[spec for...  124 us
    ppermute x29, waiting for transfers between devices, xor_step(): return lax.ppermute(v, axis, [(i, i ^ bit) for i in range(size)])  65.2 us
    ppermute x29, starting transfers between devices, xor_step(): return lax.ppermute(v, axis, [(i, i ^ bit) for i in range(size)])  22.3 us
  transfers between devices with their start and end apart: 30, of which 17 were waited for; matrix products, arithmetic and copies ran while one was open for 4% of the time, Pallas kernels for 49%

profile of v2, /device:TPU:0, one launch (start us, length us, event | category | flops | bytes accessed | tf_op | source)
XLA Modules:
  0.0 242.9 jit_solution(1891293980868058337)
XLA Ops:
  8.3 3.1 %collective-permute-start = (bf16[32,1536]{1,0:T(8,128)(2,1)S(1)}, bf16[32,1536]{1,0:T(8,128)(2,1)S(1)}, u32[]{:S(2)}, u32[]{:S(2)}) collective-permute-start(bf16[32,1536]{1,0:T(8,128)(2,1)S(1)} %dynamic-slice_convert_fusion), channel_id=1, source_target_pairs={{0,2},{1,3},{2,0},{3,1},{4,6},{5,7},{6,4},{7,5},{8,10},{9,11},{10,... | collective-permute-start | bytes 294920 | tf_op jit(solution)/shard_map/ppermute | solution.py:547
  11.3 2.6 %collective-permute-start.1 = (bf16[32,1536]{1,0:T(8,128)(2,1)S(1)}, bf16[32,1536]{1,0:T(8,128)(2,1)S(1)}, u32[]{:S(2)}, u32[]{:S(2)}) collective-permute-start(bf16[32,1536]{1,0:T(8,128)(2,1)S(1)} %dynamic-slice_convert_fusion), channel_id=1, source_target_pairs={{0,4},{1,5},{2,6},{3,7},{4,0},{5,1},{6,2},{7,3},{8,12},{9,13},{10,... | collective-permute-start | bytes 294920 | tf_op jit(solution)/shard_map/ppermute | solution.py:547
  18.0 3.8 %collective-permute-done.1 = bf16[32,1536]{1,0:T(8,128)(2,1)S(1)} collective-permute-done((bf16[32,1536]{1,0:T(8,128)(2,1)S(1)}, bf16[32,1536]{1,0:T(8,128)(2,1)S(1)}, u32[]{:S(2)}, u32[]{:S(2)}) %collective-permute-start.1) | collective-permute-done | bytes 98336 | tf_op jit(solution)/shard_map/ppermute | solution.py:547
  21.9 1.6 collective-permute-start.4
  23.5 2.6 %collective-permute-start.3 = (bf16[1,160,512]{2,1,0:T(8,128)(2,1)S(1)}, bf16[1,160,512]{2,1,0:T(8,128)(2,1)S(1)}, u32[]{:S(2)}, u32[]{:S(2)}) collective-permute-start(bf16[1,160,512]{2,1,0:T(8,128)(2,1)S(1)} %maximum_bitcast_fusion), channel_id=1, source_target_pairs={{0,4},{1,5},{2,6},{3,7},{4,0},{5,1},{6,2},{7,3},{8,12},{9,13},{10,... | collective-permute-start | bytes 491528 | tf_op jit(solution)/shard_map/ppermute | solution.py:547
  26.1 8.5 %collective-permute-done.3 = bf16[1,160,512]{2,1,0:T(8,128)(2,1)S(1)} collective-permute-done((bf16[1,160,512]{2,1,0:T(8,128)(2,1)S(1)}, bf16[1,160,512]{2,1,0:T(8,128)(2,1)S(1)}, u32[]{:S(2)}, u32[]{:S(2)}) %collective-permute-start.3) | collective-permute-done | bytes 163872 | tf_op jit(solution)/shard_map/ppermute | solution.py:547
  37.6 1.5 broadcast_select_fusion.gl_ref
  39.1 6.6 %collective-permute-done.6 = bf16[2,160,512]{2,1,0:T(8,128)(2,1)} collective-permute-done((bf16[2,160,512]{2,1,0:T(8,128)(2,1)}, bf16[2,160,512]{2,1,0:T(8,128)(2,1)}, u32[]{:S(2)}, u32[]{:S(2)}) %collective-permute-start.6) | collective-permute-done | bytes 327712 | tf_op jit(solution)/shard_map/ppermute | solution.py:547
  48.2 22.5 %f1.1 = (bf16[6,296,1536]{2,1,0:T(8,128)(2,1)}, bf16[6,296,512]{2,1,0:T(8,128)(2,1)}, bf16[6,296,512]{2,1,0:T(8,128)(2,1)}, f32[6,16,256]{2,1,0:T(8,128)}) custom-call(s32[2]{0:T(128)} %pad_add_fusion.1.idx, s32[6]{0:T(128)} %lens.3, bf16[6,296,512]{2,1,0:T(8,128)(2,1)} %tok.5, f32[8,512]{1,0:T(8,128)} %concatenate.28.norm, bf16[4,32,1536]{2,1,0:T(8,128)(2,1)} %copy-done.3, ...), custom_call_target="tpu_custom_call" | custom-call | flops 6899999744 | bytes 6900000 | tf_op jit(solution)/shard_map/f1/pallas_call | solution.py:583
  71.3 1.7 collective-permute-done.10.refs_3_
  73.9 25.6 %f2a.1 = (f32[6,296,512]{2,1,0:T(8,128)}, f32[6,296,512]{2,1,0:T(8,128)}, f32[6,296,512]{2,1,0:T(8,128)}, bf16[6,296,512]{2,1,0:T(8,128)(2,1)}, bf16[8,256,256]{...) custom-call(s32[2]{0:T(128)} %pad_add_fusion.1.idx, bf16[6,296,512]{2,1,0:T(8,128)(2,1)} %get-tuple-element.152.att_ref, ...), custom_call_target="tpu_custom_call" | custom-call | flops 7500000256 | bytes 7500000 | tf_op jit(solution)/shard_map/f2a/pallas_call | solution.py:583
  99.9 27.3 %f2b.1 = (bf16[6,296,512]{2,1,0:T(8,128)(2,1)}, f32[6,296,512]{2,1,0:T(8,128)}, bf16[6,296,512]{2,1,0:T(8,128)(2,1)}, bf16[8,320,256]{2,1,0:T(8,128)(2,1)}, bf16...) custom-call(s32[2]{0:T(128)} %pad_add_fusion.1.idx, bf16[6,296,512]{2,1,0:T(8,128)(2,1)} %get-tuple-element.152.att_ref, ...), custom_call_target="tpu_custom_call" | custom-call | flops 8099999744 | bytes 8100000 | tf_op jit(solution)/shard_map/f2b/pallas_call | solution.py:583
  127.8 2.9 %collective-permute-done.12 = bf16[8,320,256]{2,1,0:T(8,128)(2,1)S(1)} collective-permute-done((bf16[8,320,256]{2,1,0:T(8,128)(2,1)}, bf16[8,320,256]{2,1,0:T(8,128)(2,1)S(1)}, u32[]{:S(2)}, u32[]{:S(2)}) %collective-permute-start.12) | collective-permute-done | bytes 1310752 | tf_op jit(solution)/shard_map/ppermute | solution.py:547
  131.5 17.3 %b1.1 = (bf16[6,296,1536]{2,1,0:T(8,128)(2,1)}, bf16[8,192,256]{2,1,0:T(8,128)(2,1)}, bf16[8,192,256]{2,1,0:T(8,128)(2,1)}) custom-call(s32[2]{0:T(128)} %pad_add_fusion.1.idx, s32[6]{0:T(128)} %lens.3, bf16[6,296,1536]{2,1,0:T(8,128)(2,1)} %get-tuple-element.166.tri_ref, bf16[6,296,512]{2,1,0:T(8,128)(2,1)} %get-tuple-element.176.ga_ref, ...), custom_call_target="tpu_custom_call" | custom-call | flops 8099999744 | bytes 8100000 | tf_op jit(solution)/shard_map/b1/pallas_call | solution.py:583
  148.8 10.4 %collective-permute-done.13 = bf16[4,576,256]{2,1,0:T(8,128)(2,1)S(1)} collective-permute-done((bf16[4,576,256]{2,1,0:T(8,128)(2,1)S(1)}, bf16[4,576,256]{2,1,0:T(8,128)(2,1)S(1)}, u32[]{:S(2)}, u32[]{:S(2)}) %collective-permute-start.13) | collective-permute-done | bytes 1179680 | tf_op jit(solution)/shard_map/ppermute | solution.py:547
  159.5 2.2 collective-permute-done.14
  163.8 9.5 %qstat.1 = (f32[16,256]{1,0:T(8,128)}, f32[16,256]{1,0:T(8,128)}) custom-call(bf16[1776,512]{1,0:T(8,128)(2,1)} %bitcast.35, bf16[2816,512]{1,0:T(8,128)(2,1)} %vh.1, s32[11,1776]{1,0:T(8,128)} %bitcast.26, s32[1,1776]{1,0:T(1,128)} %reshape.86.cnt), custom_call_target="tpu_custom_call" | custom-call | flops 3000000000 | bytes 3000000 | tf_op jit(solution)/shard_map/qstat/pallas_call | solution.py:583
  174.2 3.1 %collective-permute-done.15 = bf16[2,576,256]{2,1,0:T(8,128)(2,1)S(1)} collective-permute-done((bf16[2,576,256]{2,1,0:T(8,128)(2,1)S(1)}, bf16[2,576,256]{2,1,0:T(8,128)(2,1)S(1)}, u32[]{:S(2)}, u32[]{:S(2)}) %collective-permute-start.15) | collective-permute-done | bytes 589856 | tf_op jit(solution)/shard_map/ppermute | solution.py:547
  179.1 1.8 collective-permute-start.17
  180.8 10.8 %b2.1 = (bf16[6,296,512]{2,1,0:T(8,128)(2,1)}, f32[8,512]{1,0:T(8,128)}) custom-call(s32[2]{0:T(128)} %pad_add_fusion.1.idx, bf16[6,296,1536]{2,1,0:T(8,128)(2,1)} %get-tuple-element.202.gtri, bf16[6,296,512]{2,1,0:T(8,128)(2,1)} %tok.5, f32[6,296,512]{2,1,0:T(8,128)} %get-tuple-element.203.gh, f32[8,512]{1,0:T(8,128)} %concatenate.28.norm, ...), custom_call_target="tpu_custom_call" | custom-call | flops 3300000000 | bytes 3300000 | tf_op jit(solution)/shard_map/b2/pallas_call | solution.py:583
  191.6 2.6 %collective-permute-done.17 = bf16[1,576,256]{2,1,0:T(8,128)(2,1)S(1)} collective-permute-done((bf16[1,576,256]{2,1,0:T(8,128)(2,1)S(1)}, bf16[1,576,256]{2,1,0:T(8,128)(2,1)S(1)}, u32[]{:S(2)}, u32[]{:S(2)}) %collective-permute-start.17) | collective-permute-done | bytes 294944 | tf_op jit(solution)/shard_map/ppermute | solution.py:547
  194.3 1.6 collective-permute-start.20
  197.2 7.0 %collective-permute-done.21 = bf16[1,192,256]{2,1,0:T(8,128)(2,1)S(1)} collective-permute-done((bf16[1,192,256]{2,1,0:T(8,128)(2,1)S(1)}, bf16[1,192,256]{2,1,0:T(8,128)(2,1)S(1)}, u32[]{:S(2)}, u32[]{:S(2)}) %collective-permute-start.21) | collective-permute-done | bytes 98336 | tf_op jit(solution)/shard_map/ppermute | solution.py:547
  204.9 1.5 collective-permute-start.24
  206.4 1.9 collective-permute-done.22
  209.2 5.0 %lamb_mlp.1 = (f32[64,512]{1,0:T(8,128)}, f32[64,512]{1,0:T(8,128)}, f32[64,512]{1,0:T(8,128)}, f32[64,2048]{1,0:T(8,128)}, f32[64,2048]{1,0:T(8,128)}, /*index=...) custom-call(s32[2]{0:T(128)} %pad_add_fusion.1.idx, ...), custom_call_target="tpu_custom_call" | custom-call | flops 1200000000 | bytes 1200000 | tf_op jit(solution)/shard_map/lamb_mlp/pallas_call | solution.py:583
  214.4 1.4 collective-permute-done.25.refs_1_
  216.5 2.8 %lamb_triple.1 = (f32[64,1536]{1,0:T(8,128)}, f32[64,1536]{1,0:T(8,128)}, f32[64,1536]{1,0:T(8,128)}, f32[8,128]{1,0:T(8,128)}) custom-call(s32[2]{0:T(128)} %pad_add_fusion.1.idx, f32[192,256]{1,0:T(8,128)} %copy-done.12, f32[192,256]{1,0:T(8,128)} %copy-done.22, f32[8,128]{1,0:T(8,128)} %get-tuple-element.232.refs_2_, f32[64,1536]{1,0:T(8,128)} %refs_0_.1, ...), custom_call_target="tpu_custom_call" | custom-call | flops 600000000 | bytes 600000 | tf_op jit(solution)/shard_map/lamb_triple/pallas_call | solution.py:583
  220.6 3.2 %collective-permute-done.26 = f32[8,512]{1,0:T(8,128)S(1)} collective-permute-done((f32[8,512]{1,0:T(8,128)S(1)}, f32[8,512]{1,0:T(8,128)S(1)}, u32[]{:S(2)}, u32[]{:S(2)}) %collective-permute-start.26) | collective-permute-done | bytes 16416 | tf_op jit(solution)/shard_map/ppermute | solution.py:547
  223.8 3.7 %collective-permute-done.27 = f32[8,512]{1,0:T(8,128)S(1)} collective-permute-done((f32[8,512]{1,0:T(8,128)S(1)}, f32[8,512]{1,0:T(8,128)S(1)}, u32[]{:S(2)}, u32[]{:S(2)}) %collective-permute-start.27) | collective-permute-done | bytes 16416 | tf_op jit(solution)/shard_map/ppermute | solution.py:547
  228.2 4.1 %collective-permute-done.28.two = f32[8,512]{1,0:T(8,128)S(1)} collective-permute-done((f32[8,512]{1,0:T(8,128)S(1)}, f32[8,512]{1,0:T(8,128)S(1)}, u32[]{:S(2)}, u32[]{:S(2)}) %collective-permute-start.28) | collective-permute-done | bytes 16416 | tf_op jit(solution)/shard_map/ppermute | solution.py:547
  232.9 3.2 %final.1 = (f32[64,1536]{1,0:T(8,128)}, f32[64,512]{1,0:T(8,128)}, f32[64,2048]{1,0:T(8,128)}, f32[256,512]{1,0:T(8,128)}, f32[4,512]{1,0:T(4,128)}, /*index=5*/...) custom-call(f32[8,512]{1,0:T(8,128)} %copy-done.15, ...), custom_call_target="tpu_custom_call" | custom-call | flops 900000000 | bytes 900000 | tf_op jit(solution)/shard_map/final/pallas_call | solution.py:583
  (133 shorter events, 24.9 us)
Async XLA Ops:
  7.2 92.7 %all-gather.3.cloned.1.call-start = ((), (), s32[]{:S(2)}) async-start(), calls=%async_computation | async-start | bytes 2162688 | tf_op jit(solution)/shard_map/all_gather | solution.py:678
  8.3 9.7 %collective-permute-start = (bf16[32,1536]{1,0:T(8,128)(2,1)S(1)}, bf16[32,1536]{1,0:T(8,128)(2,1)S(1)}, u32[]{:S(2)}, u32[]{:S(2)}) collective-permute-start(bf16[32,1536]{1,0:T(8,128)(2,1)S(1)} %dynamic-slice_convert_fusion), channel_id=1, source_target_pairs={{0,2},{1,3},{2,0},{3,1},{4,6},{5,7},{6,4},{7,5},{8,10},{9,11},{10,... | collective-permute-start | bytes 294920 | tf_op jit(solution)/shard_map/ppermute | solution.py:547
  11.3 10.4 %collective-permute-start.1 = (bf16[32,1536]{1,0:T(8,128)(2,1)S(1)}, bf16[32,1536]{1,0:T(8,128)(2,1)S(1)}, u32[]{:S(2)}, u32[]{:S(2)}) collective-permute-start(bf16[32,1536]{1,0:T(8,128)(2,1)S(1)} %dynamic-slice_convert_fusion), channel_id=1, source_target_pairs={{0,4},{1,5},{2,6},{3,7},{4,0},{5,1},{6,2},{7,3},{8,12},{9,13},{10,... | collective-permute-start | bytes 294920 | tf_op jit(solution)/shard_map/ppermute | solution.py:547
  13.9 7.8 %collective-permute-start.2 = (bf16[32,1536]{1,0:T(8,128)(2,1)S(1)}, bf16[32,1536]{1,0:T(8,128)(2,1)S(1)}, u32[]{:S(2)}, u32[]{:S(2)}) collective-permute-start(bf16[32,1536]{1,0:T(8,128)(2,1)S(1)} %dynamic-slice_convert_fusion), channel_id=1, source_target_pairs={{0,6},{1,7},{2,4},{3,5},{4,2},{5,3},{6,0},{7,1},{8,14},{9,15},{10,... | collective-permute-start | bytes 294920 | tf_op jit(solution)/shard_map/ppermute | solution.py:547
  21.9 12.7 %collective-permute-start.4 = (bf16[4,32,1536]{2,1,0:T(8,128)(2,1)S(1)}, bf16[4,32,1536]{2,1,0:T(8,128)(2,1)S(1)}, u32[]{:S(2)}, u32[]{:S(2)}) collective-permute-start(bf16[4,32,1536]{2,1,0:T(8,128)(2,1)S(1)} %pad_maximum_fusion.3.refs_0_), channel_id=1, source_target_pairs={{0,1},{1,0},{2,3},{3,2},{4,5},{5,4},{6,7},{7,6},{8,9},{9,8},{10,11... | collective-permute-start | bytes 1179656 | tf_op jit(solution)/shard_map/ppermute | solution.py:547
  23.5 11.1 %collective-permute-start.5 = (bf16[4,32,1536]{2,1,0:T(8,128)(2,1)S(1)}, bf16[4,32,1536]{2,1,0:T(8,128)(2,1)S(1)}, u32[]{:S(2)}, u32[]{:S(2)}) collective-permute-start(bf16[4,32,1536]{2,1,0:T(8,128)(2,1)S(1)} %pad_maximum_fusion.3.refs_0_), channel_id=1, source_target_pairs={{0,8},{8,0},{16,24},{24,16},{1,9},{9,1},{17,25},{25,17},{2,10},{10... | collective-permute-start | bytes 1179656 | tf_op jit(solution)/shard_map/ppermute | solution.py:547
  23.5 11.1 %collective-permute-start.3 = (bf16[1,160,512]{2,1,0:T(8,128)(2,1)S(1)}, bf16[1,160,512]{2,1,0:T(8,128)(2,1)S(1)}, u32[]{:S(2)}, u32[]{:S(2)}) collective-permute-start(bf16[1,160,512]{2,1,0:T(8,128)(2,1)S(1)} %maximum_bitcast_fusion), channel_id=1, source_target_pairs={{0,4},{1,5},{2,6},{3,7},{4,0},{5,1},{6,2},{7,3},{8,12},{9,13},{10,... | collective-permute-start | bytes 491528 | tf_op jit(solution)/shard_map/ppermute | solution.py:547
  35.5 10.3 %collective-permute-start.6 = (bf16[2,160,512]{2,1,0:T(8,128)(2,1)}, bf16[2,160,512]{2,1,0:T(8,128)(2,1)}, u32[]{:S(2)}, u32[]{:S(2)}) collective-permute-start(bf16[2,160,512]{2,1,0:T(8,128)(2,1)} %pad_maximum_fusion.4), channel_id=1, source_target_pairs={{0,2},{1,3},{2,0},{3,1},{4,6},{5,7},{6,4},{7,5},{8,10},{9,11},{10,... | collective-permute-start | bytes 983048 | tf_op jit(solution)/shard_map/ppermute | solution.py:547
  37.6 9.2 %collective-permute-start.7 = (bf16[4,32,1536]{2,1,0:T(8,128)(2,1)S(1)}, bf16[4,32,1536]{2,1,0:T(8,128)(2,1)S(1)}, u32[]{:S(2)}, u32[]{:S(2)}) collective-permute-start(bf16[4,32,1536]{2,1,0:T(8,128)(2,1)S(1)} %collective-permute-done.4.refs_1_), channel_id=1, source_target_pairs={{0,8},{8,0},{16,24},{24,16},{1,9},{9,1},{17,25},{25,17},{2,10},{10... | collective-permute-start | bytes 1179656 | tf_op jit(solution)/shard_map/ppermute | solution.py:547
  46.8 23.9 %copy-start.7 = (bf16[4,160,512]{2,1,0:T(8,128)(2,1)}, bf16[4,160,512]{2,1,0:T(8,128)(2,1)S(1)}, u32[]{:S(2)}) copy-start(bf16[4,160,512]{2,1,0:T(8,128)(2,1)S(1)} %pad_maximum_fusion.2.refs_0_) | copy-start | bytes 1966084
  46.8 23.9 %collective-permute-start.8 = (bf16[4,160,512]{2,1,0:T(8,128)(2,1)S(1)}, bf16[4,160,512]{2,1,0:T(8,128)(2,1)S(1)}, u32[]{:S(2)}, u32[]{:S(2)}) collective-permute-start(bf16[4,160,512]{2,1,0:T(8,128)(2,1)S(1)} %pad_maximum_fusion.2.refs_0_), channel_id=1, source_target_pairs={{0,1},{1,0},{2,3},{3,2},{4,5},{5,4},{6,7},{7,6},{8,9},{9,8},{10,11... | collective-permute-start | bytes 1966088 | tf_op jit(solution)/shard_map/ppermute | solution.py:547
  47.6 23.2 %collective-permute-start.9 = (bf16[4,160,512]{2,1,0:T(8,128)(2,1)S(1)}, bf16[4,160,512]{2,1,0:T(8,128)(2,1)S(1)}, u32[]{:S(2)}, u32[]{:S(2)}) collective-permute-start(bf16[4,160,512]{2,1,0:T(8,128)(2,1)S(1)} %pad_maximum_fusion.2.refs_0_), channel_id=1, source_target_pairs={{0,8},{8,0},{16,24},{24,16},{1,9},{9,1},{17,25},{25,17},{2,10},{10... | collective-permute-start | bytes 1966088 | tf_op jit(solution)/shard_map/ppermute | solution.py:547
  70.8 2.3 collective-permute-start.10
  99.5 27.8 %collective-permute-start.11 = (bf16[8,256,256]{2,1,0:T(8,128)(2,1)}, bf16[8,256,256]{2,1,0:T(8,128)(2,1)S(1)}, u32[]{:S(2)}, u32[]{:S(2)}) collective-permute-start(bf16[8,256,256]{2,1,0:T(8,128)(2,1)} %get-tuple-element.168), channel_id=1, source_target_pairs={{0,8},{8,0},{16,24},{24,16},{1,9},{9,1},{17,25},{25,17},{2,10},{10... | collective-permute-start | bytes 3145736 | tf_op jit(solution)/shard_map/ppermute | solution.py:547
  99.9 27.6 %copy-start.5 = (bf16[8,256,256]{2,1,0:T(8,128)(2,1)S(1)}, bf16[8,256,256]{2,1,0:T(8,128)(2,1)}, u32[]{:S(2)}) copy-start(bf16[8,256,256]{2,1,0:T(8,128)(2,1)} %get-tuple-element.172) | copy-start | bytes 3145732
  127.3 3.3 %collective-permute-start.12 = (bf16[8,320,256]{2,1,0:T(8,128)(2,1)}, bf16[8,320,256]{2,1,0:T(8,128)(2,1)S(1)}, u32[]{:S(2)}, u32[]{:S(2)}) collective-permute-start(bf16[8,320,256]{2,1,0:T(8,128)(2,1)} %get-tuple-element.175), channel_id=1, source_target_pairs={{0,8},{8,0},{16,24},{24,16},{1,9},{9,1},{17,25},{25,17},{2,10},{10... | collective-permute-start | bytes 3932168 | tf_op jit(solution)/shard_map/ppermute | solution.py:547
  131.2 28.1 %collective-permute-start.13 = (bf16[4,576,256]{2,1,0:T(8,128)(2,1)S(1)}, bf16[4,576,256]{2,1,0:T(8,128)(2,1)S(1)}, u32[]{:S(2)}, u32[]{:S(2)}) collective-permute-start(bf16[4,576,256]{2,1,0:T(8,128)(2,1)S(1)} %pad_maximum_fusion), channel_id=1, source_target_pairs={{0,2},{1,3},{2,0},{3,1},{4,6},{5,7},{6,4},{7,5},{8,10},{9,11},{10,... | collective-permute-start | bytes 3538952 | tf_op jit(solution)/shard_map/ppermute | solution.py:547
  159.2 2.5 %collective-permute-start.14 = (bf16[8,192,256]{2,1,0:T(8,128)(2,1)}, bf16[8,192,256]{2,1,0:T(8,128)(2,1)S(1)}, u32[]{:S(2)}, u32[]{:S(2)}) collective-permute-start(bf16[8,192,256]{2,1,0:T(8,128)(2,1)} %get-tuple-element.187), channel_id=1, source_target_pairs={{0,8},{8,0},{16,24},{24,16},{1,9},{9,1},{17,25},{25,17},{2,10},{10... | collective-permute-start | bytes 2359304 | tf_op jit(solution)/shard_map/ppermute | solution.py:547
  162.0 15.4 %collective-permute-start.15 = (bf16[2,576,256]{2,1,0:T(8,128)(2,1)S(1)}, bf16[2,576,256]{2,1,0:T(8,128)(2,1)S(1)}, u32[]{:S(2)}, u32[]{:S(2)}) collective-permute-start(bf16[2,576,256]{2,1,0:T(8,128)(2,1)S(1)} %get-tuple-element.194), channel_id=1, source_target_pairs={{0,1},{1,0},{2,3},{3,2},{4,5},{5,4},{6,7},{7,6},{8,9},{9,8},{10,11... | collective-permute-start | bytes 1769480 | tf_op jit(solution)/shard_map/ppermute | solution.py:547
  163.4 10.9 %collective-permute-start.16 = (bf16[4,192,256]{2,1,0:T(8,128)(2,1)S(1)}, bf16[4,192,256]{2,1,0:T(8,128)(2,1)S(1)}, u32[]{:S(2)}, u32[]{:S(2)}) collective-permute-start(bf16[4,192,256]{2,1,0:T(8,128)(2,1)S(1)} %get-tuple-element.196), channel_id=1, source_target_pairs={{0,2},{1,3},{2,0},{3,1},{4,6},{5,7},{6,4},{7,5},{8,10},{9,11},{10,... | collective-permute-start | bytes 1179656 | tf_op jit(solution)/shard_map/ppermute | solution.py:547
  177.6 14.0 %collective-permute-start.18 = (bf16[2,192,256]{2,1,0:T(8,128)(2,1)S(1)}, bf16[2,192,256]{2,1,0:T(8,128)(2,1)S(1)}, u32[]{:S(2)}, u32[]{:S(2)}) collective-permute-start(bf16[2,192,256]{2,1,0:T(8,128)(2,1)S(1)} %get-tuple-element.211), channel_id=1, source_target_pairs={{0,1},{1,0},{2,3},{3,2},{4,5},{5,4},{6,7},{7,6},{8,9},{9,8},{10,11... | collective-permute-start | bytes 589832 | tf_op jit(solution)/shard_map/ppermute | solution.py:547
  179.1 15.2 %collective-permute-start.17 = (bf16[1,576,256]{2,1,0:T(8,128)(2,1)S(1)}, bf16[1,576,256]{2,1,0:T(8,128)(2,1)S(1)}, u32[]{:S(2)}, u32[]{:S(2)}) collective-permute-start(bf16[1,576,256]{2,1,0:T(8,128)(2,1)S(1)} %get-tuple-element.264), channel_id=1, source_target_pairs={{0,4},{1,5},{2,6},{3,7},{4,0},{5,1},{6,2},{7,3},{8,12},{9,13},{10,... | collective-permute-start | bytes 884744 | tf_op jit(solution)/shard_map/ppermute | solution.py:547
  194.3 9.8 %collective-permute-start.20 = (bf16[576,256]{1,0:T(8,128)(2,1)S(1)}, bf16[576,256]{1,0:T(8,128)(2,1)S(1)}, u32[]{:S(2)}, u32[]{:S(2)}) collective-permute-start(bf16[576,256]{1,0:T(8,128)(2,1)S(1)} %fusion), channel_id=1, source_target_pairs={{0,16},{8,24},{16,0},{24,8},{1,17},{9,25},{17,1},{25,9},{2,18},{10... | collective-permute-start | bytes 884744 | tf_op jit(solution)/shard_map/ppermute | solution.py:547
  195.9 1.2 collective-permute-start.19
  195.9 8.2 %collective-permute-start.21 = (bf16[1,192,256]{2,1,0:T(8,128)(2,1)S(1)}, bf16[1,192,256]{2,1,0:T(8,128)(2,1)S(1)}, u32[]{:S(2)}, u32[]{:S(2)}) collective-permute-start(bf16[1,192,256]{2,1,0:T(8,128)(2,1)S(1)} %get-tuple-element.268), channel_id=1, source_target_pairs={{0,4},{1,5},{2,6},{3,7},{4,0},{5,1},{6,2},{7,3},{8,12},{9,13},{10,... | collective-permute-start | bytes 294920 | tf_op jit(solution)/shard_map/ppermute | solution.py:547
  204.3 4.1 %collective-permute-start.23 = (f32[576,256]{1,0:T(8,128)S(1)}, f32[576,256]{1,0:T(8,128)S(1)}, u32[]{:S(2)}, u32[]{:S(2)}) collective-permute-start(f32[576,256]{1,0:T(8,128)S(1)} %convert_add_fusion.refs_0_), channel_id=1, source_target_pairs={{0,8},{8,0},{16,24},{24,16},{1,9},{9,1},{17,25},{25,17},{2,10},{10... | collective-permute-start | bytes 1769480 | tf_op jit(solution)/shard_map/ppermute | solution.py:547
  204.3 4.0 %collective-permute-start.22 = (f32[8,512]{1,0:T(8,128)S(1)}, f32[8,512]{1,0:T(8,128)S(1)}, u32[]{:S(2)}, u32[]{:S(2)}) collective-permute-start(f32[8,512]{1,0:T(8,128)S(1)} %add_select_fusion.3), channel_id=1, source_target_pairs={{0,16},{8,24},{16,0},{24,8},{1,17},{9,25},{17,1},{25,9},{2,18},{10... | collective-permute-start | bytes 49160 | tf_op jit(solution)/shard_map/ppermute | solution.py:547
  204.9 9.3 %collective-permute-start.24 = (bf16[192,256]{1,0:T(8,128)(2,1)S(1)}, bf16[192,256]{1,0:T(8,128)(2,1)S(1)}, u32[]{:S(2)}, u32[]{:S(2)}) collective-permute-start(bf16[192,256]{1,0:T(8,128)(2,1)S(1)} %fusion.1), channel_id=1, source_target_pairs={{0,16},{8,24},{16,0},{24,8},{1,17},{9,25},{17,1},{25,9},{2,18},{10... | collective-permute-start | bytes 294920 | tf_op jit(solution)/shard_map/ppermute | solution.py:547
  214.3 1.5 collective-permute-start.25
  220.0 3.7 %collective-permute-start.26 = (f32[8,512]{1,0:T(8,128)S(1)}, f32[8,512]{1,0:T(8,128)S(1)}, u32[]{:S(2)}, u32[]{:S(2)}) collective-permute-start(f32[8,512]{1,0:T(8,128)S(1)} %pad_add_fusion), channel_id=1, source_target_pairs={{0,1},{1,0},{2,3},{3,2},{4,5},{5,4},{6,7},{7,6},{8,9},{9,8},{10,11... | collective-permute-start | bytes 49160 | tf_op jit(solution)/shard_map/ppermute | solution.py:547
  223.8 3.7 %collective-permute-start.27 = (f32[8,512]{1,0:T(8,128)S(1)}, f32[8,512]{1,0:T(8,128)S(1)}, u32[]{:S(2)}, u32[]{:S(2)}) collective-permute-start(f32[8,512]{1,0:T(8,128)S(1)} %add_select_fusion.1), channel_id=1, source_target_pairs={{0,2},{1,3},{2,0},{3,1},{4,6},{5,7},{6,4},{7,5},{8,10},{9,11},{10,... | collective-permute-start | bytes 49160 | tf_op jit(solution)/shard_map/ppermute | solution.py:547
  227.6 4.6 %collective-permute-start.28 = (f32[8,512]{1,0:T(8,128)S(1)}, f32[8,512]{1,0:T(8,128)S(1)}, u32[]{:S(2)}, u32[]{:S(2)}) collective-permute-start(f32[8,512]{1,0:T(8,128)S(1)} %add_select_fusion.one), channel_id=1, source_target_pairs={{0,4},{1,5},{2,6},{3,7},{4,0},{5,1},{6,2},{7,3},{8,12},{9,13},{10,... | collective-permute-start | bytes 49160 | tf_op jit(solution)/shard_map/ppermute | solution.py:547
  (22 other events, 165.2 us)
Sparse Core Ops, SparseCore 0:
  22.0 57.2 all-gather.2

commit v3 on v2

--- a/solution.py
+++ b/solution.py
@@ -25,6 +25,7 @@
 D = 512
 FF = 2048
 QB = 64
+PACK = 256
 QUAD = 256
 F32 = jnp.float32
 BF16 = jnp.bfloat16
@@ -40,6 +41,8 @@
 
 
 def pad_rows(v, rows):
+    if v.shape[0] == rows:
+        return v
     return jnp.concatenate([v, jnp.zeros((rows - v.shape[0], v.shape[1]), v.dtype)], axis=0)
 
 
@@ -66,10 +69,12 @@
     return jnp.concatenate([block * m for m in masks], axis=0)
 
 
-def pair_rows(t):
-    tt = t.T
-    lane = lax.broadcasted_iota(jnp.int32, (QB, 2 * HEAD_DIM), 1)
-    return jnp.where(lane < HEAD_DIM, tt[:QB], tt[QB:])
+def own_lanes(t):
+    head = lax.broadcasted_iota(jnp.int32, (QB, QUAD), 1) // HEAD_DIM
+    out = t[0:QB]
+    for h in range(1, 4):
+        out = jnp.where(head == h, t[QB * h : QB * (h + 1)], out)
+    return out
 
 
 def place(block, size, side, core):
@@ -129,24 +134,6 @@
             run_copies(copies, start)
 
 
-def load_ff_true(ref, n_f, parts, we, wr, sem, start):
-    hm = D // n_f // parts
-    hr = wr.shape[0] // n_f // parts
-    nc = we.shape[1] // D
-    for d in range(parts):
-        for i in range(n_f):
-            row, rowr = (i * parts + d) * hm, (i * parts + d) * hr
-            src = ref.at[d * n_f + i]
-            copies = [
-                pltpu.make_async_copy(
-                    src.at[pl.ds(hm * q, hm)], we.at[pl.ds(row, hm), pl.ds(q * D, D)], sem
-                )
-                for q in range(nc)
-            ]
-            copies.append(pltpu.make_async_copy(src.at[pl.ds(hm * nc, hr)], wr.at[pl.ds(rowr, hr)], sem))
-            run_copies(copies, start)
-
-
 def f1_kernel(plan, nw, idx, lens, tok, norm, *refs):
     w_refs, (tri_out, n1_out, att_out, lse_out, wt, tri, sem) = refs[:nw], refs[nw:]
     e = pl.program_id(0)
@@ -187,38 +174,33 @@
             lse_out[0, pl.ds(g * blocks + j, 1), :] = m + jnp.log(total)
             pb = (p * (1.0 / total)).astype(BF16)
             live = min(QB, rows - QB * j)
-            for t2 in range(2):
-                cl = 2 * D + gl + 128 * t2
-                o = mm(tri[0:ext, cl : cl + 128], pb[:, 128 * t2 : 128 * t2 + 128], TN)
-                o = pair_rows(o).astype(BF16)
-                att_out[0, QB * j : QB * j + live, gl + 128 * t2 : gl + 128 * t2 + 128] = o[:live]
-
-
-def put_rows(dst, p, at, src, row, rows):
+            o = own_lanes(mm(pb, tri[0:ext, 2 * D + gl : 2 * D + gl + QUAD], TN)).astype(BF16)
+            att_out[0, QB * j : QB * j + live, gl : gl + QUAD] = o[:live]
+
+
+def put_rows(dst, at_index, at, src, row, rows):
     for q in range(src.shape[1] // QUAD):
-        dst[p, at : at + rows] = src[pl.ds(row, rows), q * QUAD : (q + 1) * QUAD].astype(BF16)
+        dst[(*at_index, slice(at, at + rows))] = src[pl.ds(row, rows), q * QUAD : (q + 1) * QUAD].astype(BF16)
         at += rows
     return at
 
 
-def grad_sides(refs):
-    return [(refs[0], 0)] if len(refs) == 1 else [(refs[0], 1), (refs[1], 2)]
-
-
-def put_ff_grads(grads, pos, idx, acc_e, acc_r, wr, acc_m=None):
-    halves = len(grads)
+def put_ff_grads(keep, send, pos, idx, acc_e, acc_r, wr, acc_m=None):
+    halves, count = keep.shape[:2]
     hm = D // len(pos) // halves
     hr = wr.shape[0] // len(pos) // halves
     for c in range(wr.shape[0] // D):
         wr[c * D : c * D + D] = acc_r[:, c * D : c * D + D].T.astype(BF16)
     for p, rel in enumerate(pos):
         block = jnp.bitwise_xor(idx[0], rel)
-        for dst, side in grad_sides(grads):
+        dst = keep if p < count else send
+        for c in range(halves):
+            side = 0 if halves == 1 else c + 1
             row, rowr = place(block, hm, side, idx[1]), place(block, hr, side, idx[1])
-            at = put_rows(dst, p, 0, acc_e, row, hm)
-            at = put_rows(dst, p, at, wr, rowr, hr)
+            at = put_rows(dst, (c, p % count), 0, acc_e, row, hm)
+            at = put_rows(dst, (c, p % count), at, wr, rowr, hr)
             if acc_m is not None:
-                put_rows(dst, p, at, acc_m, row, hm)
+                put_rows(dst, (c, p % count), at, acc_m, row, hm)
 
 
 def ff_chunks(n2, glow, out, g2, we, wr, acc_e, acc_r):
@@ -231,21 +213,19 @@
         out = out + mm(act, wr[cs])
         gact = mm(glow, wr[cs], NT)
         ge = (gp * gact).astype(BF16)
-        g2 = g2 + mm(ge, we[:, cs], NT)
+        back = mm(ge, we[:, cs], NT)
+        g2 = back if g2 is None else g2 + back
         acc_r[:, cs] += mm(glow, act, TN)
         acc_e[:, cs] += mm(n2, ge, TN)
     return out, g2
 
 
-def f2a_kernel(plan, nw, pos, nh, idx, att_ref, tok, gl_ref, norm, *refs):
+def f2a_kernel(plan, nw, pos, idx, att_ref, tok, gl_ref, norm, *refs):
     w_refs, refs = refs[:nw], refs[nw:]
-    (hid_out, out_out, g2_out, n2_out), grads, refs = refs[:4], refs[4 : 4 + nh], refs[4 + nh :]
-    wm, we, wr, acc_e, acc_r, sem = refs
-    e = pl.program_id(0)
-    rows = tok.shape[1]
-    rows16 = -(-rows // 16) * 16
-
-    @pl.when(e == 0)
+    hid_out, out_out, g2_out, n2_out, keep, send, wm, we, wr, acc_e, acc_r, sem = refs
+    s = pl.program_id(0)
+
+    @pl.when(s == 0)
     def _():
         load_mixer(w_refs, plan, wm, sem, idx[0], idx[1], True)
         load_ff(w_refs, plan, True, we, wr, sem, idx[0], idx[1], True)
@@ -254,66 +234,59 @@
         load_mixer(w_refs, plan, wm, sem, idx[0], idx[1], False)
         load_ff(w_refs, plan, True, we, wr, sem, idx[0], idx[1], False)
 
-    att = pad_rows(att_ref[0], rows16)
-    glow = pad_rows(gl_ref[0], rows16)
-    hidden = pad_rows(tok[0].astype(F32), rows16) + mm(att, wm[...])
+    glow = gl_ref[...]
+    hidden = tok[...].astype(F32) + mm(att_ref[...], wm[...])
     xhat, _ = ln_parts(hidden)
     n2 = (xhat * norm[2:3] + norm[3:4]).astype(BF16)
-    hid_out[0] = hidden[:rows]
-    n2_out[0] = n2[:rows]
-    out, g2 = ff_chunks(n2, glow, hidden, jnp.zeros_like(hidden), we, wr, acc_e, acc_r)
-    out_out[0] = out[:rows]
-    g2_out[0] = g2[:rows]
-
-    @pl.when(e == pl.num_programs(0) - 1)
+    hid_out[...] = hidden
+    n2_out[...] = n2
+    out, g2 = ff_chunks(n2, glow, hidden, None, we, wr, acc_e, acc_r)
+    out_out[...] = out
+    g2_out[...] = g2
+
+    @pl.when(s == pl.num_programs(0) - 1)
     def _():
-        put_ff_grads(grads, pos, idx, acc_e, acc_r, wr)
-
-
-def f2b_kernel(plan, nw, parts, pos, nh, idx, att_ref, hid, out_ref, g2_ref, n2_ref, gl_ref, norm, wb, *refs):
-    w_refs, refs = refs[:nw], refs[nw:]
-    (block_out, gh_out, ga_out), grads, refs = refs[:3], refs[3 : 3 + nh], refs[3 + nh :]
-    ln_out, wm, we, wr, acc_e, acc_r, acc_m, sem = refs
-    e = pl.program_id(0)
-    rows = hid.shape[1]
-    rows16 = -(-rows // 16) * 16
-
-    @pl.when(e == 0)
+        put_ff_grads(keep, send, pos, idx, acc_e, acc_r, wr)
+
+
+def f2b_kernel(plan, nw, pos, idx, att_ref, hid, out_ref, g2_ref, n2_ref, gl_ref, norm, *refs):
+    w_refs, b_refs, refs = refs[:nw], refs[nw : 2 * nw], refs[2 * nw :]
+    block_out, gh_out, ga_out, keep, send, ln_out, wm, we, wr, acc_e, acc_r, acc_m, sem = refs
+    s = pl.program_id(0)
+
+    @pl.when(s == 0)
     def _():
         load_mixer(w_refs, plan, wm, sem, idx[0], idx[1], True)
-        load_ff_true(wb, len(pos), parts, we, wr, sem, True)
+        load_ff(b_refs, plan, False, we, wr, sem, idx[0], idx[1], True)
         acc_e[...] = jnp.zeros_like(acc_e)
         acc_r[...] = jnp.zeros_like(acc_r)
         acc_m[...] = jnp.zeros_like(acc_m)
         ln_out[...] = jnp.zeros_like(ln_out)
         load_mixer(w_refs, plan, wm, sem, idx[0], idx[1], False)
-        load_ff_true(wb, len(pos), parts, we, wr, sem, False)
+        load_ff(b_refs, plan, False, we, wr, sem, idx[0], idx[1], False)
 
     gain = norm[2:3]
-    att = pad_rows(att_ref[0], rows16)
-    glow = pad_rows(gl_ref[0], rows16)
-    n2 = pad_rows(n2_ref[0], rows16)
-    xhat, rstd = ln_parts(pad_rows(hid[0], rows16))
-    out, g2 = ff_chunks(
-        n2, glow, pad_rows(out_ref[0], rows16), pad_rows(g2_ref[0], rows16), we, wr, acc_e, acc_r
-    )
-    block_out[0] = out[:rows].astype(BF16)
+    glow = gl_ref[...]
+    out, g2 = ff_chunks(n2_ref[...], glow, out_ref[...], g2_ref[...], we, wr, acc_e, acc_r)
+    block_out[...] = out.astype(BF16)
+    xhat, rstd = ln_parts(hid[...])
     gh = glow.astype(F32) + ln_back(g2, xhat, rstd, gain)
     ln_out[0:1] += jnp.sum(g2 * xhat, axis=0, keepdims=True)
     ln_out[1:2] += jnp.sum(g2, axis=0, keepdims=True)
     gb = gh.astype(BF16)
-    gh_out[0] = gh[:rows]
-    acc_m[...] += mm(att, gb, TN)
-    ga_out[0] = mm(gb, wm[...], NT)[:rows].astype(BF16)
-
-    @pl.when(e == pl.num_programs(0) - 1)
+    gh_out[...] = gh
+    acc_m[...] += mm(att_ref[...], gb, TN)
+    ga_out[...] = mm(gb, wm[...], NT).astype(BF16)
+
+    @pl.when(s == pl.num_programs(0) - 1)
     def _():
-        put_ff_grads(grads, pos, idx, acc_e, acc_r, wr, acc_m)
+        put_ff_grads(keep, send, pos, idx, acc_e, acc_r, wr, acc_m)
 
 
 def b1_kernel(pos, nh, idx, lens, tri_ref, ga_ref, lse, n1, gtri_out, *refs):
-    grads, (tri, ga, gtri, dk, dv, acc) = refs[:nh], refs[nh:]
+    grads, (tri, ga, gtri, dk, dv, acc, n1p, gtp) = refs[:nh], refs[nh:]
     e = pl.program_id(0)
+    last = pl.num_programs(0) - 1
     rows = n1.shape[1]
     padded = tri.shape[0]
     rows16 = -(-rows // 16) * 16
@@ -355,47 +328,67 @@
                 ds = (p * (dp - delta)).astype(BF16)
                 dv[0:ext, gs] += mm(p.astype(BF16), do4)
                 dk[0:ext, gs] += mm(ds, q4)
-                for t2 in range(2):
-                    cl = D + gl + 128 * t2
-                    dq = mm(tri[0:ext, cl : cl + 128], ds[:, 128 * t2 : 128 * t2 + 128], TN)
-                    dq = pair_rows(dq) * HEAD_DIM**-0.5
-                    gtri[QB * j : QB * (j + 1), gl + 128 * t2 : gl + 128 * t2 + 128] = dq.astype(BF16)
+                dq = own_lanes(mm(ds, tri[0:ext, D + gl : D + gl + QUAD], TN)) * HEAD_DIM**-0.5
+                gtri[QB * j : QB * (j + 1), gs] = dq.astype(BF16)
 
     gtri[0:rows16, D : 2 * D] = dk[...].astype(BF16)
     gtri[0:rows16, 2 * D :] = dv[...].astype(BF16)
     gtri_out[0] = gtri[0:rows]
-    acc[...] += mm(pad_rows(n1[0], rows16), gtri[0:rows16], TN)
-
-    @pl.when(e == pl.num_programs(0) - 1)
+    start = jnp.int32(0)
+    for i in range(lens.shape[0] - 1):
+        start = start + jnp.where(i < e, (lens[i] + 15) // 16, 0)
+    at = pl.multiple_of(start * 16, 16)
+    n1p[pl.ds(at, rows16)] = pad_rows(n1[0], rows16)
+    gtp[pl.ds(at, rows16)] = gtri[0:rows16]
+
+    @pl.when(e == last)
     def _():
+        end = pl.multiple_of(at + rows16, 16)
+        n1p[pl.ds(end, PACK)] = jnp.zeros((PACK, D), BF16)
+        gtp[pl.ds(end, PACK)] = jnp.zeros((PACK, 3 * D), BF16)
+
+        def chunk(i, carry):
+            row = pl.multiple_of(i * PACK, PACK)
+            acc[...] += mm(n1p[pl.ds(row, PACK)], gtp[pl.ds(row, PACK)], TN)
+            return carry
+
+        lax.fori_loop(0, (at + length + PACK - 1) // PACK, chunk, 0)
         hm = D // len(pos) // nh
         for p, rel in enumerate(pos):
             block = jnp.bitwise_xor(idx[0], rel)
-            for dst, side in grad_sides(grads):
-                put_rows(dst, p, 0, acc, place(block, hm, side, idx[1]), hm)
-
-
-def b2_kernel(plan, nw, idx, gtri, tok, gh, norm, ln2, q_sum, q_top, *refs):
-    w_refs, (ig_out, ln_out, wt, sem) = refs[:nw], refs[nw:]
-    e = pl.program_id(0)
-
-    @pl.when(e == 0)
+            for c in range(nh):
+                side = 0 if nh == 1 else c + 1
+                put_rows(grads[c], (p,), 0, acc, place(block, hm, side, idx[1]), hm)
+
+
+def b2_kernel(plan, nw, first, idx, gtri, tok, gh, norm, *refs):
+    w_refs, refs = refs[:nw], refs[nw:]
+    if first:
+        ig_out, ln_out, wt, sem = refs
+    else:
+        _, ln1_a, ln2, q_sum, q_top, ig_out, ln_out, wt, sem = refs
+    s = pl.program_id(0)
+
+    @pl.when(s == 0)
     def _():
         load_triple(w_refs, plan, wt, sem, idx[0], idx[1], True)
         ln_out[...] = jnp.zeros_like(ln_out)
         load_triple(w_refs, plan, wt, sem, idx[0], idx[1], False)
 
-    g1 = mm(gtri[0], wt[...], NT)
-    xhat, rstd = ln_parts(tok[0].astype(F32))
-    ig_out[0] = (gh[0] + ln_back(g1, xhat, rstd, norm[0:1])).astype(BF16)
+    g1 = mm(gtri[...], wt[...], NT)
+    xhat, rstd = ln_parts(tok[...].astype(F32))
+    ig_out[...] = (gh[...] + ln_back(g1, xhat, rstd, norm[0:1])).astype(BF16)
     ln_out[0:1] += jnp.sum(g1 * xhat, axis=0, keepdims=True)
     ln_out[1:2] += jnp.sum(g1, axis=0, keepdims=True)
 
-    @pl.when(e == pl.num_programs(0) - 1)
-    def _():
-        ln_out[2:4] = ln2[0:2]
-        ln_out[4:5, 0:16] = jnp.sum(q_sum[...].T, axis=0, keepdims=True)
-        ln_out[5:6, 0:16] = jnp.max(q_top[...].T, axis=0, keepdims=True)
+    if not first:
+
+        @pl.when(s == pl.num_programs(0) - 1)
+        def _():
+            ln_out[0:2] += ln1_a[0:2]
+            ln_out[2:4] = ln2[0:2]
+            ln_out[4:5, 0:16] = jnp.sum(q_sum[...].T, axis=0, keepdims=True)
+            ln_out[5:6, 0:16] = jnp.max(q_top[...].T, axis=0, keepdims=True)
 
 
 def q_kernel(total_rows, bo, vh, bins, cnt, sum_out, top_out):
@@ -591,7 +584,7 @@
             dimension_semantics=("arbitrary",) * len(grid), vmem_limit_bytes=VMEM_LIMIT
         ),
         cost_estimate=pl.CostEstimate(
-            flops=us * 300_000_000, bytes_accessed=us * 300_000, transcendentals=0
+            flops=us * 20_000_000, bytes_accessed=us * 20_000, transcendentals=0
         ),
         name=name,
         **more,
@@ -618,7 +611,6 @@
     h2 = FF // n_f // 2
     half_ff = FF // 2
     nh = 2 if shard >= 32 else 1
-    parts = n_d if shard // n_d >= 16 else 1
     f_bits, d_bits = axis_bits(n_f), axis_bits(n_d)
     steps_f = lambda v, b: xor_step(v, "fsdp", n_f, b)
     steps_d = lambda v, b: xor_step(v, "dp", n_d, b)
@@ -627,10 +619,6 @@
         n = w.shape[0] // nh
         return lax.dynamic_slice_in_dim(w, core * n, n, 0) if nh == 2 else w
 
-    def own_part(w):
-        n = w.shape[0] // parts
-        return lax.dynamic_slice_in_dim(w, dp * n, n, 0) if parts > 1 else w
-
     def ff_half(w, h):
         return jnp.concatenate([w[:, (2 * i + h) * h2 : (2 * i + h + 1) * h2] for i in range(n_f)], axis=1)
 
@@ -638,30 +626,16 @@
         return [w[:, q * D : (q + 1) * D] for q in range(w.shape[1] // D)]
 
     own_t = own_half(w_triple).astype(BF16)
-    near, rest_bits = f_bits[0], f_bits[1:]
-    rels_a = [0]
-    for b in rest_bits:
-        rels_a = rels_a + [r ^ b for r in rels_a]
-    t_one = jnp.stack([own_t] + [steps_f(own_t, r) for r in rels_a[1:]])
-    rels_b = [r ^ near for r in rels_a]
-
-    own_e = w_expand.astype(BF16)
-    own_r = w_reduce.astype(BF16)
-    own_a = jnp.concatenate(
-        [own_half(w_mixer).astype(BF16)]
-        + under(own_half(ff_half(own_e, 0)))
-        + [own_half(own_r[:h2])],
-        axis=0,
-    )
-    own_b = jnp.concatenate(under(own_part(ff_half(own_e, 1))) + [own_part(own_r[h2:])], axis=0)
+
+    def own_piece(expand, reduce, h, first):
+        rows_h = slice(h * h2, (h + 1) * h2)
+        return jnp.concatenate(
+            first + under(ff_half(own_half(expand), h).astype(BF16)) + [own_half(reduce[rows_h]).astype(BF16)],
+            axis=0,
+        )
+
     norm_t = norm_params.T
     norm = jnp.concatenate([norm_t, jnp.zeros((4, D), F32)], axis=0)
-    places = jnp.arange(rows)
-    inside = places[None, :] < lengths[:, None]
-    glow = jnp.where(inside[:, :, None], cotangent, jnp.zeros((), BF16))
-    counted = ((valid_mask == 1) & inside).astype(jnp.int32).reshape(1, flat)
-    bins_t = action_bins.reshape(flat, ACT).T
-
     ep_block = lambda width: pl.BlockSpec((1, rows, width), lambda e: (e, 0, 0))
     ep_shape = lambda width, dtype: jax.ShapeDtypeStruct((ep, rows, width), dtype)
     low = lambda width: (ep_block(width), ep_shape(width, BF16))
@@ -672,177 +646,224 @@
     dma = pltpu.SemaphoreType.DMA
     wt_scratch = pltpu.VMEM((D, 3 * D), BF16)
 
-    waves = list(reversed(f_bits))
-    a_buf, a_rels = own_a[None], [0]
-    a_buf, own_b, t_one = sync(a_buf, own_b, t_one)
-    b_all = lax.all_gather(own_b, ("dp", "fsdp") if parts > 1 else "fsdp", axis=0)
-    t_refs, t_plan = [t_one, steps_f(t_one, near)], [(rels_a, nh - 1), (rels_b, nh - 1)]
-    got = steps_f(a_buf, waves[0])
+    near = f_bits[0]
+    rels_a = [0]
+    for b in f_bits[1:]:
+        rels_a = rels_a + [r ^ b for r in rels_a]
+    rels_b = [r ^ near for r in rels_a]
+    own_t, w_mixer_0, w_expand_0, w_reduce_0 = sync(own_t, w_mixer, w_expand, w_reduce)
+    t_got = [steps_f(own_t, r) for r in rels_a[1:]]
+    own_a = own_piece(w_expand_0, w_reduce_0, 0, [own_half(w_mixer_0).astype(BF16)])
+    t_one = jnp.stack([own_t, *t_got])
+    t_one, own_a, cotangent, valid_mask, action_bins, w_expand_1, w_reduce_1 = sync(
+        t_one, own_a, cotangent, valid_mask, action_bins, w_expand, w_reduce
+    )
+    t_two = steps_f(t_one, near)
+    t_refs, t_plan = [t_one], [(rels_a, nh - 1)]
     if nh == 2:
         t_refs.append(steps_d(t_one, 1))
         t_plan.append((rels_a, 2))
-    a_buf, got, *t_refs = sync(a_buf, got, *t_refs)
+    a_one = [own_a] + [steps_f(own_a, r) for r in rels_a[1:]]
+    own_b = own_piece(w_expand_1, w_reduce_1, 1, [])
+    b_one = [own_b] + [steps_f(own_b, r) for r in rels_a[1:]]
+    t_refs.append(t_two)
+    t_plan.append((rels_b, nh - 1))
     if nh == 2:
-        t_refs.append(steps_d(t_refs[1], 1))
+        t_refs.append(steps_d(t_two, 1))
         t_plan.append((rels_b, 2))
     nw = len(t_refs)
-    a_buf, a_rels = jnp.concatenate([a_buf, got], axis=0), a_rels + [r ^ waves[0] for r in a_rels]
-    for b in waves[1:-1]:
-        a_buf = jnp.concatenate([a_buf, steps_f(a_buf, b)], axis=0)
-        a_rels = a_rels + [r ^ b for r in a_rels]
-    glow, bins_t, counted, norm, a_buf, *t_refs = sync(glow, bins_t, counted, norm, a_buf, *t_refs)
-
-    last = waves[-1]
-    a_two = steps_f(a_buf, last)
-    a_refs, a_plan = [a_buf, a_two], [(a_rels, nh - 1), ([r ^ last for r in a_rels], nh - 1)]
+    places = jnp.arange(rows)
+    inside = places[None, :] < lengths[:, None]
+    glow = jnp.where(inside[:, :, None], cotangent, jnp.zeros((), BF16))
+    counted = ((valid_mask == 1) & inside).astype(jnp.int32).reshape(1, flat)
+    bins_t = action_bins.reshape(flat, ACT).T
+    a_one = jnp.stack(a_one)
+    glow, bins_t, counted, norm, a_one, *t_refs = sync(glow, bins_t, counted, norm, a_one, *t_refs)
+    a_two = steps_f(a_one, near)
+    a_refs, a_plan = [a_one], [(rels_a, nh - 1)]
     if nh == 2:
-        a_refs.append(steps_d(a_buf, 1))
-        a_plan.append((a_rels, 2))
+        a_refs.append(steps_d(a_one, 1))
+        a_plan.append((rels_a, 2))
     triple, n1, attended, lse = kernel_call(
         functools.partial(f1_kernel, t_plan, nw), "f1", (ep,),
         [SMEM, SMEM, ep_block(D), norm_spec] + [ANY] * nw,
         [low(3 * D), low(D), low(D), (lse_spec, jax.ShapeDtypeStruct((ep, 16, QUAD), F32))],
-        [wt_scratch, pltpu.VMEM((padded, 3 * D), BF16), dma], 23,
+        [wt_scratch, pltpu.VMEM((padded, 3 * D), BF16), dma], 18,
         (idx, lengths, tokens, norm, *t_refs),
     )
-    attended, *a_refs = sync(attended, *a_refs)
+    attended, a_two, *b_one = sync(attended, a_two, *b_one)
+    a_refs.append(a_two)
+    a_plan.append((rels_b, nh - 1))
     if nh == 2:
-        a_refs.append(steps_d(a_refs[1], 1))
-        a_plan.append((a_plan[1][0], 2))
+        a_refs.append(steps_d(a_two, 1))
+        a_plan.append((rels_b, 2))
     na = len(a_refs)
+    b_one = jnp.stack(b_one)
+    attended, b_one, *a_refs = sync(attended, b_one, *a_refs)
+    b_two = steps_f(b_one, near)
+    b_refs = [b_one] + ([steps_d(b_one, 1)] if nh == 2 else [])
 
     order = f_bits[1:2] + f_bits[:1] + f_bits[2:]
+    late = order[2:]
     pos = halving_positions(order)
     hm, hr = shard // nh, h2 // nh
     rows_a = hm * (half_ff // QUAD) + hr * (D // QUAD)
     rows_b = rows_a + hm * (D // QUAD)
     rows_t = 6 * hm
     half = n_f // 2
-    grad_out = lambda n: [(const_spec((n_f, n, QUAD)), jax.ShapeDtypeStruct((n_f, n, QUAD), BF16))] * nh
+    low_out = lambda *shape: (const_spec(shape), jax.ShapeDtypeStruct(shape, BF16))
     ff_scratch = [
         pltpu.VMEM((D, D), BF16), pltpu.VMEM((D, half_ff), BF16), pltpu.VMEM((half_ff, D), BF16),
         pltpu.VMEM((D, half_ff), F32), pltpu.VMEM((D, half_ff), F32),
     ]
-    hidden, out_part, g2_part, n2, *grads_a = kernel_call(
-        functools.partial(f2a_kernel, a_plan, na, pos, nh), "f2a", (ep,),
-        [SMEM, ep_block(D), ep_block(D), ep_block(D), norm_spec] + [ANY] * na,
-        [wide(D), wide(D), wide(D), low(D)] + grad_out(rows_a),
-        ff_scratch + [dma], 25, (idx, attended, tokens, glow, norm, *a_refs),
-    )
-
-    def chip_halves(grads, other):
-        if nh == 1:
-            return grads[0][:half], grads[0][half:]
-        return add_low(grads[0][:half], other[:half]), add_low(grads[0][half:], other[half:])
-
-    def other_core(grads):
-        return steps_d(grads[1], 1) if nh == 2 else grads[0]
+    fl = flat // 3 if flat % 48 == 0 else rows
+    fl_steps = flat // fl
+    fl_block = lambda width, at=0: pl.BlockSpec((fl, width), lambda i: (i + at, 0))
+    fl_low = lambda width: (fl_block(width), jax.ShapeDtypeStruct((flat, width), BF16))
+    fl_wide = lambda width: (fl_block(width), jax.ShapeDtypeStruct((flat, width), F32))
+    tok_flat = tokens.reshape(flat, D)
+    glow = glow.reshape(flat, D)
+    attended = attended.reshape(flat, D)
+    hidden, out_part, g2_part, n2, keep_a, send_a = kernel_call(
+        functools.partial(f2a_kernel, a_plan, na, pos), "f2a", (fl_steps,),
+        [SMEM] + [fl_block(D)] * 3 + [norm_spec] + [ANY] * na,
+        [fl_wide(D)] * 3 + [fl_low(D)] + [low_out(nh, half, rows_a, QUAD)] * 2,
+        ff_scratch + [dma], 22, (idx, attended, tok_flat, glow, norm, *a_refs),
+    )
 
     def halves(keep, got):
-        n = keep.shape[0] // 2
-        return add_low(keep[:n], got[:n]), add_low(keep[n:], got[n:])
-
-    n2, *grads_a = sync(n2, *grads_a)
-    other_a = other_core(grads_a)
-    block_out, gh, ga, *rest = kernel_call(
-        functools.partial(f2b_kernel, a_plan, na, parts, pos, nh), "f2b", (ep,),
-        [SMEM] + [ep_block(D)] * 6 + [norm_spec, ANY] + [ANY] * na,
-        [low(D), wide(D), low(D)] + grad_out(rows_b) + [whole((8, D))],
-        ff_scratch + [pltpu.VMEM((D, D), F32), dma], 27,
-        (idx, attended, hidden, out_part, g2_part, n2, glow, norm, b_all, *a_refs),
-    )
-    grads_b, ln2 = rest[:nh], rest[nh]
-    ga, other_a, *grads_b = sync(ga, other_a, *grads_b)
-    other_b = other_core(grads_b)
-    keep_a, send_a = chip_halves(grads_a, other_a)
-    keep_b, send_b = chip_halves(grads_b, other_b)
-    send = jnp.concatenate([send_a, send_b], axis=1)
-    keep = jnp.concatenate([keep_a, keep_b], axis=1)
-    ga, send, keep = sync(ga, send, keep)
-
-    got = steps_f(send, order[0])
+        n = keep.shape[-3] // 2
+        return add_low(keep[..., :n, :, :], got[..., :n, :, :]), add_low(keep[..., n:, :, :], got[..., n:, :, :])
+
+    def core_pair(total):
+        return (total[0], steps_d(total[1], 1)) if nh == 2 else (total[0], None)
+
+    def core_halves_of(pair):
+        mine, other = pair
+        n = mine.shape[0] // 2
+        return halves(mine, other) if other is not None else (mine[:n], mine[n:])
+
+    def core_add(pair):
+        return add_low(*pair) if pair[1] is not None else pair[0]
+
+    n2, keep_a, send_a, b_two, *b_refs = sync(n2, keep_a, send_a, b_two, *b_refs)
+    b_refs += [b_two] + ([steps_d(b_two, 1)] if nh == 2 else [])
+    n2, keep_a, send_a, *b_refs = sync(n2, keep_a, send_a, *b_refs)
+    got_a = steps_f(send_a, order[0])
+    block_out, gh, ga, keep_b, send_b, ln2 = kernel_call(
+        functools.partial(f2b_kernel, a_plan, na, pos), "f2b", (fl_steps,),
+        [SMEM] + [fl_block(D)] * 6 + [norm_spec] + [ANY] * (2 * na),
+        [fl_low(D), fl_wide(D), fl_low(D)] + [low_out(nh, half, rows_b, QUAD)] * 2 + [whole((8, D))],
+        ff_scratch + [pltpu.VMEM((D, D), F32), dma], 24,
+        (idx, attended, hidden, out_part, g2_part, n2, glow, norm, *a_refs, *b_refs),
+    )
+    ga, keep_a, got_a, keep_b, send_b = sync(ga, keep_a, got_a, keep_b, send_b)
+    keep_a, send_a = halves(keep_a, got_a)
+    ga, keep_a, send_a, keep_b, send_b = sync(ga, keep_a, send_a, keep_b, send_b)
+
+    got_b = steps_f(send_b, order[0])
+    got_a = steps_f(send_a, order[1])
+    pack_rows = ep * rows16 + PACK
     gtri, *grads_t = kernel_call(
         functools.partial(b1_kernel, pos, nh), "b1", (ep,),
         [SMEM, SMEM, ep_block(3 * D), ep_block(D), lse_spec, ep_block(D)],
-        [low(3 * D)] + grad_out(rows_t),
+        [low(3 * D)] + [low_out(n_f, rows_t, QUAD)] * nh,
         [
             pltpu.VMEM((padded, 3 * D), BF16), pltpu.VMEM((padded, D), BF16),
             pltpu.VMEM((padded, 3 * D), BF16), pltpu.VMEM((rows16, D), F32),
             pltpu.VMEM((rows16, D), F32), pltpu.VMEM((D, 3 * D), F32),
+            pltpu.VMEM((pack_rows, D), BF16), pltpu.VMEM((pack_rows, 3 * D), BF16),
         ],
-        27, (idx, lengths, triple, ga, lse, n1),
-    )
-    gtri, keep, got, *grads_t = sync(gtri, keep, got, *grads_t)
-    other_t = other_core(grads_t)
-    keep, send = halves(keep, got)
-    keep_t, send_t = chip_halves(grads_t, other_t)
-    block_out, keep, send, keep_t, send_t = sync(block_out, keep, send, keep_t, send_t)
-
-    got_t, got = steps_f(send_t, order[0]), steps_f(send, order[1])
+        25, (idx, lengths, triple, ga.reshape(ep, rows, D), lse, n1),
+    )
+    gtri, keep_a, got_a, keep_b, got_b, *grads_t = sync(gtri, keep_a, got_a, keep_b, got_b, *grads_t)
+
+    mine_t, other_t = core_pair(grads_t)
+    sum_a = add_low(keep_a, got_a)
+    sum_b = add_low(keep_b, got_b)
+    mine_t, other_t, sum_a, sum_b = sync(mine_t, other_t, sum_a, sum_b)
+    keep_t, send_t = core_halves_of((mine_t, other_t))
+    keep_t, send_t, sum_a, sum_b = sync(keep_t, send_t, sum_a, sum_b)
+    got_t = steps_f(send_t, order[0])
+    pair_b, pair_a = core_pair(sum_b), core_pair(sum_a)
+    keep_b, send_b = core_halves_of(pair_b)
+    block_out, keep_b, send_b = sync(block_out, keep_b, send_b)
+    got_b = steps_f(send_b, order[1])
+
     qb = 256
     steps = -(-flat // qb)
     q_sum, q_top = kernel_call(
         functools.partial(q_kernel, flat), "qstat", (steps,),
         [
-            pl.BlockSpec((qb, D), lambda s: (s, 0)), const_spec((ACT * NBINS, D)),
-            pl.BlockSpec((ACT, qb), lambda s: (0, s)), pl.BlockSpec((1, qb), lambda s: (0, s)),
+            pl.BlockSpec((qb, D), lambda i: (i, 0)), const_spec((ACT * NBINS, D)),
+            pl.BlockSpec((ACT, qb), lambda i: (0, i)), pl.BlockSpec((1, qb), lambda i: (0, i)),
         ],
-        [whole((16, qb))] * 2, [], 10, (block_out.reshape(flat, D), value_head, bins_t, counted),
-    )
-    gtri, q_sum, keep, got, keep_t, got_t = sync(gtri, q_sum, keep, got, keep_t, got_t)
-
-    late = order[2:]
+        [whole((16, qb))] * 2, [], 10, (block_out, value_head, bins_t, counted),
+    )
+    gtri, q_sum, keep_t, got_t, keep_b, got_b = sync(gtri, q_sum, keep_t, got_t, keep_b, got_b)
+    pair_a = sync(*pair_a, q_sum)[:2] if nh == 2 else pair_a
+
+    def b2_call(at, n, gtri, prior, more_in):
+        extra = [] if prior is None else [prior, *more_in]
+        specs = [] if prior is None else [ANY] + [const_spec(v.shape) for v in more_in]
+        more = {} if prior is None else {"input_output_aliases": {5 + nw: 0}}
+        return kernel_call(
+            functools.partial(b2_kernel, t_plan, nw, prior is None), "b2", (n,),
+            [SMEM, fl_block(3 * D, at), fl_block(D, at), fl_block(D, at), norm_spec] + [ANY] * nw + specs,
+            [(fl_block(D, at), jax.ShapeDtypeStruct((flat, D), BF16)), whole((8, D))],
+            [wt_scratch, dma], 6, (idx, gtri, tok_flat, gh, norm, *t_refs, *extra), **more,
+        )
+
     keep_t, send_t = halves(keep_t, got_t)
     if late:
-        keep, send = halves(keep, got)
+        keep_b, send_b = halves(keep_b, got_b)
+        keep_a, send_a = core_halves_of(pair_a)
+        keep_ab = jnp.concatenate([keep_a, keep_b], axis=1)
+        send_ab = jnp.concatenate([send_a, send_b], axis=1)
     else:
-        keep = add_low(keep, got)
-    gtri, keep, keep_t, send_t = sync(gtri, keep, keep_t, send_t)
+        keep_ab = jnp.concatenate([core_add(pair_a), add_low(keep_b, got_b)], axis=1)
+        send_ab = keep_ab
+    gtri_flat = gtri.reshape(flat, 3 * D)
+    gtri_flat, keep_t, send_t, keep_ab, send_ab = sync(gtri_flat, keep_t, send_t, keep_ab, send_ab)
     got_t = steps_f(send_t, order[1])
     if late:
-        got = steps_f(send, late[0])
-    input_grad, small = kernel_call(
-        functools.partial(b2_kernel, t_plan, nw), "b2", (ep,),
-        [SMEM, ep_block(3 * D), ep_block(D), ep_block(D), norm_spec]
-        + [const_spec((8, D)), const_spec((16, qb)), const_spec((16, qb))] + [ANY] * nw,
-        [low(D), whole((8, D))], [wt_scratch, dma], 11,
-        (idx, gtri, tokens, gh, norm, ln2, q_sum, q_top, *t_refs),
-    )
-    small, keep, got, keep_t, got_t = sync(small, keep, got, keep_t, got_t)
-
-    x_bits = d_bits[nh - 1 :]
+        got_ab = steps_f(send_ab, late[0])
+    cut = (fl_steps + 1) // 2
+    ig_part, ln1_a = b2_call(0, cut, gtri_flat, None, ())
+    ig_part, keep_t, got_t = sync(ig_part, keep_t, got_t)
+
+    def finish(keep, bits):
+        for b in bits:
+            n = keep.shape[0] // 2
+            keep = add_low(keep[:n], steps_f(keep[n:], b))
+        return keep[0]
+
     if late:
         keep_t, send_t = halves(keep_t, got_t)
-        keep = add_low(keep, got)
+        keep_t, send_t, keep_ab, got_ab, ig_part = sync(keep_t, send_t, keep_ab, got_ab, ig_part)
+        got_t = steps_f(send_t, late[0])
+        keep_ab = add_low(keep_ab, got_ab)
     else:
         keep_t = add_low(keep_t, got_t)
-    for b in late[1:]:
-        n = keep.shape[0] // 2
-        keep = add_low(keep[:n], steps_f(keep[n:], b))
-    red = keep[0]
+    x_bits = d_bits[nh - 1 :]
+    red = finish(keep_ab, late[1:])
     for b in x_bits[:-1]:
         red = add_low(red, steps_d(red, b))
-    small, red, keep_t = sync(small, red, keep_t)
-    if late:
-        got_t = steps_f(send_t, late[0])
+    red, ig_part = sync(red, ig_part)
     got_red = steps_d(red, x_bits[-1])
-    small = merge_small(small, steps_d(small, d_bits[0]))
-    small, red, got_red, keep_t, got_t = sync(small, red, got_red, keep_t, got_t)
-    red = red.astype(F32) + got_red.astype(F32)
-    if late:
-        keep_t = add_low(keep_t, got_t)
-    for b in late[1:]:
-        n = keep_t.shape[0] // 2
-        keep_t = add_low(keep_t[:n], steps_f(keep_t[n:], b))
-    red_t = keep_t[0]
+    input_grad, small = b2_call(cut, fl_steps - cut, gtri_flat, ig_part, (ln1_a, ln2, q_sum, q_top))
+    small, red, got_red, keep_t, *got_t = sync(small, red, got_red, keep_t, *([got_t] if late else []))
+
+    red_t = finish(add_low(keep_t, got_t[0]) if late else keep_t, late[1:])
     for b in x_bits[:-1]:
         red_t = add_low(red_t, steps_d(red_t, b))
-    red, red_t, small = sync(red, red_t, small)
     got_rt = steps_d(red_t, x_bits[-1])
+    red = red.astype(F32) + got_red.astype(F32)
+    red_parts = [red] + ([steps_d(red, 1)] if nh == 2 else [])
+    small = merge_small(small, steps_d(small, d_bits[0]))
+    small, red_t, *red_parts = sync(small, red_t, *red_parts)
     for b in d_bits[1:]:
         small = merge_small(small, steps_d(small, b))
-    red_parts = [red] + ([steps_d(red, 1)] if nh == 2 else [])
-
     like = lambda w: whole(w.shape)
     full = lambda *ws: [const_spec(w.shape) for w in ws]
     mlp_state = (
@@ -881,7 +902,7 @@
         [], 3, (small, small_two, norm_t, firsts_t, seconds_t, *masters, *updates),
     )
     return (
-        block_out, input_grad, *news,
+        block_out.reshape(ep, rows, D), input_grad.reshape(ep, rows, D), *news,
         tri_out[0], mlp_out[0], mlp_out[3], mlp_out[6],
         tri_out[1], mlp_out[1], mlp_out[4], mlp_out[7],
         norms_out.T, first_out.T, second_out.T, norm_table, mean.reshape(ACT), peak.reshape(ACT),

time: 244 us -> 218 us (0.89)
  waiting for transfers between devices: 65.3 us -> 49.1 us
  between operations: 14.6 us -> 1.43 us
  starting transfers between devices: 22.3 us -> 34.8 us
  Pallas kernels: 124 us -> 115 us
    ppermute x29 -> x38, waiting for transfers between devices: 65.2 us -> 49.1 us  [xor_step(): return lax.ppermute(v, axis, [(i, i ^ bit) for i in range(size)])]
    ppermute x29 -> x38, starting transfers between devices: 22.3 us -> 34.8 us  [xor_step(): return lax.ppermute(v, axis, [(i, i ^ bit) for i in range(size)])]
    pallas_call x9 -> x10, Pallas kernels: 124 us -> 115 us  [kernel_call(): pl.pallas_call(kernel, grid=grid, in_specs=in_specs, out_specs=[spec for...]
    concatenate x5 -> x3, other arithmetic: 2.68 us -> 0.08 us  [the longest x1 0.04 us: body(): keep_ab = jnp.concatenate([keep_a, keep_b], axis=1)]
  transfers between devices with their start and end apart: 30 -> 38, of which waited for: 17 -> 16; matrix products, arithmetic and copies ran while one was open for 4% -> 6% of each run, Pallas kernels for 49% -> 50%
where the time goes in v3:
time: 218 us; the launch traced here: 217 us
  Pallas kernels  115 us (53%)
  waiting for transfers between devices  49.1 us (23%)
  starting transfers between devices  34.8 us (16%)
  local copies, waits for them, and re-layouts  9.6 us (4%)
  other arithmetic  7.51 us (3%)
    pallas_call x10, Pallas kernels, kernel_call(): pl.pallas_call(kernel, grid=grid, in_specs=in_specs, out_specs=[spec for...  115 us
    ppermute x38, waiting for transfers between devices, xor_step(): return lax.ppermute(v, axis, [(i, i ^ bit) for i in range(size)])  49.1 us
    ppermute x38, starting transfers between devices, xor_step(): return lax.ppermute(v, axis, [(i, i ^ bit) for i in range(size)])  34.8 us
  transfers between devices with their start and end apart: 38, of which 16 were waited for; matrix products, arithmetic and copies ran while one was open for 6% of the time, Pallas kernels for 50%

profile of v3, /device:TPU:0, one launch (start us, length us, event | category | flops | bytes accessed | tf_op | source)
XLA Modules:
  0.0 217.3 jit_solution(5739052583330941278)
XLA Ops:
  1.7 3.1 %collective-permute-start = (bf16[32,1536]{1,0:T(8,128)(2,1)S(1)}, bf16[32,1536]{1,0:T(8,128)(2,1)S(1)}, u32[]{:S(2)}, u32[]{:S(2)}) collective-permute-start(bf16[32,1536]{1,0:T(8,128)(2,1)S(1)} %dynamic-slice_convert_fusion.2), channel_id=1, source_target_pairs={{0,2},{1,3},{2,0},{3,1},{4,6},{5,7},{6,4},{7,5},{8,10},{9,11},{10,... | collective-permute-start | bytes 294920 | tf_op jit(solution)/shard_map/ppermute | solution.py:540
  4.8 2.6 %collective-permute-start.1 = (bf16[32,1536]{1,0:T(8,128)(2,1)S(1)}, bf16[32,1536]{1,0:T(8,128)(2,1)S(1)}, u32[]{:S(2)}, u32[]{:S(2)}) collective-permute-start(bf16[32,1536]{1,0:T(8,128)(2,1)S(1)} %dynamic-slice_convert_fusion.2), channel_id=1, source_target_pairs={{0,4},{1,5},{2,6},{3,7},{4,0},{5,1},{6,2},{7,3},{8,12},{9,13},{10,... | collective-permute-start | bytes 294920 | tf_op jit(solution)/shard_map/ppermute | solution.py:540
  10.3 5.0 %collective-permute-done.1 = bf16[32,1536]{1,0:T(8,128)(2,1)S(1)} collective-permute-done((bf16[32,1536]{1,0:T(8,128)(2,1)S(1)}, bf16[32,1536]{1,0:T(8,128)(2,1)S(1)}, u32[]{:S(2)}, u32[]{:S(2)}) %collective-permute-start.1) | collective-permute-done | bytes 98336 | tf_op jit(solution)/shard_map/ppermute | solution.py:540
  15.3 1.6 collective-permute-start.7
  17.5 2.6 %collective-permute-start.4 = (bf16[160,512]{1,0:T(8,128)(2,1)S(1)}, bf16[160,512]{1,0:T(8,128)(2,1)S(1)}, u32[]{:S(2)}, u32[]{:S(2)}) collective-permute-start(bf16[160,512]{1,0:T(8,128)(2,1)S(1)} %pad_maximum_fusion.5), channel_id=1, source_target_pairs={{0,4},{1,5},{2,6},{3,7},{4,0},{5,1},{6,2},{7,3},{8,12},{9,13},{10,... | collective-permute-start | bytes 491528 | tf_op jit(solution)/shard_map/ppermute | solution.py:540
  24.3 3.3 %broadcast_select_fusion = bf16[6,296,512]{2,1,0:T(8,128)(2,1)} fusion(bf16[6,296,512]{2,1,0:T(8,128)(2,1)} %param.22, pred[6,296]{1,0:T(8,128)(4,1)S(1)} %get-tuple-element.369), kind=kLoop, calls=%fused_computation.1 | loop fusion | flops 909312 | bytes 3639024 | tf_op jit(solution)/shard_map/jit(_where)/select_n | solution.py:677
  27.6 3.5 %collective-permute-done.4 = bf16[160,512]{1,0:T(8,128)(2,1)S(1)} collective-permute-done((bf16[160,512]{1,0:T(8,128)(2,1)S(1)}, bf16[160,512]{1,0:T(8,128)(2,1)S(1)}, u32[]{:S(2)}, u32[]{:S(2)}) %collective-permute-start.4) | collective-permute-done | bytes 163872 | tf_op jit(solution)/shard_map/ppermute | solution.py:540
  33.9 2.8 %collective-permute-start.10 = (bf16[128,512]{1,0:T(8,128)(2,1)S(1)}, bf16[128,512]{1,0:T(8,128)(2,1)S(1)}, u32[]{:S(2)}, u32[]{:S(2)}) collective-permute-start(bf16[128,512]{1,0:T(8,128)(2,1)S(1)} %pad_maximum_fusion.6), channel_id=1, source_target_pairs={{0,2},{1,3},{2,0},{3,1},{4,6},{5,7},{6,4},{7,5},{8,10},{9,11},{10,... | collective-permute-start | bytes 393224 | tf_op jit(solution)/shard_map/ppermute | solution.py:540
  36.7 2.4 %collective-permute-start.12 = (bf16[128,512]{1,0:T(8,128)(2,1)S(1)}, bf16[128,512]{1,0:T(8,128)(2,1)S(1)}, u32[]{:S(2)}, u32[]{:S(2)}) collective-permute-start(bf16[128,512]{1,0:T(8,128)(2,1)S(1)} %pad_maximum_fusion.6), channel_id=1, source_target_pairs={{0,6},{1,7},{2,4},{3,5},{4,2},{5,3},{6,0},{7,1},{8,14},{9,15},{10,... | collective-permute-start | bytes 393224 | tf_op jit(solution)/shard_map/ppermute | solution.py:540
  39.8 17.6 %f1.1 = (bf16[6,296,1536]{2,1,0:T(8,128)(2,1)}, bf16[6,296,512]{2,1,0:T(8,128)(2,1)}, bf16[6,296,512]{2,1,0:T(8,128)(2,1)}, f32[6,16,256]{2,1,0:T(8,128)}) custom-call(s32[2]{0:T(128)} %pad_add_fusion.1.idx, s32[6]{0:T(128)} %lens.3, bf16[6,296,512]{2,1,0:T(8,128)(2,1)} %tok.1, f32[8,512]{1,0:T(8,128)} %concatenate.34.norm, bf16[4,32,1536]{2,1,0:T(8,128)(2,1)} %copy-done, ...), custom_call_target="tpu_custom_call" | custom-call | flops 360000000 | bytes 360000 | tf_op jit(solution)/shard_map/f1/pallas_call | solution.py:576
  58.1 1.6 collective-permute-done.14.refs_3_
  59.7 1.5 collective-permute-start.15
  61.4 22.0 %f2a.1 = (f32[1776,512]{1,0:T(8,128)}, f32[1776,512]{1,0:T(8,128)}, f32[1776,512]{1,0:T(8,128)}, bf16[1776,512]{1,0:T(8,128)(2,1)}, bf16[2,4,256,256]{3,2,1,0:T(8,128)(2,1)}, /*index=5*/bf16[2,4,256,256]{3,2,1,0:T(8,128)(2,1)}) custom-call(s32[2]{0:T(128)} %pad_add_fusion.1.idx, bf16[1776,512]{1,0:T(8,128)(2,1)} %bitcast.55, bf16[1776,512]{1,0:T(8,128)(2,1)} %bitcast.48, ...), custom_call_target="tpu_custom_call" | custom-call | flops 440000000 | bytes 440000 | tf_op jit(solution)/shard_map/f2a/pallas_call | solution.py:576
  86.5 24.9 %f2b.1 = (bf16[1776,512]{1,0:T(8,128)(2,1)}, f32[1776,512]{1,0:T(8,128)}, bf16[1776,512]{1,0:T(8,128)(2,1)}, bf16[2,4,320,256]{3,2,1,0:T(8,128)(2,1)}, bf16[2,4,...) custom-call(s32[2]{0:T(128)} %pad_add_fusion.1.idx, bf16[1776,512]{1,0:T(8,128)(2,1)} %bitcast.56, ...), custom_call_target="tpu_custom_call" | custom-call | flops 480000000 | bytes 480000 | tf_op jit(solution)/shard_map/f2b/pallas_call | solution.py:576
  113.4 15.8 %b1.1 = (bf16[6,296,1536]{2,1,0:T(8,128)(2,1)}, bf16[8,192,256]{2,1,0:T(8,128)(2,1)}, bf16[8,192,256]{2,1,0:T(8,128)(2,1)}) custom-call(s32[2]{0:T(128)} %pad_add_fusion.1.idx, s32[6]{0:T(128)} %lens.3, bf16[6,296,1536]{2,1,0:T(8,128)(2,1)} %get-tuple-element.227.tri_ref, bf16[6,296,512]{2,1,0:T(8,128)(2,1)} %bitcast.57, ...), custom_call_target="tpu_custom_call" | custom-call | flops 500000000 | bytes 500000 | tf_op jit(solution)/shard_map/b1/pallas_call | solution.py:576
  129.2 13.5 %collective-permute-done.20 = bf16[2,4,320,256]{3,2,1,0:T(8,128)(2,1)S(1)} collective-permute-done((bf16[2,4,320,256]{3,2,1,0:T(8,128)(2,1)}, bf16[2,4,320,256]{3,2,1,0:T(8,128)(2,1)S(1)}, u32[]{:S(2)}, u32[]{:S(2)}) %collective-permute-start.20) | collective-permute-done | bytes 1310752 | tf_op jit(solution)/shard_map/ppermute | solution.py:540
  143.3 2.0 collective-permute-done.21
  148.7 9.7 %qstat.1 = (f32[16,256]{1,0:T(8,128)}, f32[16,256]{1,0:T(8,128)}) custom-call(bf16[1776,512]{1,0:T(8,128)(2,1)} %get-tuple-element.259.bo, bf16[2816,512]{1,0:T(8,128)(2,1)} %vh.1, s32[11,1776]{1,0:T(8,128)} %bitcast.62, s32[1,1776]{1,0:T(1,128)} %reshape.116.cnt), custom_call_target="tpu_custom_call" | custom-call | flops 200000000 | bytes 200000 | tf_op jit(solution)/shard_map/qstat/pallas_call | solution.py:576
  158.8 1.5 collective-permute-start.26
  161.2 7.8 %b2.2 = (bf16[1776,512]{1,0:T(8,128)(2,1)}, f32[8,512]{1,0:T(8,128)}) custom-call(s32[2]{0:T(128)} %pad_add_fusion.1.idx, bf16[1776,1536]{1,0:T(8,128)(2,1)} %bitcast.51, bf16[1776,512]{1,0:T(8,128)(2,1)} %bitcast.49, f32[1776,512]{1,0:T(8,128)} %get-tuple-element.278.gh, f32[8,512]{1,0:T(8,128)} %concatenate.34.norm, bf16[4,32,1536]{2,1,0:T(8,128)(2,1)} %copy-done, ...), custom_call_target="tpu_custom_call" | custom-call | flops 120000000 | bytes 120000 | tf_op jit(solution)/shard_map/b2/pallas_call | solution.py:576
  169.0 7.3 %collective-permute-done.27 = bf16[1,576,256]{2,1,0:T(8,128)(2,1)S(1)} collective-permute-done((bf16[1,576,256]{2,1,0:T(8,128)(2,1)S(1)}, bf16[1,576,256]{2,1,0:T(8,128)(2,1)S(1)}, u32[]{:S(2)}, u32[]{:S(2)}) %collective-permute-start.27) | collective-permute-done | bytes 294944 | tf_op jit(solution)/shard_map/ppermute | solution.py:540
  176.4 1.6 collective-permute-start.28
  178.0 6.0 %b2.3 = (bf16[1776,512]{1,0:T(8,128)(2,1)}, f32[8,512]{1,0:T(8,128)}) custom-call(s32[2]{0:T(128)} %pad_add_fusion.1.idx, bf16[1776,1536]{1,0:T(8,128)(2,1)} %bitcast.52, bf16[1776,512]{1,0:T(8,128)(2,1)} %bitcast.50, f32[1776,512]{1,0:T(8,128)} %get-tuple-element.278.gh, f32[8,512]{1,0:T(8,128)} %concatenate.34.norm, ...), custom_call_target="tpu_custom_call", output_to_operand_aliasing={{0}: (9, {})} | custom-call | flops 120000000 | bytes 120000 | tf_op jit(solution)/shard_map/b2/pallas_call | solution.py:576
  185.6 1.7 collective-permute-done.30
  188.1 1.6 collective-permute-start.32
  190.1 5.1 %lamb_mlp.1 = (f32[64,512]{1,0:T(8,128)}, f32[64,512]{1,0:T(8,128)}, f32[64,512]{1,0:T(8,128)}, f32[64,2048]{1,0:T(8,128)}, f32[64,2048]{1,0:T(8,128)}, /*index=...) custom-call(s32[2]{0:T(128)} %pad_add_fusion.1.idx, ...), custom_call_target="tpu_custom_call" | custom-call | flops 80000000 | bytes 80000 | tf_op jit(solution)/shard_map/lamb_mlp/pallas_call | solution.py:576
  197.5 2.8 %lamb_triple.1 = (f32[64,1536]{1,0:T(8,128)}, f32[64,1536]{1,0:T(8,128)}, f32[64,1536]{1,0:T(8,128)}, f32[8,128]{1,0:T(8,128)}) custom-call(s32[2]{0:T(128)} %pad_add_fusion.1.idx, f32[192,256]{1,0:T(8,128)} %copy-done.13, f32[192,256]{1,0:T(8,128)} %copy-done.18, f32[8,128]{1,0:T(8,128)} %get-tuple-element.312.refs_2_, f32[64,1536]{1,0:T(8,128)} %refs_0_.1, ...), custom_call_target="tpu_custom_call" | custom-call | flops 40000000 | bytes 40000 | tf_op jit(solution)/shard_map/lamb_triple/pallas_call | solution.py:576
  201.7 3.1 %collective-permute-done.35 = f32[8,512]{1,0:T(8,128)S(1)} collective-permute-done((f32[8,512]{1,0:T(8,128)S(1)}, f32[8,512]{1,0:T(8,128)S(1)}, u32[]{:S(2)}, u32[]{:S(2)}) %collective-permute-start.35) | collective-permute-done | bytes 16416 | tf_op jit(solution)/shard_map/ppermute | solution.py:540
  205.8 2.7 %collective-permute-done.36 = f32[8,512]{1,0:T(8,128)S(1)} collective-permute-done((f32[8,512]{1,0:T(8,128)S(1)}, f32[8,512]{1,0:T(8,128)S(1)}, u32[]{:S(2)}, u32[]{:S(2)}) %collective-permute-start.36) | collective-permute-done | bytes 16416 | tf_op jit(solution)/shard_map/ppermute | solution.py:540
  208.7 2.0 collective-permute-start.37
  210.6 2.6 %collective-permute-done.37.two = f32[8,512]{1,0:T(8,128)S(1)} collective-permute-done((f32[8,512]{1,0:T(8,128)S(1)}, f32[8,512]{1,0:T(8,128)S(1)}, u32[]{:S(2)}, u32[]{:S(2)}) %collective-permute-start.37) | collective-permute-done | bytes 16416 | tf_op jit(solution)/shard_map/ppermute | solution.py:540
  213.9 3.2 %final.1 = (f32[64,1536]{1,0:T(8,128)}, f32[64,512]{1,0:T(8,128)}, f32[64,2048]{1,0:T(8,128)}, f32[256,512]{1,0:T(8,128)}, f32[4,512]{1,0:T(4,128)}, /*index=5*/...) custom-call(f32[8,512]{1,0:T(8,128)} %copy-done.20, ...), custom_call_target="tpu_custom_call" | custom-call | flops 60000000 | bytes 60000 | tf_op jit(solution)/shard_map/final/pallas_call | solution.py:576
  (147 shorter events, 31.5 us)
Async XLA Ops:
  1.7 8.5 %collective-permute-start = (bf16[32,1536]{1,0:T(8,128)(2,1)S(1)}, bf16[32,1536]{1,0:T(8,128)(2,1)S(1)}, u32[]{:S(2)}, u32[]{:S(2)}) collective-permute-start(bf16[32,1536]{1,0:T(8,128)(2,1)S(1)} %dynamic-slice_convert_fusion.2), channel_id=1, source_target_pairs={{0,2},{1,3},{2,0},{3,1},{4,6},{5,7},{6,4},{7,5},{8,10},{9,11},{10,... | collective-permute-start | bytes 294920 | tf_op jit(solution)/shard_map/ppermute | solution.py:540
  4.8 10.4 %collective-permute-start.1 = (bf16[32,1536]{1,0:T(8,128)(2,1)S(1)}, bf16[32,1536]{1,0:T(8,128)(2,1)S(1)}, u32[]{:S(2)}, u32[]{:S(2)}) collective-permute-start(bf16[32,1536]{1,0:T(8,128)(2,1)S(1)} %dynamic-slice_convert_fusion.2), channel_id=1, source_target_pairs={{0,4},{1,5},{2,6},{3,7},{4,0},{5,1},{6,2},{7,3},{8,12},{9,13},{10,... | collective-permute-start | bytes 294920 | tf_op jit(solution)/shard_map/ppermute | solution.py:540
  7.4 7.8 %collective-permute-start.2 = (bf16[32,1536]{1,0:T(8,128)(2,1)S(1)}, bf16[32,1536]{1,0:T(8,128)(2,1)S(1)}, u32[]{:S(2)}, u32[]{:S(2)}) collective-permute-start(bf16[32,1536]{1,0:T(8,128)(2,1)S(1)} %dynamic-slice_convert_fusion.2), channel_id=1, source_target_pairs={{0,6},{1,7},{2,4},{3,5},{4,2},{5,3},{6,0},{7,1},{8,14},{9,15},{10,... | collective-permute-start | bytes 294920 | tf_op jit(solution)/shard_map/ppermute | solution.py:540
  15.3 9.0 %collective-permute-start.7 = (bf16[4,32,1536]{2,1,0:T(8,128)(2,1)S(1)}, bf16[4,32,1536]{2,1,0:T(8,128)(2,1)S(1)}, u32[]{:S(2)}, u32[]{:S(2)}) collective-permute-start(bf16[4,32,1536]{2,1,0:T(8,128)(2,1)S(1)} %pad_maximum_fusion.2.refs_0_), channel_id=1, source_target_pairs={{0,1},{1,0},{2,3},{3,2},{4,5},{5,4},{6,7},{7,6},{8,9},{9,8},{10,11... | collective-permute-start | bytes 1179656 | tf_op jit(solution)/shard_map/ppermute | solution.py:540
  17.5 13.6 %collective-permute-start.4 = (bf16[160,512]{1,0:T(8,128)(2,1)S(1)}, bf16[160,512]{1,0:T(8,128)(2,1)S(1)}, u32[]{:S(2)}, u32[]{:S(2)}) collective-permute-start(bf16[160,512]{1,0:T(8,128)(2,1)S(1)} %pad_maximum_fusion.5), channel_id=1, source_target_pairs={{0,4},{1,5},{2,6},{3,7},{4,0},{5,1},{6,2},{7,3},{8,12},{9,13},{10,... | collective-permute-start | bytes 491528 | tf_op jit(solution)/shard_map/ppermute | solution.py:540
  20.1 11.0 %collective-permute-start.5 = (bf16[160,512]{1,0:T(8,128)(2,1)S(1)}, bf16[160,512]{1,0:T(8,128)(2,1)S(1)}, u32[]{:S(2)}, u32[]{:S(2)}) collective-permute-start(bf16[160,512]{1,0:T(8,128)(2,1)S(1)} %pad_maximum_fusion.5), channel_id=1, source_target_pairs={{0,6},{1,7},{2,4},{3,5},{4,2},{5,3},{6,0},{7,1},{8,14},{9,15},{10,... | collective-permute-start | bytes 491528 | tf_op jit(solution)/shard_map/ppermute | solution.py:540
  21.5 9.8 %collective-permute-start.3 = (bf16[160,512]{1,0:T(8,128)(2,1)S(1)}, bf16[160,512]{1,0:T(8,128)(2,1)S(1)}, u32[]{:S(2)}, u32[]{:S(2)}) collective-permute-start(bf16[160,512]{1,0:T(8,128)(2,1)S(1)} %pad_maximum_fusion.5), channel_id=1, source_target_pairs={{0,2},{1,3},{2,0},{3,1},{4,6},{5,7},{6,4},{7,5},{8,10},{9,11},{10,... | collective-permute-start | bytes 491528 | tf_op jit(solution)/shard_map/ppermute | solution.py:540
  21.5 9.9 %collective-permute-start.6 = (bf16[4,32,1536]{2,1,0:T(8,128)(2,1)S(1)}, bf16[4,32,1536]{2,1,0:T(8,128)(2,1)S(1)}, u32[]{:S(2)}, u32[]{:S(2)}) collective-permute-start(bf16[4,32,1536]{2,1,0:T(8,128)(2,1)S(1)} %pad_maximum_fusion.2.refs_0_), channel_id=1, source_target_pairs={{0,8},{8,0},{16,24},{24,16},{1,9},{9,1},{17,25},{25,17},{2,10},{10... | collective-permute-start | bytes 1179656 | tf_op jit(solution)/shard_map/ppermute | solution.py:540
  24.3 7.0 %collective-permute-start.8 = (bf16[4,32,1536]{2,1,0:T(8,128)(2,1)S(1)}, bf16[4,32,1536]{2,1,0:T(8,128)(2,1)S(1)}, u32[]{:S(2)}, u32[]{:S(2)}) collective-permute-start(bf16[4,32,1536]{2,1,0:T(8,128)(2,1)S(1)} %collective-permute-done.7.refs_2_), channel_id=1, source_target_pairs={{0,8},{8,0},{16,24},{24,16},{1,9},{9,1},{17,25},{25,17},{2,10},{10... | collective-permute-start | bytes 1179656 | tf_op jit(solution)/shard_map/ppermute | solution.py:540
  31.4 26.1 %collective-permute-start.9 = (bf16[4,160,512]{2,1,0:T(8,128)(2,1)S(1)}, bf16[4,160,512]{2,1,0:T(8,128)(2,1)S(1)}, u32[]{:S(2)}, u32[]{:S(2)}) collective-permute-start(bf16[4,160,512]{2,1,0:T(8,128)(2,1)S(1)} %pad_maximum_fusion.refs_0_), channel_id=1, source_target_pairs={{0,1},{1,0},{2,3},{3,2},{4,5},{5,4},{6,7},{7,6},{8,9},{9,8},{10,11... | collective-permute-start | bytes 1966088 | tf_op jit(solution)/shard_map/ppermute | solution.py:540
  33.9 23.4 %collective-permute-start.10 = (bf16[128,512]{1,0:T(8,128)(2,1)S(1)}, bf16[128,512]{1,0:T(8,128)(2,1)S(1)}, u32[]{:S(2)}, u32[]{:S(2)}) collective-permute-start(bf16[128,512]{1,0:T(8,128)(2,1)S(1)} %pad_maximum_fusion.6), channel_id=1, source_target_pairs={{0,2},{1,3},{2,0},{3,1},{4,6},{5,7},{6,4},{7,5},{8,10},{9,11},{10,... | collective-permute-start | bytes 393224 | tf_op jit(solution)/shard_map/ppermute | solution.py:540
  36.7 20.7 %collective-permute-start.11 = (bf16[128,512]{1,0:T(8,128)(2,1)S(1)}, bf16[128,512]{1,0:T(8,128)(2,1)S(1)}, u32[]{:S(2)}, u32[]{:S(2)}) collective-permute-start(bf16[128,512]{1,0:T(8,128)(2,1)S(1)} %pad_maximum_fusion.6), channel_id=1, source_target_pairs={{0,4},{1,5},{2,6},{3,7},{4,0},{5,1},{6,2},{7,3},{8,12},{9,13},{10,... | collective-permute-start | bytes 393224 | tf_op jit(solution)/shard_map/ppermute | solution.py:540
  36.7 20.7 %collective-permute-start.12 = (bf16[128,512]{1,0:T(8,128)(2,1)S(1)}, bf16[128,512]{1,0:T(8,128)(2,1)S(1)}, u32[]{:S(2)}, u32[]{:S(2)}) collective-permute-start(bf16[128,512]{1,0:T(8,128)(2,1)S(1)} %pad_maximum_fusion.6), channel_id=1, source_target_pairs={{0,6},{1,7},{2,4},{3,5},{4,2},{5,3},{6,0},{7,1},{8,14},{9,15},{10,... | collective-permute-start | bytes 393224 | tf_op jit(solution)/shard_map/ppermute | solution.py:540
  39.8 18.3 %collective-permute-start.13 = (bf16[4,160,512]{2,1,0:T(8,128)(2,1)S(1)}, bf16[4,160,512]{2,1,0:T(8,128)(2,1)S(1)}, u32[]{:S(2)}, u32[]{:S(2)}) collective-permute-start(bf16[4,160,512]{2,1,0:T(8,128)(2,1)S(1)} %pad_maximum_fusion.refs_0_), channel_id=1, source_target_pairs={{0,8},{8,0},{16,24},{24,16},{1,9},{9,1},{17,25},{25,17},{2,10},{10... | collective-permute-start | bytes 1966088 | tf_op jit(solution)/shard_map/ppermute | solution.py:540
  59.7 23.7 %collective-permute-start.15 = (bf16[4,128,512]{2,1,0:T(8,128)(2,1)S(1)}, bf16[4,128,512]{2,1,0:T(8,128)(2,1)S(1)}, u32[]{:S(2)}, u32[]{:S(2)}) collective-permute-start(bf16[4,128,512]{2,1,0:T(8,128)(2,1)S(1)} %pad_maximum_fusion.1.refs_4_), channel_id=1, source_target_pairs={{0,1},{1,0},{2,3},{3,2},{4,5},{5,4},{6,7},{7,6},{8,9},{9,8},{10,11... | collective-permute-start | bytes 1572872 | tf_op jit(solution)/shard_map/ppermute | solution.py:540
  61.3 22.1 %collective-permute-start.16 = (bf16[4,128,512]{2,1,0:T(8,128)(2,1)S(1)}, bf16[4,128,512]{2,1,0:T(8,128)(2,1)S(1)}, u32[]{:S(2)}, u32[]{:S(2)}) collective-permute-start(bf16[4,128,512]{2,1,0:T(8,128)(2,1)S(1)} %pad_maximum_fusion.1.refs_4_), channel_id=1, source_target_pairs={{0,8},{8,0},{16,24},{24,16},{1,9},{9,1},{17,25},{25,17},{2,10},{10... | collective-permute-start | bytes 1572872 | tf_op jit(solution)/shard_map/ppermute | solution.py:540
  85.5 26.0 %collective-permute-start.18 = (bf16[2,4,256,256]{3,2,1,0:T(8,128)(2,1)}, bf16[2,4,256,256]{3,2,1,0:T(8,128)(2,1)S(1)}, u32[]{:S(2)}, u32[]{:S(2)}) collective-permute-start(bf16[2,4,256,256]{3,2,1,0:T(8,128)(2,1)} %get-tuple-element.230), channel_id=1, source_target_pairs={{0,2},{1,3},{2,0},{3,1},{4,6},{5,7},{6,4},{7,5},{8,10},{9,11},{10,... | collective-permute-start | bytes 3145736 | tf_op jit(solution)/shard_map/ppermute | solution.py:540
  111.7 31.0 %collective-permute-start.20 = (bf16[2,4,320,256]{3,2,1,0:T(8,128)(2,1)}, bf16[2,4,320,256]{3,2,1,0:T(8,128)(2,1)S(1)}, u32[]{:S(2)}, u32[]{:S(2)}) collective-permute-start(bf16[2,4,320,256]{3,2,1,0:T(8,128)(2,1)} %get-tuple-element.245), channel_id=1, source_target_pairs={{0,2},{1,3},{2,0},{3,1},{4,6},{5,7},{6,4},{7,5},{8,10},{9,11},{10,... | collective-permute-start | bytes 3932168 | tf_op jit(solution)/shard_map/ppermute | solution.py:540
  112.8 16.4 %collective-permute-start.19 = (bf16[2,2,256,256]{3,2,1,0:T(8,128)(2,1)S(1)}, bf16[2,2,256,256]{3,2,1,0:T(8,128)(2,1)S(1)}, u32[]{:S(2)}, u32[]{:S(2)}) collective-permute-start(bf16[2,2,256,256]{3,2,1,0:T(8,128)(2,1)S(1)} %get-tuple-element.243), channel_id=1, source_target_pairs={{0,1},{1,0},{2,3},{3,2},{4,5},{5,4},{6,7},{7,6},{8,9},{9,8},{10,11... | collective-permute-start | bytes 1572872 | tf_op jit(solution)/shard_map/ppermute | solution.py:540
  145.7 12.7 %collective-permute-start.23 = (bf16[4,192,256]{2,1,0:T(8,128)(2,1)S(1)}, bf16[4,192,256]{2,1,0:T(8,128)(2,1)S(1)}, u32[]{:S(2)}, u32[]{:S(2)}) collective-permute-start(bf16[4,192,256]{2,1,0:T(8,128)(2,1)S(1)} %get-tuple-element.265), channel_id=1, source_target_pairs={{0,2},{1,3},{2,0},{3,1},{4,6},{5,7},{6,4},{7,5},{8,10},{9,11},{10,... | collective-permute-start | bytes 1179656 | tf_op jit(solution)/shard_map/ppermute | solution.py:540
  147.9 10.6 %collective-permute-start.24 = (bf16[2,320,256]{2,1,0:T(8,128)(2,1)S(1)}, bf16[2,320,256]{2,1,0:T(8,128)(2,1)S(1)}, u32[]{:S(2)}, u32[]{:S(2)}) collective-permute-start(bf16[2,320,256]{2,1,0:T(8,128)(2,1)S(1)} %get-tuple-element.267), channel_id=1, source_target_pairs={{0,1},{1,0},{2,3},{3,2},{4,5},{5,4},{6,7},{7,6},{8,9},{9,8},{10,11... | collective-permute-start | bytes 983048 | tf_op jit(solution)/shard_map/ppermute | solution.py:540
  148.6 9.8 %collective-permute-start.25 = (bf16[2,256,256]{2,1,0:T(8,128)(2,1)S(1)}, bf16[2,256,256]{2,1,0:T(8,128)(2,1)S(1)}, u32[]{:S(2)}, u32[]{:S(2)}) collective-permute-start(bf16[2,256,256]{2,1,0:T(8,128)(2,1)S(1)} %get-tuple-element.348), channel_id=1, source_target_pairs={{0,8},{8,0},{16,24},{24,16},{1,9},{9,1},{17,25},{25,17},{2,10},{10... | collective-permute-start | bytes 786440 | tf_op jit(solution)/shard_map/ppermute | solution.py:540
  158.8 10.2 %collective-permute-start.26 = (bf16[2,192,256]{2,1,0:T(8,128)(2,1)S(1)}, bf16[2,192,256]{2,1,0:T(8,128)(2,1)S(1)}, u32[]{:S(2)}, u32[]{:S(2)}) collective-permute-start(bf16[2,192,256]{2,1,0:T(8,128)(2,1)S(1)} %get-tuple-element.281), channel_id=1, source_target_pairs={{0,1},{1,0},{2,3},{3,2},{4,5},{5,4},{6,7},{7,6},{8,9},{9,8},{10,11... | collective-permute-start | bytes 589832 | tf_op jit(solution)/shard_map/ppermute | solution.py:540
  160.2 16.1 %collective-permute-start.27 = (bf16[1,576,256]{2,1,0:T(8,128)(2,1)S(1)}, bf16[1,576,256]{2,1,0:T(8,128)(2,1)S(1)}, u32[]{:S(2)}, u32[]{:S(2)}) collective-permute-start(bf16[1,576,256]{2,1,0:T(8,128)(2,1)S(1)} %get-tuple-element.285), channel_id=1, source_target_pairs={{0,4},{1,5},{2,6},{3,7},{4,0},{5,1},{6,2},{7,3},{8,12},{9,13},{10,... | collective-permute-start | bytes 884744 | tf_op jit(solution)/shard_map/ppermute | solution.py:540
  176.4 8.5 %collective-permute-start.28 = (bf16[576,256]{1,0:T(8,128)(2,1)S(1)}, bf16[576,256]{1,0:T(8,128)(2,1)S(1)}, u32[]{:S(2)}, u32[]{:S(2)}) collective-permute-start(bf16[576,256]{1,0:T(8,128)(2,1)S(1)} %fusion.2), channel_id=1, source_target_pairs={{0,16},{8,24},{16,0},{24,8},{1,17},{9,25},{17,1},{25,9},{2,18},{10... | collective-permute-start | bytes 884744 | tf_op jit(solution)/shard_map/ppermute | solution.py:540
  177.9 6.0 %collective-permute-start.29 = (bf16[1,192,256]{2,1,0:T(8,128)(2,1)S(1)}, bf16[1,192,256]{2,1,0:T(8,128)(2,1)S(1)}, u32[]{:S(2)}, u32[]{:S(2)}) collective-permute-start(bf16[1,192,256]{2,1,0:T(8,128)(2,1)S(1)} %get-tuple-element.298), channel_id=1, source_target_pairs={{0,4},{1,5},{2,6},{3,7},{4,0},{5,1},{6,2},{7,3},{8,12},{9,13},{10,... | collective-permute-start | bytes 294920 | tf_op jit(solution)/shard_map/ppermute | solution.py:540
  185.0 3.1 %collective-permute-start.31 = (f32[576,256]{1,0:T(8,128)S(1)}, f32[576,256]{1,0:T(8,128)S(1)}, u32[]{:S(2)}, u32[]{:S(2)}) collective-permute-start(f32[576,256]{1,0:T(8,128)S(1)} %convert_add_fusion.2.refs_0_), channel_id=1, source_target_pairs={{0,8},{8,0},{16,24},{24,16},{1,9},{9,1},{17,25},{25,17},{2,10},{10... | collective-permute-start | bytes 1769480 | tf_op jit(solution)/shard_map/ppermute | solution.py:540
  188.1 7.1 %collective-permute-start.32 = (f32[8,512]{1,0:T(8,128)S(1)}, f32[8,512]{1,0:T(8,128)S(1)}, u32[]{:S(2)}, u32[]{:S(2)}) collective-permute-start(f32[8,512]{1,0:T(8,128)S(1)} %add_select_fusion.3), channel_id=1, source_target_pairs={{0,16},{8,24},{16,0},{24,8},{1,17},{9,25},{17,1},{25,9},{2,18},{10... | collective-permute-start | bytes 49160 | tf_op jit(solution)/shard_map/ppermute | solution.py:540
  189.6 5.6 %collective-permute-start.33 = (bf16[192,256]{1,0:T(8,128)(2,1)S(1)}, bf16[192,256]{1,0:T(8,128)(2,1)S(1)}, u32[]{:S(2)}, u32[]{:S(2)}) collective-permute-start(bf16[192,256]{1,0:T(8,128)(2,1)S(1)} %fusion.3), channel_id=1, source_target_pairs={{0,16},{8,24},{16,0},{24,8},{1,17},{9,25},{17,1},{25,9},{2,18},{10... | collective-permute-start | bytes 294920 | tf_op jit(solution)/shard_map/ppermute | solution.py:540
  201.0 3.7 %collective-permute-start.35 = (f32[8,512]{1,0:T(8,128)S(1)}, f32[8,512]{1,0:T(8,128)S(1)}, u32[]{:S(2)}, u32[]{:S(2)}) collective-permute-start(f32[8,512]{1,0:T(8,128)S(1)} %pad_add_fusion), channel_id=1, source_target_pairs={{0,1},{1,0},{2,3},{3,2},{4,5},{5,4},{6,7},{7,6},{8,9},{9,8},{10,11... | collective-permute-start | bytes 49160 | tf_op jit(solution)/shard_map/ppermute | solution.py:540
  204.8 3.7 %collective-permute-start.36 = (f32[8,512]{1,0:T(8,128)S(1)}, f32[8,512]{1,0:T(8,128)S(1)}, u32[]{:S(2)}, u32[]{:S(2)}) collective-permute-start(f32[8,512]{1,0:T(8,128)S(1)} %add_select_fusion.1), channel_id=1, source_target_pairs={{0,2},{1,3},{2,0},{3,1},{4,6},{5,7},{6,4},{7,5},{8,10},{9,11},{10,... | collective-permute-start | bytes 49160 | tf_op jit(solution)/shard_map/ppermute | solution.py:540
  208.7 4.6 %collective-permute-start.37 = (f32[8,512]{1,0:T(8,128)S(1)}, f32[8,512]{1,0:T(8,128)S(1)}, u32[]{:S(2)}, u32[]{:S(2)}) collective-permute-start(f32[8,512]{1,0:T(8,128)S(1)} %add_select_fusion.one), channel_id=1, source_target_pairs={{0,4},{1,5},{2,6},{3,7},{4,0},{5,1},{6,2},{7,3},{8,12},{9,13},{10,... | collective-permute-start | bytes 49160 | tf_op jit(solution)/shard_map/ppermute | solution.py:540
  (31 other events, 249.2 us)

commit v4 on v3

--- a/solution.py
+++ b/solution.py
@@ -159,23 +159,24 @@
     masks = head_masks()
     lane = lax.broadcasted_iota(jnp.int32, (1, QUAD), 1) % QB
     blocks = -(-rows // QB)
-    for g in range(HEADS // 4):
-        gl = g * QUAD
-        for j in range(blocks):
-            ext = min(QB * (j + 1), rows16)
-            q4 = stack_heads(tri[QB * j : QB * (j + 1), gl : gl + QUAD], masks)
-            s = mm(tri[0:ext, D + gl : D + gl + QUAD], q4, NT)
-            kmax = jnp.minimum(lane + QB * j, length - 1)
-            krow = lax.broadcasted_iota(jnp.int32, (ext, QUAD), 0)
-            s = jnp.where(krow <= kmax, s, MASKED)
-            m = jnp.max(s, axis=0, keepdims=True)
-            p = jnp.exp(s - m)
-            total = jnp.sum(p, axis=0, keepdims=True)
-            lse_out[0, pl.ds(g * blocks + j, 1), :] = m + jnp.log(total)
-            pb = (p * (1.0 / total)).astype(BF16)
-            live = min(QB, rows - QB * j)
-            o = own_lanes(mm(pb, tri[0:ext, 2 * D + gl : 2 * D + gl + QUAD], TN)).astype(BF16)
-            att_out[0, QB * j : QB * j + live, gl : gl + QUAD] = o[:live]
+    chains = [(j, g * QUAD, g * blocks + j) for j in range(blocks) for g in range(HEADS // 4)]
+    exts = [min(QB * (j + 1), rows16) for j, _, _ in chains]
+    q4 = [stack_heads(tri[QB * j : QB * (j + 1), gl : gl + QUAD], masks) for j, gl, _ in chains]
+    s = [mm(tri[0:x, D + gl : D + gl + QUAD], q, NT) for (_, gl, _), x, q in zip(chains, exts, q4)]
+    pb = []
+    for (j, _, at), x, v in zip(chains, exts, s):
+        kmax = jnp.minimum(lane + QB * j, length - 1)
+        krow = lax.broadcasted_iota(jnp.int32, (x, QUAD), 0)
+        v = jnp.where(krow <= kmax, v, MASKED)
+        m = jnp.max(v, axis=0, keepdims=True)
+        p = jnp.exp(v - m)
+        total = jnp.sum(p, axis=0, keepdims=True)
+        lse_out[0, pl.ds(at, 1), :] = m + jnp.log(total)
+        pb.append((p * (1.0 / total)).astype(BF16))
+    o = [mm(v, tri[0:x, 2 * D + gl : 2 * D + gl + QUAD], TN) for (_, gl, _), x, v in zip(chains, exts, pb)]
+    for (j, gl, _), v in zip(chains, o):
+        live = min(QB, rows - QB * j)
+        att_out[0, QB * j : QB * j + live, gl : gl + QUAD] = own_lanes(v).astype(BF16)[:live]
 
 
 def put_rows(dst, at_index, at, src, row, rows):
@@ -185,22 +186,21 @@
     return at
 
 
-def put_ff_grads(keep, send, pos, idx, acc_e, acc_r, wr, acc_m=None):
-    halves, count = keep.shape[:2]
+def put_ff_grads(target, halves, pos, idx, acc_e, acc_r, wr, acc_m=None):
     hm = D // len(pos) // halves
     hr = wr.shape[0] // len(pos) // halves
     for c in range(wr.shape[0] // D):
         wr[c * D : c * D + D] = acc_r[:, c * D : c * D + D].T.astype(BF16)
     for p, rel in enumerate(pos):
         block = jnp.bitwise_xor(idx[0], rel)
-        dst = keep if p < count else send
         for c in range(halves):
             side = 0 if halves == 1 else c + 1
+            dst, where = target(c, p)
             row, rowr = place(block, hm, side, idx[1]), place(block, hr, side, idx[1])
-            at = put_rows(dst, (c, p % count), 0, acc_e, row, hm)
-            at = put_rows(dst, (c, p % count), at, wr, rowr, hr)
+            at = put_rows(dst, where, 0, acc_e, row, hm)
+            at = put_rows(dst, where, at, wr, rowr, hr)
             if acc_m is not None:
-                put_rows(dst, (c, p % count), at, acc_m, row, hm)
+                put_rows(dst, where, at, acc_m, row, hm)
 
 
 def ff_chunks(n2, glow, out, g2, we, wr, acc_e, acc_r):
@@ -220,59 +220,80 @@
     return out, g2
 
 
-def f2a_kernel(plan, nw, pos, idx, att_ref, tok, gl_ref, norm, *refs):
+def live_rows(cot, lens, rows, step):
+    count = cot.shape[0] // rows
+    row = lax.broadcasted_iota(jnp.int32, (cot.shape[0], 1), 0)
+    live = None
+    for i in range(count):
+        inside = (row >= i * rows) & (row < i * rows + lens[step * count + i])
+        live = inside if live is None else live | inside
+    return cot * jnp.where(live, 1.0, 0.0).astype(BF16)
+
+
+def f2a_kernel(plan, nw, pos, rows, idx, lens, att_ref, tok, cot, norm, *refs):
     w_refs, refs = refs[:nw], refs[nw:]
     hid_out, out_out, g2_out, n2_out, keep, send, wm, we, wr, acc_e, acc_r, sem = refs
     s = pl.program_id(0)
 
     @pl.when(s == 0)
     def _():
-        load_mixer(w_refs, plan, wm, sem, idx[0], idx[1], True)
-        load_ff(w_refs, plan, True, we, wr, sem, idx[0], idx[1], True)
+        load_mixer(w_refs, plan, wm, sem.at[0], idx[0], idx[1], True)
+        load_ff(w_refs, plan, True, we, wr, sem.at[1], idx[0], idx[1], True)
         acc_e[...] = jnp.zeros_like(acc_e)
         acc_r[...] = jnp.zeros_like(acc_r)
-        load_mixer(w_refs, plan, wm, sem, idx[0], idx[1], False)
-        load_ff(w_refs, plan, True, we, wr, sem, idx[0], idx[1], False)
-
-    glow = gl_ref[...]
+        load_mixer(w_refs, plan, wm, sem.at[0], idx[0], idx[1], False)
+
+    glow = live_rows(cot[...], lens, rows, s)
     hidden = tok[...].astype(F32) + mm(att_ref[...], wm[...])
     xhat, _ = ln_parts(hidden)
     n2 = (xhat * norm[2:3] + norm[3:4]).astype(BF16)
     hid_out[...] = hidden
     n2_out[...] = n2
+
+    @pl.when(s == 0)
+    def _():
+        load_ff(w_refs, plan, True, we, wr, sem.at[1], idx[0], idx[1], False)
+
     out, g2 = ff_chunks(n2, glow, hidden, None, we, wr, acc_e, acc_r)
     out_out[...] = out
     g2_out[...] = g2
 
     @pl.when(s == pl.num_programs(0) - 1)
     def _():
-        put_ff_grads(keep, send, pos, idx, acc_e, acc_r, wr)
-
-
-def f2b_kernel(plan, nw, pos, idx, att_ref, hid, out_ref, g2_ref, n2_ref, gl_ref, norm, *refs):
+        half = len(pos) // 2
+        target = lambda c, p: (keep if p < half else send, (c, p % half))
+        put_ff_grads(target, keep.shape[0], pos, idx, acc_e, acc_r, wr)
+
+
+def f2b_kernel(plan, nw, pos, nh, rows, idx, lens, att_ref, hid, out_ref, g2_ref, n2_ref, cot, norm, *refs):
     w_refs, b_refs, refs = refs[:nw], refs[nw : 2 * nw], refs[2 * nw :]
-    block_out, gh_out, ga_out, keep, send, ln_out, wm, we, wr, acc_e, acc_r, acc_m, sem = refs
+    (block_out, gh_out, ga_out), grads, refs = refs[:3], refs[3 : 3 + nh], refs[3 + nh :]
+    ln_out, wm, we, wr, acc_e, acc_r, acc_m, sem = refs
     s = pl.program_id(0)
 
     @pl.when(s == 0)
     def _():
-        load_mixer(w_refs, plan, wm, sem, idx[0], idx[1], True)
-        load_ff(b_refs, plan, False, we, wr, sem, idx[0], idx[1], True)
+        load_ff(b_refs, plan, False, we, wr, sem.at[1], idx[0], idx[1], True)
+        load_mixer(w_refs, plan, wm, sem.at[0], idx[0], idx[1], True)
         acc_e[...] = jnp.zeros_like(acc_e)
         acc_r[...] = jnp.zeros_like(acc_r)
         acc_m[...] = jnp.zeros_like(acc_m)
         ln_out[...] = jnp.zeros_like(ln_out)
-        load_mixer(w_refs, plan, wm, sem, idx[0], idx[1], False)
-        load_ff(b_refs, plan, False, we, wr, sem, idx[0], idx[1], False)
+        load_ff(b_refs, plan, False, we, wr, sem.at[1], idx[0], idx[1], False)
 
     gain = norm[2:3]
-    glow = gl_ref[...]
+    glow = live_rows(cot[...], lens, rows, s)
     out, g2 = ff_chunks(n2_ref[...], glow, out_ref[...], g2_ref[...], we, wr, acc_e, acc_r)
     block_out[...] = out.astype(BF16)
     xhat, rstd = ln_parts(hid[...])
     gh = glow.astype(F32) + ln_back(g2, xhat, rstd, gain)
     ln_out[0:1] += jnp.sum(g2 * xhat, axis=0, keepdims=True)
     ln_out[1:2] += jnp.sum(g2, axis=0, keepdims=True)
+
+    @pl.when(s == 0)
+    def _():
+        load_mixer(w_refs, plan, wm, sem.at[0], idx[0], idx[1], False)
+
     gb = gh.astype(BF16)
     gh_out[...] = gh
     acc_m[...] += mm(att_ref[...], gb, TN)
@@ -280,7 +301,7 @@
 
     @pl.when(s == pl.num_programs(0) - 1)
     def _():
-        put_ff_grads(keep, send, pos, idx, acc_e, acc_r, wr, acc_m)
+        put_ff_grads(lambda c, p: (grads[c], (p,)), nh, pos, idx, acc_e, acc_r, wr, acc_m)
 
 
 def b1_kernel(pos, nh, idx, lens, tri_ref, ga_ref, lse, n1, gtri_out, *refs):
@@ -308,28 +329,32 @@
     masks = head_masks()
     lane = lax.broadcasted_iota(jnp.int32, (1, QUAD), 1) % QB
     blocks = -(-rows // QB)
-    for j in range(blocks):
-
-        @pl.when(length > QB * j)
-        def _(j=j):
-            ext = min(QB * (j + 1), rows16)
-            kmax = jnp.minimum(lane + QB * j, length - 1)
-            krow = lax.broadcasted_iota(jnp.int32, (ext, QUAD), 0)
-            for g in range(HEADS // 4):
-                gl = g * QUAD
-                gs = slice(gl, gl + QUAD)
-                q4 = stack_heads(tri[QB * j : QB * (j + 1), gs], masks)
-                do4 = stack_heads(ga[QB * j : QB * (j + 1), gs], masks)
-                s = mm(tri[0:ext, D + gl : D + gl + QUAD], q4, NT)
-                s = jnp.where(krow <= kmax, s - lse[0, pl.ds(g * blocks + j, 1), :], MASKED)
-                p = jnp.exp(s)
-                dp = mm(tri[0:ext, 2 * D + gl : 2 * D + gl + QUAD], do4, NT)
-                delta = jnp.sum(p * dp, axis=0, keepdims=True)
-                ds = (p * (dp - delta)).astype(BF16)
-                dv[0:ext, gs] += mm(p.astype(BF16), do4)
-                dk[0:ext, gs] += mm(ds, q4)
-                dq = own_lanes(mm(ds, tri[0:ext, D + gl : D + gl + QUAD], TN)) * HEAD_DIM**-0.5
-                gtri[QB * j : QB * (j + 1), gs] = dq.astype(BF16)
+    for group in [tuple(range(j, min(j + 2, blocks))) for j in range(0, blocks, 2)]:
+
+        @pl.when(length > QB * group[0])
+        def _(group=group):
+            chains = [(j, g * QUAD, g * blocks + j) for j in group for g in range(HEADS // 4)]
+            exts = [min(QB * (j + 1), rows16) for j, _, _ in chains]
+            q4 = [stack_heads(tri[QB * j : QB * (j + 1), gl : gl + QUAD], masks) for j, gl, _ in chains]
+            do4 = [stack_heads(ga[QB * j : QB * (j + 1), gl : gl + QUAD], masks) for j, gl, _ in chains]
+            s = [mm(tri[0:x, D + gl : D + gl + QUAD], q, NT) for (_, gl, _), x, q in zip(chains, exts, q4)]
+            dp = [mm(tri[0:x, 2 * D + gl : 2 * D + gl + QUAD], d, NT) for (_, gl, _), x, d in zip(chains, exts, do4)]
+            p = []
+            for (j, _, at), x, v in zip(chains, exts, s):
+                kmax = jnp.minimum(lane + QB * j, length - 1)
+                krow = lax.broadcasted_iota(jnp.int32, (x, QUAD), 0)
+                p.append(jnp.exp(jnp.where(krow <= kmax, v - lse[0, pl.ds(at, 1), :], MASKED)))
+            ds = []
+            for v, w in zip(p, dp):
+                delta = jnp.sum(v * w, axis=0, keepdims=True)
+                ds.append((v * (w - delta)).astype(BF16))
+            for (_, gl, _), x, v, d in zip(chains, exts, p, do4):
+                dv[0:x, gl : gl + QUAD] += mm(v.astype(BF16), d)
+            dq = [mm(v, tri[0:x, D + gl : D + gl + QUAD], TN) for (_, gl, _), x, v in zip(chains, exts, ds)]
+            for (_, gl, _), x, v, q in zip(chains, exts, ds, q4):
+                dk[0:x, gl : gl + QUAD] += mm(v, q)
+            for (j, gl, _), v in zip(chains, dq):
+                gtri[QB * j : QB * (j + 1), gl : gl + QUAD] = (own_lanes(v) * HEAD_DIM**-0.5).astype(BF16)
 
     gtri[0:rows16, D : 2 * D] = dk[...].astype(BF16)
     gtri[0:rows16, 2 * D :] = dv[...].astype(BF16)
@@ -584,7 +609,7 @@
             dimension_semantics=("arbitrary",) * len(grid), vmem_limit_bytes=VMEM_LIMIT
         ),
         cost_estimate=pl.CostEstimate(
-            flops=us * 20_000_000, bytes_accessed=us * 20_000, transcendentals=0
+            flops=us, bytes_accessed=us, transcendentals=0
         ),
         name=name,
         **more,
@@ -655,16 +680,18 @@
     t_got = [steps_f(own_t, r) for r in rels_a[1:]]
     own_a = own_piece(w_expand_0, w_reduce_0, 0, [own_half(w_mixer_0).astype(BF16)])
     t_one = jnp.stack([own_t, *t_got])
-    t_one, own_a, cotangent, valid_mask, action_bins, w_expand_1, w_reduce_1 = sync(
-        t_one, own_a, cotangent, valid_mask, action_bins, w_expand, w_reduce
+    a_got = [steps_f(own_a, r) for r in rels_a[1:]]
+    t_one, idx, norm, valid_mask, action_bins, w_expand_1, w_reduce_1 = sync(
+        t_one, idx, norm, valid_mask, action_bins, w_expand, w_reduce
     )
     t_two = steps_f(t_one, near)
     t_refs, t_plan = [t_one], [(rels_a, nh - 1)]
     if nh == 2:
         t_refs.append(steps_d(t_one, 1))
         t_plan.append((rels_a, 2))
-    a_one = [own_a] + [steps_f(own_a, r) for r in rels_a[1:]]
+    a_one = [own_a, *a_got]
     own_b = own_piece(w_expand_1, w_reduce_1, 1, [])
+    t_two, own_b = sync(t_two, own_b)
     b_one = [own_b] + [steps_f(own_b, r) for r in rels_a[1:]]
     t_refs.append(t_two)
     t_plan.append((rels_b, nh - 1))
@@ -674,11 +701,10 @@
     nw = len(t_refs)
     places = jnp.arange(rows)
     inside = places[None, :] < lengths[:, None]
-    glow = jnp.where(inside[:, :, None], cotangent, jnp.zeros((), BF16))
     counted = ((valid_mask == 1) & inside).astype(jnp.int32).reshape(1, flat)
     bins_t = action_bins.reshape(flat, ACT).T
     a_one = jnp.stack(a_one)
-    glow, bins_t, counted, norm, a_one, *t_refs = sync(glow, bins_t, counted, norm, a_one, *t_refs)
+    bins_t, counted, norm, a_one, *t_refs = sync(bins_t, counted, norm, a_one, *t_refs)
     a_two = steps_f(a_one, near)
     a_refs, a_plan = [a_one], [(rels_a, nh - 1)]
     if nh == 2:
@@ -705,7 +731,8 @@
 
     order = f_bits[1:2] + f_bits[:1] + f_bits[2:]
     late = order[2:]
-    pos = halving_positions(order)
+    order_a = f_bits[1:3] + f_bits[:1] + f_bits[3:]
+    pos, pos_a = halving_positions(order), halving_positions(order_a)
     hm, hr = shard // nh, h2 // nh
     rows_a = hm * (half_ff // QUAD) + hr * (D // QUAD)
     rows_b = rows_a + hm * (D // QUAD)
@@ -722,13 +749,13 @@
     fl_low = lambda width: (fl_block(width), jax.ShapeDtypeStruct((flat, width), BF16))
     fl_wide = lambda width: (fl_block(width), jax.ShapeDtypeStruct((flat, width), F32))
     tok_flat = tokens.reshape(flat, D)
-    glow = glow.reshape(flat, D)
+    cot_flat = cotangent.reshape(flat, D)
     attended = attended.reshape(flat, D)
     hidden, out_part, g2_part, n2, keep_a, send_a = kernel_call(
-        functools.partial(f2a_kernel, a_plan, na, pos), "f2a", (fl_steps,),
-        [SMEM] + [fl_block(D)] * 3 + [norm_spec] + [ANY] * na,
+        functools.partial(f2a_kernel, a_plan, na, pos_a, rows), "f2a", (fl_steps,),
+        [SMEM, SMEM] + [fl_block(D)] * 3 + [norm_spec] + [ANY] * na,
         [fl_wide(D)] * 3 + [fl_low(D)] + [low_out(nh, half, rows_a, QUAD)] * 2,
-        ff_scratch + [dma], 22, (idx, attended, tok_flat, glow, norm, *a_refs),
+        ff_scratch + [pltpu.SemaphoreType.DMA((2,))], 22, (idx, lengths, attended, tok_flat, cot_flat, norm, *a_refs),
     )
 
     def halves(keep, got):
@@ -750,19 +777,24 @@
     b_refs += [b_two] + ([steps_d(b_two, 1)] if nh == 2 else [])
     n2, keep_a, send_a, *b_refs = sync(n2, keep_a, send_a, *b_refs)
     got_a = steps_f(send_a, order[0])
-    block_out, gh, ga, keep_b, send_b, ln2 = kernel_call(
-        functools.partial(f2b_kernel, a_plan, na, pos), "f2b", (fl_steps,),
-        [SMEM] + [fl_block(D)] * 6 + [norm_spec] + [ANY] * (2 * na),
-        [fl_low(D), fl_wide(D), fl_low(D)] + [low_out(nh, half, rows_b, QUAD)] * 2 + [whole((8, D))],
-        ff_scratch + [pltpu.VMEM((D, D), F32), dma], 24,
-        (idx, attended, hidden, out_part, g2_part, n2, glow, norm, *a_refs, *b_refs),
-    )
-    ga, keep_a, got_a, keep_b, send_b = sync(ga, keep_a, got_a, keep_b, send_b)
-    keep_a, send_a = halves(keep_a, got_a)
+    block_out, gh, ga, *rest = kernel_call(
+        functools.partial(f2b_kernel, a_plan, na, pos, nh, rows), "f2b", (fl_steps,),
+        [SMEM, SMEM] + [fl_block(D)] * 6 + [norm_spec] + [ANY] * (2 * na),
+        [fl_low(D), fl_wide(D), fl_low(D)] + [low_out(n_f, rows_b, QUAD)] * nh + [whole((8, D))],
+        ff_scratch + [pltpu.VMEM((D, D), F32), pltpu.SemaphoreType.DMA((2,))], 24,
+        (idx, lengths, attended, hidden, out_part, g2_part, n2, cot_flat, norm, *a_refs, *b_refs),
+    )
+    grads_b, ln2 = rest[:nh], rest[nh]
+    ga, keep_a, got_a, *grads_b = sync(ga, keep_a, got_a, *grads_b)
+    pair_b = core_pair(grads_b)
+    sum_a = add_low(keep_a, got_a)
+    pair_a = core_pair(sum_a)
+    keep_b, send_b = core_halves_of(pair_b)
+    keep_a, send_a = core_halves_of(pair_a)
     ga, keep_a, send_a, keep_b, send_b = sync(ga, keep_a, send_a, keep_b, send_b)
 
     got_b = steps_f(send_b, order[0])
-    got_a = steps_f(send_a, order[1])
+    got_a = steps_f(send_a, order_a[1])
     pack_rows = ep * rows16 + PACK
     gtri, *grads_t = kernel_call(
         functools.partial(b1_kernel, pos, nh), "b1", (ep,),
@@ -779,16 +811,22 @@
     gtri, keep_a, got_a, keep_b, got_b, *grads_t = sync(gtri, keep_a, got_a, keep_b, got_b, *grads_t)
 
     mine_t, other_t = core_pair(grads_t)
-    sum_a = add_low(keep_a, got_a)
-    sum_b = add_low(keep_b, got_b)
-    mine_t, other_t, sum_a, sum_b = sync(mine_t, other_t, sum_a, sum_b)
+    late_a = order_a[2:]
+    keep_b, send_b = halves(keep_b, got_b)
+    if late_a:
+        keep_a, send_a = halves(keep_a, got_a)
+        send_ab = jnp.concatenate([send_a.reshape(-1, QUAD), send_b.reshape(-1, QUAD)], axis=0)
+        keep_ab = jnp.concatenate([keep_a.reshape(-1, QUAD), keep_b.reshape(-1, QUAD)], axis=0)
+        cut_a = send_a.size // QUAD
+    else:
+        keep_a = add_low(keep_a, got_a)
+        send_ab, keep_ab = send_b.reshape(-1, QUAD), keep_b.reshape(-1, QUAD)
+        cut_a = 0
+    mine_t, other_t, keep_ab, send_ab = sync(mine_t, other_t, keep_ab, send_ab)
     keep_t, send_t = core_halves_of((mine_t, other_t))
-    keep_t, send_t, sum_a, sum_b = sync(keep_t, send_t, sum_a, sum_b)
+    block_out, keep_t, send_t, keep_ab, send_ab = sync(block_out, keep_t, send_t, keep_ab, send_ab)
     got_t = steps_f(send_t, order[0])
-    pair_b, pair_a = core_pair(sum_b), core_pair(sum_a)
-    keep_b, send_b = core_halves_of(pair_b)
-    block_out, keep_b, send_b = sync(block_out, keep_b, send_b)
-    got_b = steps_f(send_b, order[1])
+    got_ab = steps_f(send_ab, near)
 
     qb = 256
     steps = -(-flat // qb)
@@ -800,8 +838,7 @@
         ],
         [whole((16, qb))] * 2, [], 10, (block_out, value_head, bins_t, counted),
     )
-    gtri, q_sum, keep_t, got_t, keep_b, got_b = sync(gtri, q_sum, keep_t, got_t, keep_b, got_b)
-    pair_a = sync(*pair_a, q_sum)[:2] if nh == 2 else pair_a
+    gtri, q_sum, keep_t, got_t, keep_ab, got_ab = sync(gtri, q_sum, keep_t, got_t, keep_ab, got_ab)
 
     def b2_call(at, n, gtri, prior, more_in):
         extra = [] if prior is None else [prior, *more_in]
@@ -815,22 +852,21 @@
         )
 
     keep_t, send_t = halves(keep_t, got_t)
+    if late_a:
+        keep_a = add_low(keep_ab[:cut_a], got_ab[:cut_a]).reshape(-1, rows_a, QUAD)
+    keep_b, got_b = (v[cut_a:].reshape(-1, rows_b, QUAD) for v in (keep_ab, got_ab))
     if late:
         keep_b, send_b = halves(keep_b, got_b)
-        keep_a, send_a = core_halves_of(pair_a)
-        keep_ab = jnp.concatenate([keep_a, keep_b], axis=1)
-        send_ab = jnp.concatenate([send_a, send_b], axis=1)
     else:
-        keep_ab = jnp.concatenate([core_add(pair_a), add_low(keep_b, got_b)], axis=1)
-        send_ab = keep_ab
+        keep_b, send_b = add_low(keep_b, got_b), keep_b
     gtri_flat = gtri.reshape(flat, 3 * D)
-    gtri_flat, keep_t, send_t, keep_ab, send_ab = sync(gtri_flat, keep_t, send_t, keep_ab, send_ab)
+    gtri_flat, keep_t, send_t, keep_a, keep_b, send_b = sync(gtri_flat, keep_t, send_t, keep_a, keep_b, send_b)
     got_t = steps_f(send_t, order[1])
     if late:
-        got_ab = steps_f(send_ab, late[0])
+        got_b = steps_f(send_b, late[0])
     cut = (fl_steps + 1) // 2
     ig_part, ln1_a = b2_call(0, cut, gtri_flat, None, ())
-    ig_part, keep_t, got_t = sync(ig_part, keep_t, got_t)
+    ig_part, keep_t, got_t, keep_b, *got_b = sync(ig_part, keep_t, got_t, keep_b, *([got_b] if late else []))
 
     def finish(keep, bits):
         for b in bits:
@@ -838,18 +874,18 @@
             keep = add_low(keep[:n], steps_f(keep[n:], b))
         return keep[0]
 
+    x_bits = d_bits[nh - 1 :]
     if late:
         keep_t, send_t = halves(keep_t, got_t)
-        keep_t, send_t, keep_ab, got_ab, ig_part = sync(keep_t, send_t, keep_ab, got_ab, ig_part)
-        got_t = steps_f(send_t, late[0])
-        keep_ab = add_low(keep_ab, got_ab)
+        keep_b = add_low(keep_b, got_b[0])
     else:
         keep_t = add_low(keep_t, got_t)
-    x_bits = d_bits[nh - 1 :]
-    red = finish(keep_ab, late[1:])
+    red = jnp.concatenate([finish(keep_a, late_a[1:]), finish(keep_b, late[1:])], axis=0)
     for b in x_bits[:-1]:
         red = add_low(red, steps_d(red, b))
-    red, ig_part = sync(red, ig_part)
+    red, keep_t, ig_part = sync(red, keep_t, ig_part)
+    if late:
+        got_t = steps_f(send_t, late[0])
     got_red = steps_d(red, x_bits[-1])
     input_grad, small = b2_call(cut, fl_steps - cut, gtri_flat, ig_part, (ln1_a, ln2, q_sum, q_top))
     small, red, got_red, keep_t, *got_t = sync(small, red, got_red, keep_t, *([got_t] if late else []))
@@ -860,10 +896,8 @@
     got_rt = steps_d(red_t, x_bits[-1])
     red = red.astype(F32) + got_red.astype(F32)
     red_parts = [red] + ([steps_d(red, 1)] if nh == 2 else [])
-    small = merge_small(small, steps_d(small, d_bits[0]))
-    small, red_t, *red_parts = sync(small, red_t, *red_parts)
-    for b in d_bits[1:]:
-        small = merge_small(small, steps_d(small, b))
+    small_core = steps_d(small, d_bits[0])
+    red_t, *red_parts = sync(red_t, *red_parts)
     like = lambda w: whole(w.shape)
     full = lambda *ws: [const_spec(w.shape) for w in ws]
     mlp_state = (
@@ -876,7 +910,10 @@
         [like(w) for w in (w_mixer, w_expand, w_reduce) for _ in range(3)] + [whole((8, 128))],
         [], 4, (idx, *red_parts, *mlp_state),
     )
-    small, sq_mlp, red_t, got_rt = sync(small, sq_mlp, red_t, got_rt)
+    small, small_core, sq_mlp, red_t, got_rt = sync(small, small_core, sq_mlp, red_t, got_rt)
+    small = merge_small(small, small_core)
+    for b in d_bits[1:]:
+        small = merge_small(small, steps_d(small, b))
     red_t = red_t.astype(F32) + got_rt.astype(F32)
     parts_t = [red_t] + ([steps_d(red_t, 1)] if nh == 2 else [])
     tri_state = (w_triple, first_triple, second_triple)

time: 218 us -> 203 us (0.931)
  waiting for transfers between devices: 49.1 us -> 30.7 us
  starting transfers between devices: 34.8 us -> 42 us
  Pallas kernels: 115 us -> 110 us
  local copies, waits for them, and re-layouts: 9.6 us -> 12.3 us
  other arithmetic: 7.51 us -> 5.23 us
    ppermute x38, waiting for transfers between devices: 49.1 us -> 30.7 us  [xor_step(): return lax.ppermute(v, axis, [(i, i ^ bit) for i in range(size)])]
    ppermute x38, starting transfers between devices: 34.8 us -> 42 us  [xor_step(): return lax.ppermute(v, axis, [(i, i ^ bit) for i in range(size)])]
    pallas_call x10, Pallas kernels: 115 us -> 110 us  [kernel_call(): pl.pallas_call(kernel, grid=grid, in_specs=in_specs, out_specs=[spec for...]
    select_n x1 -> x0, other arithmetic: 3.25 us -> none  [body(): glow = jnp.where(inside[:, :, None], cotangent, jnp.zeros((), BF16))]
  transfers between devices with their start and end apart: 38 -> 38, of which waited for: 16 -> 13; matrix products, arithmetic and copies ran while one was open for 6% -> 5% of each run, Pallas kernels for 50% -> 53%
where the time goes in v4:
time: 203 us; the launch traced here: 202 us
  Pallas kernels  110 us (54%)
  starting transfers between devices  42 us (21%)
  waiting for transfers between devices  30.7 us (15%)
  local copies, waits for them, and re-layouts  12.3 us (6%)
  other arithmetic  5.23 us (3%)
    pallas_call x10, Pallas kernels, kernel_call(): pl.pallas_call(kernel, grid=grid, in_specs=in_specs, out_specs=[spec for...  110 us
    ppermute x38, starting transfers between devices, xor_step(): return lax.ppermute(v, axis, [(i, i ^ bit) for i in range(size)])  42 us
    ppermute x38, waiting for transfers between devices, xor_step(): return lax.ppermute(v, axis, [(i, i ^ bit) for i in range(size)])  30.7 us
  transfers between devices with their start and end apart: 38, of which 13 were waited for; matrix products, arithmetic and copies ran while one was open for 5% of the time, Pallas kernels for 53%

profile of v4, /device:TPU:0, one launch (start us, length us, event | category | flops | bytes accessed | tf_op | source)
XLA Modules:
  0.0 202.1 jit_solution(12145786072998995712)
XLA Ops:
  1.7 3.1 %collective-permute-start = (bf16[32,1536]{1,0:T(8,128)(2,1)S(1)}, bf16[32,1536]{1,0:T(8,128)(2,1)S(1)}, u32[]{:S(2)}, u32[]{:S(2)}) collective-permute-start(bf16[32,1536]{1,0:T(8,128)(2,1)S(1)} %dynamic-slice_convert_fusion.2), channel_id=1, source_target_pairs={{0,2},{1,3},{2,0},{3,1},{4,6},{5,7},{6,4},{7,5},{8,10},{9,11},{10,... | collective-permute-start | bytes 294920 | tf_op jit(solution)/shard_map/ppermute | solution.py:565
  4.8 2.6 %collective-permute-start.1 = (bf16[32,1536]{1,0:T(8,128)(2,1)S(1)}, bf16[32,1536]{1,0:T(8,128)(2,1)S(1)}, u32[]{:S(2)}, u32[]{:S(2)}) collective-permute-start(bf16[32,1536]{1,0:T(8,128)(2,1)S(1)} %dynamic-slice_convert_fusion.2), channel_id=1, source_target_pairs={{0,4},{1,5},{2,6},{3,7},{4,0},{5,1},{6,2},{7,3},{8,12},{9,13},{10,... | collective-permute-start | bytes 294920 | tf_op jit(solution)/shard_map/ppermute | solution.py:565
  10.2 2.0 collective-permute-start.4
  12.2 2.0 collective-permute-start.5
  16.6 5.3 %collective-permute-done.1 = bf16[32,1536]{1,0:T(8,128)(2,1)S(1)} collective-permute-done((bf16[32,1536]{1,0:T(8,128)(2,1)S(1)}, bf16[32,1536]{1,0:T(8,128)(2,1)S(1)}, u32[]{:S(2)}, u32[]{:S(2)}) %collective-permute-start.1) | collective-permute-done | bytes 98336 | tf_op jit(solution)/shard_map/ppermute | solution.py:565
  21.9 1.6 collective-permute-start.7
  26.2 3.6 %collective-permute-done.7.refs_2_ = bf16[4,32,1536]{2,1,0:T(8,128)(2,1)S(1)} collective-permute-done((bf16[4,32,1536]{2,1,0:T(8,128)(2,1)S(1)}, bf16[4,32,1536]{2,1,0:T(8,128)(2,1)S(1)}, u32[]{:S(2)}, u32[]{:S(2)}) %collective-permute-start.7) | collective-permute-done | bytes 393248 | tf_op jit(solution)/shard_map/ppermute | solution.py:565
  31.5 1.6 collective-permute-start.9
  33.1 3.2 %collective-permute-start.10 = (bf16[128,512]{1,0:T(8,128)(2,1)}, bf16[128,512]{1,0:T(8,128)(2,1)S(1)}, u32[]{:S(2)}, u32[]{:S(2)}) collective-permute-start(bf16[128,512]{1,0:T(8,128)(2,1)} %pad_maximum_fusion.7), channel_id=1, source_target_pairs={{0,2},{1,3},{2,0},{3,1},{4,6},{5,7},{6,4},{7,5},{8,10},{9,11},{10,... | collective-permute-start | bytes 393224 | tf_op jit(solution)/shard_map/ppermute | solution.py:565
  36.3 1.9 collective-permute-start.11
  39.7 15.7 %f1.1 = (bf16[6,296,1536]{2,1,0:T(8,128)(2,1)}, bf16[6,296,512]{2,1,0:T(8,128)(2,1)}, bf16[6,296,512]{2,1,0:T(8,128)(2,1)}, f32[6,16,256]{2,1,0:T(8,128)}) custom-call(s32[2]{0:T(128)} %pad_add_fusion.1.idx, s32[6]{0:T(128)} %lens.7, bf16[6,296,512]{2,1,0:T(8,128)(2,1)} %tok.1, f32[8,512]{1,0:T(8,128)} %concatenate.34.norm, bf16[4,32,1536]{2,1,0:T(8,128)(2,1)} %copy-done, ...), custom_call_target="tpu_custom_call" | custom-call | flops 18 | bytes 18 | tf_op jit(solution)/shard_map/f1/pallas_call | solution.py:601
  59.2 22.0 %f2a.1 = (f32[1776,512]{1,0:T(8,128)}, f32[1776,512]{1,0:T(8,128)}, f32[1776,512]{1,0:T(8,128)}, bf16[1776,512]{1,0:T(8,128)(2,1)}, bf16[2,4,256,256]{3,2,1,0:T(8,128)(2,1)}, /*index=5*/bf16[2,4,256,256]{3,2,1,0:T(8,128)(2,1)}) custom-call(s32[2]{0:T(128)} %pad_add_fusion.1.idx, s32[6]{0:T(128)} %lens.7, bf16[1776,512]{1,0:T(8,128)(2,1)} %bitcast.69, ...), custom_call_target="tpu_custom_call" | custom-call | flops 22 | bytes 22 | tf_op jit(solution)/shard_map/f2a/pallas_call | solution.py:601
  84.1 25.5 %f2b.1 = (bf16[1776,512]{1,0:T(8,128)(2,1)}, f32[1776,512]{1,0:T(8,128)}, bf16[1776,512]{1,0:T(8,128)(2,1)}, bf16[8,320,256]{2,1,0:T(8,128)(2,1)}, bf16[8,320,256]{2,1,0:T(8,128)(2,1)}, /*index=5*/f32[8,512]{1,0:T(8,128)}) custom-call(s32[2]{0:T(128)} %pad_add_fusion.1.idx, s32[6]{0:T(128)} %lens.7, bf16[1776,512]{1,0:T(8,128)(2,1)} %bitcast.70, ...), custom_call_target="tpu_custom_call" | custom-call | flops 24 | bytes 24 | tf_op jit(solution)/shard_map/f2b/pallas_call | solution.py:601
  110.5 2.9 %collective-permute-done.19 = bf16[4,256,256]{2,1,0:T(8,128)(2,1)S(1)} collective-permute-done((bf16[4,256,256]{2,1,0:T(8,128)(2,1)S(1)}, bf16[4,256,256]{2,1,0:T(8,128)(2,1)S(1)}, u32[]{:S(2)}, u32[]{:S(2)}) %collective-permute-start.19) | collective-permute-done | bytes 524320 | tf_op jit(solution)/shard_map/ppermute | solution.py:565
  115.3 2.0 collective-permute-start.21
  117.3 13.0 %b1.1 = (bf16[6,296,1536]{2,1,0:T(8,128)(2,1)}, bf16[8,192,256]{2,1,0:T(8,128)(2,1)}, bf16[8,192,256]{2,1,0:T(8,128)(2,1)}) custom-call(s32[2]{0:T(128)} %pad_add_fusion.1.idx, s32[6]{0:T(128)} %lens.7, bf16[6,296,1536]{2,1,0:T(8,128)(2,1)} %get-tuple-element.224.tri_ref, bf16[6,296,512]{2,1,0:T(8,128)(2,1)} %bitcast.71, ...), custom_call_target="tpu_custom_call" | custom-call | flops 25 | bytes 25 | tf_op jit(solution)/shard_map/b1/pallas_call | solution.py:601
  130.3 4.9 %collective-permute-done.21 = bf16[2,256,256]{2,1,0:T(8,128)(2,1)S(1)} collective-permute-done((bf16[2,256,256]{2,1,0:T(8,128)(2,1)S(1)}, bf16[2,256,256]{2,1,0:T(8,128)(2,1)S(1)}, u32[]{:S(2)}, u32[]{:S(2)}) %collective-permute-start.21) | collective-permute-done | bytes 262176 | tf_op jit(solution)/shard_map/ppermute | solution.py:565
  136.9 2.2 %collective-permute-done.23 = bf16[8,192,256]{2,1,0:T(8,128)(2,1)S(1)} collective-permute-done((bf16[8,192,256]{2,1,0:T(8,128)(2,1)}, bf16[8,192,256]{2,1,0:T(8,128)(2,1)S(1)}, u32[]{:S(2)}, u32[]{:S(2)}) %collective-permute-start.23) | collective-permute-done | bytes 786464 | tf_op jit(solution)/shard_map/ppermute | solution.py:565
  140.7 2.0 collective-permute-start.24
  142.8 9.5 %qstat.1 = (f32[16,256]{1,0:T(8,128)}, f32[16,256]{1,0:T(8,128)}) custom-call(bf16[1776,512]{1,0:T(8,128)(2,1)} %get-tuple-element.255.bo, bf16[2816,512]{1,0:T(8,128)(2,1)} %vh.1, s32[11,1776]{1,0:T(8,128)} %bitcast.77, s32[1,1776]{1,0:T(1,128)} %reshape.130.cnt), custom_call_target="tpu_custom_call" | custom-call | flops 10 | bytes 10 | tf_op jit(solution)/shard_map/qstat/pallas_call | solution.py:601
  153.6 2.0 collective-permute-start.27
  155.6 7.8 %b2.2 = (bf16[1776,512]{1,0:T(8,128)(2,1)}, f32[8,512]{1,0:T(8,128)}) custom-call(s32[2]{0:T(128)} %pad_add_fusion.1.idx, bf16[1776,1536]{1,0:T(8,128)(2,1)} %bitcast.65, bf16[1776,512]{1,0:T(8,128)(2,1)} %bitcast.63, f32[1776,512]{1,0:T(8,128)} %get-tuple-element.270.gh, f32[8,512]{1,0:T(8,128)} %concatenate.34.norm, bf16[4,32,1536]{2,1,0:T(8,128)(2,1)} %copy-done, ...), custom_call_target="tpu_custom_call" | custom-call | flops 6 | bytes 6 | tf_op jit(solution)/shard_map/b2/pallas_call | solution.py:601
  163.6 1.5 collective-permute-start.28
  166.0 6.0 %b2.3 = (bf16[1776,512]{1,0:T(8,128)(2,1)}, f32[8,512]{1,0:T(8,128)}) custom-call(s32[2]{0:T(128)} %pad_add_fusion.1.idx, bf16[1776,1536]{1,0:T(8,128)(2,1)} %bitcast.66, bf16[1776,512]{1,0:T(8,128)(2,1)} %bitcast.64, f32[1776,512]{1,0:T(8,128)} %get-tuple-element.270.gh, f32[8,512]{1,0:T(8,128)} %concatenate.34.norm, ...), custom_call_target="tpu_custom_call", output_to_operand_aliasing={{0}: (9, {})} | custom-call | flops 6 | bytes 6 | tf_op jit(solution)/shard_map/b2/pallas_call | solution.py:601
  175.0 5.0 %lamb_mlp.1 = (f32[64,512]{1,0:T(8,128)}, f32[64,512]{1,0:T(8,128)}, f32[64,512]{1,0:T(8,128)}, f32[64,2048]{1,0:T(8,128)}, f32[64,2048]{1,0:T(8,128)}, /*index=...) custom-call(s32[2]{0:T(128)} %pad_add_fusion.1.idx, ...), custom_call_target="tpu_custom_call" | custom-call | flops 4 | bytes 4 | tf_op jit(solution)/shard_map/lamb_mlp/pallas_call | solution.py:601
  182.3 2.8 %lamb_triple.1 = (f32[64,1536]{1,0:T(8,128)}, f32[64,1536]{1,0:T(8,128)}, f32[64,1536]{1,0:T(8,128)}, f32[8,128]{1,0:T(8,128)}) custom-call(s32[2]{0:T(128)} %pad_add_fusion.1.idx, f32[192,256]{1,0:T(8,128)} %copy-done.13, f32[192,256]{1,0:T(8,128)} %copy-done.18, f32[8,128]{1,0:T(8,128)} %get-tuple-element.304.refs_2_, f32[64,1536]{1,0:T(8,128)} %refs_0_.1, ...), custom_call_target="tpu_custom_call" | custom-call | flops 2 | bytes 2 | tf_op jit(solution)/shard_map/lamb_triple/pallas_call | solution.py:601
  186.9 2.8 %collective-permute-done.35 = f32[8,512]{1,0:T(8,128)S(1)} collective-permute-done((f32[8,512]{1,0:T(8,128)S(1)}, f32[8,512]{1,0:T(8,128)S(1)}, u32[]{:S(2)}, u32[]{:S(2)}) %collective-permute-start.35) | collective-permute-done | bytes 16416 | tf_op jit(solution)/shard_map/ppermute | solution.py:565
  189.7 2.0 %collective-permute-start.36 = (f32[8,512]{1,0:T(8,128)S(1)}, f32[8,512]{1,0:T(8,128)S(1)}, u32[]{:S(2)}, u32[]{:S(2)}) collective-permute-start(f32[8,512]{1,0:T(8,128)S(1)} %add_select_fusion.1), channel_id=1, source_target_pairs={{0,2},{1,3},{2,0},{3,1},{4,6},{5,7},{6,4},{7,5},{8,10},{9,11},{10,... | collective-permute-start | bytes 49160 | tf_op jit(solution)/shard_map/ppermute | solution.py:565
  191.7 1.7 collective-permute-done.36
  193.5 2.0 collective-permute-start.37
  195.5 2.7 %collective-permute-done.37.two = f32[8,512]{1,0:T(8,128)S(1)} collective-permute-done((f32[8,512]{1,0:T(8,128)S(1)}, f32[8,512]{1,0:T(8,128)S(1)}, u32[]{:S(2)}, u32[]{:S(2)}) %collective-permute-start.37) | collective-permute-done | bytes 16416 | tf_op jit(solution)/shard_map/ppermute | solution.py:565
  198.8 3.2 %final.1 = (f32[64,1536]{1,0:T(8,128)}, f32[64,512]{1,0:T(8,128)}, f32[64,2048]{1,0:T(8,128)}, f32[256,512]{1,0:T(8,128)}, f32[4,512]{1,0:T(4,128)}, /*index=5*/...) custom-call(f32[8,512]{1,0:T(8,128)} %copy-done.22, ...), custom_call_target="tpu_custom_call" | custom-call | flops 3 | bytes 3 | tf_op jit(solution)/shard_map/final/pallas_call | solution.py:601
  (151 shorter events, 34.7 us)
Async XLA Ops:
  1.7 14.4 %collective-permute-start = (bf16[32,1536]{1,0:T(8,128)(2,1)S(1)}, bf16[32,1536]{1,0:T(8,128)(2,1)S(1)}, u32[]{:S(2)}, u32[]{:S(2)}) collective-permute-start(bf16[32,1536]{1,0:T(8,128)(2,1)S(1)} %dynamic-slice_convert_fusion.2), channel_id=1, source_target_pairs={{0,2},{1,3},{2,0},{3,1},{4,6},{5,7},{6,4},{7,5},{8,10},{9,11},{10,... | collective-permute-start | bytes 294920 | tf_op jit(solution)/shard_map/ppermute | solution.py:565
  4.8 17.1 %collective-permute-start.1 = (bf16[32,1536]{1,0:T(8,128)(2,1)S(1)}, bf16[32,1536]{1,0:T(8,128)(2,1)S(1)}, u32[]{:S(2)}, u32[]{:S(2)}) collective-permute-start(bf16[32,1536]{1,0:T(8,128)(2,1)S(1)} %dynamic-slice_convert_fusion.2), channel_id=1, source_target_pairs={{0,4},{1,5},{2,6},{3,7},{4,0},{5,1},{6,2},{7,3},{8,12},{9,13},{10,... | collective-permute-start | bytes 294920 | tf_op jit(solution)/shard_map/ppermute | solution.py:565
  7.3 14.5 %collective-permute-start.2 = (bf16[32,1536]{1,0:T(8,128)(2,1)S(1)}, bf16[32,1536]{1,0:T(8,128)(2,1)S(1)}, u32[]{:S(2)}, u32[]{:S(2)}) collective-permute-start(bf16[32,1536]{1,0:T(8,128)(2,1)S(1)} %dynamic-slice_convert_fusion.2), channel_id=1, source_target_pairs={{0,6},{1,7},{2,4},{3,5},{4,2},{5,3},{6,0},{7,1},{8,14},{9,15},{10,... | collective-permute-start | bytes 294920 | tf_op jit(solution)/shard_map/ppermute | solution.py:565
  10.2 21.1 %collective-permute-start.4 = (bf16[160,512]{1,0:T(8,128)(2,1)S(1)}, bf16[160,512]{1,0:T(8,128)(2,1)S(1)}, u32[]{:S(2)}, u32[]{:S(2)}) collective-permute-start(bf16[160,512]{1,0:T(8,128)(2,1)S(1)} %pad_maximum_fusion.6), channel_id=1, source_target_pairs={{0,4},{1,5},{2,6},{3,7},{4,0},{5,1},{6,2},{7,3},{8,12},{9,13},{10,... | collective-permute-start | bytes 491528 | tf_op jit(solution)/shard_map/ppermute | solution.py:565
  12.2 19.2 %collective-permute-start.5 = (bf16[160,512]{1,0:T(8,128)(2,1)S(1)}, bf16[160,512]{1,0:T(8,128)(2,1)S(1)}, u32[]{:S(2)}, u32[]{:S(2)}) collective-permute-start(bf16[160,512]{1,0:T(8,128)(2,1)S(1)} %pad_maximum_fusion.6), channel_id=1, source_target_pairs={{0,6},{1,7},{2,4},{3,5},{4,2},{5,3},{6,0},{7,1},{8,14},{9,15},{10,... | collective-permute-start | bytes 491528 | tf_op jit(solution)/shard_map/ppermute | solution.py:565
  16.1 15.3 %collective-permute-start.3 = (bf16[160,512]{1,0:T(8,128)(2,1)S(1)}, bf16[160,512]{1,0:T(8,128)(2,1)S(1)}, u32[]{:S(2)}, u32[]{:S(2)}) collective-permute-start(bf16[160,512]{1,0:T(8,128)(2,1)S(1)} %pad_maximum_fusion.6), channel_id=1, source_target_pairs={{0,2},{1,3},{2,0},{3,1},{4,6},{5,7},{6,4},{7,5},{8,10},{9,11},{10,... | collective-permute-start | bytes 491528 | tf_op jit(solution)/shard_map/ppermute | solution.py:565
  21.9 7.8 %collective-permute-start.7 = (bf16[4,32,1536]{2,1,0:T(8,128)(2,1)S(1)}, bf16[4,32,1536]{2,1,0:T(8,128)(2,1)S(1)}, u32[]{:S(2)}, u32[]{:S(2)}) collective-permute-start(bf16[4,32,1536]{2,1,0:T(8,128)(2,1)S(1)} %pad_maximum_fusion.4.refs_0_), channel_id=1, source_target_pairs={{0,1},{1,0},{2,3},{3,2},{4,5},{5,4},{6,7},{7,6},{8,9},{9,8},{10,11... | collective-permute-start | bytes 1179656 | tf_op jit(solution)/shard_map/ppermute | solution.py:565
  23.5 8.0 %collective-permute-start.6 = (bf16[4,32,1536]{2,1,0:T(8,128)(2,1)S(1)}, bf16[4,32,1536]{2,1,0:T(8,128)(2,1)S(1)}, u32[]{:S(2)}, u32[]{:S(2)}) collective-permute-start(bf16[4,32,1536]{2,1,0:T(8,128)(2,1)S(1)} %pad_maximum_fusion.4.refs_0_), channel_id=1, source_target_pairs={{0,8},{8,0},{16,24},{24,16},{1,9},{9,1},{17,25},{25,17},{2,10},{10... | collective-permute-start | bytes 1179656 | tf_op jit(solution)/shard_map/ppermute | solution.py:565
  31.5 24.0 %collective-permute-start.9 = (bf16[4,160,512]{2,1,0:T(8,128)(2,1)S(1)}, bf16[4,160,512]{2,1,0:T(8,128)(2,1)S(1)}, u32[]{:S(2)}, u32[]{:S(2)}) collective-permute-start(bf16[4,160,512]{2,1,0:T(8,128)(2,1)S(1)} %pad_maximum_fusion.refs_0_), channel_id=1, source_target_pairs={{0,1},{1,0},{2,3},{3,2},{4,5},{5,4},{6,7},{7,6},{8,9},{9,8},{10,11... | collective-permute-start | bytes 1966088 | tf_op jit(solution)/shard_map/ppermute | solution.py:565
  33.1 22.3 %collective-permute-start.10 = (bf16[128,512]{1,0:T(8,128)(2,1)}, bf16[128,512]{1,0:T(8,128)(2,1)S(1)}, u32[]{:S(2)}, u32[]{:S(2)}) collective-permute-start(bf16[128,512]{1,0:T(8,128)(2,1)} %pad_maximum_fusion.7), channel_id=1, source_target_pairs={{0,2},{1,3},{2,0},{3,1},{4,6},{5,7},{6,4},{7,5},{8,10},{9,11},{10,... | collective-permute-start | bytes 393224 | tf_op jit(solution)/shard_map/ppermute | solution.py:565
  36.3 19.2 %collective-permute-start.11 = (bf16[128,512]{1,0:T(8,128)(2,1)}, bf16[128,512]{1,0:T(8,128)(2,1)S(1)}, u32[]{:S(2)}, u32[]{:S(2)}) collective-permute-start(bf16[128,512]{1,0:T(8,128)(2,1)} %pad_maximum_fusion.7), channel_id=1, source_target_pairs={{0,4},{1,5},{2,6},{3,7},{4,0},{5,1},{6,2},{7,3},{8,12},{9,13},{10,... | collective-permute-start | bytes 393224 | tf_op jit(solution)/shard_map/ppermute | solution.py:565
  38.2 17.3 %collective-permute-start.12 = (bf16[128,512]{1,0:T(8,128)(2,1)}, bf16[128,512]{1,0:T(8,128)(2,1)S(1)}, u32[]{:S(2)}, u32[]{:S(2)}) collective-permute-start(bf16[128,512]{1,0:T(8,128)(2,1)} %pad_maximum_fusion.7), channel_id=1, source_target_pairs={{0,6},{1,7},{2,4},{3,5},{4,2},{5,3},{6,0},{7,1},{8,14},{9,15},{10,... | collective-permute-start | bytes 393224 | tf_op jit(solution)/shard_map/ppermute | solution.py:565
  39.7 18.1 %collective-permute-start.13 = (bf16[4,160,512]{2,1,0:T(8,128)(2,1)S(1)}, bf16[4,160,512]{2,1,0:T(8,128)(2,1)S(1)}, u32[]{:S(2)}, u32[]{:S(2)}) collective-permute-start(bf16[4,160,512]{2,1,0:T(8,128)(2,1)S(1)} %pad_maximum_fusion.refs_0_), channel_id=1, source_target_pairs={{0,8},{8,0},{16,24},{24,16},{1,9},{9,1},{17,25},{25,17},{2,10},{10... | collective-permute-start | bytes 1966088 | tf_op jit(solution)/shard_map/ppermute | solution.py:565
  58.4 22.9 %collective-permute-start.15 = (bf16[4,128,512]{2,1,0:T(8,128)(2,1)S(1)}, bf16[4,128,512]{2,1,0:T(8,128)(2,1)S(1)}, u32[]{:S(2)}, u32[]{:S(2)}) collective-permute-start(bf16[4,128,512]{2,1,0:T(8,128)(2,1)S(1)} %pad_maximum_fusion.1.refs_4_), channel_id=1, source_target_pairs={{0,1},{1,0},{2,3},{3,2},{4,5},{5,4},{6,7},{7,6},{8,9},{9,8},{10,11... | collective-permute-start | bytes 1572872 | tf_op jit(solution)/shard_map/ppermute | solution.py:565
  58.9 22.4 %collective-permute-start.16 = (bf16[4,128,512]{2,1,0:T(8,128)(2,1)S(1)}, bf16[4,128,512]{2,1,0:T(8,128)(2,1)S(1)}, u32[]{:S(2)}, u32[]{:S(2)}) collective-permute-start(bf16[4,128,512]{2,1,0:T(8,128)(2,1)S(1)} %pad_maximum_fusion.1.refs_4_), channel_id=1, source_target_pairs={{0,8},{8,0},{16,24},{24,16},{1,9},{9,1},{17,25},{25,17},{2,10},{10... | collective-permute-start | bytes 1572872 | tf_op jit(solution)/shard_map/ppermute | solution.py:565
  83.3 26.3 %collective-permute-start.18 = (bf16[2,4,256,256]{3,2,1,0:T(8,128)(2,1)}, bf16[2,4,256,256]{3,2,1,0:T(8,128)(2,1)S(1)}, u32[]{:S(2)}, u32[]{:S(2)}) collective-permute-start(bf16[2,4,256,256]{3,2,1,0:T(8,128)(2,1)} %get-tuple-element.227), channel_id=1, source_target_pairs={{0,2},{1,3},{2,0},{3,1},{4,6},{5,7},{6,4},{7,5},{8,10},{9,11},{10,... | collective-permute-start | bytes 3145736 | tf_op jit(solution)/shard_map/ppermute | solution.py:565
  109.6 4.0 %collective-permute-start.20 = (bf16[8,320,256]{2,1,0:T(8,128)(2,1)}, bf16[8,320,256]{2,1,0:T(8,128)(2,1)S(1)}, u32[]{:S(2)}, u32[]{:S(2)}) collective-permute-start(bf16[8,320,256]{2,1,0:T(8,128)(2,1)} %get-tuple-element.234), channel_id=1, source_target_pairs={{0,8},{8,0},{16,24},{24,16},{1,9},{9,1},{17,25},{25,17},{2,10},{10... | collective-permute-start | bytes 3932168 | tf_op jit(solution)/shard_map/ppermute | solution.py:565
  110.3 3.1 %collective-permute-start.19 = (bf16[4,256,256]{2,1,0:T(8,128)(2,1)S(1)}, bf16[4,256,256]{2,1,0:T(8,128)(2,1)S(1)}, u32[]{:S(2)}, u32[]{:S(2)}) collective-permute-start(bf16[4,256,256]{2,1,0:T(8,128)(2,1)S(1)} %slice_bitcast_fusion), channel_id=1, source_target_pairs={{0,8},{8,0},{16,24},{24,16},{1,9},{9,1},{17,25},{25,17},{2,10},{10... | collective-permute-start | bytes 1572872 | tf_op jit(solution)/shard_map/ppermute | solution.py:565
  113.9 22.7 %collective-permute-start.22 = (bf16[4,320,256]{2,1,0:T(8,128)(2,1)S(1)}, bf16[4,320,256]{2,1,0:T(8,128)(2,1)S(1)}, u32[]{:S(2)}, u32[]{:S(2)}) collective-permute-start(bf16[4,320,256]{2,1,0:T(8,128)(2,1)S(1)} %get-tuple-element.242), channel_id=1, source_target_pairs={{0,2},{1,3},{2,0},{3,1},{4,6},{5,7},{6,4},{7,5},{8,10},{9,11},{10,... | collective-permute-start | bytes 1966088 | tf_op jit(solution)/shard_map/ppermute | solution.py:565
  115.3 19.9 %collective-permute-start.21 = (bf16[2,256,256]{2,1,0:T(8,128)(2,1)S(1)}, bf16[2,256,256]{2,1,0:T(8,128)(2,1)S(1)}, u32[]{:S(2)}, u32[]{:S(2)}) collective-permute-start(bf16[2,256,256]{2,1,0:T(8,128)(2,1)S(1)} %get-tuple-element.240), channel_id=1, source_target_pairs={{0,4},{1,5},{2,6},{3,7},{4,0},{5,1},{6,2},{7,3},{8,12},{9,13},{10,... | collective-permute-start | bytes 786440 | tf_op jit(solution)/shard_map/ppermute | solution.py:565
  139.3 12.9 %collective-permute-start.25 = (bf16[896,256]{1,0:T(8,128)(2,1)S(1)}, bf16[896,256]{1,0:T(8,128)(2,1)S(1)}, u32[]{:S(2)}, u32[]{:S(2)}) collective-permute-start(bf16[896,256]{1,0:T(8,128)(2,1)S(1)} %get-tuple-element.263), channel_id=1, source_target_pairs={{0,1},{1,0},{2,3},{3,2},{4,5},{5,4},{6,7},{7,6},{8,9},{9,8},{10,11... | collective-permute-start | bytes 1376264 | tf_op jit(solution)/shard_map/ppermute | solution.py:565
  140.7 11.5 %collective-permute-start.24 = (bf16[4,192,256]{2,1,0:T(8,128)(2,1)S(1)}, bf16[4,192,256]{2,1,0:T(8,128)(2,1)S(1)}, u32[]{:S(2)}, u32[]{:S(2)}) collective-permute-start(bf16[4,192,256]{2,1,0:T(8,128)(2,1)S(1)} %get-tuple-element.261), channel_id=1, source_target_pairs={{0,2},{1,3},{2,0},{3,1},{4,6},{5,7},{6,4},{7,5},{8,10},{9,11},{10,... | collective-permute-start | bytes 1179656 | tf_op jit(solution)/shard_map/ppermute | solution.py:565
  152.5 10.9 %collective-permute-start.26 = (bf16[2,192,256]{2,1,0:T(8,128)(2,1)S(1)}, bf16[2,192,256]{2,1,0:T(8,128)(2,1)S(1)}, u32[]{:S(2)}, u32[]{:S(2)}) collective-permute-start(bf16[2,192,256]{2,1,0:T(8,128)(2,1)S(1)} %get-tuple-element.274), channel_id=1, source_target_pairs={{0,1},{1,0},{2,3},{3,2},{4,5},{5,4},{6,7},{7,6},{8,9},{9,8},{10,11... | collective-permute-start | bytes 589832 | tf_op jit(solution)/shard_map/ppermute | solution.py:565
  153.6 9.8 %collective-permute-start.27 = (bf16[1,320,256]{2,1,0:T(8,128)(2,1)S(1)}, bf16[1,320,256]{2,1,0:T(8,128)(2,1)S(1)}, u32[]{:S(2)}, u32[]{:S(2)}) collective-permute-start(bf16[1,320,256]{2,1,0:T(8,128)(2,1)S(1)} %get-tuple-element.276), channel_id=1, source_target_pairs={{0,4},{1,5},{2,6},{3,7},{4,0},{5,1},{6,2},{7,3},{8,12},{9,13},{10,... | collective-permute-start | bytes 491528 | tf_op jit(solution)/shard_map/ppermute | solution.py:565
  163.6 8.5 %collective-permute-start.28 = (bf16[576,256]{1,0:T(8,128)(2,1)S(1)}, bf16[576,256]{1,0:T(8,128)(2,1)S(1)}, u32[]{:S(2)}, u32[]{:S(2)}) collective-permute-start(bf16[576,256]{1,0:T(8,128)(2,1)S(1)} %pad_maximum_fusion.5), channel_id=1, source_target_pairs={{0,16},{8,24},{16,0},{24,8},{1,17},{9,25},{17,1},{25,9},{2,18},{10... | collective-permute-start | bytes 884744 | tf_op jit(solution)/shard_map/ppermute | solution.py:565
  165.1 6.9 %collective-permute-start.29 = (bf16[1,192,256]{2,1,0:T(8,128)(2,1)S(1)}, bf16[1,192,256]{2,1,0:T(8,128)(2,1)S(1)}, u32[]{:S(2)}, u32[]{:S(2)}) collective-permute-start(bf16[1,192,256]{2,1,0:T(8,128)(2,1)S(1)} %get-tuple-element.342), channel_id=1, source_target_pairs={{0,4},{1,5},{2,6},{3,7},{4,0},{5,1},{6,2},{7,3},{8,12},{9,13},{10,... | collective-permute-start | bytes 294920 | tf_op jit(solution)/shard_map/ppermute | solution.py:565
  172.2 7.8 %collective-permute-start.32 = (bf16[192,256]{1,0:T(8,128)(2,1)S(1)}, bf16[192,256]{1,0:T(8,128)(2,1)S(1)}, u32[]{:S(2)}, u32[]{:S(2)}) collective-permute-start(bf16[192,256]{1,0:T(8,128)(2,1)S(1)} %fusion.8), channel_id=1, source_target_pairs={{0,16},{8,24},{16,0},{24,8},{1,17},{9,25},{17,1},{25,9},{2,18},{10... | collective-permute-start | bytes 294920 | tf_op jit(solution)/shard_map/ppermute | solution.py:565
  173.0 7.0 %collective-permute-start.30 = (f32[8,512]{1,0:T(8,128)}, f32[8,512]{1,0:T(8,128)S(1)}, u32[]{:S(2)}, u32[]{:S(2)}) collective-permute-start(f32[8,512]{1,0:T(8,128)} %get-tuple-element.300), channel_id=1, source_target_pairs={{0,8},{8,0},{16,24},{24,16},{1,9},{9,1},{17,25},{25,17},{2,10},{10... | collective-permute-start | bytes 49160 | tf_op jit(solution)/shard_map/ppermute | solution.py:565
  180.4 4.7 %collective-permute-start.33 = (f32[8,512]{1,0:T(8,128)S(1)}, f32[8,512]{1,0:T(8,128)S(1)}, u32[]{:S(2)}, u32[]{:S(2)}) collective-permute-start(f32[8,512]{1,0:T(8,128)S(1)} %add_select_fusion.2), channel_id=1, source_target_pairs={{0,16},{8,24},{16,0},{24,8},{1,17},{9,25},{17,1},{25,9},{2,18},{10... | collective-permute-start | bytes 49160 | tf_op jit(solution)/shard_map/ppermute | solution.py:565
  185.9 3.7 %collective-permute-start.35 = (f32[8,512]{1,0:T(8,128)S(1)}, f32[8,512]{1,0:T(8,128)S(1)}, u32[]{:S(2)}, u32[]{:S(2)}) collective-permute-start(f32[8,512]{1,0:T(8,128)S(1)} %pad_add_fusion), channel_id=1, source_target_pairs={{0,1},{1,0},{2,3},{3,2},{4,5},{5,4},{6,7},{7,6},{8,9},{9,8},{10,11... | collective-permute-start | bytes 49160 | tf_op jit(solution)/shard_map/ppermute | solution.py:565
  189.7 3.7 %collective-permute-start.36 = (f32[8,512]{1,0:T(8,128)S(1)}, f32[8,512]{1,0:T(8,128)S(1)}, u32[]{:S(2)}, u32[]{:S(2)}) collective-permute-start(f32[8,512]{1,0:T(8,128)S(1)} %add_select_fusion.1), channel_id=1, source_target_pairs={{0,2},{1,3},{2,0},{3,1},{4,6},{5,7},{6,4},{7,5},{8,10},{9,11},{10,... | collective-permute-start | bytes 49160 | tf_op jit(solution)/shard_map/ppermute | solution.py:565
  193.5 4.6 %collective-permute-start.37 = (f32[8,512]{1,0:T(8,128)S(1)}, f32[8,512]{1,0:T(8,128)S(1)}, u32[]{:S(2)}, u32[]{:S(2)}) collective-permute-start(f32[8,512]{1,0:T(8,128)S(1)} %add_select_fusion.one), channel_id=1, source_target_pairs={{0,4},{1,5},{2,6},{3,7},{4,0},{5,1},{6,2},{7,3},{8,12},{9,13},{10,... | collective-permute-start | bytes 49160 | tf_op jit(solution)/shard_map/ppermute | solution.py:565
  (33 other events, 243.6 us)

commit v5 on v4

--- a/solution.py
+++ b/solution.py
@@ -29,7 +29,7 @@
 QUAD = 256
 F32 = jnp.float32
 BF16 = jnp.bfloat16
-VMEM_LIMIT = 60 * 1024 * 1024
+MIB = 1024 * 1024
 
 NT = (((1,), (1,)), ((), ()))
 NN = (((1,), (0,)), ((), ()))
@@ -597,7 +597,7 @@
 ANY = pl.BlockSpec(memory_space=pl.ANY)
 
 
-def kernel_call(kernel, name, grid, in_specs, out, scratch, us, args, **more):
+def kernel_call(kernel, name, grid, in_specs, out, scratch, mib, args, **more):
     return pl.pallas_call(
         kernel,
         grid=grid,
@@ -606,11 +606,9 @@
         out_shape=[shape for _, shape in out],
         scratch_shapes=scratch,
         compiler_params=pltpu.CompilerParams(
-            dimension_semantics=("arbitrary",) * len(grid), vmem_limit_bytes=VMEM_LIMIT
+            dimension_semantics=("arbitrary",) * len(grid), vmem_limit_bytes=mib * MIB
         ),
-        cost_estimate=pl.CostEstimate(
-            flops=us, bytes_accessed=us, transcendentals=0
-        ),
+        cost_estimate=pl.CostEstimate(flops=1, bytes_accessed=1, transcendentals=0),
         name=name,
         **more,
     )(*args)
@@ -679,55 +677,45 @@
     own_t, w_mixer_0, w_expand_0, w_reduce_0 = sync(own_t, w_mixer, w_expand, w_reduce)
     t_got = [steps_f(own_t, r) for r in rels_a[1:]]
     own_a = own_piece(w_expand_0, w_reduce_0, 0, [own_half(w_mixer_0).astype(BF16)])
+    own_b = own_piece(w_expand_0, w_reduce_0, 1, [])
+    a_near = steps_f(own_a, near)
     t_one = jnp.stack([own_t, *t_got])
-    a_got = [steps_f(own_a, r) for r in rels_a[1:]]
-    t_one, idx, norm, valid_mask, action_bins, w_expand_1, w_reduce_1 = sync(
-        t_one, idx, norm, valid_mask, action_bins, w_expand, w_reduce
-    )
+    t_one, idx, norm, own_a, own_b, a_near = sync(t_one, idx, norm, own_a, own_b, a_near)
     t_two = steps_f(t_one, near)
     t_refs, t_plan = [t_one], [(rels_a, nh - 1)]
     if nh == 2:
         t_refs.append(steps_d(t_one, 1))
         t_plan.append((rels_a, 2))
-    a_one = [own_a, *a_got]
-    own_b = own_piece(w_expand_1, w_reduce_1, 1, [])
     t_two, own_b = sync(t_two, own_b)
-    b_one = [own_b] + [steps_f(own_b, r) for r in rels_a[1:]]
+    b_near = steps_f(own_b, near)
+    a_pair, b_pair = jnp.stack([own_a, a_near]), jnp.stack([own_b, b_near])
+    a_got = [steps_f(a_pair, r) for r in rels_a[1:]]
     t_refs.append(t_two)
     t_plan.append((rels_b, nh - 1))
     if nh == 2:
-        t_refs.append(steps_d(t_two, 1))
-        t_plan.append((rels_b, 2))
+        for i, r in enumerate(rels_b):
+            t_refs.append(steps_d(t_two[i : i + 1], 1))
+            t_plan.append(([r], 2))
     nw = len(t_refs)
-    places = jnp.arange(rows)
-    inside = places[None, :] < lengths[:, None]
-    counted = ((valid_mask == 1) & inside).astype(jnp.int32).reshape(1, flat)
-    bins_t = action_bins.reshape(flat, ACT).T
-    a_one = jnp.stack(a_one)
-    bins_t, counted, norm, a_one, *t_refs = sync(bins_t, counted, norm, a_one, *t_refs)
-    a_two = steps_f(a_one, near)
-    a_refs, a_plan = [a_one], [(rels_a, nh - 1)]
-    if nh == 2:
-        a_refs.append(steps_d(a_one, 1))
-        a_plan.append((rels_a, 2))
+    pair_plan = [([0, near], nh - 1)]
+    got_plan = [([r, r ^ near], nh - 1) for r in rels_a[1:]]
+    a_refs, a_plan = [a_pair], pair_plan + got_plan
+    norm, b_pair, *t_refs = sync(norm, b_pair, *t_refs)
+    b_refs, b_got = [b_pair], [steps_f(b_pair, r) for r in rels_a[1:]]
     triple, n1, attended, lse = kernel_call(
         functools.partial(f1_kernel, t_plan, nw), "f1", (ep,),
         [SMEM, SMEM, ep_block(D), norm_spec] + [ANY] * nw,
         [low(3 * D), low(D), low(D), (lse_spec, jax.ShapeDtypeStruct((ep, 16, QUAD), F32))],
-        [wt_scratch, pltpu.VMEM((padded, 3 * D), BF16), dma], 18,
+        [wt_scratch, pltpu.VMEM((padded, 3 * D), BF16), dma], 60,
         (idx, lengths, tokens, norm, *t_refs),
     )
-    attended, a_two, *b_one = sync(attended, a_two, *b_one)
-    a_refs.append(a_two)
-    a_plan.append((rels_b, nh - 1))
+    attended, *a_got = sync(attended, *a_got)
+    a_refs += a_got
     if nh == 2:
-        a_refs.append(steps_d(a_two, 1))
-        a_plan.append((rels_b, 2))
+        a_refs += [steps_d(v, 1) for v in [a_pair, *a_got]]
+        a_plan = a_plan + [(rels, 2) for rels, _ in a_plan]
     na = len(a_refs)
-    b_one = jnp.stack(b_one)
-    attended, b_one, *a_refs = sync(attended, b_one, *a_refs)
-    b_two = steps_f(b_one, near)
-    b_refs = [b_one] + ([steps_d(b_one, 1)] if nh == 2 else [])
+    attended, *a_refs = sync(attended, *a_refs)
 
     order = f_bits[1:2] + f_bits[:1] + f_bits[2:]
     late = order[2:]
@@ -755,7 +743,7 @@
         functools.partial(f2a_kernel, a_plan, na, pos_a, rows), "f2a", (fl_steps,),
         [SMEM, SMEM] + [fl_block(D)] * 3 + [norm_spec] + [ANY] * na,
         [fl_wide(D)] * 3 + [fl_low(D)] + [low_out(nh, half, rows_a, QUAD)] * 2,
-        ff_scratch + [pltpu.SemaphoreType.DMA((2,))], 22, (idx, lengths, attended, tok_flat, cot_flat, norm, *a_refs),
+        ff_scratch + [pltpu.SemaphoreType.DMA((2,))], 50, (idx, lengths, attended, tok_flat, cot_flat, norm, *a_refs),
     )
 
     def halves(keep, got):
@@ -773,25 +761,33 @@
     def core_add(pair):
         return add_low(*pair) if pair[1] is not None else pair[0]
 
-    n2, keep_a, send_a, b_two, *b_refs = sync(n2, keep_a, send_a, b_two, *b_refs)
-    b_refs += [b_two] + ([steps_d(b_two, 1)] if nh == 2 else [])
+    n2, keep_a, send_a, *b_got = sync(n2, keep_a, send_a, *b_got)
+    b_refs += b_got
+    if nh == 2:
+        b_refs += [steps_d(v, 1) for v in [b_pair, *b_got]]
     n2, keep_a, send_a, *b_refs = sync(n2, keep_a, send_a, *b_refs)
     got_a = steps_f(send_a, order[0])
     block_out, gh, ga, *rest = kernel_call(
         functools.partial(f2b_kernel, a_plan, na, pos, nh, rows), "f2b", (fl_steps,),
         [SMEM, SMEM] + [fl_block(D)] * 6 + [norm_spec] + [ANY] * (2 * na),
         [fl_low(D), fl_wide(D), fl_low(D)] + [low_out(n_f, rows_b, QUAD)] * nh + [whole((8, D))],
-        ff_scratch + [pltpu.VMEM((D, D), F32), pltpu.SemaphoreType.DMA((2,))], 24,
+        ff_scratch + [pltpu.VMEM((D, D), F32), pltpu.SemaphoreType.DMA((2,))], 54,
         (idx, lengths, attended, hidden, out_part, g2_part, n2, cot_flat, norm, *a_refs, *b_refs),
     )
     grads_b, ln2 = rest[:nh], rest[nh]
-    ga, keep_a, got_a, *grads_b = sync(ga, keep_a, got_a, *grads_b)
+    ga, valid_mask, action_bins, keep_a, got_a, *grads_b = sync(
+        ga, valid_mask, action_bins, keep_a, got_a, *grads_b
+    )
     pair_b = core_pair(grads_b)
+    places = jnp.arange(rows)
+    inside = places[None, :] < lengths[:, None]
+    counted = ((valid_mask == 1) & inside).astype(jnp.int32).reshape(1, flat)
+    bins_t = action_bins.reshape(flat, ACT).T
     sum_a = add_low(keep_a, got_a)
     pair_a = core_pair(sum_a)
     keep_b, send_b = core_halves_of(pair_b)
     keep_a, send_a = core_halves_of(pair_a)
-    ga, keep_a, send_a, keep_b, send_b = sync(ga, keep_a, send_a, keep_b, send_b)
+    ga, counted, bins_t, keep_a, send_a, keep_b, send_b = sync(ga, counted, bins_t, keep_a, send_a, keep_b, send_b)
 
     got_b = steps_f(send_b, order[0])
     got_a = steps_f(send_a, order_a[1])
@@ -806,7 +802,7 @@
             pltpu.VMEM((rows16, D), F32), pltpu.VMEM((D, 3 * D), F32),
             pltpu.VMEM((pack_rows, D), BF16), pltpu.VMEM((pack_rows, 3 * D), BF16),
         ],
-        25, (idx, lengths, triple, ga.reshape(ep, rows, D), lse, n1),
+        44, (idx, lengths, triple, ga.reshape(ep, rows, D), lse, n1),
     )
     gtri, keep_a, got_a, keep_b, got_b, *grads_t = sync(gtri, keep_a, got_a, keep_b, got_b, *grads_t)
 
@@ -836,7 +832,7 @@
             pl.BlockSpec((qb, D), lambda i: (i, 0)), const_spec((ACT * NBINS, D)),
             pl.BlockSpec((ACT, qb), lambda i: (0, i)), pl.BlockSpec((1, qb), lambda i: (0, i)),
         ],
-        [whole((16, qb))] * 2, [], 10, (block_out, value_head, bins_t, counted),
+        [whole((16, qb))] * 2, [], 20, (block_out, value_head, bins_t, counted),
     )
     gtri, q_sum, keep_t, got_t, keep_ab, got_ab = sync(gtri, q_sum, keep_t, got_t, keep_ab, got_ab)
 
@@ -848,7 +844,7 @@
             functools.partial(b2_kernel, t_plan, nw, prior is None), "b2", (n,),
             [SMEM, fl_block(3 * D, at), fl_block(D, at), fl_block(D, at), norm_spec] + [ANY] * nw + specs,
             [(fl_block(D, at), jax.ShapeDtypeStruct((flat, D), BF16)), whole((8, D))],
-            [wt_scratch, dma], 6, (idx, gtri, tok_flat, gh, norm, *t_refs, *extra), **more,
+            [wt_scratch, dma], 28, (idx, gtri, tok_flat, gh, norm, *t_refs, *extra), **more,
         )
 
     keep_t, send_t = halves(keep_t, got_t)
@@ -899,7 +895,7 @@
     small_core = steps_d(small, d_bits[0])
     red_t, *red_parts = sync(red_t, *red_parts)
     like = lambda w: whole(w.shape)
-    full = lambda *ws: [const_spec(w.shape) for w in ws]
+    full = lambda *ws: [pl.BlockSpec(memory_space=pltpu.VMEM)] * len(ws)
     mlp_state = (
         w_mixer, first_mixer, second_mixer, w_expand, first_expand, second_expand,
         w_reduce, first_reduce, second_reduce,
@@ -908,7 +904,7 @@
         functools.partial(lamb_mlp_kernel, n_f, nh, rows_a), "lamb_mlp", (1,),
         [SMEM] + full(*red_parts, *mlp_state),
         [like(w) for w in (w_mixer, w_expand, w_reduce) for _ in range(3)] + [whole((8, 128))],
-        [], 4, (idx, *red_parts, *mlp_state),
+        [], 20, (idx, *red_parts, *mlp_state),
     )
     small, small_core, sq_mlp, red_t, got_rt = sync(small, small_core, sq_mlp, red_t, got_rt)
     small = merge_small(small, small_core)
@@ -921,7 +917,7 @@
         functools.partial(lamb_triple_kernel, n_f, nh), "lamb_triple", (1,),
         [SMEM] + full(*parts_t, sq_mlp, *tri_state),
         [like(w_triple)] * 3 + [whole((8, 128))],
-        [], 2, (idx, *parts_t, sq_mlp, *tri_state),
+        [], 12, (idx, *parts_t, sq_mlp, *tri_state),
     )
 
     small = small + jnp.pad(squares, ((0, 0), (0, D - 128)))
@@ -936,7 +932,7 @@
         full(small, small_two, norm_t, firsts_t, seconds_t, *masters, *updates),
         [like(w) for w in masters]
         + [whole((4, D))] * 3 + [whole((2, 8)), whole((1, ACT)), whole((1, ACT))],
-        [], 3, (small, small_two, norm_t, firsts_t, seconds_t, *masters, *updates),
+        [], 16, (small, small_two, norm_t, firsts_t, seconds_t, *masters, *updates),
     )
     return (
         block_out.reshape(ep, rows, D), input_grad.reshape(ep, rows, D), *news,

time: 203 us -> 194 us (0.956)
  Pallas kernels: 110 us -> 103 us
  waiting for transfers between devices: 30.7 us -> 36.9 us
  local copies, waits for them, and re-layouts: 12.3 us -> 6.46 us
    pallas_call x10, Pallas kernels: 110 us -> 103 us  [kernel_call(): pl.pallas_call(kernel, grid=grid, in_specs=in_specs, out_specs=[spec for...]
    ppermute x38 -> x45, waiting for transfers between devices: 30.7 us -> 36.9 us  [xor_step(): return lax.ppermute(v, axis, [(i, i ^ bit) for i in range(size)])]
    unnamed x54 -> x126, local copies, waits for them, and re-layouts: 3.71 us -> 0.94 us
    ppermute x38 -> x45, starting transfers between devices: 42 us -> 42.1 us  [xor_step(): return lax.ppermute(v, axis, [(i, i ^ bit) for i in range(size)])]
  transfers between devices with their start and end apart: 38 -> 45, of which waited for: 13 -> 23; matrix products, arithmetic and copies ran while one was open for 5% -> 3% of each run, Pallas kernels for 53% -> 52%
where the time goes in v5:
time: 194 us
  Pallas kernels  103 us (53%)
  starting transfers between devices  42.1 us (22%)
  waiting for transfers between devices  36.9 us (19%)
  local copies, waits for them, and re-layouts  6.46 us (3%)
  other arithmetic  4.3 us (2%)
    pallas_call x10, Pallas kernels, kernel_call(): pl.pallas_call(kernel, grid=grid, in_specs=in_specs, out_specs=[spec for...  103 us
    ppermute x45, starting transfers between devices, xor_step(): return lax.ppermute(v, axis, [(i, i ^ bit) for i in range(size)])  42.1 us
    ppermute x45, waiting for transfers between devices, xor_step(): return lax.ppermute(v, axis, [(i, i ^ bit) for i in range(size)])  36.9 us
  transfers between devices with their start and end apart: 45, of which 23 were waited for; matrix products, arithmetic and copies ran while one was open for 3% of the time, Pallas kernels for 52%

profile of v5, /device:TPU:0, one launch (start us, length us, event | category | flops | bytes accessed | tf_op | source)
XLA Modules:
  0.0 193.9 jit_solution(10328916203232078985)
XLA Ops:
  1.6 3.1 %collective-permute-start = (bf16[32,1536]{1,0:T(8,128)(2,1)S(1)}, bf16[32,1536]{1,0:T(8,128)(2,1)S(1)}, u32[]{:S(2)}, u32[]{:S(2)}) collective-permute-start(bf16[32,1536]{1,0:T(8,128)(2,1)S(1)} %dynamic-slice_convert_fusion.1), channel_id=1, source_target_pairs={{0,2},{1,3},{2,0},{3,1},{4,6},{5,7},{6,4},{7,5},{8,10},{9,11},{10,... | collective-permute-start | bytes 294920 | tf_op jit(solution)/shard_map/ppermute | solution.py:565
  4.7 2.6 %collective-permute-start.1 = (bf16[32,1536]{1,0:T(8,128)(2,1)S(1)}, bf16[32,1536]{1,0:T(8,128)(2,1)S(1)}, u32[]{:S(2)}, u32[]{:S(2)}) collective-permute-start(bf16[32,1536]{1,0:T(8,128)(2,1)S(1)} %dynamic-slice_convert_fusion.1), channel_id=1, source_target_pairs={{0,4},{1,5},{2,6},{3,7},{4,0},{5,1},{6,2},{7,3},{8,12},{9,13},{10,... | collective-permute-start | bytes 294920 | tf_op jit(solution)/shard_map/ppermute | solution.py:565
  10.3 1.8 collective-permute-start.3
  13.3 1.8 collective-permute-done.1
  15.7 1.7 collective-permute-start.4
  18.5 3.1 %collective-permute-start.12 = (bf16[2,160,512]{2,1,0:T(8,128)(2,1)S(1)}, bf16[2,160,512]{2,1,0:T(8,128)(2,1)S(1)}, u32[]{:S(2)}, u32[]{:S(2)}) collective-permute-start(bf16[2,160,512]{2,1,0:T(8,128)(2,1)S(1)} %pad_maximum_fusion.3.refs_0_), channel_id=1, source_target_pairs={{0,4},{1,5},{2,6},{3,7},{4,0},{5,1},{6,2},{7,3},{8,12},{9,13},{10,... | collective-permute-start | bytes 983048 | tf_op jit(solution)/shard_map/ppermute | solution.py:565
  21.9 3.2 %collective-permute-done.4.refs_2_ = bf16[4,32,1536]{2,1,0:T(8,128)(2,1)S(1)} collective-permute-done((bf16[4,32,1536]{2,1,0:T(8,128)(2,1)S(1)}, bf16[4,32,1536]{2,1,0:T(8,128)(2,1)S(1)}, u32[]{:S(2)}, u32[]{:S(2)}) %collective-permute-start.4) | collective-permute-done | bytes 393248 | tf_op jit(solution)/shard_map/ppermute | solution.py:565
  28.3 2.8 %collective-permute-done.5 = bf16[128,512]{1,0:T(8,128)(2,1)S(1)} collective-permute-done((bf16[128,512]{1,0:T(8,128)(2,1)S(1)}, bf16[128,512]{1,0:T(8,128)(2,1)S(1)}, u32[]{:S(2)}, u32[]{:S(2)}) %collective-permute-start.5) | collective-permute-done | bytes 131104 | tf_op jit(solution)/shard_map/ppermute | solution.py:565
  33.1 15.7 %f1.1 = (bf16[6,296,1536]{2,1,0:T(8,128)(2,1)}, bf16[6,296,512]{2,1,0:T(8,128)(2,1)}, bf16[6,296,512]{2,1,0:T(8,128)(2,1)}, f32[6,16,256]{2,1,0:T(8,128)}) custom-call(s32[2]{0:T(128)} %pad_add_fusion.1.idx, s32[6]{0:T(128)} %lens.7, bf16[6,296,512]{2,1,0:T(8,128)(2,1)} %tok.1, f32[8,512]{1,0:T(8,128)} %concatenate.34.norm, bf16[4,32,1536]{2,1,0:T(8,128)(2,1)} %copy-done.3, ...), custom_call_target="tpu_custom_call" | custom-call | flops 1 | bytes 1 | tf_op jit(solution)/shard_map/f1/pallas_call | solution.py:601
  49.6 2.4 %collective-permute-start.18 = (bf16[2,128,512]{2,1,0:T(8,128)(2,1)S(1)}, bf16[2,128,512]{2,1,0:T(8,128)(2,1)S(1)}, u32[]{:S(2)}, u32[]{:S(2)}) collective-permute-start(bf16[2,128,512]{2,1,0:T(8,128)(2,1)S(1)} %pad_maximum_fusion.5.refs_8_), channel_id=1, source_target_pairs={{0,2},{1,3},{2,0},{3,1},{4,6},{5,7},{6,4},{7,5},{8,10},{9,11},{10,... | collective-permute-start | bytes 786440 | tf_op jit(solution)/shard_map/ppermute | solution.py:565
  52.0 1.8 collective-permute-start.19
  54.6 23.8 %f2a.1 = (f32[1776,512]{1,0:T(8,128)}, f32[1776,512]{1,0:T(8,128)}, f32[1776,512]{1,0:T(8,128)}, bf16[1776,512]{1,0:T(8,128)(2,1)}, bf16[2,4,256,256]{3,2,1,0:T(...) custom-call(s32[2]{0:T(128)S(1)} %copy-done.44, s32[6]{0:T(128)S(1)} %copy-done.48, bf16[1776,512]{1,0:T(8,128)(2,1)} %bitcast.71, ...), custom_call_target="tpu_custom_call" | custom-call | flops 1 | bytes 1 | tf_op jit(solution)/shard_map/f2a/pallas_call | solution.py:601
  82.0 25.4 %f2b.1 = (bf16[1776,512]{1,0:T(8,128)(2,1)}, f32[1776,512]{1,0:T(8,128)}, bf16[1776,512]{1,0:T(8,128)(2,1)}, bf16[8,320,256]{2,1,0:T(8,128)(2,1)}, bf16[8,320,256]{2,1,0:T(8,128)(2,1)}, /*index=5*/f32[8,512]{1,0:T(8,128)}) custom-call(s32[2]{0:T(128)} %pad_add_fusion.1.idx, s32[6]{0:T(128)} %lens.7, bf16[1776,512]{1,0:T(8,128)(2,1)} %bitcast.72, ...), custom_call_target="tpu_custom_call" | custom-call | flops 1 | bytes 1 | tf_op jit(solution)/shard_map/f2b/pallas_call | solution.py:601
  109.5 2.1 %collective-permute-done.26 = bf16[4,256,256]{2,1,0:T(8,128)(2,1)S(1)} collective-permute-done((bf16[4,256,256]{2,1,0:T(8,128)(2,1)}, bf16[4,256,256]{2,1,0:T(8,128)(2,1)S(1)}, u32[]{:S(2)}, u32[]{:S(2)}) %collective-permute-start.26) | collective-permute-done | bytes 524320 | tf_op jit(solution)/shard_map/ppermute | solution.py:565
  111.8 1.8 add_convert_fusion.1
  114.7 2.2 %collective-permute-start.28 = (bf16[2,256,256]{2,1,0:T(8,128)(2,1)S(1)}, bf16[2,256,256]{2,1,0:T(8,128)(2,1)S(1)}, u32[]{:S(2)}, u32[]{:S(2)}) collective-permute-start(bf16[2,256,256]{2,1,0:T(8,128)(2,1)S(1)} %get-tuple-element.258), channel_id=1, source_target_pairs={{0,4},{1,5},{2,6},{3,7},{4,0},{5,1},{6,2},{7,3},{8,12},{9,13},{10,... | collective-permute-start | bytes 786440 | tf_op jit(solution)/shard_map/ppermute | solution.py:565
  116.9 12.1 %b1.1 = (bf16[6,296,1536]{2,1,0:T(8,128)(2,1)}, bf16[8,192,256]{2,1,0:T(8,128)(2,1)S(1)}, bf16[8,192,256]{2,1,0:T(8,128)(2,1)S(1)}) custom-call(s32[2]{0:T(128)S(1)} %copy-done.45, s32[6]{0:T(128)S(1)} %copy-done.49, bf16[6,296,1536]{2,1,0:T(8,128)(2,1)} %get-tuple-element.240.tri_ref, bf16[6,296,512]{2,1,0:T(8,128)(2,1)S(1)} %bitcast.62, ...), custom_call_target="tpu_custom_call" | custom-call | flops 1 | bytes 1 | tf_op jit(solution)/shard_map/b1/pallas_call | solution.py:601
  129.0 5.7 %collective-permute-done.28 = bf16[2,256,256]{2,1,0:T(8,128)(2,1)S(1)} collective-permute-done((bf16[2,256,256]{2,1,0:T(8,128)(2,1)S(1)}, bf16[2,256,256]{2,1,0:T(8,128)(2,1)S(1)}, u32[]{:S(2)}, u32[]{:S(2)}) %collective-permute-start.28) | collective-permute-done | bytes 262176 | tf_op jit(solution)/shard_map/ppermute | solution.py:565
  136.4 1.9 collective-permute-done.30
  139.6 3.1 %collective-permute-start.31 = (bf16[4,192,256]{2,1,0:T(8,128)(2,1)S(1)}, bf16[4,192,256]{2,1,0:T(8,128)(2,1)S(1)}, u32[]{:S(2)}, u32[]{:S(2)}) collective-permute-start(bf16[4,192,256]{2,1,0:T(8,128)(2,1)S(1)} %get-tuple-element.279), channel_id=1, source_target_pairs={{0,2},{1,3},{2,0},{3,1},{4,6},{5,7},{6,4},{7,5},{8,10},{9,11},{10,... | collective-permute-start | bytes 1179656 | tf_op jit(solution)/shard_map/ppermute | solution.py:565
  142.8 7.2 %qstat.1 = (f32[16,256]{1,0:T(8,128)S(1)}, f32[16,256]{1,0:T(8,128)S(1)}) custom-call(bf16[1776,512]{1,0:T(8,128)(2,1)S(1)} %copy-done.16, bf16[2816,512]{1,0:T(8,128)(2,1)S(1)} %copy-done.11, s32[11,1776]{1,0:T(8,128)S(1)} %bitcast.64, s32[1,1776]{1,0:T(1,128)S(1)} %reshape.130.cnt), custom_call_target="tpu_custom_call" | custom-call | flops 1 | bytes 1 | tf_op jit(solution)/shard_map/qstat/pallas_call | solution.py:601
  150.0 1.9 collective-permute-done.31
  152.8 1.8 collective-permute-start.34
  154.7 6.9 %b2.2 = (bf16[1776,512]{1,0:T(8,128)(2,1)}, f32[8,512]{1,0:T(8,128)S(1)}) custom-call(s32[2]{0:T(128)S(1)} %copy-done.45, bf16[1776,1536]{1,0:T(8,128)(2,1)S(1)} %bitcast.60, bf16[1776,512]{1,0:T(8,128)(2,1)S(1)} %bitcast.58, f32[1776,512]{1,0:T(8,128)S(1)} %copy-done.2, f32[8,512]{1,0:T(8,128)S(1)} %copy-done.34, bf16[4,32,1536]{2,1,0:T(8,128)(2,1)S(1)} %copy-done.4, ...), custom_call_target="tpu_custom_call" | custom-call | flops 1 | bytes 1 | tf_op jit(solution)/shard_map/b2/pallas_call | solution.py:601
  164.5 5.1 %b2.3 = (bf16[1776,512]{1,0:T(8,128)(2,1)}, f32[8,512]{1,0:T(8,128)S(1)}) custom-call(s32[2]{0:T(128)S(1)} %copy-done.45, bf16[1776,1536]{1,0:T(8,128)(2,1)S(1)} %bitcast.61, bf16[1776,512]{1,0:T(8,128)(2,1)S(1)} %bitcast.59, f32[1776,512]{1,0:T(8,128)S(1)} %copy-done.2, f32[8,512]{1,0:T(8,128)S(1)} %copy-done.34, ...), custom_call_target="tpu_custom_call", output_to_operand_aliasing={{0}: (12, {})} | custom-call | flops 1 | bytes 1 | tf_op jit(solution)/shard_map/b2/pallas_call | solution.py:601
  173.0 3.1 %lamb_mlp.1 = (f32[64,512]{1,0:T(8,128)}, f32[64,512]{1,0:T(8,128)}, f32[64,512]{1,0:T(8,128)S(1)}, f32[64,2048]{1,0:T(8,128)}, f32[64,2048]{1,0:T(8,128)}, /*in...) custom-call(s32[2]{0:T(128)S(1)} %copy-done.45, ...), custom_call_target="tpu_custom_call" | custom-call | flops 1 | bytes 1 | tf_op jit(solution)/shard_map/lamb_mlp/pallas_call | solution.py:601
  177.8 1.8 lamb_triple.1
  181.2 2.8 %collective-permute-done.42 = f32[8,512]{1,0:T(8,128)S(1)} collective-permute-done((f32[8,512]{1,0:T(8,128)S(1)}, f32[8,512]{1,0:T(8,128)S(1)}, u32[]{:S(2)}, u32[]{:S(2)}) %collective-permute-start.42) | collective-permute-done | bytes 16416 | tf_op jit(solution)/shard_map/ppermute | solution.py:565
  184.1 1.7 collective-permute-start.43
  185.8 2.0 %collective-permute-done.43 = f32[8,512]{1,0:T(8,128)S(1)} collective-permute-done((f32[8,512]{1,0:T(8,128)S(1)}, f32[8,512]{1,0:T(8,128)S(1)}, u32[]{:S(2)}, u32[]{:S(2)}) %collective-permute-start.43) | collective-permute-done | bytes 16416 | tf_op jit(solution)/shard_map/ppermute | solution.py:565
  187.9 1.8 collective-permute-start.44
  189.7 2.8 %collective-permute-done.44.two = f32[8,512]{1,0:T(8,128)S(1)} collective-permute-done((f32[8,512]{1,0:T(8,128)S(1)}, f32[8,512]{1,0:T(8,128)S(1)}, u32[]{:S(2)}, u32[]{:S(2)}) %collective-permute-start.44) | collective-permute-done | bytes 16416 | tf_op jit(solution)/shard_map/ppermute | solution.py:565
  (234 shorter events, 35.1 us)
Async XLA Ops:
  1.6 11.7 %collective-permute-start = (bf16[32,1536]{1,0:T(8,128)(2,1)S(1)}, bf16[32,1536]{1,0:T(8,128)(2,1)S(1)}, u32[]{:S(2)}, u32[]{:S(2)}) collective-permute-start(bf16[32,1536]{1,0:T(8,128)(2,1)S(1)} %dynamic-slice_convert_fusion.1), channel_id=1, source_target_pairs={{0,2},{1,3},{2,0},{3,1},{4,6},{5,7},{6,4},{7,5},{8,10},{9,11},{10,... | collective-permute-start | bytes 294920 | tf_op jit(solution)/shard_map/ppermute | solution.py:565
  4.7 10.4 %collective-permute-start.1 = (bf16[32,1536]{1,0:T(8,128)(2,1)S(1)}, bf16[32,1536]{1,0:T(8,128)(2,1)S(1)}, u32[]{:S(2)}, u32[]{:S(2)}) collective-permute-start(bf16[32,1536]{1,0:T(8,128)(2,1)S(1)} %dynamic-slice_convert_fusion.1), channel_id=1, source_target_pairs={{0,4},{1,5},{2,6},{3,7},{4,0},{5,1},{6,2},{7,3},{8,12},{9,13},{10,... | collective-permute-start | bytes 294920 | tf_op jit(solution)/shard_map/ppermute | solution.py:565
  7.3 7.8 %collective-permute-start.2 = (bf16[32,1536]{1,0:T(8,128)(2,1)S(1)}, bf16[32,1536]{1,0:T(8,128)(2,1)S(1)}, u32[]{:S(2)}, u32[]{:S(2)}) collective-permute-start(bf16[32,1536]{1,0:T(8,128)(2,1)S(1)} %dynamic-slice_convert_fusion.1), channel_id=1, source_target_pairs={{0,6},{1,7},{2,4},{3,5},{4,2},{5,3},{6,0},{7,1},{8,14},{9,15},{10,... | collective-permute-start | bytes 294920 | tf_op jit(solution)/shard_map/ppermute | solution.py:565
  10.3 5.4 %collective-permute-start.3 = (bf16[160,512]{1,0:T(8,128)(2,1)S(1)}, bf16[160,512]{1,0:T(8,128)(2,1)S(1)}, u32[]{:S(2)}, u32[]{:S(2)}) collective-permute-start(bf16[160,512]{1,0:T(8,128)(2,1)S(1)} %pad_maximum_fusion.6), channel_id=1, source_target_pairs={{0,1},{1,0},{2,3},{3,2},{4,5},{5,4},{6,7},{7,6},{8,9},{9,8},{10,11... | collective-permute-start | bytes 491528 | tf_op jit(solution)/shard_map/ppermute | solution.py:565
  15.7 9.4 %collective-permute-start.4 = (bf16[4,32,1536]{2,1,0:T(8,128)(2,1)S(1)}, bf16[4,32,1536]{2,1,0:T(8,128)(2,1)S(1)}, u32[]{:S(2)}, u32[]{:S(2)}) collective-permute-start(bf16[4,32,1536]{2,1,0:T(8,128)(2,1)S(1)} %pad_maximum_fusion.2.refs_0_), channel_id=1, source_target_pairs={{0,1},{1,0},{2,3},{3,2},{4,5},{5,4},{6,7},{7,6},{8,9},{9,8},{10,11... | collective-permute-start | bytes 1179656 | tf_op jit(solution)/shard_map/ppermute | solution.py:565
  17.4 7.8 %collective-permute-start.6 = (bf16[4,32,1536]{2,1,0:T(8,128)(2,1)S(1)}, bf16[4,32,1536]{2,1,0:T(8,128)(2,1)S(1)}, u32[]{:S(2)}, u32[]{:S(2)}) collective-permute-start(bf16[4,32,1536]{2,1,0:T(8,128)(2,1)S(1)} %pad_maximum_fusion.2.refs_0_), channel_id=1, source_target_pairs={{0,8},{8,0},{16,24},{24,16},{1,9},{9,1},{17,25},{25,17},{2,10},{10... | collective-permute-start | bytes 1179656 | tf_op jit(solution)/shard_map/ppermute | solution.py:565
  17.5 31.4 %collective-permute-start.11 = (bf16[2,160,512]{2,1,0:T(8,128)(2,1)S(1)}, bf16[2,160,512]{2,1,0:T(8,128)(2,1)S(1)}, u32[]{:S(2)}, u32[]{:S(2)}) collective-permute-start(bf16[2,160,512]{2,1,0:T(8,128)(2,1)S(1)} %pad_maximum_fusion.3.refs_0_), channel_id=1, source_target_pairs={{0,2},{1,3},{2,0},{3,1},{4,6},{5,7},{6,4},{7,5},{8,10},{9,11},{10,... | collective-permute-start | bytes 983048 | tf_op jit(solution)/shard_map/ppermute | solution.py:565
  18.5 30.3 %collective-permute-start.12 = (bf16[2,160,512]{2,1,0:T(8,128)(2,1)S(1)}, bf16[2,160,512]{2,1,0:T(8,128)(2,1)S(1)}, u32[]{:S(2)}, u32[]{:S(2)}) collective-permute-start(bf16[2,160,512]{2,1,0:T(8,128)(2,1)S(1)} %pad_maximum_fusion.3.refs_0_), channel_id=1, source_target_pairs={{0,4},{1,5},{2,6},{3,7},{4,0},{5,1},{6,2},{7,3},{8,12},{9,13},{10,... | collective-permute-start | bytes 983048 | tf_op jit(solution)/shard_map/ppermute | solution.py:565
  21.7 27.2 %collective-permute-start.13 = (bf16[2,160,512]{2,1,0:T(8,128)(2,1)S(1)}, bf16[2,160,512]{2,1,0:T(8,128)(2,1)S(1)}, u32[]{:S(2)}, u32[]{:S(2)}) collective-permute-start(bf16[2,160,512]{2,1,0:T(8,128)(2,1)S(1)} %pad_maximum_fusion.3.refs_0_), channel_id=1, source_target_pairs={{0,6},{1,7},{2,4},{3,5},{4,2},{5,3},{6,0},{7,1},{8,14},{9,15},{10,... | collective-permute-start | bytes 983048 | tf_op jit(solution)/shard_map/ppermute | solution.py:565
  25.2 5.9 %collective-permute-start.5 = (bf16[128,512]{1,0:T(8,128)(2,1)S(1)}, bf16[128,512]{1,0:T(8,128)(2,1)S(1)}, u32[]{:S(2)}, u32[]{:S(2)}) collective-permute-start(bf16[128,512]{1,0:T(8,128)(2,1)S(1)} %pad_maximum_fusion.7), channel_id=1, source_target_pairs={{0,1},{1,0},{2,3},{3,2},{4,5},{5,4},{6,7},{7,6},{8,9},{9,8},{10,11... | collective-permute-start | bytes 393224 | tf_op jit(solution)/shard_map/ppermute | solution.py:565
  31.2 20.7 %collective-permute-start.14 = (bf16[2,160,512]{2,1,0:T(8,128)(2,1)S(1)}, bf16[2,160,512]{2,1,0:T(8,128)(2,1)S(1)}, u32[]{:S(2)}, u32[]{:S(2)}) collective-permute-start(bf16[2,160,512]{2,1,0:T(8,128)(2,1)S(1)} %pad_maximum_fusion.3.refs_0_), channel_id=1, source_target_pairs={{0,8},{8,0},{16,24},{24,16},{1,9},{9,1},{17,25},{25,17},{2,10},{10... | collective-permute-start | bytes 983048 | tf_op jit(solution)/shard_map/ppermute | solution.py:565
  48.9 4.8 %collective-permute-start.15 = (bf16[2,160,512]{2,1,0:T(8,128)(2,1)S(1)}, bf16[2,160,512]{2,1,0:T(8,128)(2,1)S(1)}, u32[]{:S(2)}, u32[]{:S(2)}) collective-permute-start(bf16[2,160,512]{2,1,0:T(8,128)(2,1)S(1)} %collective-permute-done.11.refs_1_), channel_id=1, source_target_pairs={{0,8},{8,0},{16,24},{24,16},{1,9},{9,1},{17,25},{25,17},{2,10},{10... | collective-permute-start | bytes 983048 | tf_op jit(solution)/shard_map/ppermute | solution.py:565
  49.1 5.4 %collective-permute-start.16 = (bf16[2,160,512]{2,1,0:T(8,128)(2,1)S(1)}, bf16[2,160,512]{2,1,0:T(8,128)(2,1)S(1)}, u32[]{:S(2)}, u32[]{:S(2)}) collective-permute-start(bf16[2,160,512]{2,1,0:T(8,128)(2,1)S(1)} %collective-permute-done.12.refs_2_), channel_id=1, source_target_pairs={{0,8},{8,0},{16,24},{24,16},{1,9},{9,1},{17,25},{25,17},{2,10},{10... | collective-permute-start | bytes 983048 | tf_op jit(solution)/shard_map/ppermute | solution.py:565
  49.5 5.1 %collective-permute-start.17 = (bf16[2,160,512]{2,1,0:T(8,128)(2,1)S(1)}, bf16[2,160,512]{2,1,0:T(8,128)(2,1)S(1)}, u32[]{:S(2)}, u32[]{:S(2)}) collective-permute-start(bf16[2,160,512]{2,1,0:T(8,128)(2,1)S(1)} %collective-permute-done.13.refs_3_), channel_id=1, source_target_pairs={{0,8},{8,0},{16,24},{24,16},{1,9},{9,1},{17,25},{25,17},{2,10},{10... | collective-permute-start | bytes 983048 | tf_op jit(solution)/shard_map/ppermute | solution.py:565
  49.6 28.9 %collective-permute-start.18 = (bf16[2,128,512]{2,1,0:T(8,128)(2,1)S(1)}, bf16[2,128,512]{2,1,0:T(8,128)(2,1)S(1)}, u32[]{:S(2)}, u32[]{:S(2)}) collective-permute-start(bf16[2,128,512]{2,1,0:T(8,128)(2,1)S(1)} %pad_maximum_fusion.5.refs_8_), channel_id=1, source_target_pairs={{0,2},{1,3},{2,0},{3,1},{4,6},{5,7},{6,4},{7,5},{8,10},{9,11},{10,... | collective-permute-start | bytes 786440 | tf_op jit(solution)/shard_map/ppermute | solution.py:565
  52.0 26.6 %collective-permute-start.19 = (bf16[2,128,512]{2,1,0:T(8,128)(2,1)S(1)}, bf16[2,128,512]{2,1,0:T(8,128)(2,1)S(1)}, u32[]{:S(2)}, u32[]{:S(2)}) collective-permute-start(bf16[2,128,512]{2,1,0:T(8,128)(2,1)S(1)} %pad_maximum_fusion.5.refs_8_), channel_id=1, source_target_pairs={{0,4},{1,5},{2,6},{3,7},{4,0},{5,1},{6,2},{7,3},{8,12},{9,13},{10,... | collective-permute-start | bytes 786440 | tf_op jit(solution)/shard_map/ppermute | solution.py:565
  53.8 24.8 %collective-permute-start.20 = (bf16[2,128,512]{2,1,0:T(8,128)(2,1)S(1)}, bf16[2,128,512]{2,1,0:T(8,128)(2,1)S(1)}, u32[]{:S(2)}, u32[]{:S(2)}) collective-permute-start(bf16[2,128,512]{2,1,0:T(8,128)(2,1)S(1)} %pad_maximum_fusion.5.refs_8_), channel_id=1, source_target_pairs={{0,6},{1,7},{2,4},{3,5},{4,2},{5,3},{6,0},{7,1},{8,14},{9,15},{10,... | collective-permute-start | bytes 786440 | tf_op jit(solution)/shard_map/ppermute | solution.py:565
  54.5 25.0 %collective-permute-start.21 = (bf16[2,128,512]{2,1,0:T(8,128)(2,1)S(1)}, bf16[2,128,512]{2,1,0:T(8,128)(2,1)S(1)}, u32[]{:S(2)}, u32[]{:S(2)}) collective-permute-start(bf16[2,128,512]{2,1,0:T(8,128)(2,1)S(1)} %pad_maximum_fusion.5.refs_8_), channel_id=1, source_target_pairs={{0,8},{8,0},{16,24},{24,16},{1,9},{9,1},{17,25},{25,17},{2,10},{10... | collective-permute-start | bytes 786440 | tf_op jit(solution)/shard_map/ppermute | solution.py:565
  81.0 26.5 %collective-permute-start.25 = (bf16[2,4,256,256]{3,2,1,0:T(8,128)(2,1)}, bf16[2,4,256,256]{3,2,1,0:T(8,128)(2,1)S(1)}, u32[]{:S(2)}, u32[]{:S(2)}) collective-permute-start(bf16[2,4,256,256]{3,2,1,0:T(8,128)(2,1)} %get-tuple-element.243), channel_id=1, source_target_pairs={{0,2},{1,3},{2,0},{3,1},{4,6},{5,7},{6,4},{7,5},{8,10},{9,11},{10,... | collective-permute-start | bytes 3145736 | tf_op jit(solution)/shard_map/ppermute | solution.py:565
  107.5 4.2 %collective-permute-start.27 = (bf16[8,320,256]{2,1,0:T(8,128)(2,1)}, bf16[8,320,256]{2,1,0:T(8,128)(2,1)}, u32[]{:S(2)}, u32[]{:S(2)}) collective-permute-start(bf16[8,320,256]{2,1,0:T(8,128)(2,1)} %get-tuple-element.252), channel_id=1, source_target_pairs={{0,8},{8,0},{16,24},{24,16},{1,9},{9,1},{17,25},{25,17},{2,10},{10... | collective-permute-start | bytes 3932168 | tf_op jit(solution)/shard_map/ppermute | solution.py:565
  113.6 22.5 %collective-permute-start.29 = (bf16[4,320,256]{2,1,0:T(8,128)(2,1)S(1)}, bf16[4,320,256]{2,1,0:T(8,128)(2,1)S(1)}, u32[]{:S(2)}, u32[]{:S(2)}) collective-permute-start(bf16[4,320,256]{2,1,0:T(8,128)(2,1)S(1)} %get-tuple-element.260), channel_id=1, source_target_pairs={{0,2},{1,3},{2,0},{3,1},{4,6},{5,7},{6,4},{7,5},{8,10},{9,11},{10,... | collective-permute-start | bytes 1966088 | tf_op jit(solution)/shard_map/ppermute | solution.py:565
  114.7 19.9 %collective-permute-start.28 = (bf16[2,256,256]{2,1,0:T(8,128)(2,1)S(1)}, bf16[2,256,256]{2,1,0:T(8,128)(2,1)S(1)}, u32[]{:S(2)}, u32[]{:S(2)}) collective-permute-start(bf16[2,256,256]{2,1,0:T(8,128)(2,1)S(1)} %get-tuple-element.258), channel_id=1, source_target_pairs={{0,4},{1,5},{2,6},{3,7},{4,0},{5,1},{6,2},{7,3},{8,12},{9,13},{10,... | collective-permute-start | bytes 786440 | tf_op jit(solution)/shard_map/ppermute | solution.py:565
  138.5 13.4 %collective-permute-start.32 = (bf16[896,256]{1,0:T(8,128)(2,1)S(1)}, bf16[896,256]{1,0:T(8,128)(2,1)S(1)}, u32[]{:S(2)}, u32[]{:S(2)}) collective-permute-start(bf16[896,256]{1,0:T(8,128)(2,1)S(1)} %get-tuple-element.281), channel_id=1, source_target_pairs={{0,1},{1,0},{2,3},{3,2},{4,5},{5,4},{6,7},{7,6},{8,9},{9,8},{10,11... | collective-permute-start | bytes 1376264 | tf_op jit(solution)/shard_map/ppermute | solution.py:565
  139.6 12.3 %collective-permute-start.31 = (bf16[4,192,256]{2,1,0:T(8,128)(2,1)S(1)}, bf16[4,192,256]{2,1,0:T(8,128)(2,1)S(1)}, u32[]{:S(2)}, u32[]{:S(2)}) collective-permute-start(bf16[4,192,256]{2,1,0:T(8,128)(2,1)S(1)} %get-tuple-element.279), channel_id=1, source_target_pairs={{0,2},{1,3},{2,0},{3,1},{4,6},{5,7},{6,4},{7,5},{8,10},{9,11},{10,... | collective-permute-start | bytes 1179656 | tf_op jit(solution)/shard_map/ppermute | solution.py:565
  152.2 10.4 %collective-permute-start.33 = (bf16[2,192,256]{2,1,0:T(8,128)(2,1)S(1)}, bf16[2,192,256]{2,1,0:T(8,128)(2,1)S(1)}, u32[]{:S(2)}, u32[]{:S(2)}) collective-permute-start(bf16[2,192,256]{2,1,0:T(8,128)(2,1)S(1)} %get-tuple-element.292), channel_id=1, source_target_pairs={{0,1},{1,0},{2,3},{3,2},{4,5},{5,4},{6,7},{7,6},{8,9},{9,8},{10,11... | collective-permute-start | bytes 589832 | tf_op jit(solution)/shard_map/ppermute | solution.py:565
  152.8 9.7 %collective-permute-start.34 = (bf16[1,320,256]{2,1,0:T(8,128)(2,1)S(1)}, bf16[1,320,256]{2,1,0:T(8,128)(2,1)S(1)}, u32[]{:S(2)}, u32[]{:S(2)}) collective-permute-start(bf16[1,320,256]{2,1,0:T(8,128)(2,1)S(1)} %get-tuple-element.294), channel_id=1, source_target_pairs={{0,4},{1,5},{2,6},{3,7},{4,0},{5,1},{6,2},{7,3},{8,12},{9,13},{10,... | collective-permute-start | bytes 491528 | tf_op jit(solution)/shard_map/ppermute | solution.py:565
  162.7 8.1 %collective-permute-start.35 = (bf16[576,256]{1,0:T(8,128)(2,1)S(1)}, bf16[576,256]{1,0:T(8,128)(2,1)S(1)}, u32[]{:S(2)}, u32[]{:S(2)}) collective-permute-start(bf16[576,256]{1,0:T(8,128)(2,1)S(1)} %pad_maximum_fusion.4), channel_id=1, source_target_pairs={{0,16},{8,24},{16,0},{24,8},{1,17},{9,25},{17,1},{25,9},{2,18},{10... | collective-permute-start | bytes 884744 | tf_op jit(solution)/shard_map/ppermute | solution.py:565
  164.2 6.6 %collective-permute-start.36 = (bf16[1,192,256]{2,1,0:T(8,128)(2,1)S(1)}, bf16[1,192,256]{2,1,0:T(8,128)(2,1)S(1)}, u32[]{:S(2)}, u32[]{:S(2)}) collective-permute-start(bf16[1,192,256]{2,1,0:T(8,128)(2,1)S(1)} %get-tuple-element.362), channel_id=1, source_target_pairs={{0,4},{1,5},{2,6},{3,7},{4,0},{5,1},{6,2},{7,3},{8,12},{9,13},{10,... | collective-permute-start | bytes 294920 | tf_op jit(solution)/shard_map/ppermute | solution.py:565
  171.0 5.3 %collective-permute-start.39 = (bf16[192,256]{1,0:T(8,128)(2,1)S(1)}, bf16[192,256]{1,0:T(8,128)(2,1)S(1)}, u32[]{:S(2)}, u32[]{:S(2)}) collective-permute-start(bf16[192,256]{1,0:T(8,128)(2,1)S(1)} %fusion.8), channel_id=1, source_target_pairs={{0,16},{8,24},{16,0},{24,8},{1,17},{9,25},{17,1},{25,9},{2,18},{10... | collective-permute-start | bytes 294920 | tf_op jit(solution)/shard_map/ppermute | solution.py:565
  171.6 4.6 %collective-permute-start.37 = (f32[8,512]{1,0:T(8,128)S(1)}, f32[8,512]{1,0:T(8,128)S(1)}, u32[]{:S(2)}, u32[]{:S(2)}) collective-permute-start(f32[8,512]{1,0:T(8,128)S(1)} %get-tuple-element.318), channel_id=1, source_target_pairs={{0,8},{8,0},{16,24},{24,16},{1,9},{9,1},{17,25},{25,17},{2,10},{10... | collective-permute-start | bytes 49160 | tf_op jit(solution)/shard_map/ppermute | solution.py:565
  180.3 3.7 %collective-permute-start.42 = (f32[8,512]{1,0:T(8,128)S(1)}, f32[8,512]{1,0:T(8,128)S(1)}, u32[]{:S(2)}, u32[]{:S(2)}) collective-permute-start(f32[8,512]{1,0:T(8,128)S(1)} %pad_add_fusion), channel_id=1, source_target_pairs={{0,1},{1,0},{2,3},{3,2},{4,5},{5,4},{6,7},{7,6},{8,9},{9,8},{10,11... | collective-permute-start | bytes 49160 | tf_op jit(solution)/shard_map/ppermute | solution.py:565
  187.9 4.6 %collective-permute-start.44 = (f32[8,512]{1,0:T(8,128)S(1)}, f32[8,512]{1,0:T(8,128)S(1)}, u32[]{:S(2)}, u32[]{:S(2)}) collective-permute-start(f32[8,512]{1,0:T(8,128)S(1)} %add_select_fusion.one), channel_id=1, source_target_pairs={{0,4},{1,5},{2,6},{3,7},{4,0},{5,1},{6,2},{7,3},{8,12},{9,13},{10,... | collective-permute-start | bytes 49160 | tf_op jit(solution)/shard_map/ppermute | solution.py:565
  (76 other events, 782.3 us)

commit v6 on v5

--- a/solution.py
+++ b/solution.py
@@ -137,46 +137,49 @@
 def f1_kernel(plan, nw, idx, lens, tok, norm, *refs):
     w_refs, (tri_out, n1_out, att_out, lse_out, wt, tri, sem) = refs[:nw], refs[nw:]
     e = pl.program_id(0)
-    rows = tok.shape[1]
-    padded = tri.shape[0]
+    count, rows = tok.shape[:2]
+    padded = tri.shape[1]
     rows16 = -(-rows // 16) * 16
 
     @pl.when(e == 0)
     def _():
         load_triple(w_refs, plan, wt, sem, idx[0], idx[1], True)
-        tri[rows16:padded] = jnp.zeros((padded - rows16, 3 * D), BF16)
+        tri[:, rows16:padded] = jnp.zeros((count, padded - rows16, 3 * D), BF16)
         load_triple(w_refs, plan, wt, sem, idx[0], idx[1], False)
 
-    xhat, _ = ln_parts(pad_rows(tok[0].astype(F32), rows16))
-    n1 = (xhat * norm[0:1] + norm[1:2]).astype(BF16)
-    n1_out[0] = n1[:rows]
-    t = mm(n1, wt[...]).astype(BF16)
-    tri[0:rows16, 0:D] = t[:, 0:D] * jnp.asarray(HEAD_DIM**-0.5, BF16)
-    tri[0:rows16, D:] = t[:, D:]
-    tri_out[0] = tri[0:rows]
-
-    length = lens[e]
+    for i in range(count):
+        xhat, _ = ln_parts(pad_rows(tok[i].astype(F32), rows16))
+        n1 = (xhat * norm[0:1] + norm[1:2]).astype(BF16)
+        n1_out[i] = n1[:rows]
+        t = mm(n1, wt[...]).astype(BF16)
+        tri[i, 0:rows16, 0:D] = t[:, 0:D] * jnp.asarray(HEAD_DIM**-0.5, BF16)
+        tri[i, 0:rows16, D:] = t[:, D:]
+        tri_out[i] = tri[i, 0:rows]
+
     masks = head_masks()
     lane = lax.broadcasted_iota(jnp.int32, (1, QUAD), 1) % QB
     blocks = -(-rows // QB)
-    chains = [(j, g * QUAD, g * blocks + j) for j in range(blocks) for g in range(HEADS // 4)]
-    exts = [min(QB * (j + 1), rows16) for j, _, _ in chains]
-    q4 = [stack_heads(tri[QB * j : QB * (j + 1), gl : gl + QUAD], masks) for j, gl, _ in chains]
-    s = [mm(tri[0:x, D + gl : D + gl + QUAD], q, NT) for (_, gl, _), x, q in zip(chains, exts, q4)]
+    chains = [
+        (i, j, g * QUAD, g * blocks + j)
+        for i in range(count) for j in range(blocks) for g in range(HEADS // 4)
+    ]
+    exts = [min(QB * (j + 1), rows16) for _, j, _, _ in chains]
+    q4 = [stack_heads(tri[i, QB * j : QB * (j + 1), gl : gl + QUAD], masks) for i, j, gl, _ in chains]
+    s = [mm(tri[i, 0:x, D + gl : D + gl + QUAD], q, NT) for (i, _, gl, _), x, q in zip(chains, exts, q4)]
     pb = []
-    for (j, _, at), x, v in zip(chains, exts, s):
-        kmax = jnp.minimum(lane + QB * j, length - 1)
+    for (i, j, _, at), x, v in zip(chains, exts, s):
+        kmax = jnp.minimum(lane + QB * j, lens[e * count + i] - 1)
         krow = lax.broadcasted_iota(jnp.int32, (x, QUAD), 0)
         v = jnp.where(krow <= kmax, v, MASKED)
         m = jnp.max(v, axis=0, keepdims=True)
         p = jnp.exp(v - m)
         total = jnp.sum(p, axis=0, keepdims=True)
-        lse_out[0, pl.ds(at, 1), :] = m + jnp.log(total)
+        lse_out[i, pl.ds(at, 1), :] = m + jnp.log(total)
         pb.append((p * (1.0 / total)).astype(BF16))
-    o = [mm(v, tri[0:x, 2 * D + gl : 2 * D + gl + QUAD], TN) for (_, gl, _), x, v in zip(chains, exts, pb)]
-    for (j, gl, _), v in zip(chains, o):
+    o = [mm(v, tri[i, 0:x, 2 * D + gl : 2 * D + gl + QUAD], TN) for (i, _, gl, _), x, v in zip(chains, exts, pb)]
+    for (i, j, gl, _), v in zip(chains, o):
         live = min(QB, rows - QB * j)
-        att_out[0, QB * j : QB * j + live, gl : gl + QUAD] = own_lanes(v).astype(BF16)[:live]
+        att_out[i, QB * j : QB * j + live, gl : gl + QUAD] = own_lanes(v).astype(BF16)[:live]
 
 
 def put_rows(dst, at_index, at, src, row, rows):
@@ -308,63 +311,72 @@
     grads, (tri, ga, gtri, dk, dv, acc, n1p, gtp) = refs[:nh], refs[nh:]
     e = pl.program_id(0)
     last = pl.num_programs(0) - 1
-    rows = n1.shape[1]
-    padded = tri.shape[0]
+    count, rows = n1.shape[:2]
+    padded = tri.shape[1]
     rows16 = -(-rows // 16) * 16
     low16 = rows // 16 * 16
 
     @pl.when(e == 0)
     def _():
         acc[...] = jnp.zeros_like(acc)
-        tri[low16:padded] = jnp.zeros((padded - low16, 3 * D), BF16)
-        ga[low16:padded] = jnp.zeros((padded - low16, D), BF16)
-
-    tri[0:rows] = tri_ref[0]
-    ga[0:rows] = ga_ref[0]
+        tri[:, low16:padded] = jnp.zeros((count, padded - low16, 3 * D), BF16)
+        ga[:, low16:padded] = jnp.zeros((count, padded - low16, D), BF16)
+
+    for i in range(count):
+        tri[i, 0:rows] = tri_ref[i]
+        ga[i, 0:rows] = ga_ref[i]
     dk[...] = jnp.zeros_like(dk)
     dv[...] = jnp.zeros_like(dv)
-    gtri[:, 0:D] = jnp.zeros((padded, D), BF16)
-
-    length = lens[e]
+    gtri[:, :, 0:D] = jnp.zeros((count, padded, D), BF16)
+
+    lengths = [lens[e * count + i] for i in range(count)]
     masks = head_masks()
     lane = lax.broadcasted_iota(jnp.int32, (1, QUAD), 1) % QB
     blocks = -(-rows // QB)
-    for group in [tuple(range(j, min(j + 2, blocks))) for j in range(0, blocks, 2)]:
-
-        @pl.when(length > QB * group[0])
-        def _(group=group):
-            chains = [(j, g * QUAD, g * blocks + j) for j in group for g in range(HEADS // 4)]
-            exts = [min(QB * (j + 1), rows16) for j, _, _ in chains]
-            q4 = [stack_heads(tri[QB * j : QB * (j + 1), gl : gl + QUAD], masks) for j, gl, _ in chains]
-            do4 = [stack_heads(ga[QB * j : QB * (j + 1), gl : gl + QUAD], masks) for j, gl, _ in chains]
-            s = [mm(tri[0:x, D + gl : D + gl + QUAD], q, NT) for (_, gl, _), x, q in zip(chains, exts, q4)]
-            dp = [mm(tri[0:x, 2 * D + gl : 2 * D + gl + QUAD], d, NT) for (_, gl, _), x, d in zip(chains, exts, do4)]
-            p = []
-            for (j, _, at), x, v in zip(chains, exts, s):
-                kmax = jnp.minimum(lane + QB * j, length - 1)
-                krow = lax.broadcasted_iota(jnp.int32, (x, QUAD), 0)
-                p.append(jnp.exp(jnp.where(krow <= kmax, v - lse[0, pl.ds(at, 1), :], MASKED)))
-            ds = []
-            for v, w in zip(p, dp):
-                delta = jnp.sum(v * w, axis=0, keepdims=True)
-                ds.append((v * (w - delta)).astype(BF16))
-            for (_, gl, _), x, v, d in zip(chains, exts, p, do4):
-                dv[0:x, gl : gl + QUAD] += mm(v.astype(BF16), d)
-            dq = [mm(v, tri[0:x, D + gl : D + gl + QUAD], TN) for (_, gl, _), x, v in zip(chains, exts, ds)]
-            for (_, gl, _), x, v, q in zip(chains, exts, ds, q4):
-                dk[0:x, gl : gl + QUAD] += mm(v, q)
-            for (j, gl, _), v in zip(chains, dq):
-                gtri[QB * j : QB * (j + 1), gl : gl + QUAD] = (own_lanes(v) * HEAD_DIM**-0.5).astype(BF16)
-
-    gtri[0:rows16, D : 2 * D] = dk[...].astype(BF16)
-    gtri[0:rows16, 2 * D :] = dv[...].astype(BF16)
-    gtri_out[0] = gtri[0:rows]
+
+    def run(chains):
+        chains = [(i, j, g * QUAD, g * blocks + j) for i, j in chains for g in range(HEADS // 4)]
+        exts = [min(QB * (j + 1), rows16) for _, j, _, _ in chains]
+        q4 = [stack_heads(tri[i, QB * j : QB * (j + 1), gl : gl + QUAD], masks) for i, j, gl, _ in chains]
+        do4 = [stack_heads(ga[i, QB * j : QB * (j + 1), gl : gl + QUAD], masks) for i, j, gl, _ in chains]
+        s = [mm(tri[i, 0:x, D + gl : D + gl + QUAD], q, NT) for (i, _, gl, _), x, q in zip(chains, exts, q4)]
+        dp = [mm(tri[i, 0:x, 2 * D + gl : 2 * D + gl + QUAD], d, NT) for (i, _, gl, _), x, d in zip(chains, exts, do4)]
+        p = []
+        for (i, j, _, at), x, v in zip(chains, exts, s):
+            kmax = jnp.minimum(lane + QB * j, lengths[i] - 1)
+            krow = lax.broadcasted_iota(jnp.int32, (x, QUAD), 0)
+            p.append(jnp.exp(jnp.where(krow <= kmax, v - lse[i, pl.ds(at, 1), :], MASKED)))
+        ds = []
+        for v, w in zip(p, dp):
+            delta = jnp.sum(v * w, axis=0, keepdims=True)
+            ds.append((v * (w - delta)).astype(BF16))
+        for (i, _, gl, _), x, v, d in zip(chains, exts, p, do4):
+            dv[i, 0:x, gl : gl + QUAD] += mm(v.astype(BF16), d)
+        dq = [mm(v, tri[i, 0:x, D + gl : D + gl + QUAD], TN) for (i, _, gl, _), x, v in zip(chains, exts, ds)]
+        for (i, _, gl, _), x, v, q in zip(chains, exts, ds, q4):
+            dk[i, 0:x, gl : gl + QUAD] += mm(v, q)
+        for (i, j, gl, _), v in zip(chains, dq):
+            gtri[i, QB * j : QB * (j + 1), gl : gl + QUAD] = (own_lanes(v) * HEAD_DIM**-0.5).astype(BF16)
+
+    run([(i, j) for i in range(count) for j in range(min(2, blocks))])
+    for i in range(count):
+        for j in range(2, blocks, 2):
+
+            @pl.when(lengths[i] > QB * j)
+            def _(i=i, j=j):
+                run([(i, k) for k in range(j, min(j + 2, blocks))])
+
     start = jnp.int32(0)
-    for i in range(lens.shape[0] - 1):
-        start = start + jnp.where(i < e, (lens[i] + 15) // 16, 0)
-    at = pl.multiple_of(start * 16, 16)
-    n1p[pl.ds(at, rows16)] = pad_rows(n1[0], rows16)
-    gtp[pl.ds(at, rows16)] = gtri[0:rows16]
+    for i in range(lens.shape[0] - count):
+        start = start + jnp.where(i < e * count, (lens[i] + 15) // 16, 0)
+    for i in range(count):
+        gtri[i, 0:rows16, D : 2 * D] = dk[i].astype(BF16)
+        gtri[i, 0:rows16, 2 * D :] = dv[i].astype(BF16)
+        gtri_out[i] = gtri[i, 0:rows]
+        at = pl.multiple_of(start * 16, 16)
+        n1p[pl.ds(at, rows16)] = pad_rows(n1[i], rows16)
+        gtp[pl.ds(at, rows16)] = gtri[i, 0:rows16]
+        start = start + (lengths[i] + 15) // 16
 
     @pl.when(e == last)
     def _():
@@ -377,7 +389,7 @@
             acc[...] += mm(n1p[pl.ds(row, PACK)], gtp[pl.ds(row, PACK)], TN)
             return carry
 
-        lax.fori_loop(0, (at + length + PACK - 1) // PACK, chunk, 0)
+        lax.fori_loop(0, (start * 16 + PACK - 1) // PACK, chunk, 0)
         hm = D // len(pos) // nh
         for p, rel in enumerate(pos):
             block = jnp.bitwise_xor(idx[0], rel)
@@ -660,6 +672,8 @@
     norm_t = norm_params.T
     norm = jnp.concatenate([norm_t, jnp.zeros((4, D), F32)], axis=0)
     ep_block = lambda width: pl.BlockSpec((1, rows, width), lambda e: (e, 0, 0))
+    eps = 2 if ep % 2 == 0 else 1
+    eps_block = lambda width: pl.BlockSpec((eps, rows, width), lambda e: (e, 0, 0))
     ep_shape = lambda width, dtype: jax.ShapeDtypeStruct((ep, rows, width), dtype)
     low = lambda width: (ep_block(width), ep_shape(width, BF16))
     wide = lambda width: (ep_block(width), ep_shape(width, F32))
@@ -693,9 +707,9 @@
     t_refs.append(t_two)
     t_plan.append((rels_b, nh - 1))
     if nh == 2:
-        for i, r in enumerate(rels_b):
-            t_refs.append(steps_d(t_two[i : i + 1], 1))
-            t_plan.append(([r], 2))
+        for i in range(0, len(rels_b), 2):
+            t_refs.append(steps_d(t_two[i : i + 2], 1))
+            t_plan.append((rels_b[i : i + 2], 2))
     nw = len(t_refs)
     pair_plan = [([0, near], nh - 1)]
     got_plan = [([r, r ^ near], nh - 1) for r in rels_a[1:]]
@@ -703,10 +717,14 @@
     norm, b_pair, *t_refs = sync(norm, b_pair, *t_refs)
     b_refs, b_got = [b_pair], [steps_f(b_pair, r) for r in rels_a[1:]]
     triple, n1, attended, lse = kernel_call(
-        functools.partial(f1_kernel, t_plan, nw), "f1", (ep,),
-        [SMEM, SMEM, ep_block(D), norm_spec] + [ANY] * nw,
-        [low(3 * D), low(D), low(D), (lse_spec, jax.ShapeDtypeStruct((ep, 16, QUAD), F32))],
-        [wt_scratch, pltpu.VMEM((padded, 3 * D), BF16), dma], 60,
+        functools.partial(f1_kernel, t_plan, nw), "f1", (ep // eps,),
+        [SMEM, SMEM, eps_block(D), norm_spec] + [ANY] * nw,
+        [
+            (eps_block(3 * D), ep_shape(3 * D, BF16)), (eps_block(D), ep_shape(D, BF16)),
+            (eps_block(D), ep_shape(D, BF16)),
+            (pl.BlockSpec((eps, 16, QUAD), lambda e: (e, 0, 0)), jax.ShapeDtypeStruct((ep, 16, QUAD), F32)),
+        ],
+        [wt_scratch, pltpu.VMEM((eps, padded, 3 * D), BF16), dma], 60,
         (idx, lengths, tokens, norm, *t_refs),
     )
     attended, *a_got = sync(attended, *a_got)
@@ -719,8 +737,7 @@
 
     order = f_bits[1:2] + f_bits[:1] + f_bits[2:]
     late = order[2:]
-    order_a = f_bits[1:3] + f_bits[:1] + f_bits[3:]
-    pos, pos_a = halving_positions(order), halving_positions(order_a)
+    pos = halving_positions(order)
     hm, hr = shard // nh, h2 // nh
     rows_a = hm * (half_ff // QUAD) + hr * (D // QUAD)
     rows_b = rows_a + hm * (D // QUAD)
@@ -740,10 +757,10 @@
     cot_flat = cotangent.reshape(flat, D)
     attended = attended.reshape(flat, D)
     hidden, out_part, g2_part, n2, keep_a, send_a = kernel_call(
-        functools.partial(f2a_kernel, a_plan, na, pos_a, rows), "f2a", (fl_steps,),
+        functools.partial(f2a_kernel, a_plan, na, pos, rows), "f2a", (fl_steps,),
         [SMEM, SMEM] + [fl_block(D)] * 3 + [norm_spec] + [ANY] * na,
         [fl_wide(D)] * 3 + [fl_low(D)] + [low_out(nh, half, rows_a, QUAD)] * 2,
-        ff_scratch + [pltpu.SemaphoreType.DMA((2,))], 50, (idx, lengths, attended, tok_flat, cot_flat, norm, *a_refs),
+        ff_scratch + [pltpu.SemaphoreType.DMA((2,))], 60, (idx, lengths, attended, tok_flat, cot_flat, norm, *a_refs),
     )
 
     def halves(keep, got):
@@ -790,39 +807,37 @@
     ga, counted, bins_t, keep_a, send_a, keep_b, send_b = sync(ga, counted, bins_t, keep_a, send_a, keep_b, send_b)
 
     got_b = steps_f(send_b, order[0])
-    got_a = steps_f(send_a, order_a[1])
+    got_a = steps_f(send_a, order[1])
     pack_rows = ep * rows16 + PACK
     gtri, *grads_t = kernel_call(
-        functools.partial(b1_kernel, pos, nh), "b1", (ep,),
-        [SMEM, SMEM, ep_block(3 * D), ep_block(D), lse_spec, ep_block(D)],
-        [low(3 * D)] + [low_out(n_f, rows_t, QUAD)] * nh,
+        functools.partial(b1_kernel, pos, nh), "b1", (ep // eps,),
+        [SMEM, SMEM, eps_block(3 * D), eps_block(D), pl.BlockSpec((eps, 16, QUAD), lambda e: (e, 0, 0)), eps_block(D)],
+        [(eps_block(3 * D), ep_shape(3 * D, BF16))] + [low_out(n_f, rows_t, QUAD)] * nh,
         [
-            pltpu.VMEM((padded, 3 * D), BF16), pltpu.VMEM((padded, D), BF16),
-            pltpu.VMEM((padded, 3 * D), BF16), pltpu.VMEM((rows16, D), F32),
-            pltpu.VMEM((rows16, D), F32), pltpu.VMEM((D, 3 * D), F32),
+            pltpu.VMEM((eps, padded, 3 * D), BF16), pltpu.VMEM((eps, padded, D), BF16),
+            pltpu.VMEM((eps, padded, 3 * D), BF16), pltpu.VMEM((eps, rows16, D), F32),
+            pltpu.VMEM((eps, rows16, D), F32), pltpu.VMEM((D, 3 * D), F32),
             pltpu.VMEM((pack_rows, D), BF16), pltpu.VMEM((pack_rows, 3 * D), BF16),
         ],
-        44, (idx, lengths, triple, ga.reshape(ep, rows, D), lse, n1),
+        48, (idx, lengths, triple, ga.reshape(ep, rows, D), lse, n1),
     )
     gtri, keep_a, got_a, keep_b, got_b, *grads_t = sync(gtri, keep_a, got_a, keep_b, got_b, *grads_t)
 
     mine_t, other_t = core_pair(grads_t)
-    late_a = order_a[2:]
     keep_b, send_b = halves(keep_b, got_b)
-    if late_a:
+    if late:
         keep_a, send_a = halves(keep_a, got_a)
-        send_ab = jnp.concatenate([send_a.reshape(-1, QUAD), send_b.reshape(-1, QUAD)], axis=0)
-        keep_ab = jnp.concatenate([keep_a.reshape(-1, QUAD), keep_b.reshape(-1, QUAD)], axis=0)
-        cut_a = send_a.size // QUAD
     else:
-        keep_a = add_low(keep_a, got_a)
-        send_ab, keep_ab = send_b.reshape(-1, QUAD), keep_b.reshape(-1, QUAD)
-        cut_a = 0
-    mine_t, other_t, keep_ab, send_ab = sync(mine_t, other_t, keep_ab, send_ab)
+        keep_a, send_a = add_low(keep_a, got_a), keep_a
+    mine_t, other_t, keep_a, send_a, keep_b, send_b = sync(mine_t, other_t, keep_a, send_a, keep_b, send_b)
     keep_t, send_t = core_halves_of((mine_t, other_t))
-    block_out, keep_t, send_t, keep_ab, send_ab = sync(block_out, keep_t, send_t, keep_ab, send_ab)
+    block_out, keep_t, send_t, keep_a, send_a, keep_b, send_b = sync(
+        block_out, keep_t, send_t, keep_a, send_a, keep_b, send_b
+    )
     got_t = steps_f(send_t, order[0])
-    got_ab = steps_f(send_ab, near)
+    got_b = steps_f(send_b, order[1])
+    if late:
+        got_a = steps_f(send_a, late[0])
 
     qb = 256
     steps = -(-flat // qb)
@@ -834,7 +849,7 @@
         ],
         [whole((16, qb))] * 2, [], 20, (block_out, value_head, bins_t, counted),
     )
-    gtri, q_sum, keep_t, got_t, keep_ab, got_ab = sync(gtri, q_sum, keep_t, got_t, keep_ab, got_ab)
+    gtri, q_sum, keep_t, got_t, keep_b, got_b = sync(gtri, q_sum, keep_t, got_t, keep_b, got_b)
 
     def b2_call(at, n, gtri, prior, more_in):
         extra = [] if prior is None else [prior, *more_in]
@@ -848,15 +863,12 @@
         )
 
     keep_t, send_t = halves(keep_t, got_t)
-    if late_a:
-        keep_a = add_low(keep_ab[:cut_a], got_ab[:cut_a]).reshape(-1, rows_a, QUAD)
-    keep_b, got_b = (v[cut_a:].reshape(-1, rows_b, QUAD) for v in (keep_ab, got_ab))
     if late:
         keep_b, send_b = halves(keep_b, got_b)
     else:
         keep_b, send_b = add_low(keep_b, got_b), keep_b
     gtri_flat = gtri.reshape(flat, 3 * D)
-    gtri_flat, keep_t, send_t, keep_a, keep_b, send_b = sync(gtri_flat, keep_t, send_t, keep_a, keep_b, send_b)
+    gtri_flat, keep_t, send_t, keep_b, send_b = sync(gtri_flat, keep_t, send_t, keep_b, send_b)
     got_t = steps_f(send_t, order[1])
     if late:
         got_b = steps_f(send_b, late[0])
@@ -873,10 +885,10 @@
     x_bits = d_bits[nh - 1 :]
     if late:
         keep_t, send_t = halves(keep_t, got_t)
-        keep_b = add_low(keep_b, got_b[0])
+        keep_b, keep_a = add_low(keep_b, got_b[0]), add_low(keep_a, got_a)
     else:
         keep_t = add_low(keep_t, got_t)
-    red = jnp.concatenate([finish(keep_a, late_a[1:]), finish(keep_b, late[1:])], axis=0)
+    red = jnp.concatenate([finish(keep_a, late[1:]), finish(keep_b, late[1:])], axis=0)
     for b in x_bits[:-1]:
         red = add_low(red, steps_d(red, b))
     red, keep_t, ig_part = sync(red, keep_t, ig_part)

time: 194 us -> 191 us (0.985); the launches traced: 194 us -> 189 us
  waiting for transfers between devices: 36.9 us -> 30.2 us
  starting transfers between devices: 42.1 us -> 46.1 us
  Pallas kernels: 103 us -> 99.4 us
    ppermute x45 -> x44, waiting for transfers between devices: 36.9 us -> 30.2 us  [xor_step(): return lax.ppermute(v, axis, [(i, i ^ bit) for i in range(size)])]
    ppermute x45 -> x44, starting transfers between devices: 42.1 us -> 46.1 us  [xor_step(): return lax.ppermute(v, axis, [(i, i ^ bit) for i in range(size)])]
    pallas_call x10, Pallas kernels: 103 us -> 99.4 us  [kernel_call(): pl.pallas_call(kernel, grid=grid, in_specs=in_specs, out_specs=[spec for...]
  transfers between devices with their start and end apart: 45 -> 44, of which waited for: 23 -> 18; matrix products, arithmetic and copies ran while one was open for 3% -> 3% of each run, Pallas kernels for 52% -> 52%
where the time goes in v6:
time: 191 us; the launch traced here: 189 us
  Pallas kernels  99.4 us (52%)
  starting transfers between devices  46.1 us (24%)
  waiting for transfers between devices  30.2 us (16%)
  local copies, waits for them, and re-layouts  7.31 us (4%)
  other arithmetic  4.32 us (2%)
    pallas_call x10, Pallas kernels, kernel_call(): pl.pallas_call(kernel, grid=grid, in_specs=in_specs, out_specs=[spec for...  99.4 us
    ppermute x44, starting transfers between devices, xor_step(): return lax.ppermute(v, axis, [(i, i ^ bit) for i in range(size)])  46.1 us
    ppermute x44, waiting for transfers between devices, xor_step(): return lax.ppermute(v, axis, [(i, i ^ bit) for i in range(size)])  30.2 us
  transfers between devices with their start and end apart: 44, of which 18 were waited for; matrix products, arithmetic and copies ran while one was open for 3% of the time, Pallas kernels for 52%

profile of v6, /device:TPU:0, one launch (start us, length us, event | category | flops | bytes accessed | tf_op | source)
XLA Modules:
  0.0 188.9 jit_solution(17869857277718723577)
XLA Ops:
  1.6 3.1 %collective-permute-start = (bf16[32,1536]{1,0:T(8,128)(2,1)S(1)}, bf16[32,1536]{1,0:T(8,128)(2,1)S(1)}, u32[]{:S(2)}, u32[]{:S(2)}) collective-permute-start(bf16[32,1536]{1,0:T(8,128)(2,1)S(1)} %dynamic-slice_convert_fusion.1), channel_id=1, source_target_pairs={{0,2},{1,3},{2,0},{3,1},{4,6},{5,7},{6,4},{7,5},{8,10},{9,11},{10,... | collective-permute-start | bytes 294920 | tf_op jit(solution)/shard_map/ppermute | solution.py:577
  4.7 2.6 %collective-permute-start.1 = (bf16[32,1536]{1,0:T(8,128)(2,1)S(1)}, bf16[32,1536]{1,0:T(8,128)(2,1)S(1)}, u32[]{:S(2)}, u32[]{:S(2)}) collective-permute-start(bf16[32,1536]{1,0:T(8,128)(2,1)S(1)} %dynamic-slice_convert_fusion.1), channel_id=1, source_target_pairs={{0,4},{1,5},{2,6},{3,7},{4,0},{5,1},{6,2},{7,3},{8,12},{9,13},{10,... | collective-permute-start | bytes 294920 | tf_op jit(solution)/shard_map/ppermute | solution.py:577
  10.3 1.8 collective-permute-start.3
  13.3 1.8 collective-permute-done.1
  15.7 1.7 collective-permute-start.4
  17.5 2.1 %collective-permute-start.10 = (bf16[2,160,512]{2,1,0:T(8,128)(2,1)S(1)}, bf16[2,160,512]{2,1,0:T(8,128)(2,1)S(1)}, u32[]{:S(2)}, u32[]{:S(2)}) collective-permute-start(bf16[2,160,512]{2,1,0:T(8,128)(2,1)S(1)} %pad_maximum_fusion.1.refs_0_), channel_id=1, source_target_pairs={{0,4},{1,5},{2,6},{3,7},{4,0},{5,1},{6,2},{7,3},{8,12},{9,13},{10,... | collective-permute-start | bytes 983048 | tf_op jit(solution)/shard_map/ppermute | solution.py:577
  19.5 1.7 collective-permute-start.11
  21.7 3.4 %collective-permute-done.4.refs_2_ = bf16[4,32,1536]{2,1,0:T(8,128)(2,1)S(1)} collective-permute-done((bf16[4,32,1536]{2,1,0:T(8,128)(2,1)S(1)}, bf16[4,32,1536]{2,1,0:T(8,128)(2,1)S(1)}, u32[]{:S(2)}, u32[]{:S(2)}) %collective-permute-start.4) | collective-permute-done | bytes 393248 | tf_op jit(solution)/shard_map/ppermute | solution.py:577
  26.8 3.3 %collective-permute-done.5 = bf16[128,512]{1,0:T(8,128)(2,1)S(1)} collective-permute-done((bf16[128,512]{1,0:T(8,128)(2,1)S(1)}, bf16[128,512]{1,0:T(8,128)(2,1)S(1)}, u32[]{:S(2)}, u32[]{:S(2)}) %collective-permute-start.5) | collective-permute-done | bytes 131104 | tf_op jit(solution)/shard_map/ppermute | solution.py:577
  32.2 14.8 %f1.1 = (bf16[6,296,1536]{2,1,0:T(8,128)(2,1)}, bf16[6,296,512]{2,1,0:T(8,128)(2,1)}, bf16[6,296,512]{2,1,0:T(8,128)(2,1)}, f32[6,16,256]{2,1,0:T(8,128)}) custom-call(s32[2]{0:T(128)} %pad_add_fusion.1.idx, s32[6]{0:T(128)} %lens.7, bf16[6,296,512]{2,1,0:T(8,128)(2,1)} %tok.1, f32[8,512]{1,0:T(8,128)} %concatenate.28.norm, bf16[4,32,1536]{2,1,0:T(8,128)(2,1)} %copy-done.3, ...), custom_call_target="tpu_custom_call" | custom-call | flops 1 | bytes 1 | tf_op jit(solution)/shard_map/f1/pallas_call | solution.py:613
  47.8 3.0 %collective-permute-start.16 = (bf16[2,128,512]{2,1,0:T(8,128)(2,1)S(1)}, bf16[2,128,512]{2,1,0:T(8,128)(2,1)S(1)}, u32[]{:S(2)}, u32[]{:S(2)}) collective-permute-start(bf16[2,128,512]{2,1,0:T(8,128)(2,1)S(1)} %pad_maximum_fusion.3.refs_8_), channel_id=1, source_target_pairs={{0,2},{1,3},{2,0},{3,1},{4,6},{5,7},{6,4},{7,5},{8,10},{9,11},{10,... | collective-permute-start | bytes 786440 | tf_op jit(solution)/shard_map/ppermute | solution.py:577
  54.8 22.1 %f2a.1 = (f32[1776,512]{1,0:T(8,128)}, f32[1776,512]{1,0:T(8,128)}, f32[1776,512]{1,0:T(8,128)}, bf16[1776,512]{1,0:T(8,128)(2,1)}, bf16[2,4,256,256]{3,2,1,0:T(8,128)(2,1)}, /*index=5*/bf16[2,4,256,256]{3,2,1,0:T(8,128)(2,1)}) custom-call(s32[2]{0:T(128)} %pad_add_fusion.1.idx, s32[6]{0:T(128)} %lens.7, bf16[1776,512]{1,0:T(8,128)(2,1)} %bitcast.60, ...), custom_call_target="tpu_custom_call" | custom-call | flops 1 | bytes 1 | tf_op jit(solution)/shard_map/f2a/pallas_call | solution.py:613
  80.0 26.0 %f2b.1 = (bf16[1776,512]{1,0:T(8,128)(2,1)}, f32[1776,512]{1,0:T(8,128)}, bf16[1776,512]{1,0:T(8,128)(2,1)}, bf16[8,320,256]{2,1,0:T(8,128)(2,1)}, bf16[8,320,256]{2,1,0:T(8,128)(2,1)}, /*index=5*/f32[8,512]{1,0:T(8,128)}) custom-call(s32[2]{0:T(128)} %pad_add_fusion.1.idx, s32[6]{0:T(128)} %lens.7, bf16[1776,512]{1,0:T(8,128)(2,1)} %bitcast.61, ...), custom_call_target="tpu_custom_call" | custom-call | flops 1 | bytes 1 | tf_op jit(solution)/shard_map/f2b/pallas_call | solution.py:613
  108.1 2.0 %collective-permute-done.24 = bf16[4,256,256]{2,1,0:T(8,128)(2,1)S(1)} collective-permute-done((bf16[4,256,256]{2,1,0:T(8,128)(2,1)}, bf16[4,256,256]{2,1,0:T(8,128)(2,1)S(1)}, u32[]{:S(2)}, u32[]{:S(2)}) %collective-permute-start.24) | collective-permute-done | bytes 524320 | tf_op jit(solution)/shard_map/ppermute | solution.py:577
  110.3 1.9 add_convert_fusion.1
  114.2 11.0 %b1.1 = (bf16[6,296,1536]{2,1,0:T(8,128)(2,1)}, bf16[8,192,256]{2,1,0:T(8,128)(2,1)S(1)}, bf16[8,192,256]{2,1,0:T(8,128)(2,1)S(1)}) custom-call(s32[2]{0:T(128)S(1)} %copy-done.31, s32[6]{0:T(128)S(1)} %copy-done.34, bf16[6,296,1536]{2,1,0:T(8,128)(2,1)} %get-tuple-element.239.tri_ref, bf16[6,296,512]{2,1,0:T(8,128)(2,1)S(1)} %bitcast.51, ...), custom_call_target="tpu_custom_call" | custom-call | flops 1 | bytes 1 | tf_op jit(solution)/shard_map/b1/pallas_call | solution.py:613
  125.2 4.0 %collective-permute-done.27 = bf16[4,320,256]{2,1,0:T(8,128)(2,1)S(1)} collective-permute-done((bf16[4,320,256]{2,1,0:T(8,128)(2,1)S(1)}, bf16[4,320,256]{2,1,0:T(8,128)(2,1)S(1)}, u32[]{:S(2)}, u32[]{:S(2)}) %collective-permute-start.27) | collective-permute-done | bytes 655392 | tf_op jit(solution)/shard_map/ppermute | solution.py:577
  129.5 2.0 %collective-permute-done.28 = bf16[8,192,256]{2,1,0:T(8,128)(2,1)S(1)} collective-permute-done((bf16[8,192,256]{2,1,0:T(8,128)(2,1)S(1)}, bf16[8,192,256]{2,1,0:T(8,128)(2,1)S(1)}, u32[]{:S(2)}, u32[]{:S(2)}) %collective-permute-start.28) | collective-permute-done | bytes 786464 | tf_op jit(solution)/shard_map/ppermute | solution.py:577
  133.5 3.0 %collective-permute-start.31 = (bf16[1,256,256]{2,1,0:T(8,128)(2,1)S(1)}, bf16[1,256,256]{2,1,0:T(8,128)(2,1)S(1)}, u32[]{:S(2)}, u32[]{:S(2)}) collective-permute-start(bf16[1,256,256]{2,1,0:T(8,128)(2,1)S(1)} %get-tuple-element.291), channel_id=1, source_target_pairs={{0,4},{1,5},{2,6},{3,7},{4,0},{5,1},{6,2},{7,3},{8,12},{9,13},{10,... | collective-permute-start | bytes 393224 | tf_op jit(solution)/shard_map/ppermute | solution.py:577
  136.5 6.9 %qstat.1 = (f32[16,256]{1,0:T(8,128)S(1)}, f32[16,256]{1,0:T(8,128)S(1)}) custom-call(bf16[1776,512]{1,0:T(8,128)(2,1)S(1)} %copy-done.15, bf16[2816,512]{1,0:T(8,128)(2,1)S(1)} %copy-done.10, s32[11,1776]{1,0:T(8,128)S(1)} %bitcast.53, s32[1,1776]{1,0:T(1,128)S(1)} %reshape.96.cnt), custom_call_target="tpu_custom_call" | custom-call | flops 1 | bytes 1 | tf_op jit(solution)/shard_map/qstat/pallas_call | solution.py:613
  143.4 2.4 %collective-permute-done.29 = bf16[4,192,256]{2,1,0:T(8,128)(2,1)S(1)} collective-permute-done((bf16[4,192,256]{2,1,0:T(8,128)(2,1)S(1)}, bf16[4,192,256]{2,1,0:T(8,128)(2,1)S(1)}, u32[]{:S(2)}, u32[]{:S(2)}) %collective-permute-start.29) | collective-permute-done | bytes 393248 | tf_op jit(solution)/shard_map/ppermute | solution.py:577
  146.6 1.8 collective-permute-start.33
  148.5 6.9 %b2.2 = (bf16[1776,512]{1,0:T(8,128)(2,1)}, f32[8,512]{1,0:T(8,128)S(1)}) custom-call(s32[2]{0:T(128)S(1)} %copy-done.31, bf16[1776,1536]{1,0:T(8,128)(2,1)S(1)} %bitcast.49, bf16[1776,512]{1,0:T(8,128)(2,1)S(1)} %bitcast.47, f32[1776,512]{1,0:T(8,128)S(1)} %copy-done.2, f32[8,512]{1,0:T(8,128)S(1)} %copy-done.21, bf16[4,32,1536]{2,1,0:T(8,128)(2,1)S(1)} %copy-done.4, ...), custom_call_target="tpu_custom_call" | custom-call | flops 1 | bytes 1 | tf_op jit(solution)/shard_map/b2/pallas_call | solution.py:613
  156.2 2.5 %collective-permute-start.34 = (bf16[576,256]{1,0:T(8,128)(2,1)S(1)}, bf16[576,256]{1,0:T(8,128)(2,1)S(1)}, u32[]{:S(2)}, u32[]{:S(2)}) collective-permute-start(bf16[576,256]{1,0:T(8,128)(2,1)S(1)} %pad_maximum_fusion.2), channel_id=1, source_target_pairs={{0,16},{8,24},{16,0},{24,8},{1,17},{9,25},{17,1},{25,9},{2,18},{10... | collective-permute-start | bytes 884744 | tf_op jit(solution)/shard_map/ppermute | solution.py:577
  159.0 5.4 %b2.3 = (bf16[1776,512]{1,0:T(8,128)(2,1)}, f32[8,512]{1,0:T(8,128)S(1)}) custom-call(s32[2]{0:T(128)S(1)} %copy-done.31, bf16[1776,1536]{1,0:T(8,128)(2,1)S(1)} %bitcast.50, bf16[1776,512]{1,0:T(8,128)(2,1)S(1)} %bitcast.48, f32[1776,512]{1,0:T(8,128)S(1)} %copy-done.2, f32[8,512]{1,0:T(8,128)S(1)} %copy-done.21, ...), custom_call_target="tpu_custom_call", output_to_operand_aliasing={{0}: (10, {})} | custom-call | flops 1 | bytes 1 | tf_op jit(solution)/shard_map/b2/pallas_call | solution.py:613
  165.0 1.8 collective-permute-start.38
  167.2 3.1 %lamb_mlp.1 = (f32[64,512]{1,0:T(8,128)}, f32[64,512]{1,0:T(8,128)}, f32[64,512]{1,0:T(8,128)S(1)}, f32[64,2048]{1,0:T(8,128)}, f32[64,2048]{1,0:T(8,128)}, /*in...) custom-call(s32[2]{0:T(128)S(1)} %copy-done.31, ...), custom_call_target="tpu_custom_call" | custom-call | flops 1 | bytes 1 | tf_op jit(solution)/shard_map/lamb_mlp/pallas_call | solution.py:613
  172.3 1.8 lamb_triple.1
  174.6 2.7 %collective-permute-start.41 = (f32[8,512]{1,0:T(8,128)S(1)}, f32[8,512]{1,0:T(8,128)S(1)}, u32[]{:S(2)}, u32[]{:S(2)}) collective-permute-start(f32[8,512]{1,0:T(8,128)S(1)} %pad_add_fusion), channel_id=1, source_target_pairs={{0,1},{1,0},{2,3},{3,2},{4,5},{5,4},{6,7},{7,6},{8,9},{9,8},{10,11... | collective-permute-start | bytes 49160 | tf_op jit(solution)/shard_map/ppermute | solution.py:577
  177.3 1.7 collective-permute-done.41
  180.8 2.1 %collective-permute-done.42 = f32[8,512]{1,0:T(8,128)S(1)} collective-permute-done((f32[8,512]{1,0:T(8,128)S(1)}, f32[8,512]{1,0:T(8,128)S(1)}, u32[]{:S(2)}, u32[]{:S(2)}) %collective-permute-start.42) | collective-permute-done | bytes 16416 | tf_op jit(solution)/shard_map/ppermute | solution.py:577
  184.5 3.0 %collective-permute-done.43.two = f32[8,512]{1,0:T(8,128)S(1)} collective-permute-done((f32[8,512]{1,0:T(8,128)S(1)}, f32[8,512]{1,0:T(8,128)S(1)}, u32[]{:S(2)}, u32[]{:S(2)}) %collective-permute-start.43) | collective-permute-done | bytes 16416 | tf_op jit(solution)/shard_map/ppermute | solution.py:577
  (219 shorter events, 33.8 us)
Async XLA Ops:
  1.6 11.7 %collective-permute-start = (bf16[32,1536]{1,0:T(8,128)(2,1)S(1)}, bf16[32,1536]{1,0:T(8,128)(2,1)S(1)}, u32[]{:S(2)}, u32[]{:S(2)}) collective-permute-start(bf16[32,1536]{1,0:T(8,128)(2,1)S(1)} %dynamic-slice_convert_fusion.1), channel_id=1, source_target_pairs={{0,2},{1,3},{2,0},{3,1},{4,6},{5,7},{6,4},{7,5},{8,10},{9,11},{10,... | collective-permute-start | bytes 294920 | tf_op jit(solution)/shard_map/ppermute | solution.py:577
  4.7 10.4 %collective-permute-start.1 = (bf16[32,1536]{1,0:T(8,128)(2,1)S(1)}, bf16[32,1536]{1,0:T(8,128)(2,1)S(1)}, u32[]{:S(2)}, u32[]{:S(2)}) collective-permute-start(bf16[32,1536]{1,0:T(8,128)(2,1)S(1)} %dynamic-slice_convert_fusion.1), channel_id=1, source_target_pairs={{0,4},{1,5},{2,6},{3,7},{4,0},{5,1},{6,2},{7,3},{8,12},{9,13},{10,... | collective-permute-start | bytes 294920 | tf_op jit(solution)/shard_map/ppermute | solution.py:577
  7.3 7.8 %collective-permute-start.2 = (bf16[32,1536]{1,0:T(8,128)(2,1)S(1)}, bf16[32,1536]{1,0:T(8,128)(2,1)S(1)}, u32[]{:S(2)}, u32[]{:S(2)}) collective-permute-start(bf16[32,1536]{1,0:T(8,128)(2,1)S(1)} %dynamic-slice_convert_fusion.1), channel_id=1, source_target_pairs={{0,6},{1,7},{2,4},{3,5},{4,2},{5,3},{6,0},{7,1},{8,14},{9,15},{10,... | collective-permute-start | bytes 294920 | tf_op jit(solution)/shard_map/ppermute | solution.py:577
  10.3 5.4 %collective-permute-start.3 = (bf16[160,512]{1,0:T(8,128)(2,1)S(1)}, bf16[160,512]{1,0:T(8,128)(2,1)S(1)}, u32[]{:S(2)}, u32[]{:S(2)}) collective-permute-start(bf16[160,512]{1,0:T(8,128)(2,1)S(1)} %pad_maximum_fusion.4), channel_id=1, source_target_pairs={{0,1},{1,0},{2,3},{3,2},{4,5},{5,4},{6,7},{7,6},{8,9},{9,8},{10,11... | collective-permute-start | bytes 491528 | tf_op jit(solution)/shard_map/ppermute | solution.py:577
  15.7 9.4 %collective-permute-start.4 = (bf16[4,32,1536]{2,1,0:T(8,128)(2,1)S(1)}, bf16[4,32,1536]{2,1,0:T(8,128)(2,1)S(1)}, u32[]{:S(2)}, u32[]{:S(2)}) collective-permute-start(bf16[4,32,1536]{2,1,0:T(8,128)(2,1)S(1)} %pad_maximum_fusion.refs_0_), channel_id=1, source_target_pairs={{0,1},{1,0},{2,3},{3,2},{4,5},{5,4},{6,7},{7,6},{8,9},{9,8},{10,11... | collective-permute-start | bytes 1179656 | tf_op jit(solution)/shard_map/ppermute | solution.py:577
  17.4 9.3 %collective-permute-start.6 = (bf16[4,32,1536]{2,1,0:T(8,128)(2,1)S(1)}, bf16[4,32,1536]{2,1,0:T(8,128)(2,1)S(1)}, u32[]{:S(2)}, u32[]{:S(2)}) collective-permute-start(bf16[4,32,1536]{2,1,0:T(8,128)(2,1)S(1)} %pad_maximum_fusion.refs_0_), channel_id=1, source_target_pairs={{0,8},{8,0},{16,24},{24,16},{1,9},{9,1},{17,25},{25,17},{2,10},{10... | collective-permute-start | bytes 1179656 | tf_op jit(solution)/shard_map/ppermute | solution.py:577
  17.5 29.6 %collective-permute-start.10 = (bf16[2,160,512]{2,1,0:T(8,128)(2,1)S(1)}, bf16[2,160,512]{2,1,0:T(8,128)(2,1)S(1)}, u32[]{:S(2)}, u32[]{:S(2)}) collective-permute-start(bf16[2,160,512]{2,1,0:T(8,128)(2,1)S(1)} %pad_maximum_fusion.1.refs_0_), channel_id=1, source_target_pairs={{0,4},{1,5},{2,6},{3,7},{4,0},{5,1},{6,2},{7,3},{8,12},{9,13},{10,... | collective-permute-start | bytes 983048 | tf_op jit(solution)/shard_map/ppermute | solution.py:577
  19.5 27.5 %collective-permute-start.11 = (bf16[2,160,512]{2,1,0:T(8,128)(2,1)S(1)}, bf16[2,160,512]{2,1,0:T(8,128)(2,1)S(1)}, u32[]{:S(2)}, u32[]{:S(2)}) collective-permute-start(bf16[2,160,512]{2,1,0:T(8,128)(2,1)S(1)} %pad_maximum_fusion.1.refs_0_), channel_id=1, source_target_pairs={{0,6},{1,7},{2,4},{3,5},{4,2},{5,3},{6,0},{7,1},{8,14},{9,15},{10,... | collective-permute-start | bytes 983048 | tf_op jit(solution)/shard_map/ppermute | solution.py:577
  21.2 25.9 %collective-permute-start.9 = (bf16[2,160,512]{2,1,0:T(8,128)(2,1)S(1)}, bf16[2,160,512]{2,1,0:T(8,128)(2,1)S(1)}, u32[]{:S(2)}, u32[]{:S(2)}) collective-permute-start(bf16[2,160,512]{2,1,0:T(8,128)(2,1)S(1)} %pad_maximum_fusion.1.refs_0_), channel_id=1, source_target_pairs={{0,2},{1,3},{2,0},{3,1},{4,6},{5,7},{6,4},{7,5},{8,10},{9,11},{10,... | collective-permute-start | bytes 983048 | tf_op jit(solution)/shard_map/ppermute | solution.py:577
  25.1 5.0 %collective-permute-start.5 = (bf16[128,512]{1,0:T(8,128)(2,1)S(1)}, bf16[128,512]{1,0:T(8,128)(2,1)S(1)}, u32[]{:S(2)}, u32[]{:S(2)}) collective-permute-start(bf16[128,512]{1,0:T(8,128)(2,1)S(1)} %pad_maximum_fusion.5), channel_id=1, source_target_pairs={{0,1},{1,0},{2,3},{3,2},{4,5},{5,4},{6,7},{7,6},{8,9},{9,8},{10,11... | collective-permute-start | bytes 393224 | tf_op jit(solution)/shard_map/ppermute | solution.py:577
  30.1 20.7 %collective-permute-start.12 = (bf16[2,160,512]{2,1,0:T(8,128)(2,1)S(1)}, bf16[2,160,512]{2,1,0:T(8,128)(2,1)S(1)}, u32[]{:S(2)}, u32[]{:S(2)}) collective-permute-start(bf16[2,160,512]{2,1,0:T(8,128)(2,1)S(1)} %pad_maximum_fusion.1.refs_0_), channel_id=1, source_target_pairs={{0,8},{8,0},{16,24},{24,16},{1,9},{9,1},{17,25},{25,17},{2,10},{10... | collective-permute-start | bytes 983048 | tf_op jit(solution)/shard_map/ppermute | solution.py:577
  47.1 5.3 %collective-permute-start.13 = (bf16[2,160,512]{2,1,0:T(8,128)(2,1)S(1)}, bf16[2,160,512]{2,1,0:T(8,128)(2,1)S(1)}, u32[]{:S(2)}, u32[]{:S(2)}) collective-permute-start(bf16[2,160,512]{2,1,0:T(8,128)(2,1)S(1)} %collective-permute-done.9.refs_1_), channel_id=1, source_target_pairs={{0,8},{8,0},{16,24},{24,16},{1,9},{9,1},{17,25},{25,17},{2,10},{10... | collective-permute-start | bytes 983048 | tf_op jit(solution)/shard_map/ppermute | solution.py:577
  47.3 6.6 %collective-permute-start.14 = (bf16[2,160,512]{2,1,0:T(8,128)(2,1)S(1)}, bf16[2,160,512]{2,1,0:T(8,128)(2,1)S(1)}, u32[]{:S(2)}, u32[]{:S(2)}) collective-permute-start(bf16[2,160,512]{2,1,0:T(8,128)(2,1)S(1)} %collective-permute-done.10.refs_2_), channel_id=1, source_target_pairs={{0,8},{8,0},{16,24},{24,16},{1,9},{9,1},{17,25},{25,17},{2,10},{10... | collective-permute-start | bytes 983048 | tf_op jit(solution)/shard_map/ppermute | solution.py:577
  47.7 6.2 %collective-permute-start.15 = (bf16[2,160,512]{2,1,0:T(8,128)(2,1)S(1)}, bf16[2,160,512]{2,1,0:T(8,128)(2,1)S(1)}, u32[]{:S(2)}, u32[]{:S(2)}) collective-permute-start(bf16[2,160,512]{2,1,0:T(8,128)(2,1)S(1)} %collective-permute-done.11.refs_3_), channel_id=1, source_target_pairs={{0,8},{8,0},{16,24},{24,16},{1,9},{9,1},{17,25},{25,17},{2,10},{10... | collective-permute-start | bytes 983048 | tf_op jit(solution)/shard_map/ppermute | solution.py:577
  47.8 29.1 %collective-permute-start.16 = (bf16[2,128,512]{2,1,0:T(8,128)(2,1)S(1)}, bf16[2,128,512]{2,1,0:T(8,128)(2,1)S(1)}, u32[]{:S(2)}, u32[]{:S(2)}) collective-permute-start(bf16[2,128,512]{2,1,0:T(8,128)(2,1)S(1)} %pad_maximum_fusion.3.refs_8_), channel_id=1, source_target_pairs={{0,2},{1,3},{2,0},{3,1},{4,6},{5,7},{6,4},{7,5},{8,10},{9,11},{10,... | collective-permute-start | bytes 786440 | tf_op jit(solution)/shard_map/ppermute | solution.py:577
  50.9 26.0 %collective-permute-start.17 = (bf16[2,128,512]{2,1,0:T(8,128)(2,1)S(1)}, bf16[2,128,512]{2,1,0:T(8,128)(2,1)S(1)}, u32[]{:S(2)}, u32[]{:S(2)}) collective-permute-start(bf16[2,128,512]{2,1,0:T(8,128)(2,1)S(1)} %pad_maximum_fusion.3.refs_8_), channel_id=1, source_target_pairs={{0,4},{1,5},{2,6},{3,7},{4,0},{5,1},{6,2},{7,3},{8,12},{9,13},{10,... | collective-permute-start | bytes 786440 | tf_op jit(solution)/shard_map/ppermute | solution.py:577
  52.4 24.5 %collective-permute-start.18 = (bf16[2,128,512]{2,1,0:T(8,128)(2,1)S(1)}, bf16[2,128,512]{2,1,0:T(8,128)(2,1)S(1)}, u32[]{:S(2)}, u32[]{:S(2)}) collective-permute-start(bf16[2,128,512]{2,1,0:T(8,128)(2,1)S(1)} %pad_maximum_fusion.3.refs_8_), channel_id=1, source_target_pairs={{0,6},{1,7},{2,4},{3,5},{4,2},{5,3},{6,0},{7,1},{8,14},{9,15},{10,... | collective-permute-start | bytes 786440 | tf_op jit(solution)/shard_map/ppermute | solution.py:577
  53.9 24.0 %collective-permute-start.19 = (bf16[2,128,512]{2,1,0:T(8,128)(2,1)S(1)}, bf16[2,128,512]{2,1,0:T(8,128)(2,1)S(1)}, u32[]{:S(2)}, u32[]{:S(2)}) collective-permute-start(bf16[2,128,512]{2,1,0:T(8,128)(2,1)S(1)} %pad_maximum_fusion.3.refs_8_), channel_id=1, source_target_pairs={{0,8},{8,0},{16,24},{24,16},{1,9},{9,1},{17,25},{25,17},{2,10},{10... | collective-permute-start | bytes 786440 | tf_op jit(solution)/shard_map/ppermute | solution.py:577
  79.3 26.7 %collective-permute-start.23 = (bf16[2,4,256,256]{3,2,1,0:T(8,128)(2,1)}, bf16[2,4,256,256]{3,2,1,0:T(8,128)(2,1)S(1)}, u32[]{:S(2)}, u32[]{:S(2)}) collective-permute-start(bf16[2,4,256,256]{3,2,1,0:T(8,128)(2,1)} %get-tuple-element.242), channel_id=1, source_target_pairs={{0,2},{1,3},{2,0},{3,1},{4,6},{5,7},{6,4},{7,5},{8,10},{9,11},{10,... | collective-permute-start | bytes 3145736 | tf_op jit(solution)/shard_map/ppermute | solution.py:577
  106.0 4.3 %collective-permute-start.25 = (bf16[8,320,256]{2,1,0:T(8,128)(2,1)}, bf16[8,320,256]{2,1,0:T(8,128)(2,1)}, u32[]{:S(2)}, u32[]{:S(2)}) collective-permute-start(bf16[8,320,256]{2,1,0:T(8,128)(2,1)} %get-tuple-element.251), channel_id=1, source_target_pairs={{0,8},{8,0},{16,24},{24,16},{1,9},{9,1},{17,25},{25,17},{2,10},{10... | collective-permute-start | bytes 3932168 | tf_op jit(solution)/shard_map/ppermute | solution.py:577
  112.2 17.1 %collective-permute-start.27 = (bf16[4,320,256]{2,1,0:T(8,128)(2,1)S(1)}, bf16[4,320,256]{2,1,0:T(8,128)(2,1)S(1)}, u32[]{:S(2)}, u32[]{:S(2)}) collective-permute-start(bf16[4,320,256]{2,1,0:T(8,128)(2,1)S(1)} %get-tuple-element.259), channel_id=1, source_target_pairs={{0,2},{1,3},{2,0},{3,1},{4,6},{5,7},{6,4},{7,5},{8,10},{9,11},{10,... | collective-permute-start | bytes 1966088 | tf_op jit(solution)/shard_map/ppermute | solution.py:577
  113.7 11.6 %collective-permute-start.26 = (bf16[2,256,256]{2,1,0:T(8,128)(2,1)S(1)}, bf16[2,256,256]{2,1,0:T(8,128)(2,1)S(1)}, u32[]{:S(2)}, u32[]{:S(2)}) collective-permute-start(bf16[2,256,256]{2,1,0:T(8,128)(2,1)S(1)} %get-tuple-element.257), channel_id=1, source_target_pairs={{0,1},{1,0},{2,3},{3,2},{4,5},{5,4},{6,7},{7,6},{8,9},{9,8},{10,11... | collective-permute-start | bytes 786440 | tf_op jit(solution)/shard_map/ppermute | solution.py:577
  131.8 14.0 %collective-permute-start.29 = (bf16[4,192,256]{2,1,0:T(8,128)(2,1)S(1)}, bf16[4,192,256]{2,1,0:T(8,128)(2,1)S(1)}, u32[]{:S(2)}, u32[]{:S(2)}) collective-permute-start(bf16[4,192,256]{2,1,0:T(8,128)(2,1)S(1)} %get-tuple-element.280), channel_id=1, source_target_pairs={{0,2},{1,3},{2,0},{3,1},{4,6},{5,7},{6,4},{7,5},{8,10},{9,11},{10,... | collective-permute-start | bytes 1179656 | tf_op jit(solution)/shard_map/ppermute | solution.py:577
  133.0 10.4 %collective-permute-start.30 = (bf16[2,320,256]{2,1,0:T(8,128)(2,1)S(1)}, bf16[2,320,256]{2,1,0:T(8,128)(2,1)S(1)}, u32[]{:S(2)}, u32[]{:S(2)}) collective-permute-start(bf16[2,320,256]{2,1,0:T(8,128)(2,1)S(1)} %get-tuple-element.282), channel_id=1, source_target_pairs={{0,1},{1,0},{2,3},{3,2},{4,5},{5,4},{6,7},{7,6},{8,9},{9,8},{10,11... | collective-permute-start | bytes 983048 | tf_op jit(solution)/shard_map/ppermute | solution.py:577
  133.5 14.8 %collective-permute-start.31 = (bf16[1,256,256]{2,1,0:T(8,128)(2,1)S(1)}, bf16[1,256,256]{2,1,0:T(8,128)(2,1)S(1)}, u32[]{:S(2)}, u32[]{:S(2)}) collective-permute-start(bf16[1,256,256]{2,1,0:T(8,128)(2,1)S(1)} %get-tuple-element.291), channel_id=1, source_target_pairs={{0,4},{1,5},{2,6},{3,7},{4,0},{5,1},{6,2},{7,3},{8,12},{9,13},{10,... | collective-permute-start | bytes 393224 | tf_op jit(solution)/shard_map/ppermute | solution.py:577
  146.0 10.1 %collective-permute-start.32 = (bf16[2,192,256]{2,1,0:T(8,128)(2,1)S(1)}, bf16[2,192,256]{2,1,0:T(8,128)(2,1)S(1)}, u32[]{:S(2)}, u32[]{:S(2)}) collective-permute-start(bf16[2,192,256]{2,1,0:T(8,128)(2,1)S(1)} %get-tuple-element.294), channel_id=1, source_target_pairs={{0,1},{1,0},{2,3},{3,2},{4,5},{5,4},{6,7},{7,6},{8,9},{9,8},{10,11... | collective-permute-start | bytes 589832 | tf_op jit(solution)/shard_map/ppermute | solution.py:577
  146.6 9.5 %collective-permute-start.33 = (bf16[1,320,256]{2,1,0:T(8,128)(2,1)S(1)}, bf16[1,320,256]{2,1,0:T(8,128)(2,1)S(1)}, u32[]{:S(2)}, u32[]{:S(2)}) collective-permute-start(bf16[1,320,256]{2,1,0:T(8,128)(2,1)S(1)} %get-tuple-element.296), channel_id=1, source_target_pairs={{0,4},{1,5},{2,6},{3,7},{4,0},{5,1},{6,2},{7,3},{8,12},{9,13},{10,... | collective-permute-start | bytes 491528 | tf_op jit(solution)/shard_map/ppermute | solution.py:577
  156.2 8.6 %collective-permute-start.34 = (bf16[576,256]{1,0:T(8,128)(2,1)S(1)}, bf16[576,256]{1,0:T(8,128)(2,1)S(1)}, u32[]{:S(2)}, u32[]{:S(2)}) collective-permute-start(bf16[576,256]{1,0:T(8,128)(2,1)S(1)} %pad_maximum_fusion.2), channel_id=1, source_target_pairs={{0,16},{8,24},{16,0},{24,8},{1,17},{9,25},{17,1},{25,9},{2,18},{10... | collective-permute-start | bytes 884744 | tf_op jit(solution)/shard_map/ppermute | solution.py:577
  158.7 5.7 %collective-permute-start.35 = (bf16[1,192,256]{2,1,0:T(8,128)(2,1)S(1)}, bf16[1,192,256]{2,1,0:T(8,128)(2,1)S(1)}, u32[]{:S(2)}, u32[]{:S(2)}) collective-permute-start(bf16[1,192,256]{2,1,0:T(8,128)(2,1)S(1)} %get-tuple-element.364), channel_id=1, source_target_pairs={{0,4},{1,5},{2,6},{3,7},{4,0},{5,1},{6,2},{7,3},{8,12},{9,13},{10,... | collective-permute-start | bytes 294920 | tf_op jit(solution)/shard_map/ppermute | solution.py:577
  165.0 5.3 %collective-permute-start.38 = (bf16[192,256]{1,0:T(8,128)(2,1)S(1)}, bf16[192,256]{1,0:T(8,128)(2,1)S(1)}, u32[]{:S(2)}, u32[]{:S(2)}) collective-permute-start(bf16[192,256]{1,0:T(8,128)(2,1)S(1)} %fusion.4), channel_id=1, source_target_pairs={{0,16},{8,24},{16,0},{24,8},{1,17},{9,25},{17,1},{25,9},{2,18},{10... | collective-permute-start | bytes 294920 | tf_op jit(solution)/shard_map/ppermute | solution.py:577
  174.6 4.4 %collective-permute-start.41 = (f32[8,512]{1,0:T(8,128)S(1)}, f32[8,512]{1,0:T(8,128)S(1)}, u32[]{:S(2)}, u32[]{:S(2)}) collective-permute-start(f32[8,512]{1,0:T(8,128)S(1)} %pad_add_fusion), channel_id=1, source_target_pairs={{0,1},{1,0},{2,3},{3,2},{4,5},{5,4},{6,7},{7,6},{8,9},{9,8},{10,11... | collective-permute-start | bytes 49160 | tf_op jit(solution)/shard_map/ppermute | solution.py:577
  182.9 4.6 %collective-permute-start.43 = (f32[8,512]{1,0:T(8,128)S(1)}, f32[8,512]{1,0:T(8,128)S(1)}, u32[]{:S(2)}, u32[]{:S(2)}) collective-permute-start(f32[8,512]{1,0:T(8,128)S(1)} %add_select_fusion.one), channel_id=1, source_target_pairs={{0,4},{1,5},{2,6},{3,7},{4,0},{5,1},{6,2},{7,3},{8,12},{9,13},{10,... | collective-permute-start | bytes 49160 | tf_op jit(solution)/shard_map/ppermute | solution.py:577
  (69 other events, 538.9 us)

commit v7 on v6

--- a/solution.py
+++ b/solution.py
@@ -547,10 +547,14 @@
     return jnp.where(row == 5, jnp.maximum(mine, other), mine + other)
 
 
-def final_kernel(one, two, norms, firsts, seconds, *refs):
+def final_kernel(count, *refs):
+    parts, (norms, firsts, seconds), refs = refs[:count], refs[count : count + 3], refs[count + 3 :]
     masters, updates, news = refs[:4], refs[4:8], refs[8:12]
     norms_out, first_out, second_out, table_out, mean_out, peak_out = refs[12:]
-    small = merge_small(one[...], two[...])
+    level = [part[...] for part in parts]
+    while len(level) > 1:
+        level = [merge_small(level[i], level[i + 1]) for i in range(0, len(level), 2)]
+    small = level[0]
     roots = jnp.sqrt(small[6:8, 0:128])
     for i in range(4):
         ratio = roots[0:1, i : i + 1] / (roots[1:2, i : i + 1] + RATIO_EPSILON)
@@ -868,13 +872,6 @@
     else:
         keep_b, send_b = add_low(keep_b, got_b), keep_b
     gtri_flat = gtri.reshape(flat, 3 * D)
-    gtri_flat, keep_t, send_t, keep_b, send_b = sync(gtri_flat, keep_t, send_t, keep_b, send_b)
-    got_t = steps_f(send_t, order[1])
-    if late:
-        got_b = steps_f(send_b, late[0])
-    cut = (fl_steps + 1) // 2
-    ig_part, ln1_a = b2_call(0, cut, gtri_flat, None, ())
-    ig_part, keep_t, got_t, keep_b, *got_b = sync(ig_part, keep_t, got_t, keep_b, *([got_b] if late else []))
 
     def finish(keep, bits):
         for b in bits:
@@ -883,26 +880,45 @@
         return keep[0]
 
     x_bits = d_bits[nh - 1 :]
+
+    def before_x(keep):
+        red = finish(keep, late[1:])
+        for b in x_bits[:-1]:
+            red = add_low(red, steps_d(red, b))
+        return red
+
+    if late:
+        keep_a = add_low(keep_a, got_a)
+    red_a = before_x(keep_a)
+    gtri_flat, keep_t, send_t, keep_b, send_b, red_a = sync(gtri_flat, keep_t, send_t, keep_b, send_b, red_a)
+    got_t = steps_f(send_t, order[1])
+    if late:
+        got_b = steps_f(send_b, late[0])
+    cut = (fl_steps + 1) // 2
+    got_ra = steps_d(red_a, x_bits[-1])
+    ig_part, ln1_a = b2_call(0, cut, gtri_flat, None, ())
+    ig_part, keep_t, got_t, got_ra, keep_b, *got_b = sync(
+        ig_part, keep_t, got_t, got_ra, keep_b, *([got_b] if late else [])
+    )
     if late:
         keep_t, send_t = halves(keep_t, got_t)
-        keep_b, keep_a = add_low(keep_b, got_b[0]), add_low(keep_a, got_a)
+        keep_b = add_low(keep_b, got_b[0])
     else:
         keep_t = add_low(keep_t, got_t)
-    red = jnp.concatenate([finish(keep_a, late[1:]), finish(keep_b, late[1:])], axis=0)
-    for b in x_bits[:-1]:
-        red = add_low(red, steps_d(red, b))
-    red, keep_t, ig_part = sync(red, keep_t, ig_part)
+    red_b = before_x(keep_b)
+    red_b, keep_t, ig_part = sync(red_b, keep_t, ig_part)
     if late:
         got_t = steps_f(send_t, late[0])
-    got_red = steps_d(red, x_bits[-1])
+    got_rb = steps_d(red_b, x_bits[-1])
     input_grad, small = b2_call(cut, fl_steps - cut, gtri_flat, ig_part, (ln1_a, ln2, q_sum, q_top))
-    small, red, got_red, keep_t, *got_t = sync(small, red, got_red, keep_t, *([got_t] if late else []))
-
-    red_t = finish(add_low(keep_t, got_t[0]) if late else keep_t, late[1:])
-    for b in x_bits[:-1]:
-        red_t = add_low(red_t, steps_d(red_t, b))
+    small, red_a, got_ra, red_b, got_rb, keep_t, *got_t = sync(
+        small, red_a, got_ra, red_b, got_rb, keep_t, *([got_t] if late else [])
+    )
+
+    red_t = before_x(add_low(keep_t, got_t[0]) if late else keep_t)
     got_rt = steps_d(red_t, x_bits[-1])
-    red = red.astype(F32) + got_red.astype(F32)
+    both_sum = lambda a, b: a.astype(F32) + b.astype(F32)
+    red = jnp.concatenate([both_sum(red_a, got_ra), both_sum(red_b, got_rb)], axis=0)
     red_parts = [red] + ([steps_d(red, 1)] if nh == 2 else [])
     small_core = steps_d(small, d_bits[0])
     red_t, *red_parts = sync(red_t, *red_parts)
@@ -933,18 +949,21 @@
     )
 
     small = small + jnp.pad(squares, ((0, 0), (0, D - 128)))
-    for b in f_bits[:-1]:
+    for b in f_bits[:-2]:
         small = merge_small(small, steps_f(small, b))
-    small_two = steps_f(small, f_bits[-1])
+    far = [0]
+    for b in f_bits[-2:]:
+        far = far + [r ^ b for r in far]
+    smalls = [small] + [steps_f(small, r) for r in far[1:]]
     masters = (w_triple, w_mixer, w_expand, w_reduce)
     updates = (tri_out[2], mlp_out[2], mlp_out[5], mlp_out[8])
     firsts_t, seconds_t = first_norms.T, second_norms.T
     *news, norms_out, first_out, second_out, norm_table, mean, peak = kernel_call(
-        final_kernel, "final", (1,),
-        full(small, small_two, norm_t, firsts_t, seconds_t, *masters, *updates),
+        functools.partial(final_kernel, len(smalls)), "final", (1,),
+        full(*smalls, norm_t, firsts_t, seconds_t, *masters, *updates),
         [like(w) for w in masters]
         + [whole((4, D))] * 3 + [whole((2, 8)), whole((1, ACT)), whole((1, ACT))],
-        [], 16, (small, small_two, norm_t, firsts_t, seconds_t, *masters, *updates),
+        [], 16, (*smalls, norm_t, firsts_t, seconds_t, *masters, *updates),
     )
     return (
         block_out.reshape(ep, rows, D), input_grad.reshape(ep, rows, D), *news,

time: 191 us -> 193 us (1.010)
  starting transfers between devices: 46.1 us -> 49.1 us
    ppermute x44 -> x46, starting transfers between devices: 46.1 us -> 49.1 us  [xor_step(): return lax.ppermute(v, axis, [(i, i ^ bit) for i in range(size)])]
    ppermute x44 -> x46, waiting for transfers between devices: 30.2 us -> 29.6 us  [xor_step(): return lax.ppermute(v, axis, [(i, i ^ bit) for i in range(size)])]
  transfers between devices with their start and end apart: 44 -> 46, of which waited for: 18 -> 18; matrix products, arithmetic and copies ran while one was open for 3% -> 3% of each run, Pallas kernels for 52% -> 51%
where the time goes in v7:
time: 193 us; the launch traced here: 191 us
  Pallas kernels  99.3 us (51%)
  starting transfers between devices  49.1 us (25%)
  waiting for transfers between devices  29.6 us (15%)
  local copies, waits for them, and re-layouts  7.28 us (4%)
  other arithmetic  4.26 us (2%)
    pallas_call x10, Pallas kernels, kernel_call(): pl.pallas_call(kernel, grid=grid, in_specs=in_specs, out_specs=[spec for...  99.3 us
    ppermute x46, starting transfers between devices, xor_step(): return lax.ppermute(v, axis, [(i, i ^ bit) for i in range(size)])  49.1 us
    ppermute x46, waiting for transfers between devices, xor_step(): return lax.ppermute(v, axis, [(i, i ^ bit) for i in range(size)])  29.6 us
  transfers between devices with their start and end apart: 46, of which 18 were waited for; matrix products, arithmetic and copies ran while one was open for 3% of the time, Pallas kernels for 51%

profile of v7, /device:TPU:0, one launch (start us, length us, event | category | flops | bytes accessed | tf_op | source)
XLA Modules:
  0.0 191.2 jit_solution(14357693018708529327)
XLA Ops:
  1.6 3.1 %collective-permute-start = (bf16[32,1536]{1,0:T(8,128)(2,1)S(1)}, bf16[32,1536]{1,0:T(8,128)(2,1)S(1)}, u32[]{:S(2)}, u32[]{:S(2)}) collective-permute-start(bf16[32,1536]{1,0:T(8,128)(2,1)S(1)} %dynamic-slice_convert_fusion.1), channel_id=1, source_target_pairs={{0,2},{1,3},{2,0},{3,1},{4,6},{5,7},{6,4},{7,5},{8,10},{9,11},{10,... | collective-permute-start | bytes 294920 | tf_op jit(solution)/shard_map/ppermute | solution.py:581
  4.7 2.6 %collective-permute-start.1 = (bf16[32,1536]{1,0:T(8,128)(2,1)S(1)}, bf16[32,1536]{1,0:T(8,128)(2,1)S(1)}, u32[]{:S(2)}, u32[]{:S(2)}) collective-permute-start(bf16[32,1536]{1,0:T(8,128)(2,1)S(1)} %dynamic-slice_convert_fusion.1), channel_id=1, source_target_pairs={{0,4},{1,5},{2,6},{3,7},{4,0},{5,1},{6,2},{7,3},{8,12},{9,13},{10,... | collective-permute-start | bytes 294920 | tf_op jit(solution)/shard_map/ppermute | solution.py:581
  10.3 1.8 collective-permute-start.3
  13.3 1.8 collective-permute-done.1
  15.7 1.7 collective-permute-start.4
  17.5 2.1 %collective-permute-start.10 = (bf16[2,160,512]{2,1,0:T(8,128)(2,1)S(1)}, bf16[2,160,512]{2,1,0:T(8,128)(2,1)S(1)}, u32[]{:S(2)}, u32[]{:S(2)}) collective-permute-start(bf16[2,160,512]{2,1,0:T(8,128)(2,1)S(1)} %pad_maximum_fusion.2.refs_0_), channel_id=1, source_target_pairs={{0,4},{1,5},{2,6},{3,7},{4,0},{5,1},{6,2},{7,3},{8,12},{9,13},{10,... | collective-permute-start | bytes 983048 | tf_op jit(solution)/shard_map/ppermute | solution.py:581
  21.7 3.4 %collective-permute-done.4.refs_2_ = bf16[4,32,1536]{2,1,0:T(8,128)(2,1)S(1)} collective-permute-done((bf16[4,32,1536]{2,1,0:T(8,128)(2,1)S(1)}, bf16[4,32,1536]{2,1,0:T(8,128)(2,1)S(1)}, u32[]{:S(2)}, u32[]{:S(2)}) %collective-permute-start.4) | collective-permute-done | bytes 393248 | tf_op jit(solution)/shard_map/ppermute | solution.py:581
  26.8 3.3 %collective-permute-done.5 = bf16[128,512]{1,0:T(8,128)(2,1)S(1)} collective-permute-done((bf16[128,512]{1,0:T(8,128)(2,1)S(1)}, bf16[128,512]{1,0:T(8,128)(2,1)S(1)}, u32[]{:S(2)}, u32[]{:S(2)}) %collective-permute-start.5) | collective-permute-done | bytes 131104 | tf_op jit(solution)/shard_map/ppermute | solution.py:581
  32.2 14.8 %f1.1 = (bf16[6,296,1536]{2,1,0:T(8,128)(2,1)}, bf16[6,296,512]{2,1,0:T(8,128)(2,1)}, bf16[6,296,512]{2,1,0:T(8,128)(2,1)}, f32[6,16,256]{2,1,0:T(8,128)}) custom-call(s32[2]{0:T(128)} %pad_add_fusion.1.idx, s32[6]{0:T(128)} %lens.7, bf16[6,296,512]{2,1,0:T(8,128)(2,1)} %tok.1, f32[8,512]{1,0:T(8,128)} %concatenate.28.norm, bf16[4,32,1536]{2,1,0:T(8,128)(2,1)} %copy-done.3, ...), custom_call_target="tpu_custom_call" | custom-call | flops 1 | bytes 1 | tf_op jit(solution)/shard_map/f1/pallas_call | solution.py:617
  47.8 3.1 %collective-permute-start.16 = (bf16[2,128,512]{2,1,0:T(8,128)(2,1)S(1)}, bf16[2,128,512]{2,1,0:T(8,128)(2,1)S(1)}, u32[]{:S(2)}, u32[]{:S(2)}) collective-permute-start(bf16[2,128,512]{2,1,0:T(8,128)(2,1)S(1)} %pad_maximum_fusion.3.refs_8_), channel_id=1, source_target_pairs={{0,2},{1,3},{2,0},{3,1},{4,6},{5,7},{6,4},{7,5},{8,10},{9,11},{10,... | collective-permute-start | bytes 786440 | tf_op jit(solution)/shard_map/ppermute | solution.py:581
  54.8 22.1 %f2a.1 = (f32[1776,512]{1,0:T(8,128)}, f32[1776,512]{1,0:T(8,128)}, f32[1776,512]{1,0:T(8,128)}, bf16[1776,512]{1,0:T(8,128)(2,1)}, bf16[2,4,256,256]{3,2,1,0:T(8,128)(2,1)}, /*index=5*/bf16[2,4,256,256]{3,2,1,0:T(8,128)(2,1)}) custom-call(s32[2]{0:T(128)} %pad_add_fusion.1.idx, s32[6]{0:T(128)} %lens.7, bf16[1776,512]{1,0:T(8,128)(2,1)} %bitcast.60, ...), custom_call_target="tpu_custom_call" | custom-call | flops 1 | bytes 1 | tf_op jit(solution)/shard_map/f2a/pallas_call | solution.py:617
  80.0 26.0 %f2b.1 = (bf16[1776,512]{1,0:T(8,128)(2,1)}, f32[1776,512]{1,0:T(8,128)}, bf16[1776,512]{1,0:T(8,128)(2,1)}, bf16[8,320,256]{2,1,0:T(8,128)(2,1)}, bf16[8,320,256]{2,1,0:T(8,128)(2,1)}, /*index=5*/f32[8,512]{1,0:T(8,128)}) custom-call(s32[2]{0:T(128)} %pad_add_fusion.1.idx, s32[6]{0:T(128)} %lens.7, bf16[1776,512]{1,0:T(8,128)(2,1)} %bitcast.61, ...), custom_call_target="tpu_custom_call" | custom-call | flops 1 | bytes 1 | tf_op jit(solution)/shard_map/f2b/pallas_call | solution.py:617
  108.0 2.0 %collective-permute-done.24 = bf16[4,256,256]{2,1,0:T(8,128)(2,1)S(1)} collective-permute-done((bf16[4,256,256]{2,1,0:T(8,128)(2,1)}, bf16[4,256,256]{2,1,0:T(8,128)(2,1)S(1)}, u32[]{:S(2)}, u32[]{:S(2)}) %collective-permute-start.24) | collective-permute-done | bytes 524320 | tf_op jit(solution)/shard_map/ppermute | solution.py:581
  110.3 1.9 add_convert_fusion.1
  114.2 11.0 %b1.1 = (bf16[6,296,1536]{2,1,0:T(8,128)(2,1)}, bf16[8,192,256]{2,1,0:T(8,128)(2,1)S(1)}, bf16[8,192,256]{2,1,0:T(8,128)(2,1)S(1)}) custom-call(s32[2]{0:T(128)S(1)} %copy-done.31, s32[6]{0:T(128)S(1)} %copy-done.34, bf16[6,296,1536]{2,1,0:T(8,128)(2,1)} %get-tuple-element.243.tri_ref, bf16[6,296,512]{2,1,0:T(8,128)(2,1)S(1)} %bitcast.51, ...), custom_call_target="tpu_custom_call" | custom-call | flops 1 | bytes 1 | tf_op jit(solution)/shard_map/b1/pallas_call | solution.py:617
  125.2 4.0 %collective-permute-done.27 = bf16[4,320,256]{2,1,0:T(8,128)(2,1)S(1)} collective-permute-done((bf16[4,320,256]{2,1,0:T(8,128)(2,1)S(1)}, bf16[4,320,256]{2,1,0:T(8,128)(2,1)S(1)}, u32[]{:S(2)}, u32[]{:S(2)}) %collective-permute-start.27) | collective-permute-done | bytes 655392 | tf_op jit(solution)/shard_map/ppermute | solution.py:581
  129.5 2.0 %collective-permute-done.28 = bf16[8,192,256]{2,1,0:T(8,128)(2,1)S(1)} collective-permute-done((bf16[8,192,256]{2,1,0:T(8,128)(2,1)S(1)}, bf16[8,192,256]{2,1,0:T(8,128)(2,1)S(1)}, u32[]{:S(2)}, u32[]{:S(2)}) %collective-permute-start.28) | collective-permute-done | bytes 786464 | tf_op jit(solution)/shard_map/ppermute | solution.py:581
  133.0 2.1 %collective-permute-start.31 = (bf16[1,256,256]{2,1,0:T(8,128)(2,1)S(1)}, bf16[1,256,256]{2,1,0:T(8,128)(2,1)S(1)}, u32[]{:S(2)}, u32[]{:S(2)}) collective-permute-start(bf16[1,256,256]{2,1,0:T(8,128)(2,1)S(1)} %get-tuple-element.293), channel_id=1, source_target_pairs={{0,4},{1,5},{2,6},{3,7},{4,0},{5,1},{6,2},{7,3},{8,12},{9,13},{10,... | collective-permute-start | bytes 393224 | tf_op jit(solution)/shard_map/ppermute | solution.py:581
  135.0 1.7 collective-permute-start.30
  136.7 6.9 %qstat.1 = (f32[16,256]{1,0:T(8,128)S(1)}, f32[16,256]{1,0:T(8,128)S(1)}) custom-call(bf16[1776,512]{1,0:T(8,128)(2,1)S(1)} %copy-done.15, bf16[2816,512]{1,0:T(8,128)(2,1)S(1)} %copy-done.10, s32[11,1776]{1,0:T(8,128)S(1)} %bitcast.53, s32[1,1776]{1,0:T(1,128)S(1)} %reshape.96.cnt), custom_call_target="tpu_custom_call" | custom-call | flops 1 | bytes 1 | tf_op jit(solution)/shard_map/qstat/pallas_call | solution.py:617
  146.5 2.1 %collective-permute-start.34 = (bf16[1,320,256]{2,1,0:T(8,128)(2,1)S(1)}, bf16[1,320,256]{2,1,0:T(8,128)(2,1)S(1)}, u32[]{:S(2)}, u32[]{:S(2)}) collective-permute-start(bf16[1,320,256]{2,1,0:T(8,128)(2,1)S(1)} %get-tuple-element.301), channel_id=1, source_target_pairs={{0,4},{1,5},{2,6},{3,7},{4,0},{5,1},{6,2},{7,3},{8,12},{9,13},{10,... | collective-permute-start | bytes 491528 | tf_op jit(solution)/shard_map/ppermute | solution.py:581
  148.6 3.7 %collective-permute-start.33 = (bf16[256,256]{1,0:T(8,128)(2,1)S(1)}, bf16[256,256]{1,0:T(8,128)(2,1)S(1)}, u32[]{:S(2)}, u32[]{:S(2)}) collective-permute-start(bf16[256,256]{1,0:T(8,128)(2,1)S(1)} %fusion.3), channel_id=1, source_target_pairs={{0,16},{8,24},{16,0},{24,8},{1,17},{9,25},{17,1},{25,9},{2,18},{10... | collective-permute-start | bytes 393224 | tf_op jit(solution)/shard_map/ppermute | solution.py:581
  152.4 6.9 %b2.2 = (bf16[1776,512]{1,0:T(8,128)(2,1)}, f32[8,512]{1,0:T(8,128)S(1)}) custom-call(s32[2]{0:T(128)S(1)} %copy-done.31, bf16[1776,1536]{1,0:T(8,128)(2,1)S(1)} %bitcast.49, bf16[1776,512]{1,0:T(8,128)(2,1)S(1)} %bitcast.47, f32[1776,512]{1,0:T(8,128)S(1)} %copy-done.2, f32[8,512]{1,0:T(8,128)S(1)} %copy-done.21, bf16[4,32,1536]{2,1,0:T(8,128)(2,1)S(1)} %copy-done.4, ...), custom_call_target="tpu_custom_call" | custom-call | flops 1 | bytes 1 | tf_op jit(solution)/shard_map/b2/pallas_call | solution.py:617
  160.3 5.4 %b2.3 = (bf16[1776,512]{1,0:T(8,128)(2,1)}, f32[8,512]{1,0:T(8,128)S(1)}) custom-call(s32[2]{0:T(128)S(1)} %copy-done.31, bf16[1776,1536]{1,0:T(8,128)(2,1)S(1)} %bitcast.50, bf16[1776,512]{1,0:T(8,128)(2,1)S(1)} %bitcast.48, f32[1776,512]{1,0:T(8,128)S(1)} %copy-done.2, f32[8,512]{1,0:T(8,128)S(1)} %copy-done.21, ...), custom_call_target="tpu_custom_call", output_to_operand_aliasing={{0}: (10, {})} | custom-call | flops 1 | bytes 1 | tf_op jit(solution)/shard_map/b2/pallas_call | solution.py:617
  166.1 1.9 %collective-permute-start.39 = (bf16[192,256]{1,0:T(8,128)(2,1)S(1)}, bf16[192,256]{1,0:T(8,128)(2,1)S(1)}, u32[]{:S(2)}, u32[]{:S(2)}) collective-permute-start(bf16[192,256]{1,0:T(8,128)(2,1)S(1)} %fusion.4), channel_id=1, source_target_pairs={{0,16},{8,24},{16,0},{24,8},{1,17},{9,25},{17,1},{25,9},{2,18},{10... | collective-permute-start | bytes 294920 | tf_op jit(solution)/shard_map/ppermute | solution.py:581
  168.4 3.1 %lamb_mlp.1 = (f32[64,512]{1,0:T(8,128)}, f32[64,512]{1,0:T(8,128)}, f32[64,512]{1,0:T(8,128)S(1)}, f32[64,2048]{1,0:T(8,128)}, f32[64,2048]{1,0:T(8,128)}, /*in...) custom-call(s32[2]{0:T(128)S(1)} %copy-done.31, ...), custom_call_target="tpu_custom_call" | custom-call | flops 1 | bytes 1 | tf_op jit(solution)/shard_map/lamb_mlp/pallas_call | solution.py:617
  173.5 1.8 lamb_triple.1
  176.9 2.7 %collective-permute-done.42 = f32[8,512]{1,0:T(8,128)S(1)} collective-permute-done((f32[8,512]{1,0:T(8,128)S(1)}, f32[8,512]{1,0:T(8,128)S(1)}, u32[]{:S(2)}, u32[]{:S(2)}) %collective-permute-start.42) | collective-permute-done | bytes 16416 | tf_op jit(solution)/shard_map/ppermute | solution.py:581
  179.7 3.0 %collective-permute-start.43 = (f32[8,512]{1,0:T(8,128)S(1)}, f32[8,512]{1,0:T(8,128)S(1)}, u32[]{:S(2)}, u32[]{:S(2)}) collective-permute-start(f32[8,512]{1,0:T(8,128)S(1)} %add_select_fusion.refs_0_), channel_id=1, source_target_pairs={{0,2},{1,3},{2,0},{3,1},{4,6},{5,7},{6,4},{7,5},{8,10},{9,11},{10,... | collective-permute-start | bytes 49160 | tf_op jit(solution)/shard_map/ppermute | solution.py:581
  182.6 1.7 collective-permute-start.44
  185.0 2.3 %collective-permute-done.44.refs_2_ = f32[8,512]{1,0:T(8,128)S(1)} collective-permute-done((f32[8,512]{1,0:T(8,128)S(1)}, f32[8,512]{1,0:T(8,128)S(1)}, u32[]{:S(2)}, u32[]{:S(2)}) %collective-permute-start.44) | collective-permute-done | bytes 16416 | tf_op jit(solution)/shard_map/ppermute | solution.py:581
  187.3 2.6 %collective-permute-done.45.refs_3_ = f32[8,512]{1,0:T(8,128)S(1)} collective-permute-done((f32[8,512]{1,0:T(8,128)S(1)}, f32[8,512]{1,0:T(8,128)S(1)}, u32[]{:S(2)}, u32[]{:S(2)}) %collective-permute-start.45) | collective-permute-done | bytes 16416 | tf_op jit(solution)/shard_map/ppermute | solution.py:581
  (223 shorter events, 35.1 us)
Async XLA Ops:
  1.6 11.7 %collective-permute-start = (bf16[32,1536]{1,0:T(8,128)(2,1)S(1)}, bf16[32,1536]{1,0:T(8,128)(2,1)S(1)}, u32[]{:S(2)}, u32[]{:S(2)}) collective-permute-start(bf16[32,1536]{1,0:T(8,128)(2,1)S(1)} %dynamic-slice_convert_fusion.1), channel_id=1, source_target_pairs={{0,2},{1,3},{2,0},{3,1},{4,6},{5,7},{6,4},{7,5},{8,10},{9,11},{10,... | collective-permute-start | bytes 294920 | tf_op jit(solution)/shard_map/ppermute | solution.py:581
  4.7 10.4 %collective-permute-start.1 = (bf16[32,1536]{1,0:T(8,128)(2,1)S(1)}, bf16[32,1536]{1,0:T(8,128)(2,1)S(1)}, u32[]{:S(2)}, u32[]{:S(2)}) collective-permute-start(bf16[32,1536]{1,0:T(8,128)(2,1)S(1)} %dynamic-slice_convert_fusion.1), channel_id=1, source_target_pairs={{0,4},{1,5},{2,6},{3,7},{4,0},{5,1},{6,2},{7,3},{8,12},{9,13},{10,... | collective-permute-start | bytes 294920 | tf_op jit(solution)/shard_map/ppermute | solution.py:581
  7.3 7.8 %collective-permute-start.2 = (bf16[32,1536]{1,0:T(8,128)(2,1)S(1)}, bf16[32,1536]{1,0:T(8,128)(2,1)S(1)}, u32[]{:S(2)}, u32[]{:S(2)}) collective-permute-start(bf16[32,1536]{1,0:T(8,128)(2,1)S(1)} %dynamic-slice_convert_fusion.1), channel_id=1, source_target_pairs={{0,6},{1,7},{2,4},{3,5},{4,2},{5,3},{6,0},{7,1},{8,14},{9,15},{10,... | collective-permute-start | bytes 294920 | tf_op jit(solution)/shard_map/ppermute | solution.py:581
  10.3 5.4 %collective-permute-start.3 = (bf16[160,512]{1,0:T(8,128)(2,1)S(1)}, bf16[160,512]{1,0:T(8,128)(2,1)S(1)}, u32[]{:S(2)}, u32[]{:S(2)}) collective-permute-start(bf16[160,512]{1,0:T(8,128)(2,1)S(1)} %pad_maximum_fusion.4), channel_id=1, source_target_pairs={{0,1},{1,0},{2,3},{3,2},{4,5},{5,4},{6,7},{7,6},{8,9},{9,8},{10,11... | collective-permute-start | bytes 491528 | tf_op jit(solution)/shard_map/ppermute | solution.py:581
  15.7 9.4 %collective-permute-start.4 = (bf16[4,32,1536]{2,1,0:T(8,128)(2,1)S(1)}, bf16[4,32,1536]{2,1,0:T(8,128)(2,1)S(1)}, u32[]{:S(2)}, u32[]{:S(2)}) collective-permute-start(bf16[4,32,1536]{2,1,0:T(8,128)(2,1)S(1)} %pad_maximum_fusion.1.refs_0_), channel_id=1, source_target_pairs={{0,1},{1,0},{2,3},{3,2},{4,5},{5,4},{6,7},{7,6},{8,9},{9,8},{10,11... | collective-permute-start | bytes 1179656 | tf_op jit(solution)/shard_map/ppermute | solution.py:581
  17.4 9.3 %collective-permute-start.6 = (bf16[4,32,1536]{2,1,0:T(8,128)(2,1)S(1)}, bf16[4,32,1536]{2,1,0:T(8,128)(2,1)S(1)}, u32[]{:S(2)}, u32[]{:S(2)}) collective-permute-start(bf16[4,32,1536]{2,1,0:T(8,128)(2,1)S(1)} %pad_maximum_fusion.1.refs_0_), channel_id=1, source_target_pairs={{0,8},{8,0},{16,24},{24,16},{1,9},{9,1},{17,25},{25,17},{2,10},{10... | collective-permute-start | bytes 1179656 | tf_op jit(solution)/shard_map/ppermute | solution.py:581
  17.5 29.6 %collective-permute-start.10 = (bf16[2,160,512]{2,1,0:T(8,128)(2,1)S(1)}, bf16[2,160,512]{2,1,0:T(8,128)(2,1)S(1)}, u32[]{:S(2)}, u32[]{:S(2)}) collective-permute-start(bf16[2,160,512]{2,1,0:T(8,128)(2,1)S(1)} %pad_maximum_fusion.2.refs_0_), channel_id=1, source_target_pairs={{0,4},{1,5},{2,6},{3,7},{4,0},{5,1},{6,2},{7,3},{8,12},{9,13},{10,... | collective-permute-start | bytes 983048 | tf_op jit(solution)/shard_map/ppermute | solution.py:581
  19.5 27.5 %collective-permute-start.11 = (bf16[2,160,512]{2,1,0:T(8,128)(2,1)S(1)}, bf16[2,160,512]{2,1,0:T(8,128)(2,1)S(1)}, u32[]{:S(2)}, u32[]{:S(2)}) collective-permute-start(bf16[2,160,512]{2,1,0:T(8,128)(2,1)S(1)} %pad_maximum_fusion.2.refs_0_), channel_id=1, source_target_pairs={{0,6},{1,7},{2,4},{3,5},{4,2},{5,3},{6,0},{7,1},{8,14},{9,15},{10,... | collective-permute-start | bytes 983048 | tf_op jit(solution)/shard_map/ppermute | solution.py:581
  21.2 25.9 %collective-permute-start.9 = (bf16[2,160,512]{2,1,0:T(8,128)(2,1)S(1)}, bf16[2,160,512]{2,1,0:T(8,128)(2,1)S(1)}, u32[]{:S(2)}, u32[]{:S(2)}) collective-permute-start(bf16[2,160,512]{2,1,0:T(8,128)(2,1)S(1)} %pad_maximum_fusion.2.refs_0_), channel_id=1, source_target_pairs={{0,2},{1,3},{2,0},{3,1},{4,6},{5,7},{6,4},{7,5},{8,10},{9,11},{10,... | collective-permute-start | bytes 983048 | tf_op jit(solution)/shard_map/ppermute | solution.py:581
  25.1 5.0 %collective-permute-start.5 = (bf16[128,512]{1,0:T(8,128)(2,1)S(1)}, bf16[128,512]{1,0:T(8,128)(2,1)S(1)}, u32[]{:S(2)}, u32[]{:S(2)}) collective-permute-start(bf16[128,512]{1,0:T(8,128)(2,1)S(1)} %pad_maximum_fusion.5), channel_id=1, source_target_pairs={{0,1},{1,0},{2,3},{3,2},{4,5},{5,4},{6,7},{7,6},{8,9},{9,8},{10,11... | collective-permute-start | bytes 393224 | tf_op jit(solution)/shard_map/ppermute | solution.py:581
  30.1 20.7 %collective-permute-start.12 = (bf16[2,160,512]{2,1,0:T(8,128)(2,1)S(1)}, bf16[2,160,512]{2,1,0:T(8,128)(2,1)S(1)}, u32[]{:S(2)}, u32[]{:S(2)}) collective-permute-start(bf16[2,160,512]{2,1,0:T(8,128)(2,1)S(1)} %pad_maximum_fusion.2.refs_0_), channel_id=1, source_target_pairs={{0,8},{8,0},{16,24},{24,16},{1,9},{9,1},{17,25},{25,17},{2,10},{10... | collective-permute-start | bytes 983048 | tf_op jit(solution)/shard_map/ppermute | solution.py:581
  47.1 5.3 %collective-permute-start.13 = (bf16[2,160,512]{2,1,0:T(8,128)(2,1)S(1)}, bf16[2,160,512]{2,1,0:T(8,128)(2,1)S(1)}, u32[]{:S(2)}, u32[]{:S(2)}) collective-permute-start(bf16[2,160,512]{2,1,0:T(8,128)(2,1)S(1)} %collective-permute-done.9.refs_1_), channel_id=1, source_target_pairs={{0,8},{8,0},{16,24},{24,16},{1,9},{9,1},{17,25},{25,17},{2,10},{10... | collective-permute-start | bytes 983048 | tf_op jit(solution)/shard_map/ppermute | solution.py:581
  47.3 6.6 %collective-permute-start.14 = (bf16[2,160,512]{2,1,0:T(8,128)(2,1)S(1)}, bf16[2,160,512]{2,1,0:T(8,128)(2,1)S(1)}, u32[]{:S(2)}, u32[]{:S(2)}) collective-permute-start(bf16[2,160,512]{2,1,0:T(8,128)(2,1)S(1)} %collective-permute-done.10.refs_2_), channel_id=1, source_target_pairs={{0,8},{8,0},{16,24},{24,16},{1,9},{9,1},{17,25},{25,17},{2,10},{10... | collective-permute-start | bytes 983048 | tf_op jit(solution)/shard_map/ppermute | solution.py:581
  47.7 6.2 %collective-permute-start.15 = (bf16[2,160,512]{2,1,0:T(8,128)(2,1)S(1)}, bf16[2,160,512]{2,1,0:T(8,128)(2,1)S(1)}, u32[]{:S(2)}, u32[]{:S(2)}) collective-permute-start(bf16[2,160,512]{2,1,0:T(8,128)(2,1)S(1)} %collective-permute-done.11.refs_3_), channel_id=1, source_target_pairs={{0,8},{8,0},{16,24},{24,16},{1,9},{9,1},{17,25},{25,17},{2,10},{10... | collective-permute-start | bytes 983048 | tf_op jit(solution)/shard_map/ppermute | solution.py:581
  47.8 29.0 %collective-permute-start.16 = (bf16[2,128,512]{2,1,0:T(8,128)(2,1)S(1)}, bf16[2,128,512]{2,1,0:T(8,128)(2,1)S(1)}, u32[]{:S(2)}, u32[]{:S(2)}) collective-permute-start(bf16[2,128,512]{2,1,0:T(8,128)(2,1)S(1)} %pad_maximum_fusion.3.refs_8_), channel_id=1, source_target_pairs={{0,2},{1,3},{2,0},{3,1},{4,6},{5,7},{6,4},{7,5},{8,10},{9,11},{10,... | collective-permute-start | bytes 786440 | tf_op jit(solution)/shard_map/ppermute | solution.py:581
  50.9 26.0 %collective-permute-start.17 = (bf16[2,128,512]{2,1,0:T(8,128)(2,1)S(1)}, bf16[2,128,512]{2,1,0:T(8,128)(2,1)S(1)}, u32[]{:S(2)}, u32[]{:S(2)}) collective-permute-start(bf16[2,128,512]{2,1,0:T(8,128)(2,1)S(1)} %pad_maximum_fusion.3.refs_8_), channel_id=1, source_target_pairs={{0,4},{1,5},{2,6},{3,7},{4,0},{5,1},{6,2},{7,3},{8,12},{9,13},{10,... | collective-permute-start | bytes 786440 | tf_op jit(solution)/shard_map/ppermute | solution.py:581
  52.4 24.5 %collective-permute-start.18 = (bf16[2,128,512]{2,1,0:T(8,128)(2,1)S(1)}, bf16[2,128,512]{2,1,0:T(8,128)(2,1)S(1)}, u32[]{:S(2)}, u32[]{:S(2)}) collective-permute-start(bf16[2,128,512]{2,1,0:T(8,128)(2,1)S(1)} %pad_maximum_fusion.3.refs_8_), channel_id=1, source_target_pairs={{0,6},{1,7},{2,4},{3,5},{4,2},{5,3},{6,0},{7,1},{8,14},{9,15},{10,... | collective-permute-start | bytes 786440 | tf_op jit(solution)/shard_map/ppermute | solution.py:581
  53.9 24.0 %collective-permute-start.19 = (bf16[2,128,512]{2,1,0:T(8,128)(2,1)S(1)}, bf16[2,128,512]{2,1,0:T(8,128)(2,1)S(1)}, u32[]{:S(2)}, u32[]{:S(2)}) collective-permute-start(bf16[2,128,512]{2,1,0:T(8,128)(2,1)S(1)} %pad_maximum_fusion.3.refs_8_), channel_id=1, source_target_pairs={{0,8},{8,0},{16,24},{24,16},{1,9},{9,1},{17,25},{25,17},{2,10},{10... | collective-permute-start | bytes 786440 | tf_op jit(solution)/shard_map/ppermute | solution.py:581
  79.3 26.7 %collective-permute-start.23 = (bf16[2,4,256,256]{3,2,1,0:T(8,128)(2,1)}, bf16[2,4,256,256]{3,2,1,0:T(8,128)(2,1)S(1)}, u32[]{:S(2)}, u32[]{:S(2)}) collective-permute-start(bf16[2,4,256,256]{3,2,1,0:T(8,128)(2,1)} %get-tuple-element.246), channel_id=1, source_target_pairs={{0,2},{1,3},{2,0},{3,1},{4,6},{5,7},{6,4},{7,5},{8,10},{9,11},{10,... | collective-permute-start | bytes 3145736 | tf_op jit(solution)/shard_map/ppermute | solution.py:581
  112.2 17.1 %collective-permute-start.27 = (bf16[4,320,256]{2,1,0:T(8,128)(2,1)S(1)}, bf16[4,320,256]{2,1,0:T(8,128)(2,1)S(1)}, u32[]{:S(2)}, u32[]{:S(2)}) collective-permute-start(bf16[4,320,256]{2,1,0:T(8,128)(2,1)S(1)} %get-tuple-element.263), channel_id=1, source_target_pairs={{0,2},{1,3},{2,0},{3,1},{4,6},{5,7},{6,4},{7,5},{8,10},{9,11},{10,... | collective-permute-start | bytes 1966088 | tf_op jit(solution)/shard_map/ppermute | solution.py:581
  113.6 11.6 %collective-permute-start.26 = (bf16[2,256,256]{2,1,0:T(8,128)(2,1)S(1)}, bf16[2,256,256]{2,1,0:T(8,128)(2,1)S(1)}, u32[]{:S(2)}, u32[]{:S(2)}) collective-permute-start(bf16[2,256,256]{2,1,0:T(8,128)(2,1)S(1)} %get-tuple-element.261), channel_id=1, source_target_pairs={{0,1},{1,0},{2,3},{3,2},{4,5},{5,4},{6,7},{7,6},{8,9},{9,8},{10,11... | collective-permute-start | bytes 786440 | tf_op jit(solution)/shard_map/ppermute | solution.py:581
  131.7 14.0 %collective-permute-start.29 = (bf16[4,192,256]{2,1,0:T(8,128)(2,1)S(1)}, bf16[4,192,256]{2,1,0:T(8,128)(2,1)S(1)}, u32[]{:S(2)}, u32[]{:S(2)}) collective-permute-start(bf16[4,192,256]{2,1,0:T(8,128)(2,1)S(1)} %get-tuple-element.284), channel_id=1, source_target_pairs={{0,2},{1,3},{2,0},{3,1},{4,6},{5,7},{6,4},{7,5},{8,10},{9,11},{10,... | collective-permute-start | bytes 1179656 | tf_op jit(solution)/shard_map/ppermute | solution.py:581
  133.0 11.5 %collective-permute-start.31 = (bf16[1,256,256]{2,1,0:T(8,128)(2,1)S(1)}, bf16[1,256,256]{2,1,0:T(8,128)(2,1)S(1)}, u32[]{:S(2)}, u32[]{:S(2)}) collective-permute-start(bf16[1,256,256]{2,1,0:T(8,128)(2,1)S(1)} %get-tuple-element.293), channel_id=1, source_target_pairs={{0,4},{1,5},{2,6},{3,7},{4,0},{5,1},{6,2},{7,3},{8,12},{9,13},{10,... | collective-permute-start | bytes 393224 | tf_op jit(solution)/shard_map/ppermute | solution.py:581
  135.0 9.4 %collective-permute-start.30 = (bf16[2,320,256]{2,1,0:T(8,128)(2,1)S(1)}, bf16[2,320,256]{2,1,0:T(8,128)(2,1)S(1)}, u32[]{:S(2)}, u32[]{:S(2)}) collective-permute-start(bf16[2,320,256]{2,1,0:T(8,128)(2,1)S(1)} %get-tuple-element.286), channel_id=1, source_target_pairs={{0,1},{1,0},{2,3},{3,2},{4,5},{5,4},{6,7},{7,6},{8,9},{9,8},{10,11... | collective-permute-start | bytes 983048 | tf_op jit(solution)/shard_map/ppermute | solution.py:581
  146.0 13.4 %collective-permute-start.32 = (bf16[2,192,256]{2,1,0:T(8,128)(2,1)S(1)}, bf16[2,192,256]{2,1,0:T(8,128)(2,1)S(1)}, u32[]{:S(2)}, u32[]{:S(2)}) collective-permute-start(bf16[2,192,256]{2,1,0:T(8,128)(2,1)S(1)} %get-tuple-element.298), channel_id=1, source_target_pairs={{0,1},{1,0},{2,3},{3,2},{4,5},{5,4},{6,7},{7,6},{8,9},{9,8},{10,11... | collective-permute-start | bytes 589832 | tf_op jit(solution)/shard_map/ppermute | solution.py:581
  146.5 12.8 %collective-permute-start.34 = (bf16[1,320,256]{2,1,0:T(8,128)(2,1)S(1)}, bf16[1,320,256]{2,1,0:T(8,128)(2,1)S(1)}, u32[]{:S(2)}, u32[]{:S(2)}) collective-permute-start(bf16[1,320,256]{2,1,0:T(8,128)(2,1)S(1)} %get-tuple-element.301), channel_id=1, source_target_pairs={{0,4},{1,5},{2,6},{3,7},{4,0},{5,1},{6,2},{7,3},{8,12},{9,13},{10,... | collective-permute-start | bytes 491528 | tf_op jit(solution)/shard_map/ppermute | solution.py:581
  148.6 10.7 %collective-permute-start.33 = (bf16[256,256]{1,0:T(8,128)(2,1)S(1)}, bf16[256,256]{1,0:T(8,128)(2,1)S(1)}, u32[]{:S(2)}, u32[]{:S(2)}) collective-permute-start(bf16[256,256]{1,0:T(8,128)(2,1)S(1)} %fusion.3), channel_id=1, source_target_pairs={{0,16},{8,24},{16,0},{24,8},{1,17},{9,25},{17,1},{25,9},{2,18},{10... | collective-permute-start | bytes 393224 | tf_op jit(solution)/shard_map/ppermute | solution.py:581
  159.5 6.4 %collective-permute-start.35 = (bf16[320,256]{1,0:T(8,128)(2,1)S(1)}, bf16[320,256]{1,0:T(8,128)(2,1)S(1)}, u32[]{:S(2)}, u32[]{:S(2)}) collective-permute-start(bf16[320,256]{1,0:T(8,128)(2,1)S(1)} %fusion.2), channel_id=1, source_target_pairs={{0,16},{8,24},{16,0},{24,8},{1,17},{9,25},{17,1},{25,9},{2,18},{10... | collective-permute-start | bytes 491528 | tf_op jit(solution)/shard_map/ppermute | solution.py:581
  160.0 5.9 %collective-permute-start.36 = (bf16[1,192,256]{2,1,0:T(8,128)(2,1)S(1)}, bf16[1,192,256]{2,1,0:T(8,128)(2,1)S(1)}, u32[]{:S(2)}, u32[]{:S(2)}) collective-permute-start(bf16[1,192,256]{2,1,0:T(8,128)(2,1)S(1)} %get-tuple-element.372), channel_id=1, source_target_pairs={{0,4},{1,5},{2,6},{3,7},{4,0},{5,1},{6,2},{7,3},{8,12},{9,13},{10,... | collective-permute-start | bytes 294920 | tf_op jit(solution)/shard_map/ppermute | solution.py:581
  166.1 5.4 %collective-permute-start.39 = (bf16[192,256]{1,0:T(8,128)(2,1)S(1)}, bf16[192,256]{1,0:T(8,128)(2,1)S(1)}, u32[]{:S(2)}, u32[]{:S(2)}) collective-permute-start(bf16[192,256]{1,0:T(8,128)(2,1)S(1)} %fusion.4), channel_id=1, source_target_pairs={{0,16},{8,24},{16,0},{24,8},{1,17},{9,25},{17,1},{25,9},{2,18},{10... | collective-permute-start | bytes 294920 | tf_op jit(solution)/shard_map/ppermute | solution.py:581
  179.7 5.4 %collective-permute-start.43 = (f32[8,512]{1,0:T(8,128)S(1)}, f32[8,512]{1,0:T(8,128)S(1)}, u32[]{:S(2)}, u32[]{:S(2)}) collective-permute-start(f32[8,512]{1,0:T(8,128)S(1)} %add_select_fusion.refs_0_), channel_id=1, source_target_pairs={{0,2},{1,3},{2,0},{3,1},{4,6},{5,7},{6,4},{7,5},{8,10},{9,11},{10,... | collective-permute-start | bytes 49160 | tf_op jit(solution)/shard_map/ppermute | solution.py:581
  184.3 5.5 %collective-permute-start.45 = (f32[8,512]{1,0:T(8,128)S(1)}, f32[8,512]{1,0:T(8,128)S(1)}, u32[]{:S(2)}, u32[]{:S(2)}) collective-permute-start(f32[8,512]{1,0:T(8,128)S(1)} %add_select_fusion.refs_0_), channel_id=1, source_target_pairs={{0,6},{1,7},{2,4},{3,5},{4,2},{5,3},{6,0},{7,1},{8,14},{9,15},{10,... | collective-permute-start | bytes 49160 | tf_op jit(solution)/shard_map/ppermute | solution.py:581
  (71 other events, 555.2 us)

commit v8 on v7

--- a/solution.py
+++ b/solution.py
@@ -897,18 +897,15 @@
     cut = (fl_steps + 1) // 2
     got_ra = steps_d(red_a, x_bits[-1])
     ig_part, ln1_a = b2_call(0, cut, gtri_flat, None, ())
-    ig_part, keep_t, got_t, got_ra, keep_b, *got_b = sync(
-        ig_part, keep_t, got_t, got_ra, keep_b, *([got_b] if late else [])
-    )
+    ig_part, keep_t, got_t, got_ra = sync(ig_part, keep_t, got_t, got_ra)
     if late:
         keep_t, send_t = halves(keep_t, got_t)
-        keep_b = add_low(keep_b, got_b[0])
+        got_t = steps_f(send_t, late[0])
+        keep_b = add_low(keep_b, got_b)
     else:
         keep_t = add_low(keep_t, got_t)
     red_b = before_x(keep_b)
-    red_b, keep_t, ig_part = sync(red_b, keep_t, ig_part)
-    if late:
-        got_t = steps_f(send_t, late[0])
+    red_b, ig_part = sync(red_b, ig_part)
     got_rb = steps_d(red_b, x_bits[-1])
     input_grad, small = b2_call(cut, fl_steps - cut, gtri_flat, ig_part, (ln1_a, ln2, q_sum, q_top))
     small, red_a, got_ra, red_b, got_rb, keep_t, *got_t = sync(

time: 193 us -> 191 us (0.990)
  waiting for transfers between devices: 29.6 us -> 27 us
    ppermute x46, waiting for transfers between devices: 29.6 us -> 27 us  [xor_step(): return lax.ppermute(v, axis, [(i, i ^ bit) for i in range(size)])]
  transfers between devices with their start and end apart: 46 -> 46, of which waited for: 18 -> 19; matrix products, arithmetic and copies ran while one was open for 3% -> 3% of each run, Pallas kernels for 51% -> 51%
where the time goes in v8:
time: 191 us
  Pallas kernels  99.4 us (52%)
  starting transfers between devices  51 us (27%)
  waiting for transfers between devices  27 us (14%)
  local copies, waits for them, and re-layouts  7.28 us (4%)
  other arithmetic  4.26 us (2%)
    pallas_call x10, Pallas kernels, kernel_call(): pl.pallas_call(kernel, grid=grid, in_specs=in_specs, out_specs=[spec for...  99.4 us
    ppermute x46, starting transfers between devices, xor_step(): return lax.ppermute(v, axis, [(i, i ^ bit) for i in range(size)])  51 us
    ppermute x46, waiting for transfers between devices, xor_step(): return lax.ppermute(v, axis, [(i, i ^ bit) for i in range(size)])  27 us
  transfers between devices with their start and end apart: 46, of which 19 were waited for; matrix products, arithmetic and copies ran while one was open for 3% of the time, Pallas kernels for 51%

profile of v8, /device:TPU:0, one launch (start us, length us, event | category | flops | bytes accessed | tf_op | source)
XLA Modules:
  0.0 190.5 jit_solution(16457818910222431653)
XLA Ops:
  1.6 3.1 %collective-permute-start = (bf16[32,1536]{1,0:T(8,128)(2,1)S(1)}, bf16[32,1536]{1,0:T(8,128)(2,1)S(1)}, u32[]{:S(2)}, u32[]{:S(2)}) collective-permute-start(bf16[32,1536]{1,0:T(8,128)(2,1)S(1)} %dynamic-slice_convert_fusion.1), channel_id=1, source_target_pairs={{0,2},{1,3},{2,0},{3,1},{4,6},{5,7},{6,4},{7,5},{8,10},{9,11},{10,... | collective-permute-start | bytes 294920 | tf_op jit(solution)/shard_map/ppermute | solution.py:581
  4.7 2.6 %collective-permute-start.1 = (bf16[32,1536]{1,0:T(8,128)(2,1)S(1)}, bf16[32,1536]{1,0:T(8,128)(2,1)S(1)}, u32[]{:S(2)}, u32[]{:S(2)}) collective-permute-start(bf16[32,1536]{1,0:T(8,128)(2,1)S(1)} %dynamic-slice_convert_fusion.1), channel_id=1, source_target_pairs={{0,4},{1,5},{2,6},{3,7},{4,0},{5,1},{6,2},{7,3},{8,12},{9,13},{10,... | collective-permute-start | bytes 294920 | tf_op jit(solution)/shard_map/ppermute | solution.py:581
  10.3 1.8 collective-permute-start.3
  13.3 1.8 collective-permute-done.1
  15.7 1.7 collective-permute-start.4
  17.5 2.1 %collective-permute-start.10 = (bf16[2,160,512]{2,1,0:T(8,128)(2,1)S(1)}, bf16[2,160,512]{2,1,0:T(8,128)(2,1)S(1)}, u32[]{:S(2)}, u32[]{:S(2)}) collective-permute-start(bf16[2,160,512]{2,1,0:T(8,128)(2,1)S(1)} %pad_maximum_fusion.2.refs_0_), channel_id=1, source_target_pairs={{0,4},{1,5},{2,6},{3,7},{4,0},{5,1},{6,2},{7,3},{8,12},{9,13},{10,... | collective-permute-start | bytes 983048 | tf_op jit(solution)/shard_map/ppermute | solution.py:581
  19.5 1.7 collective-permute-start.11
  21.7 3.4 %collective-permute-done.4.refs_2_ = bf16[4,32,1536]{2,1,0:T(8,128)(2,1)S(1)} collective-permute-done((bf16[4,32,1536]{2,1,0:T(8,128)(2,1)S(1)}, bf16[4,32,1536]{2,1,0:T(8,128)(2,1)S(1)}, u32[]{:S(2)}, u32[]{:S(2)}) %collective-permute-start.4) | collective-permute-done | bytes 393248 | tf_op jit(solution)/shard_map/ppermute | solution.py:581
  26.8 3.3 %collective-permute-done.5 = bf16[128,512]{1,0:T(8,128)(2,1)S(1)} collective-permute-done((bf16[128,512]{1,0:T(8,128)(2,1)S(1)}, bf16[128,512]{1,0:T(8,128)(2,1)S(1)}, u32[]{:S(2)}, u32[]{:S(2)}) %collective-permute-start.5) | collective-permute-done | bytes 131104 | tf_op jit(solution)/shard_map/ppermute | solution.py:581
  32.2 14.8 %f1.1 = (bf16[6,296,1536]{2,1,0:T(8,128)(2,1)}, bf16[6,296,512]{2,1,0:T(8,128)(2,1)}, bf16[6,296,512]{2,1,0:T(8,128)(2,1)}, f32[6,16,256]{2,1,0:T(8,128)}) custom-call(s32[2]{0:T(128)} %pad_add_fusion.1.idx, s32[6]{0:T(128)} %lens.7, bf16[6,296,512]{2,1,0:T(8,128)(2,1)} %tok.1, f32[8,512]{1,0:T(8,128)} %concatenate.28.norm, bf16[4,32,1536]{2,1,0:T(8,128)(2,1)} %copy-done.3, ...), custom_call_target="tpu_custom_call" | custom-call | flops 1 | bytes 1 | tf_op jit(solution)/shard_map/f1/pallas_call | solution.py:617
  47.8 3.1 %collective-permute-start.16 = (bf16[2,128,512]{2,1,0:T(8,128)(2,1)S(1)}, bf16[2,128,512]{2,1,0:T(8,128)(2,1)S(1)}, u32[]{:S(2)}, u32[]{:S(2)}) collective-permute-start(bf16[2,128,512]{2,1,0:T(8,128)(2,1)S(1)} %pad_maximum_fusion.3.refs_8_), channel_id=1, source_target_pairs={{0,2},{1,3},{2,0},{3,1},{4,6},{5,7},{6,4},{7,5},{8,10},{9,11},{10,... | collective-permute-start | bytes 786440 | tf_op jit(solution)/shard_map/ppermute | solution.py:581
  54.8 22.1 %f2a.1 = (f32[1776,512]{1,0:T(8,128)}, f32[1776,512]{1,0:T(8,128)}, f32[1776,512]{1,0:T(8,128)}, bf16[1776,512]{1,0:T(8,128)(2,1)}, bf16[2,4,256,256]{3,2,1,0:T(8,128)(2,1)}, /*index=5*/bf16[2,4,256,256]{3,2,1,0:T(8,128)(2,1)}) custom-call(s32[2]{0:T(128)} %pad_add_fusion.1.idx, s32[6]{0:T(128)} %lens.7, bf16[1776,512]{1,0:T(8,128)(2,1)} %bitcast.60, ...), custom_call_target="tpu_custom_call" | custom-call | flops 1 | bytes 1 | tf_op jit(solution)/shard_map/f2a/pallas_call | solution.py:617
  80.0 26.0 %f2b.1 = (bf16[1776,512]{1,0:T(8,128)(2,1)}, f32[1776,512]{1,0:T(8,128)}, bf16[1776,512]{1,0:T(8,128)(2,1)}, bf16[8,320,256]{2,1,0:T(8,128)(2,1)}, bf16[8,320,256]{2,1,0:T(8,128)(2,1)}, /*index=5*/f32[8,512]{1,0:T(8,128)}) custom-call(s32[2]{0:T(128)} %pad_add_fusion.1.idx, s32[6]{0:T(128)} %lens.7, bf16[1776,512]{1,0:T(8,128)(2,1)} %bitcast.61, ...), custom_call_target="tpu_custom_call" | custom-call | flops 1 | bytes 1 | tf_op jit(solution)/shard_map/f2b/pallas_call | solution.py:617
  108.0 2.0 %collective-permute-done.24 = bf16[4,256,256]{2,1,0:T(8,128)(2,1)S(1)} collective-permute-done((bf16[4,256,256]{2,1,0:T(8,128)(2,1)}, bf16[4,256,256]{2,1,0:T(8,128)(2,1)S(1)}, u32[]{:S(2)}, u32[]{:S(2)}) %collective-permute-start.24) | collective-permute-done | bytes 524320 | tf_op jit(solution)/shard_map/ppermute | solution.py:581
  110.3 1.9 add_convert_fusion.1
  114.2 11.0 %b1.1 = (bf16[6,296,1536]{2,1,0:T(8,128)(2,1)}, bf16[8,192,256]{2,1,0:T(8,128)(2,1)S(1)}, bf16[8,192,256]{2,1,0:T(8,128)(2,1)S(1)}) custom-call(s32[2]{0:T(128)S(1)} %copy-done.31, s32[6]{0:T(128)S(1)} %copy-done.34, bf16[6,296,1536]{2,1,0:T(8,128)(2,1)} %get-tuple-element.240.tri_ref, bf16[6,296,512]{2,1,0:T(8,128)(2,1)S(1)} %bitcast.51, ...), custom_call_target="tpu_custom_call" | custom-call | flops 1 | bytes 1 | tf_op jit(solution)/shard_map/b1/pallas_call | solution.py:617
  125.2 4.0 %collective-permute-done.27 = bf16[4,320,256]{2,1,0:T(8,128)(2,1)S(1)} collective-permute-done((bf16[4,320,256]{2,1,0:T(8,128)(2,1)S(1)}, bf16[4,320,256]{2,1,0:T(8,128)(2,1)S(1)}, u32[]{:S(2)}, u32[]{:S(2)}) %collective-permute-start.27) | collective-permute-done | bytes 655392 | tf_op jit(solution)/shard_map/ppermute | solution.py:581
  129.5 2.0 %collective-permute-done.28 = bf16[8,192,256]{2,1,0:T(8,128)(2,1)S(1)} collective-permute-done((bf16[8,192,256]{2,1,0:T(8,128)(2,1)S(1)}, bf16[8,192,256]{2,1,0:T(8,128)(2,1)S(1)}, u32[]{:S(2)}, u32[]{:S(2)}) %collective-permute-start.28) | collective-permute-done | bytes 786464 | tf_op jit(solution)/shard_map/ppermute | solution.py:581
  133.0 2.2 %collective-permute-start.31 = (bf16[1,256,256]{2,1,0:T(8,128)(2,1)S(1)}, bf16[1,256,256]{2,1,0:T(8,128)(2,1)S(1)}, u32[]{:S(2)}, u32[]{:S(2)}) collective-permute-start(bf16[1,256,256]{2,1,0:T(8,128)(2,1)S(1)} %get-tuple-element.290), channel_id=1, source_target_pairs={{0,4},{1,5},{2,6},{3,7},{4,0},{5,1},{6,2},{7,3},{8,12},{9,13},{10,... | collective-permute-start | bytes 393224 | tf_op jit(solution)/shard_map/ppermute | solution.py:581
  135.1 3.0 %collective-permute-start.30 = (bf16[2,320,256]{2,1,0:T(8,128)(2,1)S(1)}, bf16[2,320,256]{2,1,0:T(8,128)(2,1)S(1)}, u32[]{:S(2)}, u32[]{:S(2)}) collective-permute-start(bf16[2,320,256]{2,1,0:T(8,128)(2,1)S(1)} %get-tuple-element.283), channel_id=1, source_target_pairs={{0,1},{1,0},{2,3},{3,2},{4,5},{5,4},{6,7},{7,6},{8,9},{9,8},{10,11... | collective-permute-start | bytes 983048 | tf_op jit(solution)/shard_map/ppermute | solution.py:581
  138.1 6.9 %qstat.1 = (f32[16,256]{1,0:T(8,128)S(1)}, f32[16,256]{1,0:T(8,128)S(1)}) custom-call(bf16[1776,512]{1,0:T(8,128)(2,1)S(1)} %copy-done.15, bf16[2816,512]{1,0:T(8,128)(2,1)S(1)} %copy-done.10, s32[11,1776]{1,0:T(8,128)S(1)} %bitcast.53, s32[1,1776]{1,0:T(1,128)S(1)} %reshape.96.cnt), custom_call_target="tpu_custom_call" | custom-call | flops 1 | bytes 1 | tf_op jit(solution)/shard_map/qstat/pallas_call | solution.py:617
  146.0 2.2 %collective-permute-start.32 = (bf16[1,320,256]{2,1,0:T(8,128)(2,1)S(1)}, bf16[1,320,256]{2,1,0:T(8,128)(2,1)S(1)}, u32[]{:S(2)}, u32[]{:S(2)}) collective-permute-start(bf16[1,320,256]{2,1,0:T(8,128)(2,1)S(1)} %get-tuple-element.294), channel_id=1, source_target_pairs={{0,4},{1,5},{2,6},{3,7},{4,0},{5,1},{6,2},{7,3},{8,12},{9,13},{10,... | collective-permute-start | bytes 491528 | tf_op jit(solution)/shard_map/ppermute | solution.py:581
  148.1 1.9 %collective-permute-start.33 = (bf16[2,192,256]{2,1,0:T(8,128)(2,1)S(1)}, bf16[2,192,256]{2,1,0:T(8,128)(2,1)S(1)}, u32[]{:S(2)}, u32[]{:S(2)}) collective-permute-start(bf16[2,192,256]{2,1,0:T(8,128)(2,1)S(1)} %get-tuple-element.297), channel_id=1, source_target_pairs={{0,1},{1,0},{2,3},{3,2},{4,5},{5,4},{6,7},{7,6},{8,9},{9,8},{10,11... | collective-permute-start | bytes 589832 | tf_op jit(solution)/shard_map/ppermute | solution.py:581
  151.5 6.9 %b2.2 = (bf16[1776,512]{1,0:T(8,128)(2,1)}, f32[8,512]{1,0:T(8,128)S(1)}) custom-call(s32[2]{0:T(128)S(1)} %copy-done.31, bf16[1776,1536]{1,0:T(8,128)(2,1)S(1)} %bitcast.49, bf16[1776,512]{1,0:T(8,128)(2,1)S(1)} %bitcast.47, f32[1776,512]{1,0:T(8,128)S(1)} %copy-done.2, f32[8,512]{1,0:T(8,128)S(1)} %copy-done.21, bf16[4,32,1536]{2,1,0:T(8,128)(2,1)S(1)} %copy-done.4, ...), custom_call_target="tpu_custom_call" | custom-call | flops 1 | bytes 1 | tf_op jit(solution)/shard_map/b2/pallas_call | solution.py:617
  160.0 5.4 %b2.3 = (bf16[1776,512]{1,0:T(8,128)(2,1)}, f32[8,512]{1,0:T(8,128)S(1)}) custom-call(s32[2]{0:T(128)S(1)} %copy-done.31, bf16[1776,1536]{1,0:T(8,128)(2,1)S(1)} %bitcast.50, bf16[1776,512]{1,0:T(8,128)(2,1)S(1)} %bitcast.48, f32[1776,512]{1,0:T(8,128)S(1)} %copy-done.2, f32[8,512]{1,0:T(8,128)S(1)} %copy-done.21, ...), custom_call_target="tpu_custom_call", output_to_operand_aliasing={{0}: (10, {})} | custom-call | flops 1 | bytes 1 | tf_op jit(solution)/shard_map/b2/pallas_call | solution.py:617
  167.8 3.1 %lamb_mlp.1 = (f32[64,512]{1,0:T(8,128)}, f32[64,512]{1,0:T(8,128)}, f32[64,512]{1,0:T(8,128)S(1)}, f32[64,2048]{1,0:T(8,128)}, f32[64,2048]{1,0:T(8,128)}, /*in...) custom-call(s32[2]{0:T(128)S(1)} %copy-done.31, ...), custom_call_target="tpu_custom_call" | custom-call | flops 1 | bytes 1 | tf_op jit(solution)/shard_map/lamb_mlp/pallas_call | solution.py:617
  172.5 1.8 lamb_triple.1
  175.0 1.8 collective-permute-start.42
  176.8 1.9 %collective-permute-done.42 = f32[8,512]{1,0:T(8,128)S(1)} collective-permute-done((f32[8,512]{1,0:T(8,128)S(1)}, f32[8,512]{1,0:T(8,128)S(1)}, u32[]{:S(2)}, u32[]{:S(2)}) %collective-permute-start.42) | collective-permute-done | bytes 16416 | tf_op jit(solution)/shard_map/ppermute | solution.py:581
  178.9 4.1 %collective-permute-start.43 = (f32[8,512]{1,0:T(8,128)S(1)}, f32[8,512]{1,0:T(8,128)S(1)}, u32[]{:S(2)}, u32[]{:S(2)}) collective-permute-start(f32[8,512]{1,0:T(8,128)S(1)} %add_select_fusion.refs_0_), channel_id=1, source_target_pairs={{0,2},{1,3},{2,0},{3,1},{4,6},{5,7},{6,4},{7,5},{8,10},{9,11},{10,... | collective-permute-start | bytes 49160 | tf_op jit(solution)/shard_map/ppermute | solution.py:581
  183.6 1.7 collective-permute-start.45
  185.3 2.3 %collective-permute-done.44.refs_2_ = f32[8,512]{1,0:T(8,128)S(1)} collective-permute-done((f32[8,512]{1,0:T(8,128)S(1)}, f32[8,512]{1,0:T(8,128)S(1)}, u32[]{:S(2)}, u32[]{:S(2)}) %collective-permute-start.44) | collective-permute-done | bytes 16416 | tf_op jit(solution)/shard_map/ppermute | solution.py:581
  (223 shorter events, 35.5 us)
Async XLA Ops:
  1.6 11.7 %collective-permute-start = (bf16[32,1536]{1,0:T(8,128)(2,1)S(1)}, bf16[32,1536]{1,0:T(8,128)(2,1)S(1)}, u32[]{:S(2)}, u32[]{:S(2)}) collective-permute-start(bf16[32,1536]{1,0:T(8,128)(2,1)S(1)} %dynamic-slice_convert_fusion.1), channel_id=1, source_target_pairs={{0,2},{1,3},{2,0},{3,1},{4,6},{5,7},{6,4},{7,5},{8,10},{9,11},{10,... | collective-permute-start | bytes 294920 | tf_op jit(solution)/shard_map/ppermute | solution.py:581
  4.7 10.4 %collective-permute-start.1 = (bf16[32,1536]{1,0:T(8,128)(2,1)S(1)}, bf16[32,1536]{1,0:T(8,128)(2,1)S(1)}, u32[]{:S(2)}, u32[]{:S(2)}) collective-permute-start(bf16[32,1536]{1,0:T(8,128)(2,1)S(1)} %dynamic-slice_convert_fusion.1), channel_id=1, source_target_pairs={{0,4},{1,5},{2,6},{3,7},{4,0},{5,1},{6,2},{7,3},{8,12},{9,13},{10,... | collective-permute-start | bytes 294920 | tf_op jit(solution)/shard_map/ppermute | solution.py:581
  7.3 7.8 %collective-permute-start.2 = (bf16[32,1536]{1,0:T(8,128)(2,1)S(1)}, bf16[32,1536]{1,0:T(8,128)(2,1)S(1)}, u32[]{:S(2)}, u32[]{:S(2)}) collective-permute-start(bf16[32,1536]{1,0:T(8,128)(2,1)S(1)} %dynamic-slice_convert_fusion.1), channel_id=1, source_target_pairs={{0,6},{1,7},{2,4},{3,5},{4,2},{5,3},{6,0},{7,1},{8,14},{9,15},{10,... | collective-permute-start | bytes 294920 | tf_op jit(solution)/shard_map/ppermute | solution.py:581
  10.3 5.4 %collective-permute-start.3 = (bf16[160,512]{1,0:T(8,128)(2,1)S(1)}, bf16[160,512]{1,0:T(8,128)(2,1)S(1)}, u32[]{:S(2)}, u32[]{:S(2)}) collective-permute-start(bf16[160,512]{1,0:T(8,128)(2,1)S(1)} %pad_maximum_fusion.4), channel_id=1, source_target_pairs={{0,1},{1,0},{2,3},{3,2},{4,5},{5,4},{6,7},{7,6},{8,9},{9,8},{10,11... | collective-permute-start | bytes 491528 | tf_op jit(solution)/shard_map/ppermute | solution.py:581
  15.7 9.4 %collective-permute-start.4 = (bf16[4,32,1536]{2,1,0:T(8,128)(2,1)S(1)}, bf16[4,32,1536]{2,1,0:T(8,128)(2,1)S(1)}, u32[]{:S(2)}, u32[]{:S(2)}) collective-permute-start(bf16[4,32,1536]{2,1,0:T(8,128)(2,1)S(1)} %pad_maximum_fusion.1.refs_0_), channel_id=1, source_target_pairs={{0,1},{1,0},{2,3},{3,2},{4,5},{5,4},{6,7},{7,6},{8,9},{9,8},{10,11... | collective-permute-start | bytes 1179656 | tf_op jit(solution)/shard_map/ppermute | solution.py:581
  17.4 9.3 %collective-permute-start.6 = (bf16[4,32,1536]{2,1,0:T(8,128)(2,1)S(1)}, bf16[4,32,1536]{2,1,0:T(8,128)(2,1)S(1)}, u32[]{:S(2)}, u32[]{:S(2)}) collective-permute-start(bf16[4,32,1536]{2,1,0:T(8,128)(2,1)S(1)} %pad_maximum_fusion.1.refs_0_), channel_id=1, source_target_pairs={{0,8},{8,0},{16,24},{24,16},{1,9},{9,1},{17,25},{25,17},{2,10},{10... | collective-permute-start | bytes 1179656 | tf_op jit(solution)/shard_map/ppermute | solution.py:581
  17.5 29.6 %collective-permute-start.10 = (bf16[2,160,512]{2,1,0:T(8,128)(2,1)S(1)}, bf16[2,160,512]{2,1,0:T(8,128)(2,1)S(1)}, u32[]{:S(2)}, u32[]{:S(2)}) collective-permute-start(bf16[2,160,512]{2,1,0:T(8,128)(2,1)S(1)} %pad_maximum_fusion.2.refs_0_), channel_id=1, source_target_pairs={{0,4},{1,5},{2,6},{3,7},{4,0},{5,1},{6,2},{7,3},{8,12},{9,13},{10,... | collective-permute-start | bytes 983048 | tf_op jit(solution)/shard_map/ppermute | solution.py:581
  19.5 27.5 %collective-permute-start.11 = (bf16[2,160,512]{2,1,0:T(8,128)(2,1)S(1)}, bf16[2,160,512]{2,1,0:T(8,128)(2,1)S(1)}, u32[]{:S(2)}, u32[]{:S(2)}) collective-permute-start(bf16[2,160,512]{2,1,0:T(8,128)(2,1)S(1)} %pad_maximum_fusion.2.refs_0_), channel_id=1, source_target_pairs={{0,6},{1,7},{2,4},{3,5},{4,2},{5,3},{6,0},{7,1},{8,14},{9,15},{10,... | collective-permute-start | bytes 983048 | tf_op jit(solution)/shard_map/ppermute | solution.py:581
  21.2 25.9 %collective-permute-start.9 = (bf16[2,160,512]{2,1,0:T(8,128)(2,1)S(1)}, bf16[2,160,512]{2,1,0:T(8,128)(2,1)S(1)}, u32[]{:S(2)}, u32[]{:S(2)}) collective-permute-start(bf16[2,160,512]{2,1,0:T(8,128)(2,1)S(1)} %pad_maximum_fusion.2.refs_0_), channel_id=1, source_target_pairs={{0,2},{1,3},{2,0},{3,1},{4,6},{5,7},{6,4},{7,5},{8,10},{9,11},{10,... | collective-permute-start | bytes 983048 | tf_op jit(solution)/shard_map/ppermute | solution.py:581
  25.1 5.0 %collective-permute-start.5 = (bf16[128,512]{1,0:T(8,128)(2,1)S(1)}, bf16[128,512]{1,0:T(8,128)(2,1)S(1)}, u32[]{:S(2)}, u32[]{:S(2)}) collective-permute-start(bf16[128,512]{1,0:T(8,128)(2,1)S(1)} %pad_maximum_fusion.5), channel_id=1, source_target_pairs={{0,1},{1,0},{2,3},{3,2},{4,5},{5,4},{6,7},{7,6},{8,9},{9,8},{10,11... | collective-permute-start | bytes 393224 | tf_op jit(solution)/shard_map/ppermute | solution.py:581
  30.1 20.7 %collective-permute-start.12 = (bf16[2,160,512]{2,1,0:T(8,128)(2,1)S(1)}, bf16[2,160,512]{2,1,0:T(8,128)(2,1)S(1)}, u32[]{:S(2)}, u32[]{:S(2)}) collective-permute-start(bf16[2,160,512]{2,1,0:T(8,128)(2,1)S(1)} %pad_maximum_fusion.2.refs_0_), channel_id=1, source_target_pairs={{0,8},{8,0},{16,24},{24,16},{1,9},{9,1},{17,25},{25,17},{2,10},{10... | collective-permute-start | bytes 983048 | tf_op jit(solution)/shard_map/ppermute | solution.py:581
  47.1 5.3 %collective-permute-start.13 = (bf16[2,160,512]{2,1,0:T(8,128)(2,1)S(1)}, bf16[2,160,512]{2,1,0:T(8,128)(2,1)S(1)}, u32[]{:S(2)}, u32[]{:S(2)}) collective-permute-start(bf16[2,160,512]{2,1,0:T(8,128)(2,1)S(1)} %collective-permute-done.9.refs_1_), channel_id=1, source_target_pairs={{0,8},{8,0},{16,24},{24,16},{1,9},{9,1},{17,25},{25,17},{2,10},{10... | collective-permute-start | bytes 983048 | tf_op jit(solution)/shard_map/ppermute | solution.py:581
  47.3 6.6 %collective-permute-start.14 = (bf16[2,160,512]{2,1,0:T(8,128)(2,1)S(1)}, bf16[2,160,512]{2,1,0:T(8,128)(2,1)S(1)}, u32[]{:S(2)}, u32[]{:S(2)}) collective-permute-start(bf16[2,160,512]{2,1,0:T(8,128)(2,1)S(1)} %collective-permute-done.10.refs_2_), channel_id=1, source_target_pairs={{0,8},{8,0},{16,24},{24,16},{1,9},{9,1},{17,25},{25,17},{2,10},{10... | collective-permute-start | bytes 983048 | tf_op jit(solution)/shard_map/ppermute | solution.py:581
  47.7 6.2 %collective-permute-start.15 = (bf16[2,160,512]{2,1,0:T(8,128)(2,1)S(1)}, bf16[2,160,512]{2,1,0:T(8,128)(2,1)S(1)}, u32[]{:S(2)}, u32[]{:S(2)}) collective-permute-start(bf16[2,160,512]{2,1,0:T(8,128)(2,1)S(1)} %collective-permute-done.11.refs_3_), channel_id=1, source_target_pairs={{0,8},{8,0},{16,24},{24,16},{1,9},{9,1},{17,25},{25,17},{2,10},{10... | collective-permute-start | bytes 983048 | tf_op jit(solution)/shard_map/ppermute | solution.py:581
  47.8 29.0 %collective-permute-start.16 = (bf16[2,128,512]{2,1,0:T(8,128)(2,1)S(1)}, bf16[2,128,512]{2,1,0:T(8,128)(2,1)S(1)}, u32[]{:S(2)}, u32[]{:S(2)}) collective-permute-start(bf16[2,128,512]{2,1,0:T(8,128)(2,1)S(1)} %pad_maximum_fusion.3.refs_8_), channel_id=1, source_target_pairs={{0,2},{1,3},{2,0},{3,1},{4,6},{5,7},{6,4},{7,5},{8,10},{9,11},{10,... | collective-permute-start | bytes 786440 | tf_op jit(solution)/shard_map/ppermute | solution.py:581
  50.9 26.0 %collective-permute-start.17 = (bf16[2,128,512]{2,1,0:T(8,128)(2,1)S(1)}, bf16[2,128,512]{2,1,0:T(8,128)(2,1)S(1)}, u32[]{:S(2)}, u32[]{:S(2)}) collective-permute-start(bf16[2,128,512]{2,1,0:T(8,128)(2,1)S(1)} %pad_maximum_fusion.3.refs_8_), channel_id=1, source_target_pairs={{0,4},{1,5},{2,6},{3,7},{4,0},{5,1},{6,2},{7,3},{8,12},{9,13},{10,... | collective-permute-start | bytes 786440 | tf_op jit(solution)/shard_map/ppermute | solution.py:581
  52.4 24.5 %collective-permute-start.18 = (bf16[2,128,512]{2,1,0:T(8,128)(2,1)S(1)}, bf16[2,128,512]{2,1,0:T(8,128)(2,1)S(1)}, u32[]{:S(2)}, u32[]{:S(2)}) collective-permute-start(bf16[2,128,512]{2,1,0:T(8,128)(2,1)S(1)} %pad_maximum_fusion.3.refs_8_), channel_id=1, source_target_pairs={{0,6},{1,7},{2,4},{3,5},{4,2},{5,3},{6,0},{7,1},{8,14},{9,15},{10,... | collective-permute-start | bytes 786440 | tf_op jit(solution)/shard_map/ppermute | solution.py:581
  53.9 24.0 %collective-permute-start.19 = (bf16[2,128,512]{2,1,0:T(8,128)(2,1)S(1)}, bf16[2,128,512]{2,1,0:T(8,128)(2,1)S(1)}, u32[]{:S(2)}, u32[]{:S(2)}) collective-permute-start(bf16[2,128,512]{2,1,0:T(8,128)(2,1)S(1)} %pad_maximum_fusion.3.refs_8_), channel_id=1, source_target_pairs={{0,8},{8,0},{16,24},{24,16},{1,9},{9,1},{17,25},{25,17},{2,10},{10... | collective-permute-start | bytes 786440 | tf_op jit(solution)/shard_map/ppermute | solution.py:581
  79.3 26.7 %collective-permute-start.23 = (bf16[2,4,256,256]{3,2,1,0:T(8,128)(2,1)}, bf16[2,4,256,256]{3,2,1,0:T(8,128)(2,1)S(1)}, u32[]{:S(2)}, u32[]{:S(2)}) collective-permute-start(bf16[2,4,256,256]{3,2,1,0:T(8,128)(2,1)} %get-tuple-element.243), channel_id=1, source_target_pairs={{0,2},{1,3},{2,0},{3,1},{4,6},{5,7},{6,4},{7,5},{8,10},{9,11},{10,... | collective-permute-start | bytes 3145736 | tf_op jit(solution)/shard_map/ppermute | solution.py:581
  112.2 17.1 %collective-permute-start.27 = (bf16[4,320,256]{2,1,0:T(8,128)(2,1)S(1)}, bf16[4,320,256]{2,1,0:T(8,128)(2,1)S(1)}, u32[]{:S(2)}, u32[]{:S(2)}) collective-permute-start(bf16[4,320,256]{2,1,0:T(8,128)(2,1)S(1)} %get-tuple-element.260), channel_id=1, source_target_pairs={{0,2},{1,3},{2,0},{3,1},{4,6},{5,7},{6,4},{7,5},{8,10},{9,11},{10,... | collective-permute-start | bytes 1966088 | tf_op jit(solution)/shard_map/ppermute | solution.py:581
  113.6 11.6 %collective-permute-start.26 = (bf16[2,256,256]{2,1,0:T(8,128)(2,1)S(1)}, bf16[2,256,256]{2,1,0:T(8,128)(2,1)S(1)}, u32[]{:S(2)}, u32[]{:S(2)}) collective-permute-start(bf16[2,256,256]{2,1,0:T(8,128)(2,1)S(1)} %get-tuple-element.258), channel_id=1, source_target_pairs={{0,1},{1,0},{2,3},{3,2},{4,5},{5,4},{6,7},{7,6},{8,9},{9,8},{10,11... | collective-permute-start | bytes 786440 | tf_op jit(solution)/shard_map/ppermute | solution.py:581
  131.7 14.0 %collective-permute-start.29 = (bf16[4,192,256]{2,1,0:T(8,128)(2,1)S(1)}, bf16[4,192,256]{2,1,0:T(8,128)(2,1)S(1)}, u32[]{:S(2)}, u32[]{:S(2)}) collective-permute-start(bf16[4,192,256]{2,1,0:T(8,128)(2,1)S(1)} %get-tuple-element.281), channel_id=1, source_target_pairs={{0,2},{1,3},{2,0},{3,1},{4,6},{5,7},{6,4},{7,5},{8,10},{9,11},{10,... | collective-permute-start | bytes 1179656 | tf_op jit(solution)/shard_map/ppermute | solution.py:581
  133.0 12.1 %collective-permute-start.31 = (bf16[1,256,256]{2,1,0:T(8,128)(2,1)S(1)}, bf16[1,256,256]{2,1,0:T(8,128)(2,1)S(1)}, u32[]{:S(2)}, u32[]{:S(2)}) collective-permute-start(bf16[1,256,256]{2,1,0:T(8,128)(2,1)S(1)} %get-tuple-element.290), channel_id=1, source_target_pairs={{0,4},{1,5},{2,6},{3,7},{4,0},{5,1},{6,2},{7,3},{8,12},{9,13},{10,... | collective-permute-start | bytes 393224 | tf_op jit(solution)/shard_map/ppermute | solution.py:581
  135.1 10.6 %collective-permute-start.30 = (bf16[2,320,256]{2,1,0:T(8,128)(2,1)S(1)}, bf16[2,320,256]{2,1,0:T(8,128)(2,1)S(1)}, u32[]{:S(2)}, u32[]{:S(2)}) collective-permute-start(bf16[2,320,256]{2,1,0:T(8,128)(2,1)S(1)} %get-tuple-element.283), channel_id=1, source_target_pairs={{0,1},{1,0},{2,3},{3,2},{4,5},{5,4},{6,7},{7,6},{8,9},{9,8},{10,11... | collective-permute-start | bytes 983048 | tf_op jit(solution)/shard_map/ppermute | solution.py:581
  146.0 12.5 %collective-permute-start.32 = (bf16[1,320,256]{2,1,0:T(8,128)(2,1)S(1)}, bf16[1,320,256]{2,1,0:T(8,128)(2,1)S(1)}, u32[]{:S(2)}, u32[]{:S(2)}) collective-permute-start(bf16[1,320,256]{2,1,0:T(8,128)(2,1)S(1)} %get-tuple-element.294), channel_id=1, source_target_pairs={{0,4},{1,5},{2,6},{3,7},{4,0},{5,1},{6,2},{7,3},{8,12},{9,13},{10,... | collective-permute-start | bytes 491528 | tf_op jit(solution)/shard_map/ppermute | solution.py:581
  148.1 10.4 %collective-permute-start.33 = (bf16[2,192,256]{2,1,0:T(8,128)(2,1)S(1)}, bf16[2,192,256]{2,1,0:T(8,128)(2,1)S(1)}, u32[]{:S(2)}, u32[]{:S(2)}) collective-permute-start(bf16[2,192,256]{2,1,0:T(8,128)(2,1)S(1)} %get-tuple-element.297), channel_id=1, source_target_pairs={{0,1},{1,0},{2,3},{3,2},{4,5},{5,4},{6,7},{7,6},{8,9},{9,8},{10,11... | collective-permute-start | bytes 589832 | tf_op jit(solution)/shard_map/ppermute | solution.py:581
  150.1 8.4 %collective-permute-start.34 = (bf16[256,256]{1,0:T(8,128)(2,1)S(1)}, bf16[256,256]{1,0:T(8,128)(2,1)S(1)}, u32[]{:S(2)}, u32[]{:S(2)}) collective-permute-start(bf16[256,256]{1,0:T(8,128)(2,1)S(1)} %fusion.3), channel_id=1, source_target_pairs={{0,16},{8,24},{16,0},{24,8},{1,17},{9,25},{17,1},{25,9},{2,18},{10... | collective-permute-start | bytes 393224 | tf_op jit(solution)/shard_map/ppermute | solution.py:581
  158.5 7.0 %collective-permute-start.35 = (bf16[320,256]{1,0:T(8,128)(2,1)S(1)}, bf16[320,256]{1,0:T(8,128)(2,1)S(1)}, u32[]{:S(2)}, u32[]{:S(2)}) collective-permute-start(bf16[320,256]{1,0:T(8,128)(2,1)S(1)} %fusion.2), channel_id=1, source_target_pairs={{0,16},{8,24},{16,0},{24,8},{1,17},{9,25},{17,1},{25,9},{2,18},{10... | collective-permute-start | bytes 491528 | tf_op jit(solution)/shard_map/ppermute | solution.py:581
  159.3 6.2 %collective-permute-start.36 = (bf16[1,192,256]{2,1,0:T(8,128)(2,1)S(1)}, bf16[1,192,256]{2,1,0:T(8,128)(2,1)S(1)}, u32[]{:S(2)}, u32[]{:S(2)}) collective-permute-start(bf16[1,192,256]{2,1,0:T(8,128)(2,1)S(1)} %get-tuple-element.366), channel_id=1, source_target_pairs={{0,4},{1,5},{2,6},{3,7},{4,0},{5,1},{6,2},{7,3},{8,12},{9,13},{10,... | collective-permute-start | bytes 294920 | tf_op jit(solution)/shard_map/ppermute | solution.py:581
  165.7 5.3 %collective-permute-start.39 = (bf16[192,256]{1,0:T(8,128)(2,1)S(1)}, bf16[192,256]{1,0:T(8,128)(2,1)S(1)}, u32[]{:S(2)}, u32[]{:S(2)}) collective-permute-start(bf16[192,256]{1,0:T(8,128)(2,1)S(1)} %fusion.4), channel_id=1, source_target_pairs={{0,16},{8,24},{16,0},{24,8},{1,17},{9,25},{17,1},{25,9},{2,18},{10... | collective-permute-start | bytes 294920 | tf_op jit(solution)/shard_map/ppermute | solution.py:581
  178.9 6.5 %collective-permute-start.43 = (f32[8,512]{1,0:T(8,128)S(1)}, f32[8,512]{1,0:T(8,128)S(1)}, u32[]{:S(2)}, u32[]{:S(2)}) collective-permute-start(f32[8,512]{1,0:T(8,128)S(1)} %add_select_fusion.refs_0_), channel_id=1, source_target_pairs={{0,2},{1,3},{2,0},{3,1},{4,6},{5,7},{6,4},{7,5},{8,10},{9,11},{10,... | collective-permute-start | bytes 49160 | tf_op jit(solution)/shard_map/ppermute | solution.py:581
  183.6 5.5 %collective-permute-start.45 = (f32[8,512]{1,0:T(8,128)S(1)}, f32[8,512]{1,0:T(8,128)S(1)}, u32[]{:S(2)}, u32[]{:S(2)}) collective-permute-start(f32[8,512]{1,0:T(8,128)S(1)} %add_select_fusion.refs_0_), channel_id=1, source_target_pairs={{0,6},{1,7},{2,4},{3,5},{4,2},{5,3},{6,0},{7,1},{8,14},{9,15},{10,... | collective-permute-start | bytes 49160 | tf_op jit(solution)/shard_map/ppermute | solution.py:581
  (71 other events, 543.0 us)
